TPU v7x, 32 devices: a whole 2x2x4 slice. The times are simulated.
32 devices in a mesh: group: 8 (over z, core), dev: 4 (over y, x).
Axes of the slice: x: 2, y: 2, z: 4, core: 2. Of those that a mesh axis runs over, the one named last changes fastest.
Arguments:
- density: float32 [512, 3, 152], P(('group', 'dev')), may hold values from -6 to 6
- kernel_hat: bfloat16 [316, 2, 2304], replicated, may hold values from -6 to 6
- send_list: int32 [32, 4, 4], P(('group', 'dev')), may hold values from 0 to 15
- halo_list: int32 [32, 2, 4], P(('group', 'dev')), may hold values from 0 to 15
- inter_src: int32 [512, 32], P(('group', 'dev')), may hold values from 0 to 39, as said below
- inter_off: int32 [512, 32], P(('group', 'dev')), may hold values from 0 to 315
Outputs:
- potential: float32 [512, 3, 152], P(('group', 'dev'))
Inputs may be any that keep to these rules, and one draw needn't show every extreme that they name: `inter_src`: never names an entry of an adjacent subtree that does not exist (the previous one of the first subtree, the next one of the last).
All inputs are finite; a program needn't handle non-finite values.
Results may differ from a plain program's by a relative error of at most 0.0029.
Values may be sent and summed in bfloat16 or wider, within the bound.
No kernel may reach another device: no remote copies, remote signals or barrier semaphores. Data moves between devices by JAX's collectives and lax.ppermute only.
A program may use at most 128 MiB of HBM per device.

v0:
```python
import functools
import math

import jax
import jax.numpy as jnp
import ml_dtypes
import numpy as np
from jax import lax
from jax.experimental import pallas as pl
from jax.experimental.pallas import tpu as pltpu
from jax.sharding import PartitionSpec as P

ORDER = 6
GRID = 16
LANES = 128
HALF = GRID // 2 + 1
FREQ = GRID * GRID * HALF
TILES = FREQ // LANES
MAIN = 16
TAIL = TILES - MAIN
PITCH = MAIN + 1
TAIL_PITCH = 7
POINTS_PAD = 160
CHUNK = 256


def surface_points(edge_count):
    points = [
        (i, j, k)
        for i in range(edge_count)
        for j in range(edge_count)
        for k in range(edge_count)
        if min(i, j, k) == 0 or max(i, j, k) == edge_count - 1
    ]
    return np.array(points, dtype=np.int64)


@functools.lru_cache(maxsize=None)
def transform_tables():
    points = surface_points(ORDER)
    kx, ky, kz = (a.reshape(-1) for a in np.meshgrid(np.arange(GRID), np.arange(GRID), np.arange(HALF), indexing="ij"))
    phase = (points[:, :1] * kx + points[:, 1:2] * ky + points[:, 2:] * kz) % GRID
    angle = phase * (2.0 * math.pi / GRID)
    table = np.zeros((POINTS_PAD, 2 * FREQ), np.float64)
    table[: len(points), :FREQ] = np.cos(angle)
    table[: len(points), FREQ:] = -np.sin(angle)
    table = np.where(np.abs(table) < 1e-9, 0.0, table)
    high = table.astype(ml_dtypes.bfloat16)
    low = (table - high.astype(np.float64)).astype(ml_dtypes.bfloat16)
    edge_plane = (kz == 0) | (kz == GRID // 2)
    factor = np.where(edge_plane, 1.0, 2.0) / GRID**3 * np.where((kx + ky + kz) % 2 == 0, 1.0, -1.0)
    factor = np.concatenate([factor, factor]).astype(np.float32)[None, :]
    return np.concatenate([high, low], axis=0), factor


def pack_kernel(density, send_list, halo_list, to_peers, to_prev, to_next):
    comp_count = density.shape[0]
    peers, cap = send_list.shape
    rim = halo_list.shape[1]
    for c in range(comp_count):
        for e in range(cap):
            for q in range(peers):
                to_peers[q, c, pl.ds(e, 1), :] = density[c, pl.ds(send_list[q, e], 1), :]
        for e in range(rim):
            to_prev[c, pl.ds(e, 1), :] = density[c, pl.ds(halo_list[0, e], 1), :]
            to_next[c, pl.ds(e, 1), :] = density[c, pl.ds(halo_list[1, e], 1), :]


def translate_kernel(
    source, offset, density, peers_in, before, after, table, factor, kernel_hat, out,
    rows, hat, main, tail, total, total_tail,
):
    comp_count, box_count, surf = density.shape
    list_count = source.shape[1]
    peers, _, cap, _ = peers_in.shape
    rim = before.shape[1]
    slots = rows.shape[0] // comp_count
    row_count = rows.shape[0]
    f32, bf16 = jnp.float32, jnp.bfloat16

    rows[...] = jnp.zeros_like(rows)
    for c in range(comp_count):
        base = c * slots
        rows[base : base + box_count, :surf] = density[c]
        base += box_count
        for q in range(peers):
            rows[base + q * cap : base + (q + 1) * cap, :surf] = peers_in[q, c]
        base += peers * cap
        rows[base : base + rim, :surf] = before[c]
        rows[base + rim : base + 2 * rim, :surf] = after[c]

    step = 144
    @pl.loop(0, hat.shape[0] // step)
    def _(i):
        at = pl.ds(pl.multiple_of(i * step, 16), step)
        hat[at, :] = kernel_hat[at, :].astype(f32)

    value = rows[...]
    high = value.astype(bf16)
    low = (value - high.astype(f32)).astype(bf16)
    for part in range(2):
        for n in range(FREQ // CHUNK):
            columns = slice(part * FREQ + n * CHUNK, part * FREQ + (n + 1) * CHUNK)
            t_high = table[:POINTS_PAD, columns]
            t_low = table[POINTS_PAD:, columns]
            x = jnp.dot(high, t_high, preferred_element_type=f32)
            x = x + jnp.dot(low, t_high, preferred_element_type=f32)
            x = x + jnp.dot(high, t_low, preferred_element_type=f32)
            x = x.astype(bf16).astype(f32)
            for m in range(CHUNK // LANES):
                j = n * (CHUNK // LANES) + m
                for g in range(row_count // 8):
                    piece = x[g * 8 : (g + 1) * 8, m * LANES : (m + 1) * LANES]
                    if j < MAIN:
                        main[pl.ds((part * row_count + g * 8) * PITCH + j, 8, stride=PITCH), :] = piece
                    else:
                        c, s = divmod(g * 8, slots)
                        tail[j - MAIN, pl.ds(s * TAIL_PITCH + part * comp_count + c, 8, stride=TAIL_PITCH), :] = piece

    plus = lax.broadcasted_iota(jnp.int32, (8, LANES), 0) < comp_count
    halves = MAIN // 8

    @pl.loop(0, box_count)
    def _(t):
        def pair(w, accs):
            s = source[t, w]
            o = offset[t, w] * (2 * TILES)
            k = [
                [hat[pl.ds(o + 16 * h + r, 8, stride=2), :] for h in range(halves)] for r in range(2)
            ]
            accs = list(accs)
            at = 0
            for c in range(comp_count):
                for h in range(halves):
                    s_re = main[pl.ds((c * slots + s) * PITCH + 8 * h, 8), :]
                    s_im = main[pl.ds((row_count + c * slots + s) * PITCH + 8 * h, 8), :]
                    accs[at] = accs[at] + (k[0][h] * s_re - k[1][h] * s_im)
                    accs[at + 1] = accs[at + 1] + (k[0][h] * s_im + k[1][h] * s_re)
                    at += 2
            for j in range(TAIL):
                x = tail[j, pl.ds(s * TAIL_PITCH, 8), :]
                k_re = hat[pl.ds(o + 2 * (MAIN + j), 8, stride=0), :]
                k_im = hat[pl.ds(o + 2 * (MAIN + j) + 1, 8, stride=0), :]
                accs[at] = accs[at] + k_re * x
                accs[at + 1] = accs[at + 1] + k_im * x
                at += 2
            return tuple(accs)

        count = 2 * (comp_count * halves + TAIL)
        zero = jnp.zeros((8, LANES), f32)
        accs = lax.fori_loop(0, list_count, pair, (zero,) * count, unroll=4)
        at = 0
        for c in range(comp_count):
            for h in range(halves):
                for part in range(2):
                    row = (part * comp_count + c) * box_count + t
                    total[pl.ds(row * PITCH + 8 * h, 8), :] = accs[at + part]
                at += 2
        for j in range(TAIL):
            own, cross = accs[at], accs[at + 1]
            up = jnp.concatenate([cross[comp_count:], cross[:comp_count]], axis=0)
            down = jnp.concatenate([cross[-comp_count:], cross[:-comp_count]], axis=0)
            total_tail[j, pl.ds(t * TAIL_PITCH, 8), :] = jnp.where(plus, own - up, own + down)
            at += 2

    result = jnp.zeros((comp_count * box_count, 2 * POINTS_PAD), f32)
    rest = jnp.zeros((comp_count * box_count, POINTS_PAD), f32)
    groups = box_count // 8
    nt = (((1,), (1,)), ((), ()))
    for part in range(2):
        for n in range(FREQ // CHUNK):
            columns = slice(part * FREQ + n * CHUNK, part * FREQ + (n + 1) * CHUNK)
            lanes = []
            for m in range(CHUNK // LANES):
                j = n * (CHUNK // LANES) + m
                pieces = []
                for c in range(comp_count):
                    for g in range(groups):
                        if j < MAIN:
                            row = (part * comp_count + c) * box_count + g * 8
                            pieces.append(total[pl.ds(row * PITCH + j, 8, stride=PITCH), :])
                        else:
                            row = g * 8 * TAIL_PITCH + part * comp_count + c
                            pieces.append(total_tail[j - MAIN, pl.ds(row, 8, stride=TAIL_PITCH), :])
                lanes.append(jnp.concatenate(pieces, axis=0))
            x = jnp.concatenate(lanes, axis=1) * factor[:, columns]
            high = x.astype(bf16)
            low = (x - high.astype(f32)).astype(bf16)
            result += lax.dot_general(high, table[:, columns], nt, preferred_element_type=f32)
            rest += lax.dot_general(low, table[:POINTS_PAD, columns], nt, preferred_element_type=f32)
    result = result[:, :POINTS_PAD] + result[:, POINTS_PAD:] + rest
    for c in range(comp_count):
        out[c] = result[c * box_count : (c + 1) * box_count, :surf]


def on_device(density, kernel_hat, send_list, halo_list, inter_src, inter_off):
    table, factor = transform_tables()
    box_count, comp_count, surf = density.shape
    _, peers, cap = send_list.shape
    rim = halo_list.shape[2]
    f32 = jnp.float32
    vmem = pl.BlockSpec(memory_space=pltpu.VMEM)
    smem = pl.BlockSpec(memory_space=pltpu.SMEM)
    density = density.transpose(1, 0, 2)

    to_peers, to_prev, to_next = pl.pallas_call(
        pack_kernel,
        out_shape=(
            jax.ShapeDtypeStruct((peers, comp_count, cap, surf), f32),
            jax.ShapeDtypeStruct((comp_count, rim, surf), f32),
            jax.ShapeDtypeStruct((comp_count, rim, surf), f32),
        ),
        in_specs=[vmem, smem, smem],
        out_specs=(vmem, vmem, vmem),
        name="pack",
    )(density, send_list[0], halo_list[0])

    groups = lax.axis_size("group")
    forward = [(i, i + 1) for i in range(groups - 1)]
    backward = [(i + 1, i) for i in range(groups - 1)]
    before = lax.ppermute(to_next, "group", forward)
    after = lax.ppermute(to_prev, "group", backward)
    arrived = lax.all_to_all(to_peers, "dev", split_axis=0, concat_axis=0, tiled=True)

    offsets = kernel_hat.shape[0]
    hat = kernel_hat.reshape(offsets, 2, TILES, LANES).transpose(0, 2, 1, 3).reshape(-1, LANES)

    slots = box_count + peers * cap + 2 * rim
    row_count = comp_count * slots
    potential = pl.pallas_call(
        translate_kernel,
        out_shape=jax.ShapeDtypeStruct((comp_count, box_count, surf), f32),
        in_specs=[smem, smem] + [vmem] * 7,
        out_specs=vmem,
        scratch_shapes=[
            pltpu.VMEM((row_count, POINTS_PAD), f32),
            pltpu.VMEM(hat.shape, f32),
            pltpu.VMEM((2 * row_count * PITCH, LANES), f32),
            pltpu.VMEM((TAIL, (slots + 2) * TAIL_PITCH, LANES), f32),
            pltpu.VMEM((2 * comp_count * box_count * PITCH, LANES), f32),
            pltpu.VMEM((TAIL, (box_count + 2) * TAIL_PITCH, LANES), f32),
        ],
        compiler_params=pltpu.CompilerParams(vmem_limit_bytes=40 * 1024 * 1024),
        name="translate",
    )(inter_src, inter_off, density, arrived, before, after, jnp.asarray(table), jnp.asarray(factor), hat)
    return potential.transpose(1, 0, 2)


def solution(mesh):
    in_specs = (
        P(("group", "dev"), None, None),
        P(),
        P(("group", "dev"), None, None),
        P(("group", "dev"), None, None),
        P(("group", "dev"), None),
        P(("group", "dev"), None),
    )
    out_specs = P(("group", "dev"), None, None)
    return jax.shard_map(
        on_device, mesh=mesh, in_specs=in_specs, out_specs=out_specs, check_vma=False
    )
```

profile of v0, /device:TPU:1, one launch (start us, length us, event | category | flops | bytes accessed | tf_op | source)
XLA Modules:
  0.0 33.8 jit_solution(3165588649795797728)
XLA Ops:
  0.0 1.5 %pack.1 = (f32[4,3,4,152]{3,2,1,0:T(4,128)}, f32[3,4,152]{2,1,0:T(4,128)}, f32[3,4,152]{2,1,0:T(4,128)}) custom-call(f32[3,16,152]{2,1,0:T(8,128)} %bitcast.9, s32[4,4]{1,0:T(4,128)} %bitcast.12, s32[2,4]{1,0:T(2,128)} %bitcast.13), custom_call_target="tpu_custom_call" | custom-call | tf_op jit(solution)/shard_map/pack/pallas_call | solution.py:206
  1.5 4.3 %all-to-all-start = ((f32[4,3,4,152]{3,2,1,0:T(4,128)}), f32[4,3,4,152]{3,2,1,0:T(4,128)S(1)}, u32[]{:S(2)}, u32[]{:S(2)}) async-start(f32[4,3,4,152]{3,2,1,0:T(4,128)} %get-tuple-element.8), calls=%async_computation | async-start | bytes 98304 | tf_op jit(solution)/shard_map/all_to_all | solution.py:223
  5.8 4.0 %collective-permute-start = (f32[3,4,152]{2,1,0:T(4,128)}, f32[3,4,152]{2,1,0:T(4,128)S(1)}, u32[]{:S(2)}, u32[]{:S(2)}) collective-permute-start(f32[3,4,152]{2,1,0:T(4,128)} %get-tuple-element.9), channel_id=1, source_target_pairs={{0,4},{4,8},{8,12},{12,16},{16,20},{20,24},{24,28},{1,5},{5,9},{9,... | collective-permute-start | bytes 21896 | tf_op jit(solution)/shard_map/ppermute | solution.py:221
  9.8 1.9 %collective-permute-start.1 = (f32[3,4,152]{2,1,0:T(4,128)}, f32[3,4,152]{2,1,0:T(4,128)S(1)}, u32[]{:S(2)}, u32[]{:S(2)}) collective-permute-start(f32[3,4,152]{2,1,0:T(4,128)} %get-tuple-element.10), channel_id=1, source_target_pairs={{4,0},{8,4},{12,8},{16,12},{20,16},{24,20},{28,24},{5,1},{9,5},{13... | collective-permute-start | bytes 21896 | tf_op jit(solution)/shard_map/ppermute | solution.py:222
  11.8 2.1 %copy.10 = bf16[316,2,2304]{2,0,1:T(8,128)(2,1)S(1)} copy(bf16[316,2,2304]{2,1,0:T(2,128)(2,1)} %param.9) | data formatting | bytes 5824512 | tf_op args[1]
  13.9 2.9 %reshape.6 = bf16[316,2,18,128]{3,2,0,1:T(8,128)(2,1)} reshape(bf16[316,2,2304]{2,0,1:T(8,128)(2,1)S(1)} %copy.10) | data formatting | bytes 5824512 | tf_op jit(solution)/shard_map/reshape | solution.py:226
  16.8 0.0 copy-start.1
  16.8 0.0 copy-start.2
  16.8 0.0 copy-start.3
  16.8 0.0 copy-start.4
  16.8 5.1 %copy.11 = bf16[316,18,2,128]{3,2,1,0:T(2,128)(2,1)S(1)} copy(bf16[316,18,2,128]{3,1,0,2:T(8,128)(2,1)} %bitcast.11) | data formatting | bytes 5824512 | tf_op jit(solution)/shard_map/transpose | solution.py:226
  21.9 0.0 collective-permute-done.before
  21.9 0.0 collective-permute-done.1.after
  21.9 0.0 all-to-all-done.peers_in
  21.9 0.0 copy-done.1
  21.9 0.0 copy-done.2
  21.9 0.0 copy-done.3
  22.0 0.0 copy-done.4
  22.0 0.0 copy-start
  22.0 1.8 %copy-done = bf16[320,4608]{1,0:T(8,128)(2,1)S(1)} copy-done((bf16[320,4608]{1,0:T(8,128)(2,1)S(1)}, bf16[320,4608]{1,0:T(8,128)(2,1)}, u32[]{:S(2)}) %copy-start) | copy-done | bytes 2949144
  23.8 10.0 %translate.1 = f32[3,16,152]{2,1,0:T(8,128)} custom-call(s32[16,32]{1,0:T(8,128)S(1)} %copy-done.3, s32[16,32]{1,0:T(8,128)S(1)} %copy-done.4, f32[3,16,152]{2,1,0:T(8,128)S(1)} %bitcast.10, f32[4,3,4,152]{3,2,1,0:T(4,128)S(1)} %all-to-all-done.peers_in, f32[3,4,152]{2,1,0:T(4,128)S(1)} %collective-permute-done.before, ...), custom_call_target="tpu_custom_call" | custom-call | tf_op jit(solution)/shard_map/translate/pallas_call | solution.py:230
Async XLA Ops:
  1.5 20.4 %all-to-all-start = ((f32[4,3,4,152]{3,2,1,0:T(4,128)}), f32[4,3,4,152]{3,2,1,0:T(4,128)S(1)}, u32[]{:S(2)}, u32[]{:S(2)}) async-start(f32[4,3,4,152]{3,2,1,0:T(4,128)} %get-tuple-element.8), calls=%async_computation | async-start | bytes 98304 | tf_op jit(solution)/shard_map/all_to_all | solution.py:223
  5.8 16.1 %collective-permute-start = (f32[3,4,152]{2,1,0:T(4,128)}, f32[3,4,152]{2,1,0:T(4,128)S(1)}, u32[]{:S(2)}, u32[]{:S(2)}) collective-permute-start(f32[3,4,152]{2,1,0:T(4,128)} %get-tuple-element.9), channel_id=1, source_target_pairs={{0,4},{4,8},{8,12},{12,16},{16,20},{20,24},{24,28},{1,5},{5,9},{9,... | collective-permute-start | bytes 21896 | tf_op jit(solution)/shard_map/ppermute | solution.py:221
  9.8 12.1 %collective-permute-start.1 = (f32[3,4,152]{2,1,0:T(4,128)}, f32[3,4,152]{2,1,0:T(4,128)S(1)}, u32[]{:S(2)}, u32[]{:S(2)}) collective-permute-start(f32[3,4,152]{2,1,0:T(4,128)} %get-tuple-element.10), channel_id=1, source_target_pairs={{4,0},{8,4},{12,8},{16,12},{20,16},{24,20},{28,24},{5,1},{9,5},{13... | collective-permute-start | bytes 21896 | tf_op jit(solution)/shard_map/ppermute | solution.py:222
  16.8 5.2 %copy-start.1 = (f32[16,3,152]{2,0,1:T(8,128)S(1)}, f32[16,3,152]{2,0,1:T(8,128)}, u32[]{:S(2)}) copy-start(f32[16,3,152]{2,0,1:T(8,128)} %param.8) | copy-start | bytes 87556
  16.8 5.2 %copy-start.2 = (f32[1,4608]{1,0:T(1,128)S(1)}, f32[1,4608]{1,0:T(1,128)}, u32[]{:S(2)}) copy-start(f32[1,4608]{1,0:T(1,128)} %constant.5.clone.factor) | copy-start | bytes 55300
  16.8 5.2 %copy-start.3 = (s32[16,32]{1,0:T(8,128)S(1)}, s32[16,32]{1,0:T(8,128)}, u32[]{:S(2)}) copy-start(s32[16,32]{1,0:T(8,128)} %source.1) | copy-start | bytes 6148
  16.8 5.2 %copy-start.4 = (s32[16,32]{1,0:T(8,128)S(1)}, s32[16,32]{1,0:T(8,128)}, u32[]{:S(2)}) copy-start(s32[16,32]{1,0:T(8,128)} %offset.1) | copy-start | bytes 6148
  22.0 1.8 %copy-start = (bf16[320,4608]{1,0:T(8,128)(2,1)S(1)}, bf16[320,4608]{1,0:T(8,128)(2,1)}, u32[]{:S(2)}) copy-start(bf16[320,4608]{1,0:T(8,128)(2,1)} %constant.4.clone.table) | copy-start | bytes 8847364
where the time goes:
time: 34.1 us; the launch traced here: 33.8 us
  local copies, waits for them, and re-layouts  11.9 us (35%)
  Pallas kernels  11.5 us (34%)
  starting transfers between devices  10.2 us (30%)
    pallas_call x1, Pallas kernels, on_device(): pl.pallas_call(translate_kernel, out_shape=jax.ShapeDtypeStruct((comp_cou...  9.99 us
    transpose x1, local copies, waits for them, and re-layouts, on_device(): kernel_hat.reshape(offsets, 2, TILES, LANES).transpose(0, 2, 1, 3)  5.12 us
    all_to_all x1, starting transfers between devices, on_device(): lax.all_to_all(to_peers, 'dev', split_axis=0, concat_axis=0, tiled=True)  4.27 us
    ppermute x1, starting transfers between devices, on_device(): before = lax.ppermute(to_next, 'group', forward)  4.03 us
    unnamed x11, local copies, waits for them, and re-layouts  3.96 us
    reshape x1, local copies, waits for them, and re-layouts, on_device(): kernel_hat.reshape(offsets, 2, TILES, LANES).transpose(0, 2, 1, 3)  2.87 us
    ppermute x1, starting transfers between devices, on_device(): after = lax.ppermute(to_prev, 'group', backward)  1.92 us
    pallas_call x1, Pallas kernels, on_device(): pl.pallas_call(pack_kernel, out_shape=(jax.ShapeDtypeStruct((peers, comp_...  1.54 us
  transfers between devices with their start and end apart: 3, of which 0 were waited for; matrix products, arithmetic and copies ran while one was open for 30% of the time, Pallas kernels for 0%

commit v1 on v0

--- a/solution.py
+++ b/solution.py
@@ -53,7 +53,7 @@
     return np.concatenate([high, low], axis=0), factor
 
 
-def pack_kernel(density, send_list, halo_list, to_peers, to_prev, to_next):
+def pack_kernel(density, send_list, halo_list, to_peers, to_sides):
     comp_count = density.shape[0]
     peers, cap = send_list.shape
     rim = halo_list.shape[1]
@@ -62,18 +62,48 @@
             for q in range(peers):
                 to_peers[q, c, pl.ds(e, 1), :] = density[c, pl.ds(send_list[q, e], 1), :]
         for e in range(rim):
-            to_prev[c, pl.ds(e, 1), :] = density[c, pl.ds(halo_list[0, e], 1), :]
-            to_next[c, pl.ds(e, 1), :] = density[c, pl.ds(halo_list[1, e], 1), :]
+            for side in range(2):
+                to_sides[side, c, pl.ds(e, 1), :] = density[c, pl.ds(halo_list[side, e], 1), :]
+
+
+def prepare_kernel(kernel_hat, hat, hat_tail):
+    parts, count, _ = kernel_hat.shape
+    padded = hat_tail.shape[0] // (parts * TAIL)
+
+    def move(first, height):
+        for part in range(parts):
+            for j in range(TILES):
+                x = kernel_hat[part, pl.ds(first, height), j * LANES : (j + 1) * LANES].astype(jnp.float32)
+                for g in range(0, height, 8):
+                    size = min(8, height - g)
+                    piece = x[g : g + size]
+                    if j < MAIN:
+                        row = (part * padded + first + g) * PITCH + j
+                        hat[pl.ds(row, size, stride=PITCH), :] = piece
+                    else:
+                        row = (part * TAIL + j - MAIN) * padded + first + g
+                        hat_tail[pl.ds(row, size), :] = piece
+
+    whole = count // 16
+
+    @pl.loop(0, whole)
+    def _(i):
+        move(pl.multiple_of(i * 16, 16), 16)
+
+    if count % 16:
+        move(whole * 16, count % 16)
 
 
 def translate_kernel(
-    source, offset, density, peers_in, before, after, table, factor, kernel_hat, out,
-    rows, hat, main, tail, total, total_tail,
+    place, source, offset, density, peers_in, halos_in, table, factor, hat, hat_tail, out,
+    rows, main, tail, total, total_tail,
 ):
     comp_count, box_count, surf = density.shape
     list_count = source.shape[1]
-    peers, _, cap, _ = peers_in.shape
-    rim = before.shape[1]
+    peers, _, _, cap, _ = peers_in.shape
+    rim = halos_in.shape[3]
+    padded = hat_tail.shape[0] // (2 * TAIL)
+    member, previous, following = place[0], place[1], place[2]
     slots = rows.shape[0] // comp_count
     row_count = rows.shape[0]
     f32, bf16 = jnp.float32, jnp.bfloat16
@@ -84,16 +114,10 @@
         rows[base : base + box_count, :surf] = density[c]
         base += box_count
         for q in range(peers):
-            rows[base + q * cap : base + (q + 1) * cap, :surf] = peers_in[q, c]
+            rows[base + q * cap : base + (q + 1) * cap, :surf] = peers_in[q, member, c]
         base += peers * cap
-        rows[base : base + rim, :surf] = before[c]
-        rows[base + rim : base + 2 * rim, :surf] = after[c]
-
-    step = 144
-    @pl.loop(0, hat.shape[0] // step)
-    def _(i):
-        at = pl.ds(pl.multiple_of(i * step, 16), step)
-        hat[at, :] = kernel_hat[at, :].astype(f32)
+        rows[base : base + rim, :surf] = halos_in[previous, 1, c]
+        rows[base + rim : base + 2 * rim, :surf] = halos_in[following, 0, c]
 
     value = rows[...]
     high = value.astype(bf16)
@@ -124,9 +148,9 @@
     def _(t):
         def pair(w, accs):
             s = source[t, w]
-            o = offset[t, w] * (2 * TILES)
+            o = offset[t, w]
             k = [
-                [hat[pl.ds(o + 16 * h + r, 8, stride=2), :] for h in range(halves)] for r in range(2)
+                [hat[pl.ds((r * padded + o) * PITCH + 8 * h, 8), :] for h in range(halves)] for r in range(2)
             ]
             accs = list(accs)
             at = 0
@@ -139,8 +163,8 @@
                     at += 2
             for j in range(TAIL):
                 x = tail[j, pl.ds(s * TAIL_PITCH, 8), :]
-                k_re = hat[pl.ds(o + 2 * (MAIN + j), 8, stride=0), :]
-                k_im = hat[pl.ds(o + 2 * (MAIN + j) + 1, 8, stride=0), :]
+                k_re = hat_tail[pl.ds(j * padded + o, 8, stride=0), :]
+                k_im = hat_tail[pl.ds((TAIL + j) * padded + o, 8, stride=0), :]
                 accs[at] = accs[at] + k_re * x
                 accs[at + 1] = accs[at + 1] + k_im * x
                 at += 2
@@ -203,46 +227,57 @@
     smem = pl.BlockSpec(memory_space=pltpu.SMEM)
     density = density.transpose(1, 0, 2)
 
-    to_peers, to_prev, to_next = pl.pallas_call(
+    to_peers, to_sides = pl.pallas_call(
         pack_kernel,
         out_shape=(
             jax.ShapeDtypeStruct((peers, comp_count, cap, surf), f32),
-            jax.ShapeDtypeStruct((comp_count, rim, surf), f32),
-            jax.ShapeDtypeStruct((comp_count, rim, surf), f32),
+            jax.ShapeDtypeStruct((2, comp_count, rim, surf), f32),
         ),
         in_specs=[vmem, smem, smem],
-        out_specs=(vmem, vmem, vmem),
+        out_specs=(vmem, vmem),
         name="pack",
     )(density, send_list[0], halo_list[0])
-
-    groups = lax.axis_size("group")
-    forward = [(i, i + 1) for i in range(groups - 1)]
-    backward = [(i + 1, i) for i in range(groups - 1)]
-    before = lax.ppermute(to_next, "group", forward)
-    after = lax.ppermute(to_prev, "group", backward)
-    arrived = lax.all_to_all(to_peers, "dev", split_axis=0, concat_axis=0, tiled=True)
+    from_peers = lax.all_gather(to_peers, "dev")
+    from_sides = lax.all_gather(to_sides, "group")
 
     offsets = kernel_hat.shape[0]
-    hat = kernel_hat.reshape(offsets, 2, TILES, LANES).transpose(0, 2, 1, 3).reshape(-1, LANES)
+    padded = -(-offsets // 8) * 8
+    hat_rows = (2 * padded * PITCH, 2 * TAIL * padded)
+    hat, hat_tail = pl.pallas_call(
+        prepare_kernel,
+        out_shape=tuple(jax.ShapeDtypeStruct((n, LANES), f32) for n in hat_rows),
+        in_specs=[vmem],
+        out_specs=(vmem, vmem),
+        compiler_params=pltpu.CompilerParams(vmem_limit_bytes=16 * 1024 * 1024),
+        cost_estimate=pl.CostEstimate(flops=kernel_hat.size, bytes_accessed=6 * kernel_hat.size, transcendentals=0),
+        name="prepare",
+    )(kernel_hat.transpose(1, 0, 2))
+
+    group, groups = lax.axis_index("group"), lax.axis_size("group")
+    place = jnp.stack([
+        lax.axis_index("dev"), jnp.maximum(group - 1, 0), jnp.minimum(group + 1, groups - 1)
+    ]).astype(jnp.int32)
 
     slots = box_count + peers * cap + 2 * rim
     row_count = comp_count * slots
     potential = pl.pallas_call(
         translate_kernel,
         out_shape=jax.ShapeDtypeStruct((comp_count, box_count, surf), f32),
-        in_specs=[smem, smem] + [vmem] * 7,
+        in_specs=[smem, smem, smem] + [vmem] * 7,
         out_specs=vmem,
         scratch_shapes=[
             pltpu.VMEM((row_count, POINTS_PAD), f32),
-            pltpu.VMEM(hat.shape, f32),
             pltpu.VMEM((2 * row_count * PITCH, LANES), f32),
             pltpu.VMEM((TAIL, (slots + 2) * TAIL_PITCH, LANES), f32),
             pltpu.VMEM((2 * comp_count * box_count * PITCH, LANES), f32),
             pltpu.VMEM((TAIL, (box_count + 2) * TAIL_PITCH, LANES), f32),
         ],
-        compiler_params=pltpu.CompilerParams(vmem_limit_bytes=40 * 1024 * 1024),
+        compiler_params=pltpu.CompilerParams(vmem_limit_bytes=24 * 1024 * 1024),
         name="translate",
-    )(inter_src, inter_off, density, arrived, before, after, jnp.asarray(table), jnp.asarray(factor), hat)
+    )(
+        place, inter_src, inter_off, density, from_peers, from_sides,
+        jnp.asarray(table), jnp.asarray(factor), hat, hat_tail,
+    )
     return potential.transpose(1, 0, 2)
 
 

time: 34.1 us -> 38.9 us (1.14)
  blocking collectives: 0 us -> 24.9 us
  starting transfers between devices: 10.2 us -> 0 us
  local copies, waits for them, and re-layouts: 11.9 us -> 2.29 us
    all_gather x0 -> x2, blocking collectives: none -> 24.9 us  [the longest x1 16.9 us: on_device(): from_sides = lax.all_gather(to_sides, 'group')]
    ppermute x2 -> x0, starting transfers between devices: 5.95 us -> none  [the longest x1 4.03 us: on_device(): before = lax.ppermute(to_next, 'group', forward)]
    transpose x1 -> x0, local copies, waits for them, and re-layouts: 5.12 us -> none  [on_device(): kernel_hat.reshape(offsets, 2, TILES, LANES).transpose(0, 2, 1, 3)]
    all_to_all x1 -> x0, starting transfers between devices: 4.27 us -> none  [on_device(): lax.all_to_all(to_peers, 'dev', split_axis=0, concat_axis=0, tiled=True)]
    reshape x1 -> x0, local copies, waits for them, and re-layouts: 2.87 us -> none  [on_device(): kernel_hat.reshape(offsets, 2, TILES, LANES).transpose(0, 2, 1, 3)]
    unnamed x11, local copies, waits for them, and re-layouts: 3.96 us -> 2.29 us
    pallas_call x1, Pallas kernels: 9.99 us -> 9.22 us  [on_device(): pl.pallas_call(translate_kernel, out_shape=jax.ShapeDtypeStruct((comp_cou...]
    pallas_call x0 -> x1, Pallas kernels: none -> 0.46 us  [on_device(): pl.pallas_call(prepare_kernel, out_shape=tuple((jax.ShapeDtypeStruct((n,...]
  transfers between devices with their start and end apart: 3 -> 0, of which waited for: 0 -> 0; matrix products, arithmetic and copies ran while one was open for 30% -> 0% of each run, Pallas kernels for 0% -> 0%
where the time goes in v1:
time: 38.9 us; the launch traced here: 38.6 us
  blocking collectives  24.9 us (64%)
  Pallas kernels  11.2 us (29%)
  local copies, waits for them, and re-layouts  2.29 us (6%)
    all_gather x1, blocking collectives, on_device(): from_sides = lax.all_gather(to_sides, 'group')  16.9 us
    pallas_call x1, Pallas kernels, on_device(): pl.pallas_call(translate_kernel, out_shape=jax.ShapeDtypeStruct((comp_cou...  9.22 us
    all_gather x1, blocking collectives, on_device(): from_peers = lax.all_gather(to_peers, 'dev')  8.05 us
    unnamed x11, local copies, waits for them, and re-layouts  2.29 us
    pallas_call x1, Pallas kernels, on_device(): pl.pallas_call(pack_kernel, out_shape=(jax.ShapeDtypeStruct((peers, comp_...  1.54 us

profile of v1, /device:TPU:1, one launch (start us, length us, event | category | flops | bytes accessed | tf_op | source)
XLA Modules:
  0.0 38.6 jit_solution(11627308672133199820)
XLA Ops:
  0.0 0.1 pad_add_fusion.place
  0.1 1.5 %pack.1 = (f32[4,3,4,152]{3,2,1,0:T(4,128)}, f32[2,3,4,152]{3,2,1,0:T(4,128)}) custom-call(f32[3,16,152]{2,1,0:T(8,128)} %bitcast.15, s32[4,4]{1,0:T(4,128)} %bitcast.17, s32[2,4]{1,0:T(2,128)} %bitcast.18), custom_call_target="tpu_custom_call" | custom-call | tf_op jit(solution)/shard_map/pack/pallas_call | solution.py:230
  1.6 8.1 %all-gather = f32[16,3,4,152]{3,2,1,0:T(4,128)S(1)} all-gather(f32[4,3,4,152]{3,2,1,0:T(4,128)} %get-tuple-element.9), channel_id=2, replica_groups=mesh['group'=8,'dev'=4] {'dev'}, dimensions={0}, use_global_device_ids=true | all-gather | bytes 145920 | tf_op jit(solution)/shard_map/all_gather | solution.py:240
  9.7 16.9 %all-gather.1 = f32[16,3,4,152]{3,2,1,0:T(4,128)S(1)} all-gather(f32[2,3,4,152]{3,2,1,0:T(4,128)} %get-tuple-element.10), channel_id=3, replica_groups=mesh['group'=8,'dev'=4] {'group'}, dimensions={0}, use_global_device_ids=true | all-gather | bytes 131328 | tf_op jit(solution)/shard_map/all_gather | solution.py:241
  26.5 0.0 copy-start
  26.5 0.0 copy-start.1
  26.5 0.0 copy-start.2
  26.5 0.0 copy-start.3
  26.5 0.0 copy-start.4
  26.6 2.3 %copy.12 = bf16[316,2,2304]{2,0,1:T(8,128)(2,1)S(1)} copy(bf16[316,2,2304]{2,1,0:T(2,128)(2,1)} %param.9) | data formatting | bytes 5824512 | tf_op args[1]
  28.8 0.5 %prepare.1 = (f32[10880,128]{1,0:T(8,128)S(1)}, f32[1280,128]{1,0:T(8,128)S(1)}) custom-call(bf16[2,316,2304]{2,1,0:T(8,128)(2,1)S(1)} %bitcast.12), custom_call_target="tpu_custom_call" | custom-call | flops 1456128 | bytes 8736768 | tf_op jit(solution)/shard_map/prepare/pallas_call | solution.py:246
  29.3 0.0 copy-done
  29.3 0.0 copy-done.1
  29.3 0.0 copy-done.2
  29.3 0.0 copy-done.3
  29.3 0.0 copy-done.4
  29.3 9.2 %translate.1 = f32[3,16,152]{2,1,0:T(8,128)} custom-call(s32[3]{0:T(128)S(1)} %pad_add_fusion.place, s32[16,32]{1,0:T(8,128)S(1)} %copy-done.3, s32[16,32]{1,0:T(8,128)S(1)} %copy-done.4, f32[3,16,152]{2,1,0:T(8,128)S(1)} %bitcast.16, f32[4,4,3,4,152]{4,3,2,1,0:T(4,128)S(1)} %bitcast.14, f32[8,2,3,4,152]{4,3,2,1,0:T(4,128)S(1)} %bitcast.13, ...), custom_call_target="tpu_custom_call" | custom-call | tf_op jit(solution)/shard_map/translate/pallas_call | solution.py:263
Async XLA Ops:
  26.5 2.8 %copy-start = (bf16[320,4608]{1,0:T(8,128)(2,1)S(1)}, bf16[320,4608]{1,0:T(8,128)(2,1)}, u32[]{:S(2)}) copy-start(bf16[320,4608]{1,0:T(8,128)(2,1)} %constant.21.clone.table) | copy-start | bytes 8847364
  26.5 2.8 %copy-start.1 = (f32[16,3,152]{2,0,1:T(8,128)S(1)}, f32[16,3,152]{2,0,1:T(8,128)}, u32[]{:S(2)}) copy-start(f32[16,3,152]{2,0,1:T(8,128)} %param.8) | copy-start | bytes 87556
  26.5 2.8 %copy-start.2 = (f32[1,4608]{1,0:T(1,128)S(1)}, f32[1,4608]{1,0:T(1,128)}, u32[]{:S(2)}) copy-start(f32[1,4608]{1,0:T(1,128)} %constant.22.clone.factor) | copy-start | bytes 55300
  26.5 2.8 %copy-start.3 = (s32[16,32]{1,0:T(8,128)S(1)}, s32[16,32]{1,0:T(8,128)}, u32[]{:S(2)}) copy-start(s32[16,32]{1,0:T(8,128)} %source.1) | copy-start | bytes 6148
  26.5 2.8 %copy-start.4 = (s32[16,32]{1,0:T(8,128)S(1)}, s32[16,32]{1,0:T(8,128)}, u32[]{:S(2)}) copy-start(s32[16,32]{1,0:T(8,128)} %offset.1) | copy-start | bytes 6148

commit v2 on v1

--- a/solution.py
+++ b/solution.py
@@ -53,17 +53,16 @@
     return np.concatenate([high, low], axis=0), factor
 
 
-def pack_kernel(density, send_list, halo_list, to_peers, to_sides):
-    comp_count = density.shape[0]
+def pack_kernel(place, density, send_list, halo_list, *outs):
     peers, cap = send_list.shape
     rim = halo_list.shape[1]
-    for c in range(comp_count):
-        for e in range(cap):
-            for q in range(peers):
-                to_peers[q, c, pl.ds(e, 1), :] = density[c, pl.ds(send_list[q, e], 1), :]
-        for e in range(rim):
-            for side in range(2):
-                to_sides[side, c, pl.ds(e, 1), :] = density[c, pl.ds(halo_list[side, e], 1), :]
+    for c in range(density.shape[0]):
+        for k in range(peers):
+            for e in range(cap):
+                outs[k][c, e : e + 1, :] = density[c, pl.ds(send_list[place[k], e], 1), :]
+        for side in range(2):
+            for e in range(rim):
+                outs[peers + side][c, e : e + 1, :] = density[c, pl.ds(halo_list[side, e], 1), :]
 
 
 def prepare_kernel(kernel_hat, hat, hat_tail):
@@ -94,18 +93,13 @@
         move(whole * 16, count % 16)
 
 
-def translate_kernel(
-    place, source, offset, density, peers_in, halos_in, table, factor, hat, hat_tail, out,
-    rows, main, tail, total, total_tail,
-):
+def forward_kernel(place, density, *refs):
+    *pieces, before, after, table, main, tail, rows = refs
     comp_count, box_count, surf = density.shape
-    list_count = source.shape[1]
-    peers, _, _, cap, _ = peers_in.shape
-    rim = halos_in.shape[3]
-    padded = hat_tail.shape[0] // (2 * TAIL)
-    member, previous, following = place[0], place[1], place[2]
-    slots = rows.shape[0] // comp_count
+    cap = pieces[0].shape[1]
+    rim = before.shape[1]
     row_count = rows.shape[0]
+    slots = row_count // comp_count
     f32, bf16 = jnp.float32, jnp.bfloat16
 
     rows[...] = jnp.zeros_like(rows)
@@ -113,11 +107,12 @@
         base = c * slots
         rows[base : base + box_count, :surf] = density[c]
         base += box_count
-        for q in range(peers):
-            rows[base + q * cap : base + (q + 1) * cap, :surf] = peers_in[q, member, c]
-        base += peers * cap
-        rows[base : base + rim, :surf] = halos_in[previous, 1, c]
-        rows[base + rim : base + 2 * rim, :surf] = halos_in[following, 0, c]
+        for k, piece in enumerate(pieces):
+            for e in range(cap):
+                rows[pl.ds(base + place[k] * cap + e, 1), :surf] = piece[c, e : e + 1]
+        base += len(pieces) * cap
+        rows[base : base + rim, :surf] = before[c]
+        rows[base + rim : base + 2 * rim, :surf] = after[c]
 
     value = rows[...]
     high = value.astype(bf16)
@@ -141,6 +136,14 @@
                         c, s = divmod(g * 8, slots)
                         tail[j - MAIN, pl.ds(s * TAIL_PITCH + part * comp_count + c, 8, stride=TAIL_PITCH), :] = piece
 
+
+def interact_kernel(source, offset, hat, hat_tail, main, tail, total, total_tail):
+    box_count, list_count = source.shape
+    padded = hat_tail.shape[0] // (2 * TAIL)
+    row_count = main.shape[0] // (2 * PITCH)
+    slots = tail.shape[1] // TAIL_PITCH - 2
+    comp_count = row_count // slots
+    f32 = jnp.float32
     plus = lax.broadcasted_iota(jnp.int32, (8, LANES), 0) < comp_count
     halves = MAIN // 8
 
@@ -187,6 +190,10 @@
             total_tail[j, pl.ds(t * TAIL_PITCH, 8), :] = jnp.where(plus, own - up, own + down)
             at += 2
 
+
+def inverse_kernel(total, total_tail, table, factor, out):
+    comp_count, box_count, surf = out.shape
+    f32, bf16 = jnp.float32, jnp.bfloat16
     result = jnp.zeros((comp_count * box_count, 2 * POINTS_PAD), f32)
     rest = jnp.zeros((comp_count * box_count, POINTS_PAD), f32)
     groups = box_count // 8
@@ -227,25 +234,32 @@
     smem = pl.BlockSpec(memory_space=pltpu.SMEM)
     density = density.transpose(1, 0, 2)
 
-    to_peers, to_sides = pl.pallas_call(
+    member = lax.axis_index("dev")
+    place = jnp.bitwise_xor(member, jnp.arange(peers, dtype=jnp.int32)).astype(jnp.int32)
+    boxes = jax.ShapeDtypeStruct((comp_count, cap, surf), f32)
+    side = jax.ShapeDtypeStruct((comp_count, rim, surf), f32)
+    *to_peers, to_prev, to_next = pl.pallas_call(
         pack_kernel,
-        out_shape=(
-            jax.ShapeDtypeStruct((peers, comp_count, cap, surf), f32),
-            jax.ShapeDtypeStruct((2, comp_count, rim, surf), f32),
-        ),
-        in_specs=[vmem, smem, smem],
-        out_specs=(vmem, vmem),
+        out_shape=(boxes,) * peers + (side,) * 2,
+        in_specs=[smem, vmem, smem, smem],
+        out_specs=(vmem,) * (peers + 2),
         name="pack",
-    )(density, send_list[0], halo_list[0])
-    from_peers = lax.all_gather(to_peers, "dev")
-    from_sides = lax.all_gather(to_sides, "group")
+    )(place, density, send_list[0], halo_list[0])
+    pieces = [to_peers[0]]
+    for k in range(1, peers):
+        pieces.append(lax.ppermute(to_peers[k], "dev", [(i, i ^ k) for i in range(peers)]))
+    groups = lax.axis_size("group")
+    before = lax.ppermute(to_next, "group", [(i, i + 1) for i in range(groups - 1)])
+    after = lax.ppermute(to_prev, "group", [(i + 1, i) for i in range(groups - 1)])
 
     offsets = kernel_hat.shape[0]
     padded = -(-offsets // 8) * 8
-    hat_rows = (2 * padded * PITCH, 2 * TAIL * padded)
     hat, hat_tail = pl.pallas_call(
         prepare_kernel,
-        out_shape=tuple(jax.ShapeDtypeStruct((n, LANES), f32) for n in hat_rows),
+        out_shape=(
+            jax.ShapeDtypeStruct((2 * padded * PITCH, LANES), f32),
+            jax.ShapeDtypeStruct((2 * TAIL * padded, LANES), f32),
+        ),
         in_specs=[vmem],
         out_specs=(vmem, vmem),
         compiler_params=pltpu.CompilerParams(vmem_limit_bytes=16 * 1024 * 1024),
@@ -253,31 +267,41 @@
         name="prepare",
     )(kernel_hat.transpose(1, 0, 2))
 
-    group, groups = lax.axis_index("group"), lax.axis_size("group")
-    place = jnp.stack([
-        lax.axis_index("dev"), jnp.maximum(group - 1, 0), jnp.minimum(group + 1, groups - 1)
-    ]).astype(jnp.int32)
-
     slots = box_count + peers * cap + 2 * rim
     row_count = comp_count * slots
+    params = pltpu.CompilerParams(vmem_limit_bytes=24 * 1024 * 1024)
+    table = jnp.asarray(table)
+    main, tail = pl.pallas_call(
+        forward_kernel,
+        out_shape=(
+            jax.ShapeDtypeStruct((2 * row_count * PITCH, LANES), f32),
+            jax.ShapeDtypeStruct((TAIL, (slots + 2) * TAIL_PITCH, LANES), f32),
+        ),
+        in_specs=[smem] + [vmem] * (peers + 4),
+        out_specs=(vmem, vmem),
+        scratch_shapes=[pltpu.VMEM((row_count, POINTS_PAD), f32)],
+        compiler_params=params,
+        name="forward",
+    )(place, density, *pieces, before, after, table)
+    total, total_tail = pl.pallas_call(
+        interact_kernel,
+        out_shape=(
+            jax.ShapeDtypeStruct((2 * comp_count * box_count * PITCH, LANES), f32),
+            jax.ShapeDtypeStruct((TAIL, (box_count + 2) * TAIL_PITCH, LANES), f32),
+        ),
+        in_specs=[smem, smem] + [vmem] * 4,
+        out_specs=(vmem, vmem),
+        compiler_params=params,
+        name="interact",
+    )(inter_src, inter_off, hat, hat_tail, main, tail)
     potential = pl.pallas_call(
-        translate_kernel,
+        inverse_kernel,
         out_shape=jax.ShapeDtypeStruct((comp_count, box_count, surf), f32),
-        in_specs=[smem, smem, smem] + [vmem] * 7,
+        in_specs=[vmem] * 4,
         out_specs=vmem,
-        scratch_shapes=[
-            pltpu.VMEM((row_count, POINTS_PAD), f32),
-            pltpu.VMEM((2 * row_count * PITCH, LANES), f32),
-            pltpu.VMEM((TAIL, (slots + 2) * TAIL_PITCH, LANES), f32),
-            pltpu.VMEM((2 * comp_count * box_count * PITCH, LANES), f32),
-            pltpu.VMEM((TAIL, (box_count + 2) * TAIL_PITCH, LANES), f32),
-        ],
-        compiler_params=pltpu.CompilerParams(vmem_limit_bytes=24 * 1024 * 1024),
-        name="translate",
-    )(
-        place, inter_src, inter_off, density, from_peers, from_sides,
-        jnp.asarray(table), jnp.asarray(factor), hat, hat_tail,
-    )
+        compiler_params=params,
+        name="inverse",
+    )(total, total_tail, table, jnp.asarray(factor))
     return potential.transpose(1, 0, 2)
 
 

time: 38.9 us -> 26 us (0.67)
  blocking collectives: 24.9 us -> 0 us
  starting transfers between devices: 0 us -> 10.3 us
  Pallas kernels: 11.2 us -> 12 us
  waiting for transfers between devices: 0 us -> 0.66 us
  other arithmetic: 0.08 us -> 0.51 us
    all_gather x2 -> x0, blocking collectives: 24.9 us -> none  [the longest x1 16.9 us: on_device(): from_sides = lax.all_gather(to_sides, 'group')]
    ppermute x0 -> x5, starting transfers between devices: none -> 10.3 us  [the longest x1 4.78 us: on_device(): lax.ppermute(to_next, 'group', [(i, i + 1) for i in range(groups - 1)])]
    pallas_call x3 -> x5, Pallas kernels: 11.2 us -> 12 us  [the longest x1 6.23 us: on_device(): pl.pallas_call(interact_kernel, out_shape=(jax.ShapeDtypeStruct((2 * comp...]
    ppermute x0 -> x5, waiting for transfers between devices: none -> 0.66 us  [the longest x1 0.64 us: on_device(): lax.ppermute(to_prev, 'group', [(i + 1, i) for i in range(groups - 1)])]
    xor x0 -> x1, other arithmetic: none -> 0.51 us  [on_device(): jnp.bitwise_xor(member, jnp.arange(peers, dtype=jnp.int32))]
    unnamed x11 -> x15, local copies, waits for them, and re-layouts: 2.29 us -> 2.16 us
  transfers between devices with their start and end apart: 0 -> 5, of which waited for: 0 -> 1; matrix products, arithmetic and copies ran while one was open for 0% -> 8% of each run, Pallas kernels for 0% -> 2%
where the time goes in v2:
time: 26 us; the launch traced here: 25.7 us
  Pallas kernels  12 us (46%)
  starting transfers between devices  10.3 us (40%)
  local copies, waits for them, and re-layouts  2.16 us (8%)
  waiting for transfers between devices  0.66 us (3%)
  other arithmetic  0.51 us (2%)
    pallas_call x1, Pallas kernels, on_device(): pl.pallas_call(interact_kernel, out_shape=(jax.ShapeDtypeStruct((2 * comp...  6.23 us
    ppermute x1, starting transfers between devices, on_device(): lax.ppermute(to_next, 'group', [(i, i + 1) for i in range(groups - 1)])  4.78 us
    ppermute x3, starting transfers between devices, on_device(): lax.ppermute(to_peers[k], 'dev', [(i, i ^ k) for i in range(peers)])  3.29 us
    ppermute x1, starting transfers between devices, on_device(): lax.ppermute(to_prev, 'group', [(i + 1, i) for i in range(groups - 1)])  2.18 us
    unnamed x15, local copies, waits for them, and re-layouts  2.16 us
    pallas_call x1, Pallas kernels, on_device(): pl.pallas_call(inverse_kernel, out_shape=jax.ShapeDtypeStruct((comp_count...  2.02 us
    pallas_call x1, Pallas kernels, on_device(): pl.pallas_call(forward_kernel, out_shape=(jax.ShapeDtypeStruct((2 * row_c...  1.68 us
    pallas_call x1, Pallas kernels, on_device(): pl.pallas_call(pack_kernel, out_shape=(boxes,) * peers + (side,) * 2, in_...  1.59 us
  transfers between devices with their start and end apart: 5, of which 1 were waited for; matrix products, arithmetic and copies ran while one was open for 8% of the time, Pallas kernels for 2%

profile of v2, /device:TPU:1, one launch (start us, length us, event | category | flops | bytes accessed | tf_op | source)
XLA Modules:
  0.0 25.7 jit_solution(7344585042769707102)
XLA Ops:
  0.0 0.5 %iota_xor_fusion.place = s32[4]{0:T(128)} fusion(s32[]{:T(128)S(6)} %axis_index.12), kind=kLoop, calls=%fused_computation.1 | loop fusion | flops 4 | bytes 20 | tf_op jit(solution)/shard_map/xor | solution.py:238
  0.5 1.6 %pack.1 = (f32[3,4,152]{2,1,0:T(4,128)}, f32[3,4,152]{2,1,0:T(4,128)}, f32[3,4,152]{2,1,0:T(4,128)}, f32[3,4,152]{2,1,0:T(4,128)}, f32[3,4,152]{2,1,0:T(4,128)}, /*index=5*/f32[3,4,152]{2,1,0:T(4,128)}) custom-call(s32[4]{0:T(128)} %iota_xor_fusion.place, f32[3,16,152]{2,1,0:T(8,128)} %bitcast.8, s32[4,4]{1,0:T(4,128)} %bitcast.10, s32[2,4]{1,0:T(2,128)} %bitcast.11), custom_call_target="tpu_custom_call" | custom-call | tf_op jit(solution)/shard_map/pack/pallas_call | solution.py:241
  2.1 2.0 %collective-permute-start = (f32[3,4,152]{2,1,0:T(4,128)}, f32[3,4,152]{2,1,0:T(4,128)S(1)}, u32[]{:S(2)}, u32[]{:S(2)}) collective-permute-start(f32[3,4,152]{2,1,0:T(4,128)} %get-tuple-element.20), channel_id=1, source_target_pairs={{0,1},{1,0},{2,3},{3,2},{4,5},{5,4},{6,7},{7,6},{8,9},{9,8},{10,11... | collective-permute-start | bytes 21896 | tf_op jit(solution)/shard_map/ppermute | solution.py:250
  4.1 1.2 %collective-permute-start.1 = (f32[3,4,152]{2,1,0:T(4,128)}, f32[3,4,152]{2,1,0:T(4,128)S(1)}, u32[]{:S(2)}, u32[]{:S(2)}) collective-permute-start(f32[3,4,152]{2,1,0:T(4,128)} %get-tuple-element.21), channel_id=1, source_target_pairs={{0,2},{1,3},{2,0},{3,1},{4,6},{5,7},{6,4},{7,5},{8,10},{9,11},{10,... | collective-permute-start | bytes 21896 | tf_op jit(solution)/shard_map/ppermute | solution.py:250
  5.4 0.0 collective-permute-start.2
  5.4 4.8 %collective-permute-start.3 = (f32[3,4,152]{2,1,0:T(4,128)}, f32[3,4,152]{2,1,0:T(4,128)S(1)}, u32[]{:S(2)}, u32[]{:S(2)}) collective-permute-start(f32[3,4,152]{2,1,0:T(4,128)} %get-tuple-element.23), channel_id=1, source_target_pairs={{0,4},{4,8},{8,12},{12,16},{16,20},{20,24},{24,28},{1,5},{5,9},{9,... | collective-permute-start | bytes 21896 | tf_op jit(solution)/shard_map/ppermute | solution.py:252
  10.2 0.0 copy-start
  10.2 0.0 copy-start.1
  10.2 0.0 copy-start.3
  10.2 0.0 copy-start.6
  10.2 2.2 %collective-permute-start.4 = (f32[3,4,152]{2,1,0:T(4,128)}, f32[3,4,152]{2,1,0:T(4,128)S(1)}, u32[]{:S(2)}, u32[]{:S(2)}) collective-permute-start(f32[3,4,152]{2,1,0:T(4,128)} %get-tuple-element.24), channel_id=1, source_target_pairs={{4,0},{8,4},{12,8},{16,12},{20,16},{24,20},{28,24},{5,1},{9,5},{13... | collective-permute-start | bytes 21896 | tf_op jit(solution)/shard_map/ppermute | solution.py:253
  12.4 2.1 %copy.11 = bf16[316,2,2304]{2,0,1:T(8,128)(2,1)S(1)} copy(bf16[316,2,2304]{2,1,0:T(2,128)(2,1)} %param.9) | data formatting | bytes 5824512 | tf_op args[1]
  14.5 0.0 copy-start.4
  14.5 0.0 copy-start.5
  14.6 0.5 %prepare.1 = (f32[10880,128]{1,0:T(8,128)S(1)}, f32[1280,128]{1,0:T(8,128)S(1)}) custom-call(bf16[2,316,2304]{2,1,0:T(8,128)(2,1)S(1)} %bitcast.7), custom_call_target="tpu_custom_call" | custom-call | flops 1456128 | bytes 8736768 | tf_op jit(solution)/shard_map/prepare/pallas_call | solution.py:257
  15.0 0.0 collective-permute-done.refs_1_
  15.0 0.0 collective-permute-done.1.refs_2_
  15.1 0.0 collective-permute-done.2.refs_3_
  15.1 0.0 collective-permute-done.3.refs_4_
  15.1 0.6 %collective-permute-done.4.refs_5_ = f32[3,4,152]{2,1,0:T(4,128)S(1)} collective-permute-done((f32[3,4,152]{2,1,0:T(4,128)}, f32[3,4,152]{2,1,0:T(4,128)S(1)}, u32[]{:S(2)}, u32[]{:S(2)}) %collective-permute-start.4) | collective-permute-done | bytes 7328 | tf_op jit(solution)/shard_map/ppermute | solution.py:253
  15.7 0.0 copy-done
  15.7 0.0 copy-done.1
  15.7 0.0 copy-done.3
  15.7 0.0 copy-done.6
  15.7 1.7 %forward.1 = (f32[4080,128]{1,0:T(8,128)S(1)}, f32[2,294,128]{2,1,0:T(8,128)S(1)}) custom-call(s32[4]{0:T(128)S(1)} %copy-done.6, f32[3,16,152]{2,1,0:T(8,128)S(1)} %bitcast.9, f32[3,4,152]{2,1,0:T(4,128)S(1)} %copy-done.3, f32[3,4,152]{2,1,0:T(4,128)S(1)} %collective-permute-done.refs_1_, f32[3,4,152]{2,1,0:T(4,128)S(1)} %collective-permute-done.1.refs_2_, ...), custom_call_target="tpu_custom_call" | custom-call | tf_op jit(solution)/shard_map/forward/pallas_call | solution.py:274
  17.4 0.0 copy-done.4
  17.4 0.0 copy-done.5
  17.4 0.0 copy-start.2
  17.5 6.2 %interact.1 = (f32[1632,128]{1,0:T(8,128)S(1)}, f32[2,126,128]{2,1,0:T(8,128)S(1)}) custom-call(s32[16,32]{1,0:T(8,128)S(1)} %copy-done.4, s32[16,32]{1,0:T(8,128)S(1)} %copy-done.5, f32[10880,128]{1,0:T(8,128)S(1)} %get-tuple-element.17.hat, f32[1280,128]{1,0:T(8,128)S(1)} %get-tuple-element.18.hat_tail, f32[4080,128]{1,0:T(8,128)S(1)} %get-tuple-element.25.main, ...), custom_call_target="tpu_custom_call" | custom-call | tf_op jit(solution)/shard_map/interact/pallas_call | solution.py:286
  23.7 0.0 copy-done.2
  23.7 2.0 %inverse.1 = f32[3,16,152]{2,1,0:T(8,128)} custom-call(f32[1632,128]{1,0:T(8,128)S(1)} %get-tuple-element.27.total, f32[2,126,128]{2,1,0:T(8,128)S(1)} %get-tuple-element.28.total_tail, bf16[320,4608]{1,0:T(8,128)(2,1)S(1)} %copy-done, f32[1,4608]{1,0:T(1,128)S(1)} %copy-done.2), custom_call_target="tpu_custom_call" | custom-call | tf_op jit(solution)/shard_map/inverse/pallas_call | solution.py:297
Async XLA Ops:
  2.1 12.9 %collective-permute-start = (f32[3,4,152]{2,1,0:T(4,128)}, f32[3,4,152]{2,1,0:T(4,128)S(1)}, u32[]{:S(2)}, u32[]{:S(2)}) collective-permute-start(f32[3,4,152]{2,1,0:T(4,128)} %get-tuple-element.20), channel_id=1, source_target_pairs={{0,1},{1,0},{2,3},{3,2},{4,5},{5,4},{6,7},{7,6},{8,9},{9,8},{10,11... | collective-permute-start | bytes 21896 | tf_op jit(solution)/shard_map/ppermute | solution.py:250
  4.1 10.9 %collective-permute-start.1 = (f32[3,4,152]{2,1,0:T(4,128)}, f32[3,4,152]{2,1,0:T(4,128)S(1)}, u32[]{:S(2)}, u32[]{:S(2)}) collective-permute-start(f32[3,4,152]{2,1,0:T(4,128)} %get-tuple-element.21), channel_id=1, source_target_pairs={{0,2},{1,3},{2,0},{3,1},{4,6},{5,7},{6,4},{7,5},{8,10},{9,11},{10,... | collective-permute-start | bytes 21896 | tf_op jit(solution)/shard_map/ppermute | solution.py:250
  5.4 9.7 %collective-permute-start.2 = (f32[3,4,152]{2,1,0:T(4,128)}, f32[3,4,152]{2,1,0:T(4,128)S(1)}, u32[]{:S(2)}, u32[]{:S(2)}) collective-permute-start(f32[3,4,152]{2,1,0:T(4,128)} %get-tuple-element.22), channel_id=1, source_target_pairs={{0,3},{1,2},{2,1},{3,0},{4,7},{5,6},{6,5},{7,4},{8,11},{9,10},{10,... | collective-permute-start | bytes 21896 | tf_op jit(solution)/shard_map/ppermute | solution.py:250
  5.4 9.7 %collective-permute-start.3 = (f32[3,4,152]{2,1,0:T(4,128)}, f32[3,4,152]{2,1,0:T(4,128)S(1)}, u32[]{:S(2)}, u32[]{:S(2)}) collective-permute-start(f32[3,4,152]{2,1,0:T(4,128)} %get-tuple-element.23), channel_id=1, source_target_pairs={{0,4},{4,8},{8,12},{12,16},{16,20},{20,24},{24,28},{1,5},{5,9},{9,... | collective-permute-start | bytes 21896 | tf_op jit(solution)/shard_map/ppermute | solution.py:252
  10.2 5.5 %copy-start = (bf16[320,4608]{1,0:T(8,128)(2,1)S(1)}, bf16[320,4608]{1,0:T(8,128)(2,1)}, u32[]{:S(2)}) copy-start(bf16[320,4608]{1,0:T(8,128)(2,1)} %constant.8.clone.refs_6_.table) | copy-start | bytes 8847364
  10.2 5.5 %copy-start.1 = (f32[16,3,152]{2,0,1:T(8,128)S(1)}, f32[16,3,152]{2,0,1:T(8,128)}, u32[]{:S(2)}) copy-start(f32[16,3,152]{2,0,1:T(8,128)} %param.8) | copy-start | bytes 87556
  10.2 5.5 %copy-start.3 = (f32[3,4,152]{2,1,0:T(4,128)S(1)}, f32[3,4,152]{2,1,0:T(4,128)}, u32[]{:S(2)}) copy-start(f32[3,4,152]{2,1,0:T(4,128)} %get-tuple-element.19.refs_0_) | copy-start | bytes 21892
  10.2 5.5 %copy-start.6 = (s32[4]{0:T(128)S(1)}, s32[4]{0:T(128)}, u32[]{:S(2)}) copy-start(s32[4]{0:T(128)} %iota_xor_fusion.place) | copy-start | bytes 52
  10.2 5.5 %collective-permute-start.4 = (f32[3,4,152]{2,1,0:T(4,128)}, f32[3,4,152]{2,1,0:T(4,128)S(1)}, u32[]{:S(2)}, u32[]{:S(2)}) collective-permute-start(f32[3,4,152]{2,1,0:T(4,128)} %get-tuple-element.24), channel_id=1, source_target_pairs={{4,0},{8,4},{12,8},{16,12},{20,16},{24,20},{28,24},{5,1},{9,5},{13... | collective-permute-start | bytes 21896 | tf_op jit(solution)/shard_map/ppermute | solution.py:253
  14.5 2.9 %copy-start.4 = (s32[16,32]{1,0:T(8,128)S(1)}, s32[16,32]{1,0:T(8,128)}, u32[]{:S(2)}) copy-start(s32[16,32]{1,0:T(8,128)} %source.1) | copy-start | bytes 6148
  14.5 2.9 %copy-start.5 = (s32[16,32]{1,0:T(8,128)S(1)}, s32[16,32]{1,0:T(8,128)}, u32[]{:S(2)}) copy-start(s32[16,32]{1,0:T(8,128)} %offset.1) | copy-start | bytes 6148
  17.4 6.2 %copy-start.2 = (f32[1,4608]{1,0:T(1,128)S(1)}, f32[1,4608]{1,0:T(1,128)}, u32[]{:S(2)}) copy-start(f32[1,4608]{1,0:T(1,128)} %constant.9.clone.factor) | copy-start | bytes 55300

commit v3 on v2

--- a/solution.py
+++ b/solution.py
@@ -18,7 +18,7 @@
 TILES = FREQ // LANES
 MAIN = 16
 TAIL = TILES - MAIN
-PITCH = MAIN + 1
+PITCH = MAIN
 TAIL_PITCH = 7
 POINTS_PAD = 160
 CHUNK = 256
@@ -53,16 +53,19 @@
     return np.concatenate([high, low], axis=0), factor
 
 
-def pack_kernel(place, density, send_list, halo_list, *outs):
+def pack_kernel(density, send_list, halo_list, to_pair, to_other):
     peers, cap = send_list.shape
     rim = halo_list.shape[1]
+    member = lax.axis_index("dev")
+    parity = lax.rem(lax.axis_index("group"), 2)
+    mine, partner = parity * peers, (1 - parity) * peers + member
     for c in range(density.shape[0]):
-        for k in range(peers):
+        for q in range(peers):
             for e in range(cap):
-                outs[k][c, e : e + 1, :] = density[c, pl.ds(send_list[place[k], e], 1), :]
-        for side in range(2):
-            for e in range(rim):
-                outs[peers + side][c, e : e + 1, :] = density[c, pl.ds(halo_list[side, e], 1), :]
+                to_pair[mine + q, c, e : e + 1, :] = density[c, pl.ds(send_list[q, e], 1), :]
+        for e in range(rim):
+            to_pair[partner, c, e : e + 1, :] = density[c, pl.ds(halo_list[1 - parity, e], 1), :]
+            to_other[c, e : e + 1, :] = density[c, pl.ds(halo_list[parity, e], 1), :]
 
 
 def prepare_kernel(kernel_hat, hat, hat_tail):
@@ -93,26 +96,28 @@
         move(whole * 16, count % 16)
 
 
-def forward_kernel(place, density, *refs):
-    *pieces, before, after, table, main, tail, rows = refs
+def forward_kernel(density, send_list, from_pair, from_other, table, main, tail, rows):
     comp_count, box_count, surf = density.shape
-    cap = pieces[0].shape[1]
-    rim = before.shape[1]
+    peers, cap = send_list.shape
+    rim = from_other.shape[1]
     row_count = rows.shape[0]
     slots = row_count // comp_count
     f32, bf16 = jnp.float32, jnp.bfloat16
 
+    member = lax.axis_index("dev")
+    parity = lax.rem(lax.axis_index("group"), 2)
+    mine, partner = parity * peers, (1 - parity) * peers + member
     rows[...] = jnp.zeros_like(rows)
     for c in range(comp_count):
         base = c * slots
         rows[base : base + box_count, :surf] = density[c]
         base += box_count
-        for k, piece in enumerate(pieces):
-            for e in range(cap):
-                rows[pl.ds(base + place[k] * cap + e, 1), :surf] = piece[c, e : e + 1]
-        base += len(pieces) * cap
-        rows[base : base + rim, :surf] = before[c]
-        rows[base + rim : base + 2 * rim, :surf] = after[c]
+        for q in range(peers):
+            rows[base : base + cap, :surf] = from_pair[mine + q, c, :cap]
+            base += cap
+        for e in range(rim):
+            rows[pl.ds(base + (1 - parity) * rim + e, 1), :surf] = from_pair[partner, c, e : e + 1]
+            rows[pl.ds(base + parity * rim + e, 1), :surf] = from_other[c, e : e + 1]
 
     value = rows[...]
     high = value.astype(bf16)
@@ -234,23 +239,22 @@
     smem = pl.BlockSpec(memory_space=pltpu.SMEM)
     density = density.transpose(1, 0, 2)
 
-    member = lax.axis_index("dev")
-    place = jnp.bitwise_xor(member, jnp.arange(peers, dtype=jnp.int32)).astype(jnp.int32)
-    boxes = jax.ShapeDtypeStruct((comp_count, cap, surf), f32)
-    side = jax.ShapeDtypeStruct((comp_count, rim, surf), f32)
-    *to_peers, to_prev, to_next = pl.pallas_call(
+    groups = lax.axis_size("group")
+    high = max(cap, rim)
+    to_pair, to_other = pl.pallas_call(
         pack_kernel,
-        out_shape=(boxes,) * peers + (side,) * 2,
-        in_specs=[smem, vmem, smem, smem],
-        out_specs=(vmem,) * (peers + 2),
+        out_shape=(
+            jax.ShapeDtypeStruct((2 * peers, comp_count, high, surf), f32),
+            jax.ShapeDtypeStruct((comp_count, rim, surf), f32),
+        ),
+        in_specs=[vmem, smem, smem],
+        out_specs=(vmem, vmem),
         name="pack",
-    )(place, density, send_list[0], halo_list[0])
-    pieces = [to_peers[0]]
-    for k in range(1, peers):
-        pieces.append(lax.ppermute(to_peers[k], "dev", [(i, i ^ k) for i in range(peers)]))
-    groups = lax.axis_size("group")
-    before = lax.ppermute(to_next, "group", [(i, i + 1) for i in range(groups - 1)])
-    after = lax.ppermute(to_prev, "group", [(i + 1, i) for i in range(groups - 1)])
+    )(density, send_list[0], halo_list[0])
+    pairs = [list(range(i, i + 2 * peers)) for i in range(0, groups * peers, 2 * peers)]
+    from_pair = lax.all_to_all(to_pair, ("group", "dev"), 0, 0, axis_index_groups=pairs, tiled=True)
+    swaps = [(i, i + 1) for i in range(1, groups - 1, 2)]
+    from_other = lax.ppermute(to_other, "group", swaps + [(j, i) for i, j in swaps])
 
     offsets = kernel_hat.shape[0]
     padded = -(-offsets // 8) * 8
@@ -277,12 +281,12 @@
             jax.ShapeDtypeStruct((2 * row_count * PITCH, LANES), f32),
             jax.ShapeDtypeStruct((TAIL, (slots + 2) * TAIL_PITCH, LANES), f32),
         ),
-        in_specs=[smem] + [vmem] * (peers + 4),
+        in_specs=[vmem, smem, vmem, vmem, vmem],
         out_specs=(vmem, vmem),
         scratch_shapes=[pltpu.VMEM((row_count, POINTS_PAD), f32)],
         compiler_params=params,
         name="forward",
-    )(place, density, *pieces, before, after, table)
+    )(density, send_list[0], from_pair, from_other, table)
     total, total_tail = pl.pallas_call(
         interact_kernel,
         out_shape=(

time: 26 us -> 30.2 us (1.16)
  local copies, waits for them, and re-layouts: 2.16 us -> 7.8 us
  starting transfers between devices: 10.3 us -> 8.6 us
  Pallas kernels: 12 us -> 13.3 us
  waiting for transfers between devices: 0.66 us -> 0.01 us
  other arithmetic: 0.51 us -> 0 us
    ppermute x5 -> x1, starting transfers between devices: 10.3 us -> 3.37 us  [on_device(): lax.ppermute(to_other, 'group', swaps + [(j, i) for i, j in swaps])]
    unnamed x15 -> x21, local copies, waits for them, and re-layouts: 2.16 us -> 7.8 us
    all_to_all x0 -> x1, starting transfers between devices: none -> 5.23 us  [on_device(): lax.all_to_all(to_pair, ('group', 'dev'), 0, 0, axis_index_groups=pairs,...]
    pallas_call x1, Pallas kernels: 0.46 us -> 1.65 us  [on_device(): pl.pallas_call(prepare_kernel, out_shape=(jax.ShapeDtypeStruct((2 * padde...]
    ppermute x5 -> x1, waiting for transfers between devices: 0.66 us -> 0.01 us  [on_device(): lax.ppermute(to_other, 'group', swaps + [(j, i) for i, j in swaps])]
    xor x1 -> x0, other arithmetic: 0.51 us -> none  [on_device(): jnp.bitwise_xor(member, jnp.arange(peers, dtype=jnp.int32))]
  transfers between devices with their start and end apart: 5 -> 2, of which waited for: 1 -> 0; matrix products, arithmetic and copies ran while one was open for 8% -> 7% of each run, Pallas kernels for 2% -> 6%
where the time goes in v3:
time: 30.2 us; the launch traced here: 29.9 us
  Pallas kernels  13.3 us (44%)
  starting transfers between devices  8.6 us (28%)
  local copies, waits for them, and re-layouts  7.8 us (26%)
    unnamed x21, local copies, waits for them, and re-layouts  7.8 us
    pallas_call x1, Pallas kernels, on_device(): pl.pallas_call(interact_kernel, out_shape=(jax.ShapeDtypeStruct((2 * comp...  6.13 us
    all_to_all x1, starting transfers between devices, on_device(): lax.all_to_all(to_pair, ('group', 'dev'), 0, 0, axis_index_groups=pairs,...  5.23 us
    ppermute x1, starting transfers between devices, on_device(): lax.ppermute(to_other, 'group', swaps + [(j, i) for i, j in swaps])  3.37 us
    pallas_call x1, Pallas kernels, on_device(): pl.pallas_call(inverse_kernel, out_shape=jax.ShapeDtypeStruct((comp_count...  2.02 us
    pallas_call x1, Pallas kernels, on_device(): pl.pallas_call(forward_kernel, out_shape=(jax.ShapeDtypeStruct((2 * row_c...  1.93 us
    pallas_call x1, Pallas kernels, on_device(): pl.pallas_call(prepare_kernel, out_shape=(jax.ShapeDtypeStruct((2 * padde...  1.65 us
    pallas_call x1, Pallas kernels, on_device(): pl.pallas_call(pack_kernel, out_shape=(jax.ShapeDtypeStruct((2 * peers, c...  1.6 us
  transfers between devices with their start and end apart: 2, of which 0 were waited for; matrix products, arithmetic and copies ran while one was open for 7% of the time, Pallas kernels for 6%

profile of v3, /device:TPU:1, one launch (start us, length us, event | category | flops | bytes accessed | tf_op | source)
XLA Modules:
  0.0 29.9 jit_solution(5448907428560531832)
XLA Ops:
  0.0 1.6 %pack.1 = (f32[8,3,4,152]{3,2,1,0:T(4,128)}, f32[3,4,152]{2,1,0:T(4,128)}) custom-call(f32[3,16,152]{2,1,0:T(8,128)} %bitcast.8, s32[4,4]{1,0:T(4,128)} %bitcast.10, s32[2,4]{1,0:T(2,128)} %bitcast.12), custom_call_target="tpu_custom_call" | custom-call | tf_op jit(solution)/shard_map/pack/pallas_call | solution.py:244
  1.6 5.2 %all-to-all-start = ((f32[8,3,4,152]{3,2,1,0:T(4,128)}), f32[8,3,4,152]{3,2,1,0:T(4,128)S(1)}, u32[]{:S(2)}, u32[]{:S(2)}) async-start(f32[8,3,4,152]{3,2,1,0:T(4,128)} %get-tuple-element.15), calls=%async_computation | async-start | bytes 196608 | tf_op jit(solution)/shard_map/all_to_all | solution.py:255
  6.8 0.0 copy-start
  6.8 0.0 copy-start.5
  6.8 0.0 copy-start.9
  6.8 3.4 %collective-permute-start = (f32[3,4,152]{2,1,0:T(4,128)}, f32[3,4,152]{2,1,0:T(4,128)S(1)}, u32[]{:S(2)}, u32[]{:S(2)}) collective-permute-start(f32[3,4,152]{2,1,0:T(4,128)} %get-tuple-element.16), channel_id=1, source_target_pairs={{4,8},{12,16},{20,24},{8,4},{16,12},{24,20},{5,9},{13,17},{21,25},... | collective-permute-start | bytes 21896 | tf_op jit(solution)/shard_map/ppermute | solution.py:257
  10.2 2.1 %copy.11 = bf16[316,2,2304]{2,0,1:T(8,128)(2,1)S(1)} copy(bf16[316,2,2304]{2,1,0:T(2,128)(2,1)} %param.9) | data formatting | bytes 5824512 | tf_op args[1]
  12.3 0.0 copy-start.7
  12.3 0.0 copy-start.8
  12.4 1.6 %prepare.1 = (f32[10240,128]{1,0:T(8,128)S(1)}, f32[1280,128]{1,0:T(8,128)S(1)}) custom-call(bf16[2,316,2304]{2,1,0:T(8,128)(2,1)S(1)} %bitcast.7), custom_call_target="tpu_custom_call" | custom-call | flops 1456128 | bytes 8736768 | tf_op jit(solution)/shard_map/prepare/pallas_call | solution.py:261
  14.0 0.0 copy-start.1
  14.0 2.3 %copy-done.1 = f32[10240,128]{1,0:T(8,128)} copy-done((f32[10240,128]{1,0:T(8,128)}, f32[10240,128]{1,0:T(8,128)S(1)}, u32[]{:S(2)}) %copy-start.1) | copy-done | bytes 5242904
  16.3 0.0 copy-start.3
  16.3 0.9 %copy-done.3 = f32[1280,128]{1,0:T(8,128)} copy-done((f32[1280,128]{1,0:T(8,128)}, f32[1280,128]{1,0:T(8,128)S(1)}, u32[]{:S(2)}) %copy-start.3) | copy-done | bytes 655384
  17.2 0.0 collective-permute-done.from_other
  17.2 0.0 all-to-all-done.from_pair
  17.2 0.0 copy-done
  17.2 0.0 copy-done.5
  17.2 0.0 copy-done.9
  17.2 0.0 copy-start.4
  17.2 1.9 %forward.1 = (f32[3840,128]{1,0:T(8,128)S(1)}, f32[2,294,128]{2,1,0:T(8,128)S(1)}) custom-call(f32[3,16,152]{2,1,0:T(8,128)S(1)} %bitcast.9, s32[4,4]{1,0:T(4,128)S(1)} %bitcast.11, f32[8,3,4,152]{3,2,1,0:T(4,128)S(1)} %all-to-all-done.from_pair, f32[3,4,152]{2,1,0:T(4,128)S(1)} %collective-permute-done.from_other, bf16[320,4608]{1,0:T(8,128)(2,1)S(1)} %copy-done), custom_call_target="tpu_custom_call" | custom-call | tf_op jit(solution)/shard_map/forward/pallas_call | solution.py:278
  19.2 0.0 copy-done.7
  19.2 0.0 copy-done.8
  19.2 0.0 copy-done.4
  19.2 0.0 copy-start.2
  19.2 2.5 %copy-done.2 = f32[10240,128]{1,0:T(8,128)S(1)} copy-done((f32[10240,128]{1,0:T(8,128)S(1)}, f32[10240,128]{1,0:T(8,128)}, u32[]{:S(2)}) %copy-start.2) | copy-done | bytes 5242904
  21.7 0.0 copy-start.6
  21.7 6.1 %interact.1 = (f32[1536,128]{1,0:T(8,128)S(1)}, f32[2,126,128]{2,1,0:T(8,128)S(1)}) custom-call(s32[16,32]{1,0:T(8,128)S(1)} %copy-done.7, s32[16,32]{1,0:T(8,128)S(1)} %copy-done.8, f32[10240,128]{1,0:T(8,128)S(1)} %copy-done.2, f32[1280,128]{1,0:T(8,128)S(1)} %copy-done.4, f32[3840,128]{1,0:T(8,128)S(1)} %get-tuple-element.17.main, ...), custom_call_target="tpu_custom_call" | custom-call | tf_op jit(solution)/shard_map/interact/pallas_call | solution.py:290
  27.8 0.0 copy-done.6
  27.8 2.0 %inverse.1 = f32[3,16,152]{2,1,0:T(8,128)} custom-call(f32[1536,128]{1,0:T(8,128)S(1)} %get-tuple-element.19.total, f32[2,126,128]{2,1,0:T(8,128)S(1)} %get-tuple-element.20.total_tail, bf16[320,4608]{1,0:T(8,128)(2,1)S(1)} %copy-done, f32[1,4608]{1,0:T(1,128)S(1)} %copy-done.6), custom_call_target="tpu_custom_call" | custom-call | tf_op jit(solution)/shard_map/inverse/pallas_call | solution.py:301
Async XLA Ops:
  1.6 15.6 %all-to-all-start = ((f32[8,3,4,152]{3,2,1,0:T(4,128)}), f32[8,3,4,152]{3,2,1,0:T(4,128)S(1)}, u32[]{:S(2)}, u32[]{:S(2)}) async-start(f32[8,3,4,152]{3,2,1,0:T(4,128)} %get-tuple-element.15), calls=%async_computation | async-start | bytes 196608 | tf_op jit(solution)/shard_map/all_to_all | solution.py:255
  6.8 10.4 %copy-start = (bf16[320,4608]{1,0:T(8,128)(2,1)S(1)}, bf16[320,4608]{1,0:T(8,128)(2,1)}, u32[]{:S(2)}) copy-start(bf16[320,4608]{1,0:T(8,128)(2,1)} %constant.4.clone.table) | copy-start | bytes 8847364
  6.8 10.4 %copy-start.5 = (f32[16,3,152]{2,0,1:T(8,128)S(1)}, f32[16,3,152]{2,0,1:T(8,128)}, u32[]{:S(2)}) copy-start(f32[16,3,152]{2,0,1:T(8,128)} %param.8) | copy-start | bytes 87556
  6.8 10.4 %copy-start.9 = (s32[1,4,4]{2,1,0:T(4,128)S(1)}, s32[1,4,4]{2,1,0:T(4,128)}, u32[]{:S(2)}) copy-start(s32[1,4,4]{2,1,0:T(4,128)} %param.10) | copy-start | bytes 196
  6.8 10.4 %collective-permute-start = (f32[3,4,152]{2,1,0:T(4,128)}, f32[3,4,152]{2,1,0:T(4,128)S(1)}, u32[]{:S(2)}, u32[]{:S(2)}) collective-permute-start(f32[3,4,152]{2,1,0:T(4,128)} %get-tuple-element.16), channel_id=1, source_target_pairs={{4,8},{12,16},{20,24},{8,4},{16,12},{24,20},{5,9},{13,17},{21,25},... | collective-permute-start | bytes 21896 | tf_op jit(solution)/shard_map/ppermute | solution.py:257
  12.3 6.9 %copy-start.7 = (s32[16,32]{1,0:T(8,128)S(1)}, s32[16,32]{1,0:T(8,128)}, u32[]{:S(2)}) copy-start(s32[16,32]{1,0:T(8,128)} %source.1) | copy-start | bytes 6148
  12.3 6.8 %copy-start.8 = (s32[16,32]{1,0:T(8,128)S(1)}, s32[16,32]{1,0:T(8,128)}, u32[]{:S(2)}) copy-start(s32[16,32]{1,0:T(8,128)} %offset.1) | copy-start | bytes 6148
  14.0 2.3 %copy-start.1 = (f32[10240,128]{1,0:T(8,128)}, f32[10240,128]{1,0:T(8,128)S(1)}, u32[]{:S(2)}) copy-start(f32[10240,128]{1,0:T(8,128)S(1)} %get-tuple-element.13.hat) | copy-start | bytes 15728644
  16.3 0.9 %copy-start.3 = (f32[1280,128]{1,0:T(8,128)}, f32[1280,128]{1,0:T(8,128)S(1)}, u32[]{:S(2)}) copy-start(f32[1280,128]{1,0:T(8,128)S(1)} %get-tuple-element.14.hat_tail) | copy-start | bytes 1966084
  17.2 2.0 %copy-start.4 = (f32[1280,128]{1,0:T(8,128)S(1)}, f32[1280,128]{1,0:T(8,128)}, u32[]{:S(2)}) copy-start(f32[1280,128]{1,0:T(8,128)} %copy-done.3) | copy-start | bytes 1966084
  19.2 2.5 %copy-start.2 = (f32[10240,128]{1,0:T(8,128)S(1)}, f32[10240,128]{1,0:T(8,128)}, u32[]{:S(2)}) copy-start(f32[10240,128]{1,0:T(8,128)} %copy-done.1) | copy-start | bytes 15728644
  21.7 6.1 %copy-start.6 = (f32[1,4608]{1,0:T(1,128)S(1)}, f32[1,4608]{1,0:T(1,128)}, u32[]{:S(2)}) copy-start(f32[1,4608]{1,0:T(1,128)} %constant.5.clone.factor) | copy-start | bytes 55300

commit v4 on v0

v4 whole, which is shorter than its diff:
```python
import functools
import math

import jax
import jax.numpy as jnp
import ml_dtypes
import numpy as np
from jax import lax
from jax.experimental import pallas as pl
from jax.experimental.pallas import tpu as pltpu
from jax.sharding import PartitionSpec as P

ORDER = 6
GRID = 16
LANES = 128
HALF = GRID // 2 + 1
FREQ = GRID * GRID * HALF
TILES = FREQ // LANES
MAIN = 16
TAIL = TILES - MAIN
PITCH = MAIN + 1
TAIL_PITCH = 7
POINTS_PAD = 160
CHUNK = 256
PIECE = 512


def surface_points(edge_count):
    points = [
        (i, j, k)
        for i in range(edge_count)
        for j in range(edge_count)
        for k in range(edge_count)
        if min(i, j, k) == 0 or max(i, j, k) == edge_count - 1
    ]
    return np.array(points, dtype=np.int64)


@functools.lru_cache(maxsize=None)
def transform_tables():
    points = surface_points(ORDER)
    kx, ky, kz = (a.reshape(-1) for a in np.meshgrid(np.arange(GRID), np.arange(GRID), np.arange(HALF), indexing="ij"))
    phase = (points[:, :1] * kx + points[:, 1:2] * ky + points[:, 2:] * kz) % GRID
    angle = phase * (2.0 * math.pi / GRID)
    table = np.zeros((POINTS_PAD, 2 * FREQ), np.float64)
    table[: len(points), :FREQ] = np.cos(angle)
    table[: len(points), FREQ:] = -np.sin(angle)
    table = np.where(np.abs(table) < 1e-9, 0.0, table)
    high = table.astype(ml_dtypes.bfloat16)
    low = (table - high.astype(np.float64)).astype(ml_dtypes.bfloat16)
    edge_plane = (kz == 0) | (kz == GRID // 2)
    factor = np.where(edge_plane, 1.0, 2.0) / GRID**3 * np.where((kx + ky + kz) % 2 == 0, 1.0, -1.0)
    factor = np.concatenate([factor, factor]).astype(np.float32)[None, :]
    return np.concatenate([high, low], axis=0), factor


def pack_kernel(density, send_list, halo_list, to_pair, to_other):
    peers, cap = send_list.shape
    rim = halo_list.shape[1]
    member = lax.axis_index("dev")
    parity = lax.rem(lax.axis_index("group"), 2)
    mine, partner = parity * peers, (1 - parity) * peers + member
    for c in range(density.shape[0]):
        for q in range(peers):
            for e in range(cap):
                to_pair[mine + q, c, e : e + 1, :] = density[c, pl.ds(send_list[q, e], 1), :]
        for e in range(rim):
            to_pair[partner, c, e : e + 1, :] = density[c, pl.ds(halo_list[1 - parity, e], 1), :]
            to_other[c, e : e + 1, :] = density[c, pl.ds(halo_list[parity, e], 1), :]


def translate_kernel(
    source, offset, send_list, density, from_pair, from_other, factor, table_hbm, kernel_hbm, out,
    table, raw, hat, hat_tail, rows, main, tail, total, total_tail, table_sem, raw_sem,
):
    comp_count, box_count, surf = density.shape
    list_count = source.shape[1]
    peers, cap = send_list.shape
    rim = from_other.shape[1]
    row_count = rows.shape[0]
    slots = row_count // comp_count
    offsets, padded = kernel_hbm.shape[0], raw.shape[1]
    f32, bf16 = jnp.float32, jnp.bfloat16

    def table_copy(n):
        columns = pl.ds(n * PIECE, PIECE)
        return pltpu.make_async_copy(table_hbm.at[:, columns], table.at[:, columns], table_sem.at[n])

    def raw_copy(j):
        return pltpu.make_async_copy(
            kernel_hbm.at[:, :, pl.ds(j * LANES, LANES)], raw.at[j, pl.ds(0, offsets)], raw_sem.at[j]
        )

    for n in range(2 * FREQ // PIECE):
        table_copy(n).start()
    for j in range(TILES):
        raw_copy(j).start()

    member = lax.axis_index("dev")
    parity = lax.rem(lax.axis_index("group"), 2)
    mine, partner = parity * peers, (1 - parity) * peers + member
    rows[...] = jnp.zeros_like(rows)
    for c in range(comp_count):
        base = c * slots
        rows[base : base + box_count, :surf] = density[c]
        base += box_count
        for q in range(peers):
            rows[base : base + cap, :surf] = from_pair[mine + q, c, :cap]
            base += cap
        for e in range(rim):
            rows[pl.ds(base + (1 - parity) * rim + e, 1), :surf] = from_pair[partner, c, e : e + 1]
            rows[pl.ds(base + parity * rim + e, 1), :surf] = from_other[c, e : e + 1]

    value = rows[...]
    high = value.astype(bf16)
    low = (value - high.astype(f32)).astype(bf16)
    both = jnp.concatenate([high, low], axis=0)
    for n in range(2 * FREQ // CHUNK):
        if n * CHUNK % PIECE == 0:
            table_copy(n * CHUNK // PIECE).wait()
        columns = slice(n * CHUNK, (n + 1) * CHUNK)
        x = jnp.dot(both, table[:POINTS_PAD, columns], preferred_element_type=f32)
        x = x[:row_count] + x[row_count:]
        x = x + jnp.dot(high, table[POINTS_PAD:, columns], preferred_element_type=f32)
        x = x.astype(bf16).astype(f32)
        for m in range(CHUNK // LANES):
            part, j = divmod(n * (CHUNK // LANES) + m, TILES)
            for g in range(row_count // 8):
                piece = x[g * 8 : (g + 1) * 8, m * LANES : (m + 1) * LANES]
                if j < MAIN:
                    main[pl.ds((part * row_count + g * 8) * PITCH + j, 8, stride=PITCH), :] = piece
                else:
                    c, s = divmod(g * 8, slots)
                    tail[j - MAIN, pl.ds(s * TAIL_PITCH + part * comp_count + c, 8, stride=TAIL_PITCH), :] = piece

    for j in range(TILES):
        raw_copy(j).wait()
    flat = raw.reshape(TILES * padded * 2, LANES)

    @pl.loop(0, padded * 2 // 16)
    def _(i):
        for j in range(TILES):
            x = flat[pl.ds(pl.multiple_of(j * padded * 2 + i * 16, 16), 16), :].astype(f32)
            for g in range(2):
                row = i * 16 + g * 8
                if j < MAIN:
                    hat[pl.ds(row * PITCH + j, 8, stride=PITCH), :] = x[g * 8 : g * 8 + 8]
                else:
                    hat_tail[pl.ds((j - MAIN) * padded * 2 + row, 8), :] = x[g * 8 : g * 8 + 8]

    plus = lax.broadcasted_iota(jnp.int32, (8, LANES), 0) < comp_count
    halves = MAIN // 8

    @pl.loop(0, box_count)
    def _(t):
        def pair(w, accs):
            s = source[t, w]
            o = offset[t, w]
            k = [
                [hat[pl.ds((2 * o + r) * PITCH + 8 * h, 8), :] for h in range(halves)] for r in range(2)
            ]
            accs = list(accs)
            at = 0
            for c in range(comp_count):
                for h in range(halves):
                    s_re = main[pl.ds((c * slots + s) * PITCH + 8 * h, 8), :]
                    s_im = main[pl.ds((row_count + c * slots + s) * PITCH + 8 * h, 8), :]
                    accs[at] = accs[at] + (k[0][h] * s_re - k[1][h] * s_im)
                    accs[at + 1] = accs[at + 1] + (k[0][h] * s_im + k[1][h] * s_re)
                    at += 2
            for j in range(TAIL):
                x = tail[j, pl.ds(s * TAIL_PITCH, 8), :]
                k_re = hat_tail[pl.ds(2 * (j * padded + o), 8, stride=0), :]
                k_im = hat_tail[pl.ds(2 * (j * padded + o) + 1, 8, stride=0), :]
                accs[at] = accs[at] + k_re * x
                accs[at + 1] = accs[at + 1] + k_im * x
                at += 2
            return tuple(accs)

        count = 2 * (comp_count * halves + TAIL)
        zero = jnp.zeros((8, LANES), f32)
        accs = lax.fori_loop(0, list_count, pair, (zero,) * count, unroll=True)
        at = 0
        for c in range(comp_count):
            for h in range(halves):
                for part in range(2):
                    row = (part * comp_count + c) * box_count + t
                    total[pl.ds(row * PITCH + 8 * h, 8), :] = accs[at + part]
                at += 2
        for j in range(TAIL):
            own, cross = accs[at], accs[at + 1]
            up = jnp.concatenate([cross[comp_count:], cross[:comp_count]], axis=0)
            down = jnp.concatenate([cross[-comp_count:], cross[:-comp_count]], axis=0)
            total_tail[j, pl.ds(t * TAIL_PITCH, 8), :] = jnp.where(plus, own - up, own + down)
            at += 2

    groups = box_count // 8
    count = comp_count * box_count
    nt = (((1,), (1,)), ((), ()))
    result = jnp.zeros((2 * POINTS_PAD, 2 * count), f32)
    for n in range(2 * FREQ // PIECE):
        lanes = []
        for m in range(PIECE // LANES):
            part, j = divmod(n * (PIECE // LANES) + m, TILES)
            pieces = []
            for c in range(comp_count):
                for g in range(groups):
                    if j < MAIN:
                        row = (part * comp_count + c) * box_count + g * 8
                        pieces.append(total[pl.ds(row * PITCH + j, 8, stride=PITCH), :])
                    else:
                        row = g * 8 * TAIL_PITCH + part * comp_count + c
                        pieces.append(total_tail[j - MAIN, pl.ds(row, 8, stride=TAIL_PITCH), :])
            lanes.append(jnp.concatenate(pieces, axis=0))
        columns = slice(n * PIECE, (n + 1) * PIECE)
        x = jnp.concatenate(lanes, axis=1) * factor[:, columns]
        high = x.astype(bf16)
        low = (x - high.astype(f32)).astype(bf16)
        both = jnp.concatenate([high, low], axis=0)
        result += lax.dot_general(table[:, columns], both, nt, preferred_element_type=f32)
    result = result[:POINTS_PAD, :count] + result[:POINTS_PAD, count:] + result[POINTS_PAD:, :count]
    result = result.T
    for c in range(comp_count):
        out[c] = result[c * box_count : (c + 1) * box_count, :surf]


def on_device(density, kernel_hat, send_list, halo_list, inter_src, inter_off):
    table, factor = transform_tables()
    box_count, comp_count, surf = density.shape
    _, peers, cap = send_list.shape
    rim = halo_list.shape[2]
    f32 = jnp.float32
    vmem = pl.BlockSpec(memory_space=pltpu.VMEM)
    smem = pl.BlockSpec(memory_space=pltpu.SMEM)
    density = density.transpose(1, 0, 2)

    groups = lax.axis_size("group")
    high = max(cap, rim)
    to_pair, to_other = pl.pallas_call(
        pack_kernel,
        out_shape=(
            jax.ShapeDtypeStruct((2 * peers, comp_count, high, surf), f32),
            jax.ShapeDtypeStruct((comp_count, rim, surf), f32),
        ),
        in_specs=[vmem, smem, smem],
        out_specs=(vmem, vmem),
        name="pack",
    )(density, send_list[0], halo_list[0])
    pairs = [list(range(i, i + 2 * peers)) for i in range(0, groups * peers, 2 * peers)]
    from_pair = lax.all_to_all(to_pair, ("group", "dev"), 0, 0, axis_index_groups=pairs, tiled=True)
    swaps = [(i, i + 1) for i in range(1, groups - 1, 2)]
    from_other = lax.ppermute(to_other, "group", swaps + [(j, i) for i, j in swaps])

    padded = -(-kernel_hat.shape[0] // 8) * 8
    slots = box_count + peers * cap + 2 * rim
    row_count = comp_count * slots
    hbm = pl.BlockSpec(memory_space=pl.ANY)
    potential = pl.pallas_call(
        translate_kernel,
        out_shape=jax.ShapeDtypeStruct((comp_count, box_count, surf), f32),
        in_specs=[smem] * 3 + [vmem] * 4 + [hbm] * 2,
        out_specs=vmem,
        scratch_shapes=[
            pltpu.VMEM(table.shape, jnp.bfloat16),
            pltpu.VMEM((TILES, padded, 2, LANES), jnp.bfloat16),
            pltpu.VMEM((2 * padded * PITCH, LANES), f32),
            pltpu.VMEM((TAIL * padded * 2 + 8, LANES), f32),
            pltpu.VMEM((row_count, POINTS_PAD), f32),
            pltpu.VMEM((2 * row_count * PITCH, LANES), f32),
            pltpu.VMEM((TAIL, (slots + 2) * TAIL_PITCH, LANES), f32),
            pltpu.VMEM((2 * comp_count * box_count * PITCH, LANES), f32),
            pltpu.VMEM((TAIL, (box_count + 2) * TAIL_PITCH, LANES), f32),
            pltpu.SemaphoreType.DMA((2 * FREQ // PIECE,)),
            pltpu.SemaphoreType.DMA((TILES,)),
        ],
        compiler_params=pltpu.CompilerParams(vmem_limit_bytes=60 * 1024 * 1024),
        name="translate",
    )(
        inter_src, inter_off, send_list[0], density, from_pair, from_other,
        jnp.asarray(factor), jnp.asarray(table), kernel_hat,
    )
    return potential.transpose(1, 0, 2)


def solution(mesh):
    in_specs = (
        P(("group", "dev"), None, None),
        P(),
        P(("group", "dev"), None, None),
        P(("group", "dev"), None, None),
        P(("group", "dev"), None),
        P(("group", "dev"), None),
    )
    out_specs = P(("group", "dev"), None, None)
    return jax.shard_map(
        on_device, mesh=mesh, in_specs=in_specs, out_specs=out_specs, check_vma=False
    )
```

time: 34.1 us -> 30.5 us (0.89)
  local copies, waits for them, and re-layouts: 11.9 us -> 1.22 us
  Pallas kernels: 11.5 us -> 18.6 us
  waiting for transfers between devices: 0.01 us -> 2.13 us
  starting transfers between devices: 10.2 us -> 8.31 us
    pallas_call x1, Pallas kernels: 9.99 us -> 17 us  [on_device(): pl.pallas_call(translate_kernel, out_shape=jax.ShapeDtypeStruct((comp_cou...]
    transpose x1 -> x0, local copies, waits for them, and re-layouts: 5.12 us -> none  [on_device(): kernel_hat.reshape(offsets, 2, TILES, LANES).transpose(0, 2, 1, 3)]
    reshape x1 -> x0, local copies, waits for them, and re-layouts: 2.87 us -> none  [on_device(): kernel_hat.reshape(offsets, 2, TILES, LANES).transpose(0, 2, 1, 3)]
    ppermute x2 -> x1, starting transfers between devices: 5.95 us -> 3.08 us  [on_device(): lax.ppermute(to_other, 'group', swaps + [(j, i) for i, j in swaps])]
    unnamed x11 -> x4, local copies, waits for them, and re-layouts: 3.96 us -> 1.22 us
    ppermute x2 -> x1, waiting for transfers between devices: 0.01 us -> 2.12 us  [on_device(): lax.ppermute(to_other, 'group', swaps + [(j, i) for i, j in swaps])]
    all_to_all x1, starting transfers between devices: 4.27 us -> 5.23 us  [on_device(): lax.all_to_all(to_pair, ('group', 'dev'), 0, 0, axis_index_groups=pairs,...]
  transfers between devices with their start and end apart: 3 -> 2, of which waited for: 0 -> 1; matrix products, arithmetic and copies ran while one was open for 30% -> 0% of each run, Pallas kernels for 0% -> 0%
where the time goes in v4:
time: 30.5 us; the launch traced here: 30.2 us
  Pallas kernels  18.6 us (61%)
  starting transfers between devices  8.31 us (27%)
  waiting for transfers between devices  2.13 us (7%)
  local copies, waits for them, and re-layouts  1.22 us (4%)
    pallas_call x1, Pallas kernels, on_device(): pl.pallas_call(translate_kernel, out_shape=jax.ShapeDtypeStruct((comp_cou...  17 us
    all_to_all x1, starting transfers between devices, on_device(): lax.all_to_all(to_pair, ('group', 'dev'), 0, 0, axis_index_groups=pairs,...  5.23 us
    ppermute x1, starting transfers between devices, on_device(): lax.ppermute(to_other, 'group', swaps + [(j, i) for i, j in swaps])  3.08 us
    ppermute x1, waiting for transfers between devices, on_device(): lax.ppermute(to_other, 'group', swaps + [(j, i) for i, j in swaps])  2.12 us
    pallas_call x1, Pallas kernels, on_device(): pl.pallas_call(pack_kernel, out_shape=(jax.ShapeDtypeStruct((2 * peers, c...  1.59 us
    unnamed x4, local copies, waits for them, and re-layouts  1.22 us
  transfers between devices with their start and end apart: 2, of which 1 were waited for; matrix products, arithmetic and copies ran while one was open for 0% of the time, Pallas kernels for 0%

profile of v4, /device:TPU:1, one launch (start us, length us, event | category | flops | bytes accessed | tf_op | source)
XLA Modules:
  0.0 30.2 jit_solution(9101998626006907634)
XLA Ops:
  0.0 1.6 %pack.1 = (f32[8,3,4,152]{3,2,1,0:T(4,128)}, f32[3,4,152]{2,1,0:T(4,128)}) custom-call(f32[3,16,152]{2,1,0:T(8,128)} %bitcast.4, s32[4,4]{1,0:T(4,128)} %bitcast.6, s32[2,4]{1,0:T(2,128)} %bitcast.8), custom_call_target="tpu_custom_call" | custom-call | tf_op jit(solution)/shard_map/pack/pallas_call | solution.py:239
  1.6 5.2 %all-to-all-start = ((f32[8,3,4,152]{3,2,1,0:T(4,128)}), f32[8,3,4,152]{3,2,1,0:T(4,128)S(1)}, u32[]{:S(2)}, u32[]{:S(2)}) async-start(f32[8,3,4,152]{3,2,1,0:T(4,128)} %get-tuple-element.7), calls=%async_computation | async-start | bytes 196608 | tf_op jit(solution)/shard_map/all_to_all | solution.py:250
  6.8 3.1 %collective-permute-start = (f32[3,4,152]{2,1,0:T(4,128)}, f32[3,4,152]{2,1,0:T(4,128)S(1)}, u32[]{:S(2)}, u32[]{:S(2)}) collective-permute-start(f32[3,4,152]{2,1,0:T(4,128)} %get-tuple-element.8), channel_id=1, source_target_pairs={{4,8},{12,16},{20,24},{8,4},{16,12},{24,20},{5,9},{13,17},{21,25},... | collective-permute-start | bytes 21896 | tf_op jit(solution)/shard_map/ppermute | solution.py:252
  9.9 2.1 %collective-permute-done.from_other = f32[3,4,152]{2,1,0:T(4,128)S(1)} collective-permute-done((f32[3,4,152]{2,1,0:T(4,128)}, f32[3,4,152]{2,1,0:T(4,128)S(1)}, u32[]{:S(2)}, u32[]{:S(2)}) %collective-permute-start) | collective-permute-done | bytes 7328 | tf_op jit(solution)/shard_map/ppermute | solution.py:252
  12.0 0.0 copy-start.1
  12.0 0.0 all-to-all-done.from_pair
  12.0 0.6 %copy-done.1 = f32[3,4,152]{2,1,0:T(4,128)} copy-done((f32[3,4,152]{2,1,0:T(4,128)}, f32[3,4,152]{2,1,0:T(4,128)S(1)}, u32[]{:S(2)}) %copy-start.1) | copy-done | bytes 7320
  12.6 0.0 copy-start
  12.6 0.6 %copy-done = f32[8,3,4,152]{3,2,1,0:T(4,128)} copy-done((f32[8,3,4,152]{3,2,1,0:T(4,128)}, f32[8,3,4,152]{3,2,1,0:T(4,128)S(1)}, u32[]{:S(2)}) %copy-start) | copy-done | bytes 58392
  13.3 17.0 %translate.1 = f32[3,16,152]{2,1,0:T(8,128)} custom-call(s32[16,32]{1,0:T(8,128)} %source.1, s32[16,32]{1,0:T(8,128)} %offset.1, s32[4,4]{1,0:T(4,128)} %bitcast.7, f32[3,16,152]{2,1,0:T(8,128)} %bitcast.5, f32[8,3,4,152]{3,2,1,0:T(4,128)} %copy-done, f32[3,4,152]{2,1,0:T(4,128)} %copy-done.1, f32[1,4608]{1,0:T(1,128)} %constant.4.clone.factor, ...), custom_call_target="tpu_custom_call" | custom-call | tf_op jit(solution)/shard_map/translate/pallas_call | solution.py:258
Async XLA Ops:
  1.6 10.4 %all-to-all-start = ((f32[8,3,4,152]{3,2,1,0:T(4,128)}), f32[8,3,4,152]{3,2,1,0:T(4,128)S(1)}, u32[]{:S(2)}, u32[]{:S(2)}) async-start(f32[8,3,4,152]{3,2,1,0:T(4,128)} %get-tuple-element.7), calls=%async_computation | async-start | bytes 196608 | tf_op jit(solution)/shard_map/all_to_all | solution.py:250
  6.8 5.2 %collective-permute-start = (f32[3,4,152]{2,1,0:T(4,128)}, f32[3,4,152]{2,1,0:T(4,128)S(1)}, u32[]{:S(2)}, u32[]{:S(2)}) collective-permute-start(f32[3,4,152]{2,1,0:T(4,128)} %get-tuple-element.8), channel_id=1, source_target_pairs={{4,8},{12,16},{20,24},{8,4},{16,12},{24,20},{5,9},{13,17},{21,25},... | collective-permute-start | bytes 21896 | tf_op jit(solution)/shard_map/ppermute | solution.py:252
  12.0 0.6 %copy-start.1 = (f32[3,4,152]{2,1,0:T(4,128)}, f32[3,4,152]{2,1,0:T(4,128)S(1)}, u32[]{:S(2)}) copy-start(f32[3,4,152]{2,1,0:T(4,128)S(1)} %collective-permute-done.from_other) | copy-start | bytes 21892
  12.6 0.6 %copy-start = (f32[8,3,4,152]{3,2,1,0:T(4,128)}, f32[8,3,4,152]{3,2,1,0:T(4,128)S(1)}, u32[]{:S(2)}) copy-start(f32[8,3,4,152]{3,2,1,0:T(4,128)S(1)} %all-to-all-done.from_pair) | copy-start | bytes 175108

commit v5 on v3

--- a/solution.py
+++ b/solution.py
@@ -18,10 +18,11 @@
 TILES = FREQ // LANES
 MAIN = 16
 TAIL = TILES - MAIN
-PITCH = MAIN
+PITCH = MAIN + 1
 TAIL_PITCH = 7
 POINTS_PAD = 160
 CHUNK = 256
+PIECE = 512
 
 
 def surface_points(edge_count):
@@ -53,19 +54,21 @@
     return np.concatenate([high, low], axis=0), factor
 
 
-def pack_kernel(density, send_list, halo_list, to_pair, to_other):
+def pack_kernel(density, send_list, halo_list, *outs):
     peers, cap = send_list.shape
     rim = halo_list.shape[1]
     member = lax.axis_index("dev")
     parity = lax.rem(lax.axis_index("group"), 2)
-    mine, partner = parity * peers, (1 - parity) * peers + member
+    to_near, *to_far, to_first, to_second = outs
     for c in range(density.shape[0]):
-        for q in range(peers):
-            for e in range(cap):
-                to_pair[mine + q, c, e : e + 1, :] = density[c, pl.ds(send_list[q, e], 1), :]
+        for e in range(cap):
+            for part, k in enumerate((1, 3)):
+                to_near[part, c, e : e + 1, :] = density[c, pl.ds(send_list[member ^ k, e], 1), :]
+            for k, out in zip((2, *range(4, peers)), to_far):
+                out[c, e : e + 1, :] = density[c, pl.ds(send_list[member ^ k, e], 1), :]
         for e in range(rim):
-            to_pair[partner, c, e : e + 1, :] = density[c, pl.ds(halo_list[1 - parity, e], 1), :]
-            to_other[c, e : e + 1, :] = density[c, pl.ds(halo_list[parity, e], 1), :]
+            to_first[c, e : e + 1, :] = density[c, pl.ds(halo_list[1 - parity, e], 1), :]
+            to_second[c, e : e + 1, :] = density[c, pl.ds(halo_list[parity, e], 1), :]
 
 
 def prepare_kernel(kernel_hat, hat, hat_tail):
@@ -96,50 +99,52 @@
         move(whole * 16, count % 16)
 
 
-def forward_kernel(density, send_list, from_pair, from_other, table, main, tail, rows):
+def forward_kernel(send_list, density, from_near, relayed, *refs):
+    *from_far, from_first, from_second, table, main, tail, rows = refs
     comp_count, box_count, surf = density.shape
     peers, cap = send_list.shape
-    rim = from_other.shape[1]
+    rim = from_first.shape[1]
     row_count = rows.shape[0]
     slots = row_count // comp_count
     f32, bf16 = jnp.float32, jnp.bfloat16
 
     member = lax.axis_index("dev")
     parity = lax.rem(lax.axis_index("group"), 2)
-    mine, partner = parity * peers, (1 - parity) * peers + member
     rows[...] = jnp.zeros_like(rows)
+    pieces = {1: from_near.at[0], 3: relayed.at[1]}
+    pieces.update(zip((2, *range(4, peers)), from_far))
     for c in range(comp_count):
         base = c * slots
         rows[base : base + box_count, :surf] = density[c]
         base += box_count
-        for q in range(peers):
-            rows[base : base + cap, :surf] = from_pair[mine + q, c, :cap]
-            base += cap
+        for e in range(cap):
+            rows[pl.ds(base + member * cap + e, 1), :surf] = density[c, pl.ds(send_list[member, e], 1), :]
+            for k, piece in pieces.items():
+                rows[pl.ds(base + (member ^ k) * cap + e, 1), :surf] = piece[c, e : e + 1]
+        base += peers * cap
         for e in range(rim):
-            rows[pl.ds(base + (1 - parity) * rim + e, 1), :surf] = from_pair[partner, c, e : e + 1]
-            rows[pl.ds(base + parity * rim + e, 1), :surf] = from_other[c, e : e + 1]
+            rows[pl.ds(base + (1 - parity) * rim + e, 1), :surf] = from_first[c, e : e + 1]
+            rows[pl.ds(base + parity * rim + e, 1), :surf] = from_second[c, e : e + 1]
 
     value = rows[...]
     high = value.astype(bf16)
     low = (value - high.astype(f32)).astype(bf16)
-    for part in range(2):
-        for n in range(FREQ // CHUNK):
-            columns = slice(part * FREQ + n * CHUNK, part * FREQ + (n + 1) * CHUNK)
-            t_high = table[:POINTS_PAD, columns]
-            t_low = table[POINTS_PAD:, columns]
-            x = jnp.dot(high, t_high, preferred_element_type=f32)
-            x = x + jnp.dot(low, t_high, preferred_element_type=f32)
-            x = x + jnp.dot(high, t_low, preferred_element_type=f32)
-            x = x.astype(bf16).astype(f32)
-            for m in range(CHUNK // LANES):
-                j = n * (CHUNK // LANES) + m
-                for g in range(row_count // 8):
-                    piece = x[g * 8 : (g + 1) * 8, m * LANES : (m + 1) * LANES]
-                    if j < MAIN:
-                        main[pl.ds((part * row_count + g * 8) * PITCH + j, 8, stride=PITCH), :] = piece
-                    else:
-                        c, s = divmod(g * 8, slots)
-                        tail[j - MAIN, pl.ds(s * TAIL_PITCH + part * comp_count + c, 8, stride=TAIL_PITCH), :] = piece
+    both = jnp.concatenate([high, low], axis=0)
+    for n in range(2 * FREQ // CHUNK):
+        columns = slice(n * CHUNK, (n + 1) * CHUNK)
+        x = jnp.dot(both, table[:POINTS_PAD, columns], preferred_element_type=f32)
+        x = x[:row_count] + x[row_count:]
+        x = x + jnp.dot(high, table[POINTS_PAD:, columns], preferred_element_type=f32)
+        x = x.astype(bf16).astype(f32)
+        for m in range(CHUNK // LANES):
+            part, j = divmod(n * (CHUNK // LANES) + m, TILES)
+            for g in range(row_count // 8):
+                piece = x[g * 8 : (g + 1) * 8, m * LANES : (m + 1) * LANES]
+                if j < MAIN:
+                    main[pl.ds((part * row_count + g * 8) * PITCH + j, 8, stride=PITCH), :] = piece
+                else:
+                    c, s = divmod(g * 8, slots)
+                    tail[j - MAIN, pl.ds(s * TAIL_PITCH + part * comp_count + c, 8, stride=TAIL_PITCH), :] = piece
 
 
 def interact_kernel(source, offset, hat, hat_tail, main, tail, total, total_tail):
@@ -180,7 +185,7 @@
 
         count = 2 * (comp_count * halves + TAIL)
         zero = jnp.zeros((8, LANES), f32)
-        accs = lax.fori_loop(0, list_count, pair, (zero,) * count, unroll=4)
+        accs = lax.fori_loop(0, list_count, pair, (zero,) * count, unroll=True)
         at = 0
         for c in range(comp_count):
             for h in range(halves):
@@ -199,32 +204,32 @@
 def inverse_kernel(total, total_tail, table, factor, out):
     comp_count, box_count, surf = out.shape
     f32, bf16 = jnp.float32, jnp.bfloat16
-    result = jnp.zeros((comp_count * box_count, 2 * POINTS_PAD), f32)
-    rest = jnp.zeros((comp_count * box_count, POINTS_PAD), f32)
     groups = box_count // 8
+    count = comp_count * box_count
     nt = (((1,), (1,)), ((), ()))
-    for part in range(2):
-        for n in range(FREQ // CHUNK):
-            columns = slice(part * FREQ + n * CHUNK, part * FREQ + (n + 1) * CHUNK)
-            lanes = []
-            for m in range(CHUNK // LANES):
-                j = n * (CHUNK // LANES) + m
-                pieces = []
-                for c in range(comp_count):
-                    for g in range(groups):
-                        if j < MAIN:
-                            row = (part * comp_count + c) * box_count + g * 8
-                            pieces.append(total[pl.ds(row * PITCH + j, 8, stride=PITCH), :])
-                        else:
-                            row = g * 8 * TAIL_PITCH + part * comp_count + c
-                            pieces.append(total_tail[j - MAIN, pl.ds(row, 8, stride=TAIL_PITCH), :])
-                lanes.append(jnp.concatenate(pieces, axis=0))
-            x = jnp.concatenate(lanes, axis=1) * factor[:, columns]
-            high = x.astype(bf16)
-            low = (x - high.astype(f32)).astype(bf16)
-            result += lax.dot_general(high, table[:, columns], nt, preferred_element_type=f32)
-            rest += lax.dot_general(low, table[:POINTS_PAD, columns], nt, preferred_element_type=f32)
-    result = result[:, :POINTS_PAD] + result[:, POINTS_PAD:] + rest
+    result = jnp.zeros((2 * POINTS_PAD, 2 * count), f32)
+    for n in range(2 * FREQ // PIECE):
+        lanes = []
+        for m in range(PIECE // LANES):
+            part, j = divmod(n * (PIECE // LANES) + m, TILES)
+            pieces = []
+            for c in range(comp_count):
+                for g in range(groups):
+                    if j < MAIN:
+                        row = (part * comp_count + c) * box_count + g * 8
+                        pieces.append(total[pl.ds(row * PITCH + j, 8, stride=PITCH), :])
+                    else:
+                        row = g * 8 * TAIL_PITCH + part * comp_count + c
+                        pieces.append(total_tail[j - MAIN, pl.ds(row, 8, stride=TAIL_PITCH), :])
+            lanes.append(jnp.concatenate(pieces, axis=0))
+        columns = slice(n * PIECE, (n + 1) * PIECE)
+        x = jnp.concatenate(lanes, axis=1) * factor[:, columns]
+        high = x.astype(bf16)
+        low = (x - high.astype(f32)).astype(bf16)
+        both = jnp.concatenate([high, low], axis=0)
+        result += lax.dot_general(table[:, columns], both, nt, preferred_element_type=f32)
+    result = result[:POINTS_PAD, :count] + result[:POINTS_PAD, count:] + result[POINTS_PAD:, :count]
+    result = result.T
     for c in range(comp_count):
         out[c] = result[c * box_count : (c + 1) * box_count, :surf]
 
@@ -239,22 +244,29 @@
     smem = pl.BlockSpec(memory_space=pltpu.SMEM)
     density = density.transpose(1, 0, 2)
 
-    groups = lax.axis_size("group")
-    high = max(cap, rim)
-    to_pair, to_other = pl.pallas_call(
+    boxes = jax.ShapeDtypeStruct((comp_count, cap, surf), f32)
+    side = jax.ShapeDtypeStruct((comp_count, rim, surf), f32)
+    to_near, *to_far, to_first, to_second = pl.pallas_call(
         pack_kernel,
-        out_shape=(
-            jax.ShapeDtypeStruct((2 * peers, comp_count, high, surf), f32),
-            jax.ShapeDtypeStruct((comp_count, rim, surf), f32),
-        ),
+        out_shape=(jax.ShapeDtypeStruct((2, *boxes.shape), f32),) + (boxes,) * (peers - 3) + (side,) * 2,
         in_specs=[vmem, smem, smem],
-        out_specs=(vmem, vmem),
+        out_specs=(vmem,) * peers,
         name="pack",
     )(density, send_list[0], halo_list[0])
-    pairs = [list(range(i, i + 2 * peers)) for i in range(0, groups * peers, 2 * peers)]
-    from_pair = lax.all_to_all(to_pair, ("group", "dev"), 0, 0, axis_index_groups=pairs, tiled=True)
-    swaps = [(i, i + 1) for i in range(1, groups - 1, 2)]
-    from_other = lax.ppermute(to_other, "group", swaps + [(j, i) for i, j in swaps])
+
+    def swap(x, k):
+        return lax.ppermute(x, "dev", [(i, i ^ k) for i in range(peers)])
+
+    def swap_groups(x, start):
+        pairs = [(i, i + 1) for i in range(start, lax.axis_size("group") - 1, 2)]
+        return lax.ppermute(x, "group", pairs + [(j, i) for i, j in pairs])
+
+    from_near = swap(to_near, 1)
+    from_far = [swap(x, k) for x, k in zip(to_far, (2, *range(4, peers)))]
+    from_first = swap_groups(to_first, 0)
+    from_second = swap_groups(to_second, 1)
+    by_part, near = lax.optimization_barrier((kernel_hat.transpose(1, 0, 2), from_near))
+    relayed = swap(near, 2)
 
     offsets = kernel_hat.shape[0]
     padded = -(-offsets // 8) * 8
@@ -269,24 +281,25 @@
         compiler_params=pltpu.CompilerParams(vmem_limit_bytes=16 * 1024 * 1024),
         cost_estimate=pl.CostEstimate(flops=kernel_hat.size, bytes_accessed=6 * kernel_hat.size, transcendentals=0),
         name="prepare",
-    )(kernel_hat.transpose(1, 0, 2))
+    )(by_part)
 
     slots = box_count + peers * cap + 2 * rim
     row_count = comp_count * slots
     params = pltpu.CompilerParams(vmem_limit_bytes=24 * 1024 * 1024)
     table = jnp.asarray(table)
+    arrays = (send_list[0], density, from_near, relayed, *from_far, from_first, from_second, table)
     main, tail = pl.pallas_call(
         forward_kernel,
         out_shape=(
             jax.ShapeDtypeStruct((2 * row_count * PITCH, LANES), f32),
             jax.ShapeDtypeStruct((TAIL, (slots + 2) * TAIL_PITCH, LANES), f32),
         ),
-        in_specs=[vmem, smem, vmem, vmem, vmem],
+        in_specs=[smem] + [vmem] * (len(arrays) - 1),
         out_specs=(vmem, vmem),
         scratch_shapes=[pltpu.VMEM((row_count, POINTS_PAD), f32)],
         compiler_params=params,
         name="forward",
-    )(density, send_list[0], from_pair, from_other, table)
+    )(*arrays)
     total, total_tail = pl.pallas_call(
         interact_kernel,
         out_shape=(

time: 30.2 us -> 26.3 us (0.87)
  local copies, waits for them, and re-layouts: 7.8 us -> 2.15 us
  waiting for transfers between devices: 0.01 us -> 1.17 us
  Pallas kernels: 13.3 us -> 14 us
    unnamed x21 -> x19, local copies, waits for them, and re-layouts: 7.8 us -> 2.15 us
    ppermute x1 -> x5, starting transfers between devices: 3.37 us -> 8.63 us  [the longest x2 4.99 us: swap_groups(): return lax.ppermute(x, 'group', pairs + [(j, i) for i, j in pairs])]
    all_to_all x1 -> x0, starting transfers between devices: 5.23 us -> none  [on_device(): lax.all_to_all(to_pair, ('group', 'dev'), 0, 0, axis_index_groups=pairs,...]
    pallas_call x1, Pallas kernels: 6.13 us -> 8.55 us  [on_device(): pl.pallas_call(interact_kernel, out_shape=(jax.ShapeDtypeStruct((2 * comp...]
    pallas_call x1, Pallas kernels: 1.65 us -> 0.46 us  [on_device(): pl.pallas_call(prepare_kernel, out_shape=(jax.ShapeDtypeStruct((2 * padde...]
    ppermute x1 -> x5, waiting for transfers between devices: 0.01 us -> 1.17 us  [the longest x2 1.16 us: swap_groups(): return lax.ppermute(x, 'group', pairs + [(j, i) for i, j in pairs])]
    pallas_call x1, Pallas kernels: 2.02 us -> 1.65 us  [on_device(): pl.pallas_call(inverse_kernel, out_shape=jax.ShapeDtypeStruct((comp_count...]
  transfers between devices with their start and end apart: 2 -> 5, of which waited for: 0 -> 1; matrix products, arithmetic and copies ran while one was open for 7% -> 8% of each run, Pallas kernels for 6% -> 2%
where the time goes in v5:
time: 26.3 us; the launch traced here: 26.1 us
  Pallas kernels  14 us (53%)
  starting transfers between devices  8.63 us (33%)
  local copies, waits for them, and re-layouts  2.15 us (8%)
  waiting for transfers between devices  1.17 us (4%)
    pallas_call x1, Pallas kernels, on_device(): pl.pallas_call(interact_kernel, out_shape=(jax.ShapeDtypeStruct((2 * comp...  8.55 us
    ppermute x2, starting transfers between devices, swap_groups(): return lax.ppermute(x, 'group', pairs + [(j, i) for i, j in pairs])  4.99 us
    ppermute x3, starting transfers between devices, swap(): return lax.ppermute(x, 'dev', [(i, i ^ k) for i in range(peers)])  3.64 us
    unnamed x19, local copies, waits for them, and re-layouts  2.15 us
    pallas_call x1, Pallas kernels, on_device(): pl.pallas_call(forward_kernel, out_shape=(jax.ShapeDtypeStruct((2 * row_c...  1.76 us
    pallas_call x1, Pallas kernels, on_device(): pl.pallas_call(inverse_kernel, out_shape=jax.ShapeDtypeStruct((comp_count...  1.65 us
    pallas_call x1, Pallas kernels, on_device(): pl.pallas_call(pack_kernel, out_shape=(jax.ShapeDtypeStruct((2, *boxes.sh...  1.59 us
    ppermute x2, waiting for transfers between devices, swap_groups(): return lax.ppermute(x, 'group', pairs + [(j, i) for i, j in pairs])  1.16 us
  transfers between devices with their start and end apart: 5, of which 1 were waited for; matrix products, arithmetic and copies ran while one was open for 8% of the time, Pallas kernels for 2%

profile of v5, /device:TPU:1, one launch (start us, length us, event | category | flops | bytes accessed | tf_op | source)
XLA Modules:
  0.0 26.1 jit_solution(9701142178435930005)
XLA Ops:
  0.0 1.6 %pack.1 = (f32[2,3,4,152]{3,2,1,0:T(4,128)}, f32[3,4,152]{2,1,0:T(4,128)}, f32[3,4,152]{2,1,0:T(4,128)}, f32[3,4,152]{2,1,0:T(4,128)}) custom-call(f32[3,16,152]{2,1,0:T(8,128)} %bitcast.8, s32[4,4]{1,0:T(4,128)} %bitcast.10, s32[2,4]{1,0:T(2,128)} %bitcast.12), custom_call_target="tpu_custom_call" | custom-call | tf_op jit(solution)/shard_map/pack/pallas_call | solution.py:249
  1.6 0.0 copy-start.8
  1.6 0.0 copy-start.7
  1.6 0.0 copy-start.6
  1.6 0.0 copy-start
  1.6 0.0 copy-start.1
  1.6 0.0 copy-start.3
  1.6 2.1 %collective-permute-start = (f32[2,3,4,152]{3,2,1,0:T(4,128)}, f32[2,3,4,152]{3,2,1,0:T(4,128)S(1)}, u32[]{:S(2)}, u32[]{:S(2)}) collective-permute-start(f32[2,3,4,152]{3,2,1,0:T(4,128)} %get-tuple-element.17), channel_id=1, source_target_pairs={{0,1},{1,0},{2,3},{3,2},{4,5},{5,4},{6,7},{7,6},{8,9},{9,8},{10,11... | collective-permute-start | bytes 43784 | tf_op jit(solution)/shard_map/ppermute | solution.py:258
  3.8 2.1 %copy.11 = bf16[316,2,2304]{2,0,1:T(8,128)(2,1)S(1)} copy(bf16[316,2,2304]{2,1,0:T(2,128)(2,1)} %param.9) | data formatting | bytes 5824512 | tf_op args[1]
  5.9 0.0 collective-permute-done.from_near
  5.9 1.3 %collective-permute-start.1 = (f32[2,3,4,152]{3,2,1,0:T(4,128)S(1)}, f32[2,3,4,152]{3,2,1,0:T(4,128)S(1)}, u32[]{:S(2)}, u32[]{:S(2)}) collective-permute-start(f32[2,3,4,152]{3,2,1,0:T(4,128)S(1)} %collective-permute-done.from_near), channel_id=1, source_target_pairs={{0,2},{1,3},{2,0},{3,1},{4,6},{5,7},{6,4},{7,5},{8,10},{9,11},{10,... | collective-permute-start | bytes 43784 | tf_op jit(solution)/shard_map/ppermute | solution.py:258
  7.2 0.0 copy-done.8
  7.2 0.2 collective-permute-start.2
  7.4 0.0 copy-done.7
  7.4 1.5 %collective-permute-start.3 = (f32[3,4,152]{2,1,0:T(4,128)S(1)}, f32[3,4,152]{2,1,0:T(4,128)S(1)}, u32[]{:S(2)}, u32[]{:S(2)}) collective-permute-start(f32[3,4,152]{2,1,0:T(4,128)S(1)} %copy-done.7), channel_id=1, source_target_pairs={{0,4},{8,12},{16,20},{24,28},{4,0},{12,8},{20,16},{28,24},{1,5},{9... | collective-permute-start | bytes 21896 | tf_op jit(solution)/shard_map/ppermute | solution.py:262
  8.9 0.0 copy-done.6
  8.9 3.5 %collective-permute-start.4 = (f32[3,4,152]{2,1,0:T(4,128)S(1)}, f32[3,4,152]{2,1,0:T(4,128)S(1)}, u32[]{:S(2)}, u32[]{:S(2)}) collective-permute-start(f32[3,4,152]{2,1,0:T(4,128)S(1)} %copy-done.6), channel_id=1, source_target_pairs={{4,8},{12,16},{20,24},{8,4},{16,12},{24,20},{5,9},{13,17},{21,25},... | collective-permute-start | bytes 21896 | tf_op jit(solution)/shard_map/ppermute | solution.py:262
  12.4 0.5 %prepare.1 = (f32[10880,128]{1,0:T(8,128)S(1)}, f32[1280,128]{1,0:T(8,128)S(1)}) custom-call(bf16[2,316,2304]{2,1,0:T(8,128)(2,1)S(1)} %bitcast.7), custom_call_target="tpu_custom_call" | custom-call | flops 1456128 | bytes 8736768 | tf_op jit(solution)/shard_map/prepare/pallas_call | solution.py:273
  12.9 0.0 collective-permute-done.2.refs_0_
  12.9 0.0 collective-permute-done.3.refs_1_
  12.9 1.2 %collective-permute-done.4.refs_2_ = f32[3,4,152]{2,1,0:T(4,128)S(1)} collective-permute-done((f32[3,4,152]{2,1,0:T(4,128)S(1)}, f32[3,4,152]{2,1,0:T(4,128)S(1)}, u32[]{:S(2)}, u32[]{:S(2)}) %collective-permute-start.4) | collective-permute-done | bytes 7328 | tf_op jit(solution)/shard_map/ppermute | solution.py:262
  14.1 0.0 collective-permute-done.1.relayed
  14.1 0.0 copy-done
  14.1 0.0 copy-done.1
  14.1 0.0 copy-done.3
  14.1 1.8 %forward.1 = (f32[4080,128]{1,0:T(8,128)S(1)}, f32[2,294,128]{2,1,0:T(8,128)S(1)}) custom-call(s32[4,4]{1,0:T(4,128)S(1)} %bitcast.11, f32[3,16,152]{2,1,0:T(8,128)S(1)} %bitcast.9, f32[2,3,4,152]{3,2,1,0:T(4,128)S(1)} %collective-permute-done.from_near, f32[2,3,4,152]{3,2,1,0:T(4,128)S(1)} %collective-permute-done.1.relayed, ...), custom_call_target="tpu_custom_call" | custom-call | tf_op jit(solution)/shard_map/forward/pallas_call | solution.py:291
  15.9 0.0 copy-done.4
  15.9 0.0 copy-done.5
  15.9 0.0 copy-start.2
  15.9 8.5 %interact.1 = (f32[1632,128]{1,0:T(8,128)S(1)}, f32[2,126,128]{2,1,0:T(8,128)S(1)}) custom-call(s32[16,32]{1,0:T(8,128)S(1)} %copy-done.4, s32[16,32]{1,0:T(8,128)S(1)} %copy-done.5, f32[10880,128]{1,0:T(8,128)S(1)} %get-tuple-element.19.hat, f32[1280,128]{1,0:T(8,128)S(1)} %get-tuple-element.20.hat_tail, f32[4080,128]{1,0:T(8,128)S(1)} %get-tuple-element.25.main, ...), custom_call_target="tpu_custom_call" | custom-call | tf_op jit(solution)/shard_map/interact/pallas_call | solution.py:303
  24.4 0.0 copy-done.2
  24.5 1.6 %inverse.1 = f32[3,16,152]{2,1,0:T(8,128)} custom-call(f32[1632,128]{1,0:T(8,128)S(1)} %get-tuple-element.27.total, f32[2,126,128]{2,1,0:T(8,128)S(1)} %get-tuple-element.28.total_tail, bf16[320,4608]{1,0:T(8,128)(2,1)S(1)} %copy-done, f32[1,4608]{1,0:T(1,128)S(1)} %copy-done.2), custom_call_target="tpu_custom_call" | custom-call | tf_op jit(solution)/shard_map/inverse/pallas_call | solution.py:314
  (2 shorter events, 0.0 us)
Async XLA Ops:
  1.6 5.6 %copy-start.8 = (f32[3,4,152]{2,1,0:T(4,128)S(1)}, f32[3,4,152]{2,1,0:T(4,128)}, u32[]{:S(2)}) copy-start(f32[3,4,152]{2,1,0:T(4,128)} %get-tuple-element.22) | copy-start | bytes 21892
  1.6 5.8 %copy-start.7 = (f32[3,4,152]{2,1,0:T(4,128)S(1)}, f32[3,4,152]{2,1,0:T(4,128)}, u32[]{:S(2)}) copy-start(f32[3,4,152]{2,1,0:T(4,128)} %get-tuple-element.23) | copy-start | bytes 21892
  1.6 7.3 %copy-start.6 = (f32[3,4,152]{2,1,0:T(4,128)S(1)}, f32[3,4,152]{2,1,0:T(4,128)}, u32[]{:S(2)}) copy-start(f32[3,4,152]{2,1,0:T(4,128)} %get-tuple-element.24) | copy-start | bytes 21892
  1.6 12.5 %copy-start = (bf16[320,4608]{1,0:T(8,128)(2,1)S(1)}, bf16[320,4608]{1,0:T(8,128)(2,1)}, u32[]{:S(2)}) copy-start(bf16[320,4608]{1,0:T(8,128)(2,1)} %constant.4.clone.refs_3_.table) | copy-start | bytes 8847364
  1.6 12.5 %copy-start.1 = (f32[16,3,152]{2,0,1:T(8,128)S(1)}, f32[16,3,152]{2,0,1:T(8,128)}, u32[]{:S(2)}) copy-start(f32[16,3,152]{2,0,1:T(8,128)} %param.8) | copy-start | bytes 87556
  1.6 12.4 %copy-start.3 = (s32[1,4,4]{2,1,0:T(4,128)S(1)}, s32[1,4,4]{2,1,0:T(4,128)}, u32[]{:S(2)}) copy-start(s32[1,4,4]{2,1,0:T(4,128)} %param.10) | copy-start | bytes 196
  1.6 4.2 %collective-permute-start = (f32[2,3,4,152]{3,2,1,0:T(4,128)}, f32[2,3,4,152]{3,2,1,0:T(4,128)S(1)}, u32[]{:S(2)}, u32[]{:S(2)}) collective-permute-start(f32[2,3,4,152]{3,2,1,0:T(4,128)} %get-tuple-element.17), channel_id=1, source_target_pairs={{0,1},{1,0},{2,3},{3,2},{4,5},{5,4},{6,7},{7,6},{8,9},{9,8},{10,11... | collective-permute-start | bytes 43784 | tf_op jit(solution)/shard_map/ppermute | solution.py:258
  5.9 8.2 %collective-permute-start.1 = (f32[2,3,4,152]{3,2,1,0:T(4,128)S(1)}, f32[2,3,4,152]{3,2,1,0:T(4,128)S(1)}, u32[]{:S(2)}, u32[]{:S(2)}) collective-permute-start(f32[2,3,4,152]{3,2,1,0:T(4,128)S(1)} %collective-permute-done.from_near), channel_id=1, source_target_pairs={{0,2},{1,3},{2,0},{3,1},{4,6},{5,7},{6,4},{7,5},{8,10},{9,11},{10,... | collective-permute-start | bytes 43784 | tf_op jit(solution)/shard_map/ppermute | solution.py:258
  7.2 5.7 %collective-permute-start.2 = (f32[3,4,152]{2,1,0:T(4,128)S(1)}, f32[3,4,152]{2,1,0:T(4,128)S(1)}, u32[]{:S(2)}, u32[]{:S(2)}) collective-permute-start(f32[3,4,152]{2,1,0:T(4,128)S(1)} %copy-done.8), channel_id=1, source_target_pairs={{0,2},{1,3},{2,0},{3,1},{4,6},{5,7},{6,4},{7,5},{8,10},{9,11},{10,... | collective-permute-start | bytes 21896 | tf_op jit(solution)/shard_map/ppermute | solution.py:258
  7.4 5.5 %collective-permute-start.3 = (f32[3,4,152]{2,1,0:T(4,128)S(1)}, f32[3,4,152]{2,1,0:T(4,128)S(1)}, u32[]{:S(2)}, u32[]{:S(2)}) collective-permute-start(f32[3,4,152]{2,1,0:T(4,128)S(1)} %copy-done.7), channel_id=1, source_target_pairs={{0,4},{8,12},{16,20},{24,28},{4,0},{12,8},{20,16},{28,24},{1,5},{9... | collective-permute-start | bytes 21896 | tf_op jit(solution)/shard_map/ppermute | solution.py:262
  8.9 6.9 %copy-start.4 = (s32[16,32]{1,0:T(8,128)S(1)}, s32[16,32]{1,0:T(8,128)}, u32[]{:S(2)}) copy-start(s32[16,32]{1,0:T(8,128)} %source.1) | copy-start | bytes 6148
  8.9 6.9 %copy-start.5 = (s32[16,32]{1,0:T(8,128)S(1)}, s32[16,32]{1,0:T(8,128)}, u32[]{:S(2)}) copy-start(s32[16,32]{1,0:T(8,128)} %offset.1) | copy-start | bytes 6148
  8.9 5.1 %collective-permute-start.4 = (f32[3,4,152]{2,1,0:T(4,128)S(1)}, f32[3,4,152]{2,1,0:T(4,128)S(1)}, u32[]{:S(2)}, u32[]{:S(2)}) collective-permute-start(f32[3,4,152]{2,1,0:T(4,128)S(1)} %copy-done.6), channel_id=1, source_target_pairs={{4,8},{12,16},{20,24},{8,4},{16,12},{24,20},{5,9},{13,17},{21,25},... | collective-permute-start | bytes 21896 | tf_op jit(solution)/shard_map/ppermute | solution.py:262
  15.9 8.6 %copy-start.2 = (f32[1,4608]{1,0:T(1,128)S(1)}, f32[1,4608]{1,0:T(1,128)}, u32[]{:S(2)}) copy-start(f32[1,4608]{1,0:T(1,128)} %constant.5.clone.factor) | copy-start | bytes 55300

commit v6 on v5

--- a/solution.py
+++ b/solution.py
@@ -20,6 +20,7 @@
 TAIL = TILES - MAIN
 PITCH = MAIN + 1
 TAIL_PITCH = 7
+HAT_ROWS = 2 * TILES + 1
 POINTS_PAD = 160
 CHUNK = 256
 PIECE = 512
@@ -54,6 +55,16 @@
     return np.concatenate([high, low], axis=0), factor
 
 
+def source_rows(comp_count):
+    return (2 * comp_count * MAIN + TAIL * 8) | 1
+
+
+def source_row(comp_count, which, tile):
+    if tile < MAIN:
+        return which * MAIN + tile
+    return 2 * comp_count * MAIN + (tile - MAIN) * 8 + which
+
+
 def pack_kernel(density, send_list, halo_list, *outs):
     peers, cap = send_list.shape
     rim = halo_list.shape[1]
@@ -71,9 +82,8 @@
             to_second[c, e : e + 1, :] = density[c, pl.ds(halo_list[parity, e], 1), :]
 
 
-def prepare_kernel(kernel_hat, hat, hat_tail):
+def prepare_kernel(kernel_hat, hat):
     parts, count, _ = kernel_hat.shape
-    padded = hat_tail.shape[0] // (parts * TAIL)
 
     def move(first, height):
         for part in range(parts):
@@ -82,12 +92,8 @@
                 for g in range(0, height, 8):
                     size = min(8, height - g)
                     piece = x[g : g + size]
-                    if j < MAIN:
-                        row = (part * padded + first + g) * PITCH + j
-                        hat[pl.ds(row, size, stride=PITCH), :] = piece
-                    else:
-                        row = (part * TAIL + j - MAIN) * padded + first + g
-                        hat_tail[pl.ds(row, size), :] = piece
+                    row = (first + g) * HAT_ROWS + part * TILES + j
+                    hat[pl.ds(row, size, stride=HAT_ROWS), :] = piece
 
     whole = count // 16
 
@@ -100,12 +106,13 @@
 
 
 def forward_kernel(send_list, density, from_near, relayed, *refs):
-    *from_far, from_first, from_second, table, main, tail, rows = refs
+    *from_far, from_first, from_second, table, main, rows = refs
     comp_count, box_count, surf = density.shape
     peers, cap = send_list.shape
     rim = from_first.shape[1]
     row_count = rows.shape[0]
     slots = row_count // comp_count
+    pitch = source_rows(comp_count)
     f32, bf16 = jnp.float32, jnp.bfloat16
 
     member = lax.axis_index("dev")
@@ -140,19 +147,14 @@
             part, j = divmod(n * (CHUNK // LANES) + m, TILES)
             for g in range(row_count // 8):
                 piece = x[g * 8 : (g + 1) * 8, m * LANES : (m + 1) * LANES]
-                if j < MAIN:
-                    main[pl.ds((part * row_count + g * 8) * PITCH + j, 8, stride=PITCH), :] = piece
-                else:
-                    c, s = divmod(g * 8, slots)
-                    tail[j - MAIN, pl.ds(s * TAIL_PITCH + part * comp_count + c, 8, stride=TAIL_PITCH), :] = piece
-
-
-def interact_kernel(source, offset, hat, hat_tail, main, tail, total, total_tail):
+                c, s = divmod(g * 8, slots)
+                row = source_row(comp_count, part * comp_count + c, j)
+                main[pl.ds(s * pitch + row, 8, stride=pitch), :] = piece
+
+
+def interact_kernel(comp_count, source, offset, hat, main, total, total_tail):
     box_count, list_count = source.shape
-    padded = hat_tail.shape[0] // (2 * TAIL)
-    row_count = main.shape[0] // (2 * PITCH)
-    slots = tail.shape[1] // TAIL_PITCH - 2
-    comp_count = row_count // slots
+    pitch = source_rows(comp_count)
     f32 = jnp.float32
     plus = lax.broadcasted_iota(jnp.int32, (8, LANES), 0) < comp_count
     halves = MAIN // 8
@@ -160,24 +162,22 @@
     @pl.loop(0, box_count)
     def _(t):
         def pair(w, accs):
-            s = source[t, w]
-            o = offset[t, w]
-            k = [
-                [hat[pl.ds((r * padded + o) * PITCH + 8 * h, 8), :] for h in range(halves)] for r in range(2)
-            ]
+            s = source[t, w] * pitch
+            o = offset[t, w] * HAT_ROWS
+            k = [[hat[pl.ds(o + (r * TILES + 8 * h), 8), :] for h in range(halves)] for r in range(2)]
             accs = list(accs)
             at = 0
             for c in range(comp_count):
                 for h in range(halves):
-                    s_re = main[pl.ds((c * slots + s) * PITCH + 8 * h, 8), :]
-                    s_im = main[pl.ds((row_count + c * slots + s) * PITCH + 8 * h, 8), :]
+                    s_re = main[pl.ds(s + (source_row(comp_count, c, 8 * h)), 8), :]
+                    s_im = main[pl.ds(s + (source_row(comp_count, comp_count + c, 8 * h)), 8), :]
                     accs[at] = accs[at] + (k[0][h] * s_re - k[1][h] * s_im)
                     accs[at + 1] = accs[at + 1] + (k[0][h] * s_im + k[1][h] * s_re)
                     at += 2
-            for j in range(TAIL):
-                x = tail[j, pl.ds(s * TAIL_PITCH, 8), :]
-                k_re = hat_tail[pl.ds(j * padded + o, 8, stride=0), :]
-                k_im = hat_tail[pl.ds((TAIL + j) * padded + o, 8, stride=0), :]
+            for j in range(MAIN, TILES):
+                x = main[pl.ds(s + source_row(comp_count, 0, j), 8), :]
+                k_re = hat[pl.ds(o + j, 8, stride=0), :]
+                k_im = hat[pl.ds(o + TILES + j, 8, stride=0), :]
                 accs[at] = accs[at] + k_re * x
                 accs[at + 1] = accs[at + 1] + k_im * x
                 at += 2
@@ -185,7 +185,7 @@
 
         count = 2 * (comp_count * halves + TAIL)
         zero = jnp.zeros((8, LANES), f32)
-        accs = lax.fori_loop(0, list_count, pair, (zero,) * count, unroll=True)
+        accs = lax.fori_loop(0, list_count, pair, (zero,) * count, unroll=4)
         at = 0
         for c in range(comp_count):
             for h in range(halves):
@@ -269,15 +269,11 @@
     relayed = swap(near, 2)
 
     offsets = kernel_hat.shape[0]
-    padded = -(-offsets // 8) * 8
-    hat, hat_tail = pl.pallas_call(
+    hat = pl.pallas_call(
         prepare_kernel,
-        out_shape=(
-            jax.ShapeDtypeStruct((2 * padded * PITCH, LANES), f32),
-            jax.ShapeDtypeStruct((2 * TAIL * padded, LANES), f32),
-        ),
+        out_shape=jax.ShapeDtypeStruct((offsets * HAT_ROWS + 8, LANES), f32),
         in_specs=[vmem],
-        out_specs=(vmem, vmem),
+        out_specs=vmem,
         compiler_params=pltpu.CompilerParams(vmem_limit_bytes=16 * 1024 * 1024),
         cost_estimate=pl.CostEstimate(flops=kernel_hat.size, bytes_accessed=6 * kernel_hat.size, transcendentals=0),
         name="prepare",
@@ -288,29 +284,26 @@
     params = pltpu.CompilerParams(vmem_limit_bytes=24 * 1024 * 1024)
     table = jnp.asarray(table)
     arrays = (send_list[0], density, from_near, relayed, *from_far, from_first, from_second, table)
-    main, tail = pl.pallas_call(
+    main = pl.pallas_call(
         forward_kernel,
-        out_shape=(
-            jax.ShapeDtypeStruct((2 * row_count * PITCH, LANES), f32),
-            jax.ShapeDtypeStruct((TAIL, (slots + 2) * TAIL_PITCH, LANES), f32),
-        ),
+        out_shape=jax.ShapeDtypeStruct((slots * source_rows(comp_count) + 8, LANES), f32),
         in_specs=[smem] + [vmem] * (len(arrays) - 1),
-        out_specs=(vmem, vmem),
+        out_specs=vmem,
         scratch_shapes=[pltpu.VMEM((row_count, POINTS_PAD), f32)],
         compiler_params=params,
         name="forward",
     )(*arrays)
     total, total_tail = pl.pallas_call(
-        interact_kernel,
+        functools.partial(interact_kernel, comp_count),
         out_shape=(
             jax.ShapeDtypeStruct((2 * comp_count * box_count * PITCH, LANES), f32),
             jax.ShapeDtypeStruct((TAIL, (box_count + 2) * TAIL_PITCH, LANES), f32),
         ),
-        in_specs=[smem, smem] + [vmem] * 4,
+        in_specs=[smem, smem] + [vmem] * 2,
         out_specs=(vmem, vmem),
         compiler_params=params,
         name="interact",
-    )(inter_src, inter_off, hat, hat_tail, main, tail)
+    )(inter_src, inter_off, hat, main)
     potential = pl.pallas_call(
         inverse_kernel,
         out_shape=jax.ShapeDtypeStruct((comp_count, box_count, surf), f32),

time: 26.3 us -> 24 us (0.913)
  Pallas kernels: 14 us -> 11.6 us
  starting transfers between devices: 8.63 us -> 8.9 us
    pallas_call x3, Pallas kernels: 10.8 us -> 8.35 us  [the longest x1 6.13 us: on_device(): pl.pallas_call(functools.partial(interact_kernel, comp_count), out_shape=...]
    ppermute x2, starting transfers between devices: 4.99 us -> 5.26 us  [swap_groups(): return lax.ppermute(x, 'group', pairs + [(j, i) for i, j in pairs])]
  transfers between devices with their start and end apart: 5 -> 5, of which waited for: 1 -> 1; matrix products, arithmetic and copies ran while one was open for 8% -> 9% of each run, Pallas kernels for 2% -> 2%
where the time goes in v6:
time: 24 us; the launch traced here: 23.8 us
  Pallas kernels  11.6 us (48%)
  starting transfers between devices  8.9 us (37%)
  local copies, waits for them, and re-layouts  2.15 us (9%)
  waiting for transfers between devices  1.02 us (4%)
    pallas_call x1, Pallas kernels, on_device(): pl.pallas_call(functools.partial(interact_kernel, comp_count), out_shape=...  6.13 us
    ppermute x2, starting transfers between devices, swap_groups(): return lax.ppermute(x, 'group', pairs + [(j, i) for i, j in pairs])  5.26 us
    ppermute x3, starting transfers between devices, swap(): return lax.ppermute(x, 'dev', [(i, i ^ k) for i in range(peers)])  3.64 us
    unnamed x19, local copies, waits for them, and re-layouts  2.15 us
    pallas_call x1, Pallas kernels, on_device(): pl.pallas_call(forward_kernel, out_shape=jax.ShapeDtypeStruct((slots * so...  1.76 us
    pallas_call x1, Pallas kernels, on_device(): pl.pallas_call(inverse_kernel, out_shape=jax.ShapeDtypeStruct((comp_count...  1.66 us
    pallas_call x1, Pallas kernels, on_device(): pl.pallas_call(pack_kernel, out_shape=(jax.ShapeDtypeStruct((2, *boxes.sh...  1.6 us
    ppermute x2, waiting for transfers between devices, swap_groups(): return lax.ppermute(x, 'group', pairs + [(j, i) for i, j in pairs])  1.01 us
  transfers between devices with their start and end apart: 5, of which 1 were waited for; matrix products, arithmetic and copies ran while one was open for 9% of the time, Pallas kernels for 2%

profile of v6, /device:TPU:1, one launch (start us, length us, event | category | flops | bytes accessed | tf_op | source)
XLA Modules:
  0.0 23.8 jit_solution(8632952559363098424)
XLA Ops:
  0.0 1.6 %pack.1 = (f32[2,3,4,152]{3,2,1,0:T(4,128)}, f32[3,4,152]{2,1,0:T(4,128)}, f32[3,4,152]{2,1,0:T(4,128)}, f32[3,4,152]{2,1,0:T(4,128)}) custom-call(f32[3,16,152]{2,1,0:T(8,128)} %bitcast.8, s32[4,4]{1,0:T(4,128)} %bitcast.10, s32[2,4]{1,0:T(2,128)} %bitcast.12), custom_call_target="tpu_custom_call" | custom-call | tf_op jit(solution)/shard_map/pack/pallas_call | solution.py:249
  1.6 0.0 copy-start.8
  1.6 0.0 copy-start.7
  1.6 0.0 copy-start.6
  1.6 2.1 %collective-permute-start = (f32[2,3,4,152]{3,2,1,0:T(4,128)}, f32[2,3,4,152]{3,2,1,0:T(4,128)S(1)}, u32[]{:S(2)}, u32[]{:S(2)}) collective-permute-start(f32[2,3,4,152]{3,2,1,0:T(4,128)} %get-tuple-element.13), channel_id=1, source_target_pairs={{0,1},{1,0},{2,3},{3,2},{4,5},{5,4},{6,7},{7,6},{8,9},{9,8},{10,11... | collective-permute-start | bytes 43784 | tf_op jit(solution)/shard_map/ppermute | solution.py:258
  3.7 2.1 %copy.11 = bf16[316,2,2304]{2,0,1:T(8,128)(2,1)S(1)} copy(bf16[316,2,2304]{2,1,0:T(2,128)(2,1)} %param.9) | data formatting | bytes 5824512 | tf_op args[1]
  5.8 0.0 collective-permute-done.from_near
  5.8 1.3 %collective-permute-start.1 = (f32[2,3,4,152]{3,2,1,0:T(4,128)S(1)}, f32[2,3,4,152]{3,2,1,0:T(4,128)S(1)}, u32[]{:S(2)}, u32[]{:S(2)}) collective-permute-start(f32[2,3,4,152]{3,2,1,0:T(4,128)S(1)} %collective-permute-done.from_near), channel_id=1, source_target_pairs={{0,2},{1,3},{2,0},{3,1},{4,6},{5,7},{6,4},{7,5},{8,10},{9,11},{10,... | collective-permute-start | bytes 43784 | tf_op jit(solution)/shard_map/ppermute | solution.py:258
  7.1 0.0 copy-done.8
  7.1 0.2 collective-permute-start.2
  7.4 0.0 copy-done.7
  7.4 1.5 %collective-permute-start.3 = (f32[3,4,152]{2,1,0:T(4,128)S(1)}, f32[3,4,152]{2,1,0:T(4,128)S(1)}, u32[]{:S(2)}, u32[]{:S(2)}) collective-permute-start(f32[3,4,152]{2,1,0:T(4,128)S(1)} %copy-done.7), channel_id=1, source_target_pairs={{0,4},{8,12},{16,20},{24,28},{4,0},{12,8},{20,16},{28,24},{1,5},{9... | collective-permute-start | bytes 21896 | tf_op jit(solution)/shard_map/ppermute | solution.py:262
  8.9 0.0 copy-done.6
  8.9 0.0 copy-start
  8.9 3.7 %collective-permute-start.4 = (f32[3,4,152]{2,1,0:T(4,128)S(1)}, f32[3,4,152]{2,1,0:T(4,128)S(1)}, u32[]{:S(2)}, u32[]{:S(2)}) collective-permute-start(f32[3,4,152]{2,1,0:T(4,128)S(1)} %copy-done.6), channel_id=1, source_target_pairs={{4,8},{12,16},{20,24},{8,4},{16,12},{24,20},{5,9},{13,17},{21,25},... | collective-permute-start | bytes 21896 | tf_op jit(solution)/shard_map/ppermute | solution.py:262
  12.7 0.5 %prepare.1.hat = f32[11700,128]{1,0:T(8,128)S(1)} custom-call(bf16[2,316,2304]{2,1,0:T(8,128)(2,1)S(1)} %bitcast.7), custom_call_target="tpu_custom_call" | custom-call | flops 1456128 | bytes 8736768 | tf_op jit(solution)/shard_map/prepare/pallas_call | solution.py:272
  13.1 0.0 copy-start.4
  13.1 0.0 copy-start.5
  13.2 0.0 collective-permute-done.2.refs_0_
  13.2 0.0 collective-permute-done.3.refs_1_
  13.2 1.0 %collective-permute-done.4.refs_2_ = f32[3,4,152]{2,1,0:T(4,128)S(1)} collective-permute-done((f32[3,4,152]{2,1,0:T(4,128)S(1)}, f32[3,4,152]{2,1,0:T(4,128)S(1)}, u32[]{:S(2)}, u32[]{:S(2)}) %collective-permute-start.4) | collective-permute-done | bytes 7328 | tf_op jit(solution)/shard_map/ppermute | solution.py:262
  14.2 0.0 collective-permute-done.1.relayed
  14.2 0.0 copy-done
  14.2 0.0 copy-done.1
  14.2 0.0 copy-done.3
  14.2 1.8 %forward.1.main = f32[4528,128]{1,0:T(8,128)S(1)} custom-call(s32[4,4]{1,0:T(4,128)S(1)} %bitcast.11, f32[3,16,152]{2,1,0:T(8,128)S(1)} %bitcast.9, f32[2,3,4,152]{3,2,1,0:T(4,128)S(1)} %collective-permute-done.from_near, f32[2,3,4,152]{3,2,1,0:T(4,128)S(1)} %collective-permute-done.1.relayed, f32[3,4,152]{2,1,0:T(4,128)S(1)} %collective-permute-done.2.refs_0_, ...), custom_call_target="tpu_custom_call" | custom-call | tf_op jit(solution)/shard_map/forward/pallas_call | solution.py:287
  16.0 0.0 copy-done.4
  16.0 0.0 copy-done.5
  16.0 0.0 copy-start.2
  16.0 6.1 %interact.1 = (f32[1632,128]{1,0:T(8,128)S(1)}, f32[2,126,128]{2,1,0:T(8,128)S(1)}) custom-call(s32[16,32]{1,0:T(8,128)S(1)} %copy-done.4, s32[16,32]{1,0:T(8,128)S(1)} %copy-done.5, f32[11700,128]{1,0:T(8,128)S(1)} %prepare.1.hat, f32[4528,128]{1,0:T(8,128)S(1)} %forward.1.main), custom_call_target="tpu_custom_call" | custom-call | tf_op jit(solution)/shard_map/interact/pallas_call | solution.py:296
  22.1 0.0 copy-done.2
  22.1 1.7 %inverse.1 = f32[3,16,152]{2,1,0:T(8,128)} custom-call(f32[1632,128]{1,0:T(8,128)S(1)} %get-tuple-element.19.total, f32[2,126,128]{2,1,0:T(8,128)S(1)} %get-tuple-element.20.total_tail, bf16[320,4608]{1,0:T(8,128)(2,1)S(1)} %copy-done, f32[1,4608]{1,0:T(1,128)S(1)} %copy-done.2), custom_call_target="tpu_custom_call" | custom-call | tf_op jit(solution)/shard_map/inverse/pallas_call | solution.py:307
  (2 shorter events, 0.0 us)
Async XLA Ops:
  1.6 5.5 %copy-start.8 = (f32[3,4,152]{2,1,0:T(4,128)S(1)}, f32[3,4,152]{2,1,0:T(4,128)}, u32[]{:S(2)}) copy-start(f32[3,4,152]{2,1,0:T(4,128)} %get-tuple-element.16) | copy-start | bytes 21892
  1.6 5.8 %copy-start.7 = (f32[3,4,152]{2,1,0:T(4,128)S(1)}, f32[3,4,152]{2,1,0:T(4,128)}, u32[]{:S(2)}) copy-start(f32[3,4,152]{2,1,0:T(4,128)} %get-tuple-element.17) | copy-start | bytes 21892
  1.6 7.3 %copy-start.6 = (f32[3,4,152]{2,1,0:T(4,128)S(1)}, f32[3,4,152]{2,1,0:T(4,128)}, u32[]{:S(2)}) copy-start(f32[3,4,152]{2,1,0:T(4,128)} %get-tuple-element.18) | copy-start | bytes 21892
  1.6 4.2 %collective-permute-start = (f32[2,3,4,152]{3,2,1,0:T(4,128)}, f32[2,3,4,152]{3,2,1,0:T(4,128)S(1)}, u32[]{:S(2)}, u32[]{:S(2)}) collective-permute-start(f32[2,3,4,152]{3,2,1,0:T(4,128)} %get-tuple-element.13), channel_id=1, source_target_pairs={{0,1},{1,0},{2,3},{3,2},{4,5},{5,4},{6,7},{7,6},{8,9},{9,8},{10,11... | collective-permute-start | bytes 43784 | tf_op jit(solution)/shard_map/ppermute | solution.py:258
  5.8 8.3 %collective-permute-start.1 = (f32[2,3,4,152]{3,2,1,0:T(4,128)S(1)}, f32[2,3,4,152]{3,2,1,0:T(4,128)S(1)}, u32[]{:S(2)}, u32[]{:S(2)}) collective-permute-start(f32[2,3,4,152]{3,2,1,0:T(4,128)S(1)} %collective-permute-done.from_near), channel_id=1, source_target_pairs={{0,2},{1,3},{2,0},{3,1},{4,6},{5,7},{6,4},{7,5},{8,10},{9,11},{10,... | collective-permute-start | bytes 43784 | tf_op jit(solution)/shard_map/ppermute | solution.py:258
  7.1 6.0 %collective-permute-start.2 = (f32[3,4,152]{2,1,0:T(4,128)S(1)}, f32[3,4,152]{2,1,0:T(4,128)S(1)}, u32[]{:S(2)}, u32[]{:S(2)}) collective-permute-start(f32[3,4,152]{2,1,0:T(4,128)S(1)} %copy-done.8), channel_id=1, source_target_pairs={{0,2},{1,3},{2,0},{3,1},{4,6},{5,7},{6,4},{7,5},{8,10},{9,11},{10,... | collective-permute-start | bytes 21896 | tf_op jit(solution)/shard_map/ppermute | solution.py:258
  7.4 5.8 %collective-permute-start.3 = (f32[3,4,152]{2,1,0:T(4,128)S(1)}, f32[3,4,152]{2,1,0:T(4,128)S(1)}, u32[]{:S(2)}, u32[]{:S(2)}) collective-permute-start(f32[3,4,152]{2,1,0:T(4,128)S(1)} %copy-done.7), channel_id=1, source_target_pairs={{0,4},{8,12},{16,20},{24,28},{4,0},{12,8},{20,16},{28,24},{1,5},{9... | collective-permute-start | bytes 21896 | tf_op jit(solution)/shard_map/ppermute | solution.py:262
  8.9 5.3 %copy-start = (bf16[320,4608]{1,0:T(8,128)(2,1)S(1)}, bf16[320,4608]{1,0:T(8,128)(2,1)}, u32[]{:S(2)}) copy-start(bf16[320,4608]{1,0:T(8,128)(2,1)} %constant.4.clone.refs_3_.table) | copy-start | bytes 8847364
  8.9 5.3 %copy-start.1 = (f32[16,3,152]{2,0,1:T(8,128)S(1)}, f32[16,3,152]{2,0,1:T(8,128)}, u32[]{:S(2)}) copy-start(f32[16,3,152]{2,0,1:T(8,128)} %param.8) | copy-start | bytes 87556
  8.9 5.3 %copy-start.3 = (s32[1,4,4]{2,1,0:T(4,128)S(1)}, s32[1,4,4]{2,1,0:T(4,128)}, u32[]{:S(2)}) copy-start(s32[1,4,4]{2,1,0:T(4,128)} %param.10) | copy-start | bytes 196
  8.9 5.3 %collective-permute-start.4 = (f32[3,4,152]{2,1,0:T(4,128)S(1)}, f32[3,4,152]{2,1,0:T(4,128)S(1)}, u32[]{:S(2)}, u32[]{:S(2)}) collective-permute-start(f32[3,4,152]{2,1,0:T(4,128)S(1)} %copy-done.6), channel_id=1, source_target_pairs={{4,8},{12,16},{20,24},{8,4},{16,12},{24,20},{5,9},{13,17},{21,25},... | collective-permute-start | bytes 21896 | tf_op jit(solution)/shard_map/ppermute | solution.py:262
  13.1 2.8 %copy-start.4 = (s32[16,32]{1,0:T(8,128)S(1)}, s32[16,32]{1,0:T(8,128)}, u32[]{:S(2)}) copy-start(s32[16,32]{1,0:T(8,128)} %source.1) | copy-start | bytes 6148
  13.1 2.8 %copy-start.5 = (s32[16,32]{1,0:T(8,128)S(1)}, s32[16,32]{1,0:T(8,128)}, u32[]{:S(2)}) copy-start(s32[16,32]{1,0:T(8,128)} %offset.1) | copy-start | bytes 6148
  16.0 6.1 %copy-start.2 = (f32[1,4608]{1,0:T(1,128)S(1)}, f32[1,4608]{1,0:T(1,128)}, u32[]{:S(2)}) copy-start(f32[1,4608]{1,0:T(1,128)} %constant.5.clone.factor) | copy-start | bytes 55300

commit v7 on v6

--- a/solution.py
+++ b/solution.py
@@ -20,7 +20,7 @@
 TAIL = TILES - MAIN
 PITCH = MAIN + 1
 TAIL_PITCH = 7
-HAT_ROWS = 2 * TILES + 1
+HAT_ROWS = 2 * TILES
 POINTS_PAD = 160
 CHUNK = 256
 PIECE = 512
@@ -83,26 +83,19 @@
 
 
 def prepare_kernel(kernel_hat, hat):
-    parts, count, _ = kernel_hat.shape
+    count = kernel_hat.shape[0]
+    step = 8
 
     def move(first, height):
-        for part in range(parts):
-            for j in range(TILES):
-                x = kernel_hat[part, pl.ds(first, height), j * LANES : (j + 1) * LANES].astype(jnp.float32)
-                for g in range(0, height, 8):
-                    size = min(8, height - g)
-                    piece = x[g : g + size]
-                    row = (first + g) * HAT_ROWS + part * TILES + j
-                    hat[pl.ds(row, size, stride=HAT_ROWS), :] = piece
-
-    whole = count // 16
-
-    @pl.loop(0, whole)
+        for j in range(TILES):
+            hat[pl.ds(first, height), j] = kernel_hat[pl.ds(first, height), :, j * LANES : (j + 1) * LANES].astype(jnp.float32)
+
+    @pl.loop(0, count // step)
     def _(i):
-        move(pl.multiple_of(i * 16, 16), 16)
-
-    if count % 16:
-        move(whole * 16, count % 16)
+        move(i * step, step)
+
+    if count % step:
+        move(count - count % step, count % step)
 
 
 def forward_kernel(send_list, density, from_near, relayed, *refs):
@@ -159,46 +152,47 @@
     plus = lax.broadcasted_iota(jnp.int32, (8, LANES), 0) < comp_count
     halves = MAIN // 8
 
+    flat = hat.reshape(-1, LANES)
+    zero = jnp.zeros((8, LANES), f32)
+
     @pl.loop(0, box_count)
     def _(t):
-        def pair(w, accs):
+        for h in range(halves):
+            def pair(w, accs):
+                s = source[t, w] * pitch
+                o = offset[t, w] * HAT_ROWS
+                k_re = flat[pl.ds(o + 16 * h, 8, stride=2), :]
+                k_im = flat[pl.ds(o + (16 * h + 1), 8, stride=2), :]
+                done = []
+                for c in range(comp_count):
+                    s_re = main[pl.ds(s + (source_row(comp_count, c, 8 * h)), 8), :]
+                    s_im = main[pl.ds(s + (source_row(comp_count, comp_count + c, 8 * h)), 8), :]
+                    done.append(accs[2 * c] + (k_re * s_re - k_im * s_im))
+                    done.append(accs[2 * c + 1] + (k_re * s_im + k_im * s_re))
+                return tuple(done)
+
+            accs = lax.fori_loop(0, list_count, pair, (zero,) * (2 * comp_count), unroll=8)
+            for c in range(comp_count):
+                for part in range(2):
+                    row = (part * comp_count + c) * box_count + t
+                    total[pl.ds(row * PITCH + 8 * h, 8), :] = accs[2 * c + part]
+
+        def pair_tail(w, accs):
             s = source[t, w] * pitch
             o = offset[t, w] * HAT_ROWS
-            k = [[hat[pl.ds(o + (r * TILES + 8 * h), 8), :] for h in range(halves)] for r in range(2)]
-            accs = list(accs)
-            at = 0
-            for c in range(comp_count):
-                for h in range(halves):
-                    s_re = main[pl.ds(s + (source_row(comp_count, c, 8 * h)), 8), :]
-                    s_im = main[pl.ds(s + (source_row(comp_count, comp_count + c, 8 * h)), 8), :]
-                    accs[at] = accs[at] + (k[0][h] * s_re - k[1][h] * s_im)
-                    accs[at + 1] = accs[at + 1] + (k[0][h] * s_im + k[1][h] * s_re)
-                    at += 2
+            done = []
             for j in range(MAIN, TILES):
                 x = main[pl.ds(s + source_row(comp_count, 0, j), 8), :]
-                k_re = hat[pl.ds(o + j, 8, stride=0), :]
-                k_im = hat[pl.ds(o + TILES + j, 8, stride=0), :]
-                accs[at] = accs[at] + k_re * x
-                accs[at + 1] = accs[at + 1] + k_im * x
-                at += 2
-            return tuple(accs)
-
-        count = 2 * (comp_count * halves + TAIL)
-        zero = jnp.zeros((8, LANES), f32)
-        accs = lax.fori_loop(0, list_count, pair, (zero,) * count, unroll=4)
-        at = 0
-        for c in range(comp_count):
-            for h in range(halves):
-                for part in range(2):
-                    row = (part * comp_count + c) * box_count + t
-                    total[pl.ds(row * PITCH + 8 * h, 8), :] = accs[at + part]
-                at += 2
+                done.append(accs[len(done)] + flat[pl.ds(o + 2 * j, 8, stride=0), :] * x)
+                done.append(accs[len(done)] + flat[pl.ds(o + (2 * j + 1), 8, stride=0), :] * x)
+            return tuple(done)
+
+        accs = lax.fori_loop(0, list_count, pair_tail, (zero,) * (2 * TAIL), unroll=8)
         for j in range(TAIL):
-            own, cross = accs[at], accs[at + 1]
+            own, cross = accs[2 * j], accs[2 * j + 1]
             up = jnp.concatenate([cross[comp_count:], cross[:comp_count]], axis=0)
             down = jnp.concatenate([cross[-comp_count:], cross[:-comp_count]], axis=0)
             total_tail[j, pl.ds(t * TAIL_PITCH, 8), :] = jnp.where(plus, own - up, own + down)
-            at += 2
 
 
 def inverse_kernel(total, total_tail, table, factor, out):
@@ -265,19 +259,18 @@
     from_far = [swap(x, k) for x, k in zip(to_far, (2, *range(4, peers)))]
     from_first = swap_groups(to_first, 0)
     from_second = swap_groups(to_second, 1)
-    by_part, near = lax.optimization_barrier((kernel_hat.transpose(1, 0, 2), from_near))
-    relayed = swap(near, 2)
-
     offsets = kernel_hat.shape[0]
     hat = pl.pallas_call(
         prepare_kernel,
-        out_shape=jax.ShapeDtypeStruct((offsets * HAT_ROWS + 8, LANES), f32),
+        out_shape=jax.ShapeDtypeStruct((offsets, TILES, 2, LANES), f32),
         in_specs=[vmem],
         out_specs=vmem,
         compiler_params=pltpu.CompilerParams(vmem_limit_bytes=16 * 1024 * 1024),
         cost_estimate=pl.CostEstimate(flops=kernel_hat.size, bytes_accessed=6 * kernel_hat.size, transcendentals=0),
         name="prepare",
-    )(by_part)
+    )(kernel_hat)
+    hat, near = lax.optimization_barrier((hat, from_near))
+    relayed = swap(near, 2)
 
     slots = box_count + peers * cap + 2 * rim
     row_count = comp_count * slots

time: 24 us -> 27 us (1.12)
  Pallas kernels: 11.6 us -> 14.7 us
  waiting for transfers between devices: 1.02 us -> 1.89 us
  starting transfers between devices: 8.9 us -> 8.18 us
  local copies, waits for them, and re-layouts: 2.15 us -> 1.87 us
    pallas_call x1, Pallas kernels: 0.46 us -> 2.14 us  [on_device(): pl.pallas_call(prepare_kernel, out_shape=jax.ShapeDtypeStruct((offsets, T...]
    pallas_call x1, Pallas kernels: 6.13 us -> 7.59 us  [on_device(): pl.pallas_call(functools.partial(interact_kernel, comp_count), out_shape=...]
    ppermute x2, waiting for transfers between devices: 1.01 us -> 1.88 us  [swap_groups(): return lax.ppermute(x, 'group', pairs + [(j, i) for i, j in pairs])]
    ppermute x2, starting transfers between devices: 5.26 us -> 4.61 us  [swap_groups(): return lax.ppermute(x, 'group', pairs + [(j, i) for i, j in pairs])]
    unnamed x19 -> x20, local copies, waits for them, and re-layouts: 2.15 us -> 1.87 us
  transfers between devices with their start and end apart: 5 -> 5, of which waited for: 1 -> 1; matrix products, arithmetic and copies ran while one was open for 9% -> 0% of each run, Pallas kernels for 2% -> 8%
where the time goes in v7:
time: 27 us; the launch traced here: 26.8 us
  Pallas kernels  14.7 us (54%)
  starting transfers between devices  8.18 us (30%)
  waiting for transfers between devices  1.89 us (7%)
  local copies, waits for them, and re-layouts  1.87 us (7%)
    pallas_call x1, Pallas kernels, on_device(): pl.pallas_call(functools.partial(interact_kernel, comp_count), out_shape=...  7.59 us
    ppermute x2, starting transfers between devices, swap_groups(): return lax.ppermute(x, 'group', pairs + [(j, i) for i, j in pairs])  4.61 us
    ppermute x3, starting transfers between devices, swap(): return lax.ppermute(x, 'dev', [(i, i ^ k) for i in range(peers)])  3.57 us
    pallas_call x1, Pallas kernels, on_device(): pl.pallas_call(prepare_kernel, out_shape=jax.ShapeDtypeStruct((offsets, T...  2.14 us
    ppermute x2, waiting for transfers between devices, swap_groups(): return lax.ppermute(x, 'group', pairs + [(j, i) for i, j in pairs])  1.88 us
    unnamed x20, local copies, waits for them, and re-layouts  1.87 us
    pallas_call x1, Pallas kernels, on_device(): pl.pallas_call(forward_kernel, out_shape=jax.ShapeDtypeStruct((slots * so...  1.76 us
    pallas_call x1, Pallas kernels, on_device(): pl.pallas_call(inverse_kernel, out_shape=jax.ShapeDtypeStruct((comp_count...  1.64 us
  transfers between devices with their start and end apart: 5, of which 1 were waited for; matrix products, arithmetic and copies ran while one was open for 0% of the time, Pallas kernels for 8%

profile of v7, /device:TPU:1, one launch (start us, length us, event | category | flops | bytes accessed | tf_op | source)
XLA Modules:
  0.0 26.8 jit_solution(8915998685389042456)
XLA Ops:
  0.0 1.6 %pack.1 = (f32[2,3,4,152]{3,2,1,0:T(4,128)}, f32[3,4,152]{2,1,0:T(4,128)}, f32[3,4,152]{2,1,0:T(4,128)}, f32[3,4,152]{2,1,0:T(4,128)}) custom-call(f32[3,16,152]{2,1,0:T(8,128)} %bitcast.4, s32[4,4]{1,0:T(4,128)} %bitcast.6, s32[2,4]{1,0:T(2,128)} %bitcast.8), custom_call_target="tpu_custom_call" | custom-call | tf_op jit(solution)/shard_map/pack/pallas_call | solution.py:243
  1.6 0.0 copy-start
  1.6 2.0 %collective-permute-start = (f32[2,3,4,152]{3,2,1,0:T(4,128)}, f32[2,3,4,152]{3,2,1,0:T(4,128)S(1)}, u32[]{:S(2)}, u32[]{:S(2)}) collective-permute-start(f32[2,3,4,152]{3,2,1,0:T(4,128)} %get-tuple-element.13), channel_id=1, source_target_pairs={{0,1},{1,0},{2,3},{3,2},{4,5},{5,4},{6,7},{7,6},{8,9},{9,8},{10,11... | collective-permute-start | bytes 43784 | tf_op jit(solution)/shard_map/ppermute | solution.py:252
  3.6 0.0 copy-start.1
  3.6 1.8 %copy-done.1 = bf16[316,2,2304]{2,1,0:T(2,128)(2,1)S(1)} copy-done((bf16[316,2,2304]{2,1,0:T(2,128)(2,1)S(1)}, bf16[316,2,2304]{2,1,0:T(2,128)(2,1)}, u32[]{:S(2)}) %copy-start.1) | copy-done | bytes 2912280
  5.5 0.0 copy-start.8
  5.5 0.0 copy-start.4
  5.5 2.1 %prepare.1.hat = f32[316,18,2,128]{3,2,1,0:T(2,128)S(1)} custom-call(bf16[316,2,2304]{2,1,0:T(2,128)(2,1)S(1)} %copy-done.1), custom_call_target="tpu_custom_call" | custom-call | flops 1456128 | bytes 8736768 | tf_op jit(solution)/shard_map/prepare/pallas_call | solution.py:263
  7.6 0.0 copy-start.5
  7.6 0.0 copy-start.6
  7.7 0.0 collective-permute-done.from_near
  7.7 1.3 %collective-permute-start.1 = (f32[2,3,4,152]{3,2,1,0:T(4,128)S(1)}, f32[2,3,4,152]{3,2,1,0:T(4,128)S(1)}, u32[]{:S(2)}, u32[]{:S(2)}) collective-permute-start(f32[2,3,4,152]{3,2,1,0:T(4,128)S(1)} %collective-permute-done.from_near), channel_id=1, source_target_pairs={{0,2},{1,3},{2,0},{3,1},{4,6},{5,7},{6,4},{7,5},{8,10},{9,11},{10,... | collective-permute-start | bytes 43784 | tf_op jit(solution)/shard_map/ppermute | solution.py:252
  9.0 0.0 copy-done.9
  9.0 0.2 collective-permute-start.2
  9.2 0.0 copy-done.8
  9.2 1.5 %collective-permute-start.3 = (f32[3,4,152]{2,1,0:T(4,128)S(1)}, f32[3,4,152]{2,1,0:T(4,128)S(1)}, u32[]{:S(2)}, u32[]{:S(2)}) collective-permute-start(f32[3,4,152]{2,1,0:T(4,128)S(1)} %copy-done.8), channel_id=1, source_target_pairs={{0,4},{8,12},{16,20},{24,28},{4,0},{12,8},{20,16},{28,24},{1,5},{9... | collective-permute-start | bytes 21896 | tf_op jit(solution)/shard_map/ppermute | solution.py:256
  10.7 0.0 copy-done.7
  10.7 3.1 %collective-permute-start.4 = (f32[3,4,152]{2,1,0:T(4,128)S(1)}, f32[3,4,152]{2,1,0:T(4,128)S(1)}, u32[]{:S(2)}, u32[]{:S(2)}) collective-permute-start(f32[3,4,152]{2,1,0:T(4,128)S(1)} %copy-done.7), channel_id=1, source_target_pairs={{4,8},{12,16},{20,24},{8,4},{16,12},{24,20},{5,9},{13,17},{21,25},... | collective-permute-start | bytes 21896 | tf_op jit(solution)/shard_map/ppermute | solution.py:256
  13.8 0.0 collective-permute-done.2.refs_0_
  13.8 0.0 collective-permute-done.3.refs_1_
  13.8 1.9 %collective-permute-done.4.refs_2_ = f32[3,4,152]{2,1,0:T(4,128)S(1)} collective-permute-done((f32[3,4,152]{2,1,0:T(4,128)S(1)}, f32[3,4,152]{2,1,0:T(4,128)S(1)}, u32[]{:S(2)}, u32[]{:S(2)}) %collective-permute-start.4) | collective-permute-done | bytes 7328 | tf_op jit(solution)/shard_map/ppermute | solution.py:256
  15.7 0.0 collective-permute-done.1.relayed
  15.7 0.0 copy-done
  15.7 0.0 copy-done.2
  15.7 0.0 copy-done.4
  15.7 1.8 %forward.1.main = f32[4528,128]{1,0:T(8,128)S(1)} custom-call(s32[4,4]{1,0:T(4,128)S(1)} %bitcast.7, f32[3,16,152]{2,1,0:T(8,128)S(1)} %bitcast.5, f32[2,3,4,152]{3,2,1,0:T(4,128)S(1)} %collective-permute-done.from_near, f32[2,3,4,152]{3,2,1,0:T(4,128)S(1)} %collective-permute-done.1.relayed, f32[3,4,152]{2,1,0:T(4,128)S(1)} %collective-permute-done.2.refs_0_, ...), custom_call_target="tpu_custom_call" | custom-call | tf_op jit(solution)/shard_map/forward/pallas_call | solution.py:280
  17.5 0.0 copy-done.5
  17.5 0.0 copy-done.6
  17.5 0.0 copy-start.3
  17.5 7.6 %interact.1 = (f32[1632,128]{1,0:T(8,128)S(1)}, f32[2,126,128]{2,1,0:T(8,128)S(1)}) custom-call(s32[16,32]{1,0:T(8,128)S(1)} %copy-done.5, s32[16,32]{1,0:T(8,128)S(1)} %copy-done.6, f32[316,18,2,128]{3,2,1,0:T(2,128)S(1)} %prepare.1.hat, f32[4528,128]{1,0:T(8,128)S(1)} %forward.1.main), custom_call_target="tpu_custom_call" | custom-call | tf_op jit(solution)/shard_map/interact/pallas_call | solution.py:289
  25.1 0.0 copy-done.3
  25.2 1.6 %inverse.1 = f32[3,16,152]{2,1,0:T(8,128)} custom-call(f32[1632,128]{1,0:T(8,128)S(1)} %get-tuple-element.19.total, f32[2,126,128]{2,1,0:T(8,128)S(1)} %get-tuple-element.20.total_tail, bf16[320,4608]{1,0:T(8,128)(2,1)S(1)} %copy-done, f32[1,4608]{1,0:T(1,128)S(1)} %copy-done.3), custom_call_target="tpu_custom_call" | custom-call | tf_op jit(solution)/shard_map/inverse/pallas_call | solution.py:300
  (3 shorter events, 0.0 us)
Async XLA Ops:
  1.6 14.1 %copy-start = (bf16[320,4608]{1,0:T(8,128)(2,1)S(1)}, bf16[320,4608]{1,0:T(8,128)(2,1)}, u32[]{:S(2)}) copy-start(bf16[320,4608]{1,0:T(8,128)(2,1)} %constant.4.clone.refs_3_.table) | copy-start | bytes 8847364
  1.6 6.1 %collective-permute-start = (f32[2,3,4,152]{3,2,1,0:T(4,128)}, f32[2,3,4,152]{3,2,1,0:T(4,128)S(1)}, u32[]{:S(2)}, u32[]{:S(2)}) collective-permute-start(f32[2,3,4,152]{3,2,1,0:T(4,128)} %get-tuple-element.13), channel_id=1, source_target_pairs={{0,1},{1,0},{2,3},{3,2},{4,5},{5,4},{6,7},{7,6},{8,9},{9,8},{10,11... | collective-permute-start | bytes 43784 | tf_op jit(solution)/shard_map/ppermute | solution.py:252
  3.6 1.8 %copy-start.1 = (bf16[316,2,2304]{2,1,0:T(2,128)(2,1)S(1)}, bf16[316,2,2304]{2,1,0:T(2,128)(2,1)}, u32[]{:S(2)}) copy-start(bf16[316,2,2304]{2,1,0:T(2,128)(2,1)} %kernel_hat.1) | copy-start | bytes 8736772
  5.5 3.5 %copy-start.9 = (f32[3,4,152]{2,1,0:T(4,128)S(1)}, f32[3,4,152]{2,1,0:T(4,128)}, u32[]{:S(2)}) copy-start(f32[3,4,152]{2,1,0:T(4,128)} %get-tuple-element.16) | copy-start | bytes 21892
  5.5 3.7 %copy-start.8 = (f32[3,4,152]{2,1,0:T(4,128)S(1)}, f32[3,4,152]{2,1,0:T(4,128)}, u32[]{:S(2)}) copy-start(f32[3,4,152]{2,1,0:T(4,128)} %get-tuple-element.17) | copy-start | bytes 21892
  5.5 5.3 %copy-start.7 = (f32[3,4,152]{2,1,0:T(4,128)S(1)}, f32[3,4,152]{2,1,0:T(4,128)}, u32[]{:S(2)}) copy-start(f32[3,4,152]{2,1,0:T(4,128)} %get-tuple-element.18) | copy-start | bytes 21892
  5.5 10.3 %copy-start.2 = (f32[16,3,152]{2,0,1:T(8,128)S(1)}, f32[16,3,152]{2,0,1:T(8,128)}, u32[]{:S(2)}) copy-start(f32[16,3,152]{2,0,1:T(8,128)} %param.8) | copy-start | bytes 87556
  5.5 10.3 %copy-start.4 = (s32[1,4,4]{2,1,0:T(4,128)S(1)}, s32[1,4,4]{2,1,0:T(4,128)}, u32[]{:S(2)}) copy-start(s32[1,4,4]{2,1,0:T(4,128)} %param.10) | copy-start | bytes 196
  7.6 9.9 %copy-start.5 = (s32[16,32]{1,0:T(8,128)S(1)}, s32[16,32]{1,0:T(8,128)}, u32[]{:S(2)}) copy-start(s32[16,32]{1,0:T(8,128)} %source.1) | copy-start | bytes 6148
  7.6 9.9 %copy-start.6 = (s32[16,32]{1,0:T(8,128)S(1)}, s32[16,32]{1,0:T(8,128)}, u32[]{:S(2)}) copy-start(s32[16,32]{1,0:T(8,128)} %offset.1) | copy-start | bytes 6148
  7.7 8.1 %collective-permute-start.1 = (f32[2,3,4,152]{3,2,1,0:T(4,128)S(1)}, f32[2,3,4,152]{3,2,1,0:T(4,128)S(1)}, u32[]{:S(2)}, u32[]{:S(2)}) collective-permute-start(f32[2,3,4,152]{3,2,1,0:T(4,128)S(1)} %collective-permute-done.from_near), channel_id=1, source_target_pairs={{0,2},{1,3},{2,0},{3,1},{4,6},{5,7},{6,4},{7,5},{8,10},{9,11},{10,... | collective-permute-start | bytes 43784 | tf_op jit(solution)/shard_map/ppermute | solution.py:252
  9.0 4.9 %collective-permute-start.2 = (f32[3,4,152]{2,1,0:T(4,128)S(1)}, f32[3,4,152]{2,1,0:T(4,128)S(1)}, u32[]{:S(2)}, u32[]{:S(2)}) collective-permute-start(f32[3,4,152]{2,1,0:T(4,128)S(1)} %copy-done.9), channel_id=1, source_target_pairs={{0,2},{1,3},{2,0},{3,1},{4,6},{5,7},{6,4},{7,5},{8,10},{9,11},{10,... | collective-permute-start | bytes 21896 | tf_op jit(solution)/shard_map/ppermute | solution.py:252
  9.2 4.6 %collective-permute-start.3 = (f32[3,4,152]{2,1,0:T(4,128)S(1)}, f32[3,4,152]{2,1,0:T(4,128)S(1)}, u32[]{:S(2)}, u32[]{:S(2)}) collective-permute-start(f32[3,4,152]{2,1,0:T(4,128)S(1)} %copy-done.8), channel_id=1, source_target_pairs={{0,4},{8,12},{16,20},{24,28},{4,0},{12,8},{20,16},{28,24},{1,5},{9... | collective-permute-start | bytes 21896 | tf_op jit(solution)/shard_map/ppermute | solution.py:256
  10.7 5.0 %collective-permute-start.4 = (f32[3,4,152]{2,1,0:T(4,128)S(1)}, f32[3,4,152]{2,1,0:T(4,128)S(1)}, u32[]{:S(2)}, u32[]{:S(2)}) collective-permute-start(f32[3,4,152]{2,1,0:T(4,128)S(1)} %copy-done.7), channel_id=1, source_target_pairs={{4,8},{12,16},{20,24},{8,4},{16,12},{24,20},{5,9},{13,17},{21,25},... | collective-permute-start | bytes 21896 | tf_op jit(solution)/shard_map/ppermute | solution.py:256
  17.5 7.6 %copy-start.3 = (f32[1,4608]{1,0:T(1,128)S(1)}, f32[1,4608]{1,0:T(1,128)}, u32[]{:S(2)}) copy-start(f32[1,4608]{1,0:T(1,128)} %constant.5.clone.factor) | copy-start | bytes 55300

commit v8 on v6

--- a/solution.py
+++ b/solution.py
@@ -24,6 +24,7 @@
 POINTS_PAD = 160
 CHUNK = 256
 PIECE = 512
+UNROLL = 8
 
 
 def surface_points(edge_count):
@@ -161,9 +162,12 @@
 
     @pl.loop(0, box_count)
     def _(t):
-        def pair(w, accs):
-            s = source[t, w] * pitch
-            o = offset[t, w] * HAT_ROWS
+        def rows_of(first):
+            return tuple(
+                (source[t, first + u] * pitch, offset[t, first + u] * HAT_ROWS) for u in range(UNROLL)
+            )
+
+        def pair(s, o, accs):
             k = [[hat[pl.ds(o + (r * TILES + 8 * h), 8), :] for h in range(halves)] for r in range(2)]
             accs = list(accs)
             at = 0
@@ -185,7 +189,15 @@
 
         count = 2 * (comp_count * halves + TAIL)
         zero = jnp.zeros((8, LANES), f32)
-        accs = lax.fori_loop(0, list_count, pair, (zero,) * count, unroll=4)
+
+        def block(i, carry):
+            accs, here = carry
+            ahead = rows_of(lax.rem((i + 1) * UNROLL, list_count))
+            for s, o in here:
+                accs = pair(s, o, accs)
+            return accs, ahead
+
+        accs, _ = lax.fori_loop(0, list_count // UNROLL, block, ((zero,) * count, rows_of(0)))
         at = 0
         for c in range(comp_count):
             for h in range(halves):
@@ -251,6 +263,7 @@
         out_shape=(jax.ShapeDtypeStruct((2, *boxes.shape), f32),) + (boxes,) * (peers - 3) + (side,) * 2,
         in_specs=[vmem, smem, smem],
         out_specs=(vmem,) * peers,
+        compiler_params=pltpu.CompilerParams(vmem_limit_bytes=4 * 1024 * 1024),
         name="pack",
     )(density, send_list[0], halo_list[0])
 

time: 24 us -> 24.7 us (1.029)
  local copies, waits for them, and re-layouts: 2.15 us -> 4.3 us
  Pallas kernels: 11.6 us -> 10.1 us
    unnamed x19, local copies, waits for them, and re-layouts: 2.15 us -> 4.3 us
    pallas_call x1, Pallas kernels: 1.6 us -> 0.71 us  [on_device(): pl.pallas_call(pack_kernel, out_shape=(jax.ShapeDtypeStruct((2, *boxes.sh...]
    pallas_call x1, Pallas kernels: 6.13 us -> 5.56 us  [on_device(): pl.pallas_call(functools.partial(interact_kernel, comp_count), out_shape=...]
where the time goes in v8:
time: 24.7 us; the launch traced here: 24.5 us
  Pallas kernels  10.1 us (41%)
  starting transfers between devices  8.66 us (35%)
  local copies, waits for them, and re-layouts  4.3 us (17%)
  waiting for transfers between devices  1.24 us (5%)
    pallas_call x1, Pallas kernels, on_device(): pl.pallas_call(functools.partial(interact_kernel, comp_count), out_shape=...  5.56 us
    ppermute x2, starting transfers between devices, swap_groups(): return lax.ppermute(x, 'group', pairs + [(j, i) for i, j in pairs])  5.02 us
    unnamed x19, local copies, waits for them, and re-layouts  4.3 us
    ppermute x3, starting transfers between devices, swap(): return lax.ppermute(x, 'dev', [(i, i ^ k) for i in range(peers)])  3.64 us
    pallas_call x1, Pallas kernels, on_device(): pl.pallas_call(forward_kernel, out_shape=jax.ShapeDtypeStruct((slots * so...  1.76 us
    pallas_call x1, Pallas kernels, on_device(): pl.pallas_call(inverse_kernel, out_shape=jax.ShapeDtypeStruct((comp_count...  1.66 us
    ppermute x2, waiting for transfers between devices, swap_groups(): return lax.ppermute(x, 'group', pairs + [(j, i) for i, j in pairs])  1.23 us
    pallas_call x1, Pallas kernels, on_device(): pl.pallas_call(pack_kernel, out_shape=(jax.ShapeDtypeStruct((2, *boxes.sh...  0.71 us
  transfers between devices with their start and end apart: 5, of which 1 were waited for; matrix products, arithmetic and copies ran while one was open for 9% of the time, Pallas kernels for 2%

profile of v8, /device:TPU:1, one launch (start us, length us, event | category | flops | bytes accessed | tf_op | source)
XLA Modules:
  0.0 24.5 jit_solution(5906698598624790076)
XLA Ops:
  0.0 0.0 copy-start.1
  0.0 0.8 %copy-done.1 = f32[16,3,152]{2,0,1:T(8,128)S(1)} copy-done((f32[16,3,152]{2,0,1:T(8,128)S(1)}, f32[16,3,152]{2,0,1:T(8,128)}, u32[]{:S(2)}) %copy-start.1) | copy-done | bytes 29208
  0.8 0.0 copy-start.4
  0.8 0.7 %copy-done.4 = s32[1,4,4]{2,1,0:T(4,128)S(1)} copy-done((s32[1,4,4]{2,1,0:T(4,128)S(1)}, s32[1,4,4]{2,1,0:T(4,128)}, u32[]{:S(2)}) %copy-start.4) | copy-done | bytes 88
  1.5 0.0 copy-start.8
  1.5 0.7 %copy-done.8 = s32[1,2,4]{2,1,0:T(2,128)S(1)} copy-done((s32[1,2,4]{2,1,0:T(2,128)S(1)}, s32[1,2,4]{2,1,0:T(2,128)}, u32[]{:S(2)}) %copy-start.8) | copy-done | bytes 56
  2.2 0.7 %pack.1 = (f32[2,3,4,152]{3,2,1,0:T(4,128)S(1)}, f32[3,4,152]{2,1,0:T(4,128)S(1)}, f32[3,4,152]{2,1,0:T(4,128)S(1)}, f32[3,4,152]{2,1,0:T(4,128)S(1)}) custom-call(f32[3,16,152]{2,1,0:T(8,128)S(1)} %bitcast.8, s32[4,4]{1,0:T(4,128)S(1)} %bitcast.10, s32[2,4]{1,0:T(2,128)S(1)} %bitcast.12), custom_call_target="tpu_custom_call" | custom-call | tf_op jit(solution)/shard_map/pack/pallas_call | solution.py:261
  2.9 2.1 %collective-permute-start = (f32[2,3,4,152]{3,2,1,0:T(4,128)S(1)}, f32[2,3,4,152]{3,2,1,0:T(4,128)S(1)}, u32[]{:S(2)}, u32[]{:S(2)}) collective-permute-start(f32[2,3,4,152]{3,2,1,0:T(4,128)S(1)} %get-tuple-element.13), channel_id=1, source_target_pairs={{0,1},{1,0},{2,3},{3,2},{4,5},{5,4},{6,7},{7,6},{8,9},{9,8},{10,11... | collective-permute-start | bytes 43784 | tf_op jit(solution)/shard_map/ppermute | solution.py:271
  5.0 2.1 %copy.11 = bf16[316,2,2304]{2,0,1:T(8,128)(2,1)S(1)} copy(bf16[316,2,2304]{2,1,0:T(2,128)(2,1)} %param.9) | data formatting | bytes 5824512 | tf_op args[1]
  7.1 0.0 collective-permute-done.from_near
  7.1 1.3 %collective-permute-start.1 = (f32[2,3,4,152]{3,2,1,0:T(4,128)S(1)}, f32[2,3,4,152]{3,2,1,0:T(4,128)S(1)}, u32[]{:S(2)}, u32[]{:S(2)}) collective-permute-start(f32[2,3,4,152]{3,2,1,0:T(4,128)S(1)} %collective-permute-done.from_near), channel_id=1, source_target_pairs={{0,2},{1,3},{2,0},{3,1},{4,6},{5,7},{6,4},{7,5},{8,10},{9,11},{10,... | collective-permute-start | bytes 43784 | tf_op jit(solution)/shard_map/ppermute | solution.py:271
  8.4 0.2 collective-permute-start.2
  8.6 1.5 %collective-permute-start.3 = (f32[3,4,152]{2,1,0:T(4,128)S(1)}, f32[3,4,152]{2,1,0:T(4,128)S(1)}, u32[]{:S(2)}, u32[]{:S(2)}) collective-permute-start(f32[3,4,152]{2,1,0:T(4,128)S(1)} %get-tuple-element.17), channel_id=1, source_target_pairs={{0,4},{8,12},{16,20},{24,28},{4,0},{12,8},{20,16},{28,24},{1,5},{9... | collective-permute-start | bytes 21896 | tf_op jit(solution)/shard_map/ppermute | solution.py:275
  10.2 0.0 copy-start
  10.2 3.5 %collective-permute-start.4 = (f32[3,4,152]{2,1,0:T(4,128)S(1)}, f32[3,4,152]{2,1,0:T(4,128)S(1)}, u32[]{:S(2)}, u32[]{:S(2)}) collective-permute-start(f32[3,4,152]{2,1,0:T(4,128)S(1)} %get-tuple-element.18), channel_id=1, source_target_pairs={{4,8},{12,16},{20,24},{8,4},{16,12},{24,20},{5,9},{13,17},{21,25},... | collective-permute-start | bytes 21896 | tf_op jit(solution)/shard_map/ppermute | solution.py:275
  13.7 0.5 %prepare.1.hat = f32[11700,128]{1,0:T(8,128)S(1)} custom-call(bf16[2,316,2304]{2,1,0:T(8,128)(2,1)S(1)} %bitcast.7), custom_call_target="tpu_custom_call" | custom-call | flops 1456128 | bytes 8736768 | tf_op jit(solution)/shard_map/prepare/pallas_call | solution.py:285
  14.1 0.0 copy-start.6
  14.2 0.0 copy-start.7
  14.2 0.0 collective-permute-done.2.refs_0_
  14.2 0.0 collective-permute-done.3.refs_1_
  14.2 1.2 %collective-permute-done.4.refs_2_ = f32[3,4,152]{2,1,0:T(4,128)S(1)} collective-permute-done((f32[3,4,152]{2,1,0:T(4,128)S(1)}, f32[3,4,152]{2,1,0:T(4,128)S(1)}, u32[]{:S(2)}, u32[]{:S(2)}) %collective-permute-start.4) | collective-permute-done | bytes 7328 | tf_op jit(solution)/shard_map/ppermute | solution.py:275
  15.4 0.0 collective-permute-done.1.relayed
  15.4 0.0 copy-done
  15.4 0.0 copy-done.2
  15.4 0.0 copy-done.5
  15.4 1.8 %forward.1.main = f32[4528,128]{1,0:T(8,128)S(1)} custom-call(s32[4,4]{1,0:T(4,128)S(1)} %bitcast.11, f32[3,16,152]{2,1,0:T(8,128)S(1)} %bitcast.9, f32[2,3,4,152]{3,2,1,0:T(4,128)S(1)} %collective-permute-done.from_near, f32[2,3,4,152]{3,2,1,0:T(4,128)S(1)} %collective-permute-done.1.relayed, f32[3,4,152]{2,1,0:T(4,128)S(1)} %collective-permute-done.2.refs_0_, ...), custom_call_target="tpu_custom_call" | custom-call | tf_op jit(solution)/shard_map/forward/pallas_call | solution.py:300
  17.2 0.0 copy-done.6
  17.2 0.0 copy-done.7
  17.2 0.0 copy-start.3
  17.2 5.6 %interact.1 = (f32[1632,128]{1,0:T(8,128)S(1)}, f32[2,126,128]{2,1,0:T(8,128)S(1)}) custom-call(s32[16,32]{1,0:T(8,128)S(1)} %copy-done.6, s32[16,32]{1,0:T(8,128)S(1)} %copy-done.7, f32[11700,128]{1,0:T(8,128)S(1)} %prepare.1.hat, f32[4528,128]{1,0:T(8,128)S(1)} %forward.1.main), custom_call_target="tpu_custom_call" | custom-call | tf_op jit(solution)/shard_map/interact/pallas_call | solution.py:309
  22.8 0.0 copy-done.3
  22.8 1.7 %inverse.1 = f32[3,16,152]{2,1,0:T(8,128)} custom-call(f32[1632,128]{1,0:T(8,128)S(1)} %get-tuple-element.19.total, f32[2,126,128]{2,1,0:T(8,128)S(1)} %get-tuple-element.20.total_tail, bf16[320,4608]{1,0:T(8,128)(2,1)S(1)} %copy-done, f32[1,4608]{1,0:T(1,128)S(1)} %copy-done.3), custom_call_target="tpu_custom_call" | custom-call | tf_op jit(solution)/shard_map/inverse/pallas_call | solution.py:320
  (2 shorter events, 0.0 us)
Async XLA Ops:
  0.0 0.8 %copy-start.1 = (f32[16,3,152]{2,0,1:T(8,128)S(1)}, f32[16,3,152]{2,0,1:T(8,128)}, u32[]{:S(2)}) copy-start(f32[16,3,152]{2,0,1:T(8,128)} %param.8) | copy-start | bytes 87556
  0.8 0.7 %copy-start.4 = (s32[1,4,4]{2,1,0:T(4,128)S(1)}, s32[1,4,4]{2,1,0:T(4,128)}, u32[]{:S(2)}) copy-start(s32[1,4,4]{2,1,0:T(4,128)} %param.10) | copy-start | bytes 196
  1.5 0.7 %copy-start.8 = (s32[1,2,4]{2,1,0:T(2,128)S(1)}, s32[1,2,4]{2,1,0:T(2,128)}, u32[]{:S(2)}) copy-start(s32[1,2,4]{2,1,0:T(2,128)} %param.11) | copy-start | bytes 100
  2.9 4.2 %collective-permute-start = (f32[2,3,4,152]{3,2,1,0:T(4,128)S(1)}, f32[2,3,4,152]{3,2,1,0:T(4,128)S(1)}, u32[]{:S(2)}, u32[]{:S(2)}) collective-permute-start(f32[2,3,4,152]{3,2,1,0:T(4,128)S(1)} %get-tuple-element.13), channel_id=1, source_target_pairs={{0,1},{1,0},{2,3},{3,2},{4,5},{5,4},{6,7},{7,6},{8,9},{9,8},{10,11... | collective-permute-start | bytes 43784 | tf_op jit(solution)/shard_map/ppermute | solution.py:271
  7.1 8.3 %collective-permute-start.1 = (f32[2,3,4,152]{3,2,1,0:T(4,128)S(1)}, f32[2,3,4,152]{3,2,1,0:T(4,128)S(1)}, u32[]{:S(2)}, u32[]{:S(2)}) collective-permute-start(f32[2,3,4,152]{3,2,1,0:T(4,128)S(1)} %collective-permute-done.from_near), channel_id=1, source_target_pairs={{0,2},{1,3},{2,0},{3,1},{4,6},{5,7},{6,4},{7,5},{8,10},{9,11},{10,... | collective-permute-start | bytes 43784 | tf_op jit(solution)/shard_map/ppermute | solution.py:271
  8.4 5.8 %collective-permute-start.2 = (f32[3,4,152]{2,1,0:T(4,128)S(1)}, f32[3,4,152]{2,1,0:T(4,128)S(1)}, u32[]{:S(2)}, u32[]{:S(2)}) collective-permute-start(f32[3,4,152]{2,1,0:T(4,128)S(1)} %get-tuple-element.16), channel_id=1, source_target_pairs={{0,2},{1,3},{2,0},{3,1},{4,6},{5,7},{6,4},{7,5},{8,10},{9,11},{10,... | collective-permute-start | bytes 21896 | tf_op jit(solution)/shard_map/ppermute | solution.py:271
  8.6 5.5 %collective-permute-start.3 = (f32[3,4,152]{2,1,0:T(4,128)S(1)}, f32[3,4,152]{2,1,0:T(4,128)S(1)}, u32[]{:S(2)}, u32[]{:S(2)}) collective-permute-start(f32[3,4,152]{2,1,0:T(4,128)S(1)} %get-tuple-element.17), channel_id=1, source_target_pairs={{0,4},{8,12},{16,20},{24,28},{4,0},{12,8},{20,16},{28,24},{1,5},{9... | collective-permute-start | bytes 21896 | tf_op jit(solution)/shard_map/ppermute | solution.py:275
  10.2 5.3 %copy-start = (bf16[320,4608]{1,0:T(8,128)(2,1)S(1)}, bf16[320,4608]{1,0:T(8,128)(2,1)}, u32[]{:S(2)}) copy-start(bf16[320,4608]{1,0:T(8,128)(2,1)} %constant.4.clone.refs_3_.table) | copy-start | bytes 8847364
  10.2 5.3 %copy-start.2 = (f32[16,3,152]{2,0,1:T(8,128)S(1)}, f32[16,3,152]{2,0,1:T(8,128)}, u32[]{:S(2)}) copy-start(f32[16,3,152]{2,0,1:T(8,128)} %param.8) | copy-start | bytes 87556
  10.2 5.3 %copy-start.5 = (s32[1,4,4]{2,1,0:T(4,128)S(1)}, s32[1,4,4]{2,1,0:T(4,128)}, u32[]{:S(2)}) copy-start(s32[1,4,4]{2,1,0:T(4,128)} %param.10) | copy-start | bytes 196
  10.2 5.3 %collective-permute-start.4 = (f32[3,4,152]{2,1,0:T(4,128)S(1)}, f32[3,4,152]{2,1,0:T(4,128)S(1)}, u32[]{:S(2)}, u32[]{:S(2)}) collective-permute-start(f32[3,4,152]{2,1,0:T(4,128)S(1)} %get-tuple-element.18), channel_id=1, source_target_pairs={{4,8},{12,16},{20,24},{8,4},{16,12},{24,20},{5,9},{13,17},{21,25},... | collective-permute-start | bytes 21896 | tf_op jit(solution)/shard_map/ppermute | solution.py:275
  14.1 3.1 %copy-start.6 = (s32[16,32]{1,0:T(8,128)S(1)}, s32[16,32]{1,0:T(8,128)}, u32[]{:S(2)}) copy-start(s32[16,32]{1,0:T(8,128)} %source.1) | copy-start | bytes 6148
  14.2 3.1 %copy-start.7 = (s32[16,32]{1,0:T(8,128)S(1)}, s32[16,32]{1,0:T(8,128)}, u32[]{:S(2)}) copy-start(s32[16,32]{1,0:T(8,128)} %offset.1) | copy-start | bytes 6148
  17.2 5.6 %copy-start.3 = (f32[1,4608]{1,0:T(1,128)S(1)}, f32[1,4608]{1,0:T(1,128)}, u32[]{:S(2)}) copy-start(f32[1,4608]{1,0:T(1,128)} %constant.5.clone.factor) | copy-start | bytes 55300

commit v9 on v6

--- a/solution.py
+++ b/solution.py
@@ -161,9 +161,7 @@
 
     @pl.loop(0, box_count)
     def _(t):
-        def pair(w, accs):
-            s = source[t, w] * pitch
-            o = offset[t, w] * HAT_ROWS
+        def pair(s, o, accs):
             k = [[hat[pl.ds(o + (r * TILES + 8 * h), 8), :] for h in range(halves)] for r in range(2)]
             accs = list(accs)
             at = 0
@@ -185,7 +183,12 @@
 
         count = 2 * (comp_count * halves + TAIL)
         zero = jnp.zeros((8, LANES), f32)
-        accs = lax.fori_loop(0, list_count, pair, (zero,) * count, unroll=4)
+
+        accs, last = (zero,) * count, t
+        for w in range(list_count):
+            s = source[t, w + jnp.minimum(last, 0)]
+            last = offset[t, w + jnp.minimum(s, 0)]
+            accs = pair(s * pitch, last * HAT_ROWS, accs)
         at = 0
         for c in range(comp_count):
             for h in range(halves):

time: 24 us -> 31.2 us (1.30)
  Pallas kernels: 11.6 us -> 18.8 us
    pallas_call x1, Pallas kernels: 6.13 us -> 13.3 us  [on_device(): pl.pallas_call(functools.partial(interact_kernel, comp_count), out_shape=...]
  transfers between devices with their start and end apart: 5 -> 5, of which waited for: 1 -> 1; matrix products, arithmetic and copies ran while one was open for 9% -> 7% of each run, Pallas kernels for 2% -> 1%
where the time goes in v9:
time: 31.2 us; the launch traced here: 31 us
  Pallas kernels  18.8 us (60%)
  starting transfers between devices  8.9 us (29%)
  local copies, waits for them, and re-layouts  2.15 us (7%)
  waiting for transfers between devices  1.02 us (3%)
    pallas_call x1, Pallas kernels, on_device(): pl.pallas_call(functools.partial(interact_kernel, comp_count), out_shape=...  13.3 us
    ppermute x2, starting transfers between devices, swap_groups(): return lax.ppermute(x, 'group', pairs + [(j, i) for i, j in pairs])  5.26 us
    ppermute x3, starting transfers between devices, swap(): return lax.ppermute(x, 'dev', [(i, i ^ k) for i in range(peers)])  3.64 us
    unnamed x19, local copies, waits for them, and re-layouts  2.15 us
    pallas_call x1, Pallas kernels, on_device(): pl.pallas_call(forward_kernel, out_shape=jax.ShapeDtypeStruct((slots * so...  1.76 us
    pallas_call x1, Pallas kernels, on_device(): pl.pallas_call(inverse_kernel, out_shape=jax.ShapeDtypeStruct((comp_count...  1.66 us
    pallas_call x1, Pallas kernels, on_device(): pl.pallas_call(pack_kernel, out_shape=(jax.ShapeDtypeStruct((2, *boxes.sh...  1.6 us
    ppermute x2, waiting for transfers between devices, swap_groups(): return lax.ppermute(x, 'group', pairs + [(j, i) for i, j in pairs])  1.01 us
  transfers between devices with their start and end apart: 5, of which 1 were waited for; matrix products, arithmetic and copies ran while one was open for 7% of the time, Pallas kernels for 1%

profile of v9, /device:TPU:1, one launch (start us, length us, event | category | flops | bytes accessed | tf_op | source)
XLA Modules:
  0.0 31.0 jit_solution(5218079179499233737)
XLA Ops:
  0.0 1.6 %pack.1 = (f32[2,3,4,152]{3,2,1,0:T(4,128)}, f32[3,4,152]{2,1,0:T(4,128)}, f32[3,4,152]{2,1,0:T(4,128)}, f32[3,4,152]{2,1,0:T(4,128)}) custom-call(f32[3,16,152]{2,1,0:T(8,128)} %bitcast.8, s32[4,4]{1,0:T(4,128)} %bitcast.10, s32[2,4]{1,0:T(2,128)} %bitcast.12), custom_call_target="tpu_custom_call" | custom-call | tf_op jit(solution)/shard_map/pack/pallas_call | solution.py:252
  1.6 0.0 copy-start.8
  1.6 0.0 copy-start.7
  1.6 0.0 copy-start.6
  1.6 2.1 %collective-permute-start = (f32[2,3,4,152]{3,2,1,0:T(4,128)}, f32[2,3,4,152]{3,2,1,0:T(4,128)S(1)}, u32[]{:S(2)}, u32[]{:S(2)}) collective-permute-start(f32[2,3,4,152]{3,2,1,0:T(4,128)} %get-tuple-element.13), channel_id=1, source_target_pairs={{0,1},{1,0},{2,3},{3,2},{4,5},{5,4},{6,7},{7,6},{8,9},{9,8},{10,11... | collective-permute-start | bytes 43784 | tf_op jit(solution)/shard_map/ppermute | solution.py:261
  3.7 2.1 %copy.11 = bf16[316,2,2304]{2,0,1:T(8,128)(2,1)S(1)} copy(bf16[316,2,2304]{2,1,0:T(2,128)(2,1)} %param.9) | data formatting | bytes 5824512 | tf_op args[1]
  5.8 0.0 collective-permute-done.from_near
  5.8 1.3 %collective-permute-start.1 = (f32[2,3,4,152]{3,2,1,0:T(4,128)S(1)}, f32[2,3,4,152]{3,2,1,0:T(4,128)S(1)}, u32[]{:S(2)}, u32[]{:S(2)}) collective-permute-start(f32[2,3,4,152]{3,2,1,0:T(4,128)S(1)} %collective-permute-done.from_near), channel_id=1, source_target_pairs={{0,2},{1,3},{2,0},{3,1},{4,6},{5,7},{6,4},{7,5},{8,10},{9,11},{10,... | collective-permute-start | bytes 43784 | tf_op jit(solution)/shard_map/ppermute | solution.py:261
  7.1 0.0 copy-done.8
  7.1 0.2 collective-permute-start.2
  7.4 0.0 copy-done.7
  7.4 1.5 %collective-permute-start.3 = (f32[3,4,152]{2,1,0:T(4,128)S(1)}, f32[3,4,152]{2,1,0:T(4,128)S(1)}, u32[]{:S(2)}, u32[]{:S(2)}) collective-permute-start(f32[3,4,152]{2,1,0:T(4,128)S(1)} %copy-done.7), channel_id=1, source_target_pairs={{0,4},{8,12},{16,20},{24,28},{4,0},{12,8},{20,16},{28,24},{1,5},{9... | collective-permute-start | bytes 21896 | tf_op jit(solution)/shard_map/ppermute | solution.py:265
  8.9 0.0 copy-done.6
  8.9 0.0 copy-start
  8.9 3.7 %collective-permute-start.4 = (f32[3,4,152]{2,1,0:T(4,128)S(1)}, f32[3,4,152]{2,1,0:T(4,128)S(1)}, u32[]{:S(2)}, u32[]{:S(2)}) collective-permute-start(f32[3,4,152]{2,1,0:T(4,128)S(1)} %copy-done.6), channel_id=1, source_target_pairs={{4,8},{12,16},{20,24},{8,4},{16,12},{24,20},{5,9},{13,17},{21,25},... | collective-permute-start | bytes 21896 | tf_op jit(solution)/shard_map/ppermute | solution.py:265
  12.7 0.5 %prepare.1.hat = f32[11700,128]{1,0:T(8,128)S(1)} custom-call(bf16[2,316,2304]{2,1,0:T(8,128)(2,1)S(1)} %bitcast.7), custom_call_target="tpu_custom_call" | custom-call | flops 1456128 | bytes 8736768 | tf_op jit(solution)/shard_map/prepare/pallas_call | solution.py:275
  13.1 0.0 copy-start.4
  13.1 0.0 copy-start.5
  13.2 0.0 collective-permute-done.2.refs_0_
  13.2 0.0 collective-permute-done.3.refs_1_
  13.2 1.0 %collective-permute-done.4.refs_2_ = f32[3,4,152]{2,1,0:T(4,128)S(1)} collective-permute-done((f32[3,4,152]{2,1,0:T(4,128)S(1)}, f32[3,4,152]{2,1,0:T(4,128)S(1)}, u32[]{:S(2)}, u32[]{:S(2)}) %collective-permute-start.4) | collective-permute-done | bytes 7328 | tf_op jit(solution)/shard_map/ppermute | solution.py:265
  14.2 0.0 collective-permute-done.1.relayed
  14.2 0.0 copy-done
  14.2 0.0 copy-done.1
  14.2 0.0 copy-done.3
  14.2 1.8 %forward.1.main = f32[4528,128]{1,0:T(8,128)S(1)} custom-call(s32[4,4]{1,0:T(4,128)S(1)} %bitcast.11, f32[3,16,152]{2,1,0:T(8,128)S(1)} %bitcast.9, f32[2,3,4,152]{3,2,1,0:T(4,128)S(1)} %collective-permute-done.from_near, f32[2,3,4,152]{3,2,1,0:T(4,128)S(1)} %collective-permute-done.1.relayed, f32[3,4,152]{2,1,0:T(4,128)S(1)} %collective-permute-done.2.refs_0_, ...), custom_call_target="tpu_custom_call" | custom-call | tf_op jit(solution)/shard_map/forward/pallas_call | solution.py:290
  16.0 0.0 copy-done.4
  16.0 0.0 copy-done.5
  16.0 0.0 copy-start.2
  16.0 13.3 %interact.1 = (f32[1632,128]{1,0:T(8,128)S(1)}, f32[2,126,128]{2,1,0:T(8,128)S(1)}) custom-call(s32[16,32]{1,0:T(8,128)S(1)} %copy-done.4, s32[16,32]{1,0:T(8,128)S(1)} %copy-done.5, f32[11700,128]{1,0:T(8,128)S(1)} %prepare.1.hat, f32[4528,128]{1,0:T(8,128)S(1)} %forward.1.main), custom_call_target="tpu_custom_call" | custom-call | tf_op jit(solution)/shard_map/interact/pallas_call | solution.py:299
  29.4 0.0 copy-done.2
  29.4 1.7 %inverse.1 = f32[3,16,152]{2,1,0:T(8,128)} custom-call(f32[1632,128]{1,0:T(8,128)S(1)} %get-tuple-element.19.total, f32[2,126,128]{2,1,0:T(8,128)S(1)} %get-tuple-element.20.total_tail, bf16[320,4608]{1,0:T(8,128)(2,1)S(1)} %copy-done, f32[1,4608]{1,0:T(1,128)S(1)} %copy-done.2), custom_call_target="tpu_custom_call" | custom-call | tf_op jit(solution)/shard_map/inverse/pallas_call | solution.py:310
  (2 shorter events, 0.0 us)
Async XLA Ops:
  1.6 5.5 %copy-start.8 = (f32[3,4,152]{2,1,0:T(4,128)S(1)}, f32[3,4,152]{2,1,0:T(4,128)}, u32[]{:S(2)}) copy-start(f32[3,4,152]{2,1,0:T(4,128)} %get-tuple-element.16) | copy-start | bytes 21892
  1.6 5.8 %copy-start.7 = (f32[3,4,152]{2,1,0:T(4,128)S(1)}, f32[3,4,152]{2,1,0:T(4,128)}, u32[]{:S(2)}) copy-start(f32[3,4,152]{2,1,0:T(4,128)} %get-tuple-element.17) | copy-start | bytes 21892
  1.6 7.3 %copy-start.6 = (f32[3,4,152]{2,1,0:T(4,128)S(1)}, f32[3,4,152]{2,1,0:T(4,128)}, u32[]{:S(2)}) copy-start(f32[3,4,152]{2,1,0:T(4,128)} %get-tuple-element.18) | copy-start | bytes 21892
  1.6 4.2 %collective-permute-start = (f32[2,3,4,152]{3,2,1,0:T(4,128)}, f32[2,3,4,152]{3,2,1,0:T(4,128)S(1)}, u32[]{:S(2)}, u32[]{:S(2)}) collective-permute-start(f32[2,3,4,152]{3,2,1,0:T(4,128)} %get-tuple-element.13), channel_id=1, source_target_pairs={{0,1},{1,0},{2,3},{3,2},{4,5},{5,4},{6,7},{7,6},{8,9},{9,8},{10,11... | collective-permute-start | bytes 43784 | tf_op jit(solution)/shard_map/ppermute | solution.py:261
  5.8 8.3 %collective-permute-start.1 = (f32[2,3,4,152]{3,2,1,0:T(4,128)S(1)}, f32[2,3,4,152]{3,2,1,0:T(4,128)S(1)}, u32[]{:S(2)}, u32[]{:S(2)}) collective-permute-start(f32[2,3,4,152]{3,2,1,0:T(4,128)S(1)} %collective-permute-done.from_near), channel_id=1, source_target_pairs={{0,2},{1,3},{2,0},{3,1},{4,6},{5,7},{6,4},{7,5},{8,10},{9,11},{10,... | collective-permute-start | bytes 43784 | tf_op jit(solution)/shard_map/ppermute | solution.py:261
  7.1 6.0 %collective-permute-start.2 = (f32[3,4,152]{2,1,0:T(4,128)S(1)}, f32[3,4,152]{2,1,0:T(4,128)S(1)}, u32[]{:S(2)}, u32[]{:S(2)}) collective-permute-start(f32[3,4,152]{2,1,0:T(4,128)S(1)} %copy-done.8), channel_id=1, source_target_pairs={{0,2},{1,3},{2,0},{3,1},{4,6},{5,7},{6,4},{7,5},{8,10},{9,11},{10,... | collective-permute-start | bytes 21896 | tf_op jit(solution)/shard_map/ppermute | solution.py:261
  7.4 5.8 %collective-permute-start.3 = (f32[3,4,152]{2,1,0:T(4,128)S(1)}, f32[3,4,152]{2,1,0:T(4,128)S(1)}, u32[]{:S(2)}, u32[]{:S(2)}) collective-permute-start(f32[3,4,152]{2,1,0:T(4,128)S(1)} %copy-done.7), channel_id=1, source_target_pairs={{0,4},{8,12},{16,20},{24,28},{4,0},{12,8},{20,16},{28,24},{1,5},{9... | collective-permute-start | bytes 21896 | tf_op jit(solution)/shard_map/ppermute | solution.py:265
  8.9 5.3 %copy-start = (bf16[320,4608]{1,0:T(8,128)(2,1)S(1)}, bf16[320,4608]{1,0:T(8,128)(2,1)}, u32[]{:S(2)}) copy-start(bf16[320,4608]{1,0:T(8,128)(2,1)} %constant.4.clone.refs_3_.table) | copy-start | bytes 8847364
  8.9 5.3 %copy-start.1 = (f32[16,3,152]{2,0,1:T(8,128)S(1)}, f32[16,3,152]{2,0,1:T(8,128)}, u32[]{:S(2)}) copy-start(f32[16,3,152]{2,0,1:T(8,128)} %param.8) | copy-start | bytes 87556
  8.9 5.3 %copy-start.3 = (s32[1,4,4]{2,1,0:T(4,128)S(1)}, s32[1,4,4]{2,1,0:T(4,128)}, u32[]{:S(2)}) copy-start(s32[1,4,4]{2,1,0:T(4,128)} %param.10) | copy-start | bytes 196
  8.9 5.3 %collective-permute-start.4 = (f32[3,4,152]{2,1,0:T(4,128)S(1)}, f32[3,4,152]{2,1,0:T(4,128)S(1)}, u32[]{:S(2)}, u32[]{:S(2)}) collective-permute-start(f32[3,4,152]{2,1,0:T(4,128)S(1)} %copy-done.6), channel_id=1, source_target_pairs={{4,8},{12,16},{20,24},{8,4},{16,12},{24,20},{5,9},{13,17},{21,25},... | collective-permute-start | bytes 21896 | tf_op jit(solution)/shard_map/ppermute | solution.py:265
  13.1 2.8 %copy-start.4 = (s32[16,32]{1,0:T(8,128)S(1)}, s32[16,32]{1,0:T(8,128)}, u32[]{:S(2)}) copy-start(s32[16,32]{1,0:T(8,128)} %source.1) | copy-start | bytes 6148
  13.1 2.8 %copy-start.5 = (s32[16,32]{1,0:T(8,128)S(1)}, s32[16,32]{1,0:T(8,128)}, u32[]{:S(2)}) copy-start(s32[16,32]{1,0:T(8,128)} %offset.1) | copy-start | bytes 6148
  16.0 13.4 %copy-start.2 = (f32[1,4608]{1,0:T(1,128)S(1)}, f32[1,4608]{1,0:T(1,128)}, u32[]{:S(2)}) copy-start(f32[1,4608]{1,0:T(1,128)} %constant.5.clone.factor) | copy-start | bytes 55300

commit v10 on v9

--- a/solution.py
+++ b/solution.py
@@ -24,6 +24,7 @@
 POINTS_PAD = 160
 CHUNK = 256
 PIECE = 512
+GROUP = 2
 
 
 def surface_points(edge_count):
@@ -136,12 +137,11 @@
     value = rows[...]
     high = value.astype(bf16)
     low = (value - high.astype(f32)).astype(bf16)
-    both = jnp.concatenate([high, low], axis=0)
+    twice = jnp.concatenate([high, high], axis=1)
     for n in range(2 * FREQ // CHUNK):
         columns = slice(n * CHUNK, (n + 1) * CHUNK)
-        x = jnp.dot(both, table[:POINTS_PAD, columns], preferred_element_type=f32)
-        x = x[:row_count] + x[row_count:]
-        x = x + jnp.dot(high, table[POINTS_PAD:, columns], preferred_element_type=f32)
+        x = jnp.dot(twice, table[:, columns], preferred_element_type=f32)
+        x = x + jnp.dot(low, table[:POINTS_PAD, columns], preferred_element_type=f32)
         x = x.astype(bf16).astype(f32)
         for m in range(CHUNK // LANES):
             part, j = divmod(n * (CHUNK // LANES) + m, TILES)
@@ -185,10 +185,12 @@
         zero = jnp.zeros((8, LANES), f32)
 
         accs, last = (zero,) * count, t
-        for w in range(list_count):
-            s = source[t, w + jnp.minimum(last, 0)]
-            last = offset[t, w + jnp.minimum(s, 0)]
-            accs = pair(s * pitch, last * HAT_ROWS, accs)
+        for first in range(0, list_count, GROUP):
+            ahead = jnp.minimum(last, 0)
+            pairs = [(source[t, w + ahead], offset[t, w + ahead]) for w in range(first, first + GROUP)]
+            last = pairs[-1][1]
+            for s, o in pairs:
+                accs = pair(s * pitch, o * HAT_ROWS, accs)
         at = 0
         for c in range(comp_count):
             for h in range(halves):

time: 31.2 us -> 25.8 us (0.83)
  Pallas kernels: 18.8 us -> 13.4 us
    pallas_call x1, Pallas kernels: 13.3 us -> 7.87 us  [on_device(): pl.pallas_call(functools.partial(interact_kernel, comp_count), out_shape=...]
  transfers between devices with their start and end apart: 5 -> 5, of which waited for: 1 -> 1; matrix products, arithmetic and copies ran while one was open for 7% -> 8% of each run, Pallas kernels for 1% -> 2%
where the time goes in v10:
time: 25.8 us; the launch traced here: 25.6 us
  Pallas kernels  13.4 us (52%)
  starting transfers between devices  8.9 us (34%)
  local copies, waits for them, and re-layouts  2.15 us (8%)
  waiting for transfers between devices  1.02 us (4%)
    pallas_call x1, Pallas kernels, on_device(): pl.pallas_call(functools.partial(interact_kernel, comp_count), out_shape=...  7.87 us
    ppermute x2, starting transfers between devices, swap_groups(): return lax.ppermute(x, 'group', pairs + [(j, i) for i, j in pairs])  5.26 us
    ppermute x3, starting transfers between devices, swap(): return lax.ppermute(x, 'dev', [(i, i ^ k) for i in range(peers)])  3.64 us
    unnamed x19, local copies, waits for them, and re-layouts  2.15 us
    pallas_call x1, Pallas kernels, on_device(): pl.pallas_call(forward_kernel, out_shape=jax.ShapeDtypeStruct((slots * so...  1.81 us
    pallas_call x1, Pallas kernels, on_device(): pl.pallas_call(inverse_kernel, out_shape=jax.ShapeDtypeStruct((comp_count...  1.66 us
    pallas_call x1, Pallas kernels, on_device(): pl.pallas_call(pack_kernel, out_shape=(jax.ShapeDtypeStruct((2, *boxes.sh...  1.6 us
    ppermute x2, waiting for transfers between devices, swap_groups(): return lax.ppermute(x, 'group', pairs + [(j, i) for i, j in pairs])  1.01 us
  transfers between devices with their start and end apart: 5, of which 1 were waited for; matrix products, arithmetic and copies ran while one was open for 8% of the time, Pallas kernels for 2%

profile of v10, /device:TPU:1, one launch (start us, length us, event | category | flops | bytes accessed | tf_op | source)
XLA Modules:
  0.0 25.6 jit_solution(11812511163684838774)
XLA Ops:
  0.0 1.6 %pack.1 = (f32[2,3,4,152]{3,2,1,0:T(4,128)}, f32[3,4,152]{2,1,0:T(4,128)}, f32[3,4,152]{2,1,0:T(4,128)}, f32[3,4,152]{2,1,0:T(4,128)}) custom-call(f32[3,16,152]{2,1,0:T(8,128)} %bitcast.8, s32[4,4]{1,0:T(4,128)} %bitcast.10, s32[2,4]{1,0:T(2,128)} %bitcast.12), custom_call_target="tpu_custom_call" | custom-call | tf_op jit(solution)/shard_map/pack/pallas_call | solution.py:254
  1.6 0.0 copy-start.8
  1.6 0.0 copy-start.7
  1.6 0.0 copy-start.6
  1.6 2.1 %collective-permute-start = (f32[2,3,4,152]{3,2,1,0:T(4,128)}, f32[2,3,4,152]{3,2,1,0:T(4,128)S(1)}, u32[]{:S(2)}, u32[]{:S(2)}) collective-permute-start(f32[2,3,4,152]{3,2,1,0:T(4,128)} %get-tuple-element.13), channel_id=1, source_target_pairs={{0,1},{1,0},{2,3},{3,2},{4,5},{5,4},{6,7},{7,6},{8,9},{9,8},{10,11... | collective-permute-start | bytes 43784 | tf_op jit(solution)/shard_map/ppermute | solution.py:263
  3.7 2.1 %copy.11 = bf16[316,2,2304]{2,0,1:T(8,128)(2,1)S(1)} copy(bf16[316,2,2304]{2,1,0:T(2,128)(2,1)} %param.9) | data formatting | bytes 5824512 | tf_op args[1]
  5.8 0.0 collective-permute-done.from_near
  5.8 1.3 %collective-permute-start.1 = (f32[2,3,4,152]{3,2,1,0:T(4,128)S(1)}, f32[2,3,4,152]{3,2,1,0:T(4,128)S(1)}, u32[]{:S(2)}, u32[]{:S(2)}) collective-permute-start(f32[2,3,4,152]{3,2,1,0:T(4,128)S(1)} %collective-permute-done.from_near), channel_id=1, source_target_pairs={{0,2},{1,3},{2,0},{3,1},{4,6},{5,7},{6,4},{7,5},{8,10},{9,11},{10,... | collective-permute-start | bytes 43784 | tf_op jit(solution)/shard_map/ppermute | solution.py:263
  7.1 0.0 copy-done.8
  7.1 0.2 collective-permute-start.2
  7.4 0.0 copy-done.7
  7.4 1.5 %collective-permute-start.3 = (f32[3,4,152]{2,1,0:T(4,128)S(1)}, f32[3,4,152]{2,1,0:T(4,128)S(1)}, u32[]{:S(2)}, u32[]{:S(2)}) collective-permute-start(f32[3,4,152]{2,1,0:T(4,128)S(1)} %copy-done.7), channel_id=1, source_target_pairs={{0,4},{8,12},{16,20},{24,28},{4,0},{12,8},{20,16},{28,24},{1,5},{9... | collective-permute-start | bytes 21896 | tf_op jit(solution)/shard_map/ppermute | solution.py:267
  8.9 0.0 copy-done.6
  8.9 0.0 copy-start
  8.9 3.7 %collective-permute-start.4 = (f32[3,4,152]{2,1,0:T(4,128)S(1)}, f32[3,4,152]{2,1,0:T(4,128)S(1)}, u32[]{:S(2)}, u32[]{:S(2)}) collective-permute-start(f32[3,4,152]{2,1,0:T(4,128)S(1)} %copy-done.6), channel_id=1, source_target_pairs={{4,8},{12,16},{20,24},{8,4},{16,12},{24,20},{5,9},{13,17},{21,25},... | collective-permute-start | bytes 21896 | tf_op jit(solution)/shard_map/ppermute | solution.py:267
  12.7 0.5 %prepare.1.hat = f32[11700,128]{1,0:T(8,128)S(1)} custom-call(bf16[2,316,2304]{2,1,0:T(8,128)(2,1)S(1)} %bitcast.7), custom_call_target="tpu_custom_call" | custom-call | flops 1456128 | bytes 8736768 | tf_op jit(solution)/shard_map/prepare/pallas_call | solution.py:277
  13.1 0.0 copy-start.4
  13.1 0.0 copy-start.5
  13.2 0.0 collective-permute-done.2.refs_0_
  13.2 0.0 collective-permute-done.3.refs_1_
  13.2 1.0 %collective-permute-done.4.refs_2_ = f32[3,4,152]{2,1,0:T(4,128)S(1)} collective-permute-done((f32[3,4,152]{2,1,0:T(4,128)S(1)}, f32[3,4,152]{2,1,0:T(4,128)S(1)}, u32[]{:S(2)}, u32[]{:S(2)}) %collective-permute-start.4) | collective-permute-done | bytes 7328 | tf_op jit(solution)/shard_map/ppermute | solution.py:267
  14.2 0.0 collective-permute-done.1.relayed
  14.2 0.0 copy-done
  14.2 0.0 copy-done.1
  14.2 0.0 copy-done.3
  14.2 1.8 %forward.1.main = f32[4528,128]{1,0:T(8,128)S(1)} custom-call(s32[4,4]{1,0:T(4,128)S(1)} %bitcast.11, f32[3,16,152]{2,1,0:T(8,128)S(1)} %bitcast.9, f32[2,3,4,152]{3,2,1,0:T(4,128)S(1)} %collective-permute-done.from_near, f32[2,3,4,152]{3,2,1,0:T(4,128)S(1)} %collective-permute-done.1.relayed, f32[3,4,152]{2,1,0:T(4,128)S(1)} %collective-permute-done.2.refs_0_, ...), custom_call_target="tpu_custom_call" | custom-call | tf_op jit(solution)/shard_map/forward/pallas_call | solution.py:292
  16.0 0.0 copy-done.4
  16.0 0.0 copy-done.5
  16.0 0.0 copy-start.2
  16.1 7.9 %interact.1 = (f32[1632,128]{1,0:T(8,128)S(1)}, f32[2,126,128]{2,1,0:T(8,128)S(1)}) custom-call(s32[16,32]{1,0:T(8,128)S(1)} %copy-done.4, s32[16,32]{1,0:T(8,128)S(1)} %copy-done.5, f32[11700,128]{1,0:T(8,128)S(1)} %prepare.1.hat, f32[4528,128]{1,0:T(8,128)S(1)} %forward.1.main), custom_call_target="tpu_custom_call" | custom-call | tf_op jit(solution)/shard_map/interact/pallas_call | solution.py:301
  23.9 0.0 copy-done.2
  23.9 1.7 %inverse.1 = f32[3,16,152]{2,1,0:T(8,128)} custom-call(f32[1632,128]{1,0:T(8,128)S(1)} %get-tuple-element.19.total, f32[2,126,128]{2,1,0:T(8,128)S(1)} %get-tuple-element.20.total_tail, bf16[320,4608]{1,0:T(8,128)(2,1)S(1)} %copy-done, f32[1,4608]{1,0:T(1,128)S(1)} %copy-done.2), custom_call_target="tpu_custom_call" | custom-call | tf_op jit(solution)/shard_map/inverse/pallas_call | solution.py:312
  (2 shorter events, 0.0 us)
Async XLA Ops:
  1.6 5.5 %copy-start.8 = (f32[3,4,152]{2,1,0:T(4,128)S(1)}, f32[3,4,152]{2,1,0:T(4,128)}, u32[]{:S(2)}) copy-start(f32[3,4,152]{2,1,0:T(4,128)} %get-tuple-element.16) | copy-start | bytes 21892
  1.6 5.8 %copy-start.7 = (f32[3,4,152]{2,1,0:T(4,128)S(1)}, f32[3,4,152]{2,1,0:T(4,128)}, u32[]{:S(2)}) copy-start(f32[3,4,152]{2,1,0:T(4,128)} %get-tuple-element.17) | copy-start | bytes 21892
  1.6 7.3 %copy-start.6 = (f32[3,4,152]{2,1,0:T(4,128)S(1)}, f32[3,4,152]{2,1,0:T(4,128)}, u32[]{:S(2)}) copy-start(f32[3,4,152]{2,1,0:T(4,128)} %get-tuple-element.18) | copy-start | bytes 21892
  1.6 4.2 %collective-permute-start = (f32[2,3,4,152]{3,2,1,0:T(4,128)}, f32[2,3,4,152]{3,2,1,0:T(4,128)S(1)}, u32[]{:S(2)}, u32[]{:S(2)}) collective-permute-start(f32[2,3,4,152]{3,2,1,0:T(4,128)} %get-tuple-element.13), channel_id=1, source_target_pairs={{0,1},{1,0},{2,3},{3,2},{4,5},{5,4},{6,7},{7,6},{8,9},{9,8},{10,11... | collective-permute-start | bytes 43784 | tf_op jit(solution)/shard_map/ppermute | solution.py:263
  5.8 8.3 %collective-permute-start.1 = (f32[2,3,4,152]{3,2,1,0:T(4,128)S(1)}, f32[2,3,4,152]{3,2,1,0:T(4,128)S(1)}, u32[]{:S(2)}, u32[]{:S(2)}) collective-permute-start(f32[2,3,4,152]{3,2,1,0:T(4,128)S(1)} %collective-permute-done.from_near), channel_id=1, source_target_pairs={{0,2},{1,3},{2,0},{3,1},{4,6},{5,7},{6,4},{7,5},{8,10},{9,11},{10,... | collective-permute-start | bytes 43784 | tf_op jit(solution)/shard_map/ppermute | solution.py:263
  7.1 6.0 %collective-permute-start.2 = (f32[3,4,152]{2,1,0:T(4,128)S(1)}, f32[3,4,152]{2,1,0:T(4,128)S(1)}, u32[]{:S(2)}, u32[]{:S(2)}) collective-permute-start(f32[3,4,152]{2,1,0:T(4,128)S(1)} %copy-done.8), channel_id=1, source_target_pairs={{0,2},{1,3},{2,0},{3,1},{4,6},{5,7},{6,4},{7,5},{8,10},{9,11},{10,... | collective-permute-start | bytes 21896 | tf_op jit(solution)/shard_map/ppermute | solution.py:263
  7.4 5.8 %collective-permute-start.3 = (f32[3,4,152]{2,1,0:T(4,128)S(1)}, f32[3,4,152]{2,1,0:T(4,128)S(1)}, u32[]{:S(2)}, u32[]{:S(2)}) collective-permute-start(f32[3,4,152]{2,1,0:T(4,128)S(1)} %copy-done.7), channel_id=1, source_target_pairs={{0,4},{8,12},{16,20},{24,28},{4,0},{12,8},{20,16},{28,24},{1,5},{9... | collective-permute-start | bytes 21896 | tf_op jit(solution)/shard_map/ppermute | solution.py:267
  8.9 5.3 %copy-start = (bf16[320,4608]{1,0:T(8,128)(2,1)S(1)}, bf16[320,4608]{1,0:T(8,128)(2,1)}, u32[]{:S(2)}) copy-start(bf16[320,4608]{1,0:T(8,128)(2,1)} %constant.4.clone.refs_3_.table) | copy-start | bytes 8847364
  8.9 5.3 %copy-start.1 = (f32[16,3,152]{2,0,1:T(8,128)S(1)}, f32[16,3,152]{2,0,1:T(8,128)}, u32[]{:S(2)}) copy-start(f32[16,3,152]{2,0,1:T(8,128)} %param.8) | copy-start | bytes 87556
  8.9 5.3 %copy-start.3 = (s32[1,4,4]{2,1,0:T(4,128)S(1)}, s32[1,4,4]{2,1,0:T(4,128)}, u32[]{:S(2)}) copy-start(s32[1,4,4]{2,1,0:T(4,128)} %param.10) | copy-start | bytes 196
  8.9 5.3 %collective-permute-start.4 = (f32[3,4,152]{2,1,0:T(4,128)S(1)}, f32[3,4,152]{2,1,0:T(4,128)S(1)}, u32[]{:S(2)}, u32[]{:S(2)}) collective-permute-start(f32[3,4,152]{2,1,0:T(4,128)S(1)} %copy-done.6), channel_id=1, source_target_pairs={{4,8},{12,16},{20,24},{8,4},{16,12},{24,20},{5,9},{13,17},{21,25},... | collective-permute-start | bytes 21896 | tf_op jit(solution)/shard_map/ppermute | solution.py:267
  13.1 2.9 %copy-start.4 = (s32[16,32]{1,0:T(8,128)S(1)}, s32[16,32]{1,0:T(8,128)}, u32[]{:S(2)}) copy-start(s32[16,32]{1,0:T(8,128)} %source.1) | copy-start | bytes 6148
  13.1 2.9 %copy-start.5 = (s32[16,32]{1,0:T(8,128)S(1)}, s32[16,32]{1,0:T(8,128)}, u32[]{:S(2)}) copy-start(s32[16,32]{1,0:T(8,128)} %offset.1) | copy-start | bytes 6148
  16.0 7.9 %copy-start.2 = (f32[1,4608]{1,0:T(1,128)S(1)}, f32[1,4608]{1,0:T(1,128)}, u32[]{:S(2)}) copy-start(f32[1,4608]{1,0:T(1,128)} %constant.5.clone.factor) | copy-start | bytes 55300

commit v11 on v8

--- a/solution.py
+++ b/solution.py
@@ -20,9 +20,9 @@
 TAIL = TILES - MAIN
 PITCH = MAIN + 1
 TAIL_PITCH = 7
-HAT_ROWS = 2 * TILES + 1
+HAT_ROWS = 40
 POINTS_PAD = 160
-CHUNK = 256
+CHUNK = 768
 PIECE = 512
 UNROLL = 8
 
@@ -57,7 +57,11 @@
 
 
 def source_rows(comp_count):
-    return (2 * comp_count * MAIN + TAIL * 8) | 1
+    return ((2 * comp_count * MAIN // 8 + TAIL) | 1) * 8
+
+
+def kernel_row(part, tile):
+    return part * MAIN + tile if tile < MAIN else 2 * MAIN + (tile - MAIN) * 2 + part
 
 
 def source_row(comp_count, which, tile):
@@ -85,6 +89,7 @@
 
 def prepare_kernel(kernel_hat, hat):
     parts, count, _ = kernel_hat.shape
+    flat = hat.reshape(count * HAT_ROWS, LANES)
 
     def move(first, height):
         for part in range(parts):
@@ -93,8 +98,7 @@
                 for g in range(0, height, 8):
                     size = min(8, height - g)
                     piece = x[g : g + size]
-                    row = (first + g) * HAT_ROWS + part * TILES + j
-                    hat[pl.ds(row, size, stride=HAT_ROWS), :] = piece
+                    flat[pl.ds((first + g) * HAT_ROWS + kernel_row(part, j), size, stride=HAT_ROWS), :] = piece
 
     whole = count // 16
 
@@ -114,6 +118,7 @@
     row_count = rows.shape[0]
     slots = row_count // comp_count
     pitch = source_rows(comp_count)
+    flat = main.reshape(slots * pitch, LANES)
     f32, bf16 = jnp.float32, jnp.bfloat16
 
     member = lax.axis_index("dev")
@@ -150,12 +155,11 @@
                 piece = x[g * 8 : (g + 1) * 8, m * LANES : (m + 1) * LANES]
                 c, s = divmod(g * 8, slots)
                 row = source_row(comp_count, part * comp_count + c, j)
-                main[pl.ds(s * pitch + row, 8, stride=pitch), :] = piece
+                flat[pl.ds(s * pitch + row, 8, stride=pitch), :] = piece
 
 
 def interact_kernel(comp_count, source, offset, hat, main, total, total_tail):
     box_count, list_count = source.shape
-    pitch = source_rows(comp_count)
     f32 = jnp.float32
     plus = lax.broadcasted_iota(jnp.int32, (8, LANES), 0) < comp_count
     halves = MAIN // 8
@@ -164,26 +168,31 @@
     def _(t):
         def rows_of(first):
             return tuple(
-                (source[t, first + u] * pitch, offset[t, first + u] * HAT_ROWS) for u in range(UNROLL)
+                (source[t, first + u], offset[t, first + u]) for u in range(UNROLL)
             )
 
         def pair(s, o, accs):
-            k = [[hat[pl.ds(o + (r * TILES + 8 * h), 8), :] for h in range(halves)] for r in range(2)]
+            def kernel_tiles(part, tile):
+                row = kernel_row(part, tile)
+                return hat[o, row : row + 8, :]
+
+            def source_tiles(which, tile):
+                row = source_row(comp_count, which, tile)
+                return main[s, row : row + 8, :]
+
+            k = [[kernel_tiles(r, 8 * h) for h in range(halves)] for r in range(2)]
             accs = list(accs)
             at = 0
             for c in range(comp_count):
                 for h in range(halves):
-                    s_re = main[pl.ds(s + (source_row(comp_count, c, 8 * h)), 8), :]
-                    s_im = main[pl.ds(s + (source_row(comp_count, comp_count + c, 8 * h)), 8), :]
+                    s_re, s_im = source_tiles(c, 8 * h), source_tiles(comp_count + c, 8 * h)
                     accs[at] = accs[at] + (k[0][h] * s_re - k[1][h] * s_im)
                     accs[at + 1] = accs[at + 1] + (k[0][h] * s_im + k[1][h] * s_re)
                     at += 2
             for j in range(MAIN, TILES):
-                x = main[pl.ds(s + source_row(comp_count, 0, j), 8), :]
-                k_re = hat[pl.ds(o + j, 8, stride=0), :]
-                k_im = hat[pl.ds(o + TILES + j, 8, stride=0), :]
-                accs[at] = accs[at] + k_re * x
-                accs[at + 1] = accs[at + 1] + k_im * x
+                x = source_tiles(0, j)
+                for r in range(2):
+                    accs[at + r] = accs[at + r] + hat[o, pl.ds(kernel_row(r, j), 8, stride=0), :] * x
                 at += 2
             return tuple(accs)
 
@@ -263,7 +272,6 @@
         out_shape=(jax.ShapeDtypeStruct((2, *boxes.shape), f32),) + (boxes,) * (peers - 3) + (side,) * 2,
         in_specs=[vmem, smem, smem],
         out_specs=(vmem,) * peers,
-        compiler_params=pltpu.CompilerParams(vmem_limit_bytes=4 * 1024 * 1024),
         name="pack",
     )(density, send_list[0], halo_list[0])
 
@@ -284,7 +292,7 @@
     offsets = kernel_hat.shape[0]
     hat = pl.pallas_call(
         prepare_kernel,
-        out_shape=jax.ShapeDtypeStruct((offsets * HAT_ROWS + 8, LANES), f32),
+        out_shape=jax.ShapeDtypeStruct((offsets, HAT_ROWS, LANES), f32),
         in_specs=[vmem],
         out_specs=vmem,
         compiler_params=pltpu.CompilerParams(vmem_limit_bytes=16 * 1024 * 1024),
@@ -299,7 +307,7 @@
     arrays = (send_list[0], density, from_near, relayed, *from_far, from_first, from_second, table)
     main = pl.pallas_call(
         forward_kernel,
-        out_shape=jax.ShapeDtypeStruct((slots * source_rows(comp_count) + 8, LANES), f32),
+        out_shape=jax.ShapeDtypeStruct((slots, source_rows(comp_count), LANES), f32),
         in_specs=[smem] + [vmem] * (len(arrays) - 1),
         out_specs=vmem,
         scratch_shapes=[pltpu.VMEM((row_count, POINTS_PAD), f32)],

time: 24.7 us -> 24.2 us (0.980)
  Pallas kernels: 10.1 us -> 12.3 us
  local copies, waits for them, and re-layouts: 4.3 us -> 2.15 us
  waiting for transfers between devices: 1.24 us -> 0.54 us
    unnamed x19, local copies, waits for them, and re-layouts: 4.3 us -> 2.15 us
    pallas_call x1, Pallas kernels: 0.71 us -> 1.6 us  [on_device(): pl.pallas_call(pack_kernel, out_shape=(jax.ShapeDtypeStruct((2, *boxes.sh...]
    ppermute x2, waiting for transfers between devices: 1.23 us -> 0.53 us  [swap_groups(): return lax.ppermute(x, 'group', pairs + [(j, i) for i, j in pairs])]
    pallas_call x1, Pallas kernels: 5.56 us -> 6.25 us  [on_device(): pl.pallas_call(functools.partial(interact_kernel, comp_count), out_shape=...]
    pallas_call x2, Pallas kernels: 2.22 us -> 2.77 us  [the longest x1 1.82 us: on_device(): pl.pallas_call(forward_kernel, out_shape=jax.ShapeDtypeStruct((slots, sou...]
  transfers between devices with their start and end apart: 5 -> 5, of which waited for: 1 -> 1; matrix products, arithmetic and copies ran while one was open for 9% -> 9% of each run, Pallas kernels for 2% -> 4%
where the time goes in v11:
time: 24.2 us; the launch traced here: 24 us
  Pallas kernels  12.3 us (51%)
  starting transfers between devices  8.9 us (37%)
  local copies, waits for them, and re-layouts  2.15 us (9%)
  waiting for transfers between devices  0.54 us (2%)
    pallas_call x1, Pallas kernels, on_device(): pl.pallas_call(functools.partial(interact_kernel, comp_count), out_shape=...  6.25 us
    ppermute x2, starting transfers between devices, swap_groups(): return lax.ppermute(x, 'group', pairs + [(j, i) for i, j in pairs])  5.26 us
    ppermute x3, starting transfers between devices, swap(): return lax.ppermute(x, 'dev', [(i, i ^ k) for i in range(peers)])  3.64 us
    unnamed x19, local copies, waits for them, and re-layouts  2.15 us
    pallas_call x1, Pallas kernels, on_device(): pl.pallas_call(forward_kernel, out_shape=jax.ShapeDtypeStruct((slots, sou...  1.82 us
    pallas_call x1, Pallas kernels, on_device(): pl.pallas_call(inverse_kernel, out_shape=jax.ShapeDtypeStruct((comp_count...  1.65 us
    pallas_call x1, Pallas kernels, on_device(): pl.pallas_call(pack_kernel, out_shape=(jax.ShapeDtypeStruct((2, *boxes.sh...  1.6 us
    pallas_call x1, Pallas kernels, on_device(): pl.pallas_call(prepare_kernel, out_shape=jax.ShapeDtypeStruct((offsets, H...  0.95 us
  transfers between devices with their start and end apart: 5, of which 1 were waited for; matrix products, arithmetic and copies ran while one was open for 9% of the time, Pallas kernels for 4%

profile of v11, /device:TPU:1, one launch (start us, length us, event | category | flops | bytes accessed | tf_op | source)
XLA Modules:
  0.0 24.0 jit_solution(4526837377392224552)
XLA Ops:
  0.0 1.6 %pack.1 = (f32[2,3,4,152]{3,2,1,0:T(4,128)}, f32[3,4,152]{2,1,0:T(4,128)}, f32[3,4,152]{2,1,0:T(4,128)}, f32[3,4,152]{2,1,0:T(4,128)}) custom-call(f32[3,16,152]{2,1,0:T(8,128)} %bitcast.8, s32[4,4]{1,0:T(4,128)} %bitcast.10, s32[2,4]{1,0:T(2,128)} %bitcast.12), custom_call_target="tpu_custom_call" | custom-call | tf_op jit(solution)/shard_map/pack/pallas_call | solution.py:270
  1.6 0.0 copy-start.8
  1.6 0.0 copy-start.7
  1.6 2.1 %collective-permute-start = (f32[2,3,4,152]{3,2,1,0:T(4,128)}, f32[2,3,4,152]{3,2,1,0:T(4,128)S(1)}, u32[]{:S(2)}, u32[]{:S(2)}) collective-permute-start(f32[2,3,4,152]{3,2,1,0:T(4,128)} %get-tuple-element.13), channel_id=1, source_target_pairs={{0,1},{1,0},{2,3},{3,2},{4,5},{5,4},{6,7},{7,6},{8,9},{9,8},{10,11... | collective-permute-start | bytes 43784 | tf_op jit(solution)/shard_map/ppermute | solution.py:279
  3.7 2.1 %copy.11 = bf16[316,2,2304]{2,0,1:T(8,128)(2,1)S(1)} copy(bf16[316,2,2304]{2,1,0:T(2,128)(2,1)} %param.9) | data formatting | bytes 5824512 | tf_op args[1]
  5.8 0.0 collective-permute-done.from_near
  5.8 1.3 %collective-permute-start.1 = (f32[2,3,4,152]{3,2,1,0:T(4,128)S(1)}, f32[2,3,4,152]{3,2,1,0:T(4,128)S(1)}, u32[]{:S(2)}, u32[]{:S(2)}) collective-permute-start(f32[2,3,4,152]{3,2,1,0:T(4,128)S(1)} %collective-permute-done.from_near), channel_id=1, source_target_pairs={{0,2},{1,3},{2,0},{3,1},{4,6},{5,7},{6,4},{7,5},{8,10},{9,11},{10,... | collective-permute-start | bytes 43784 | tf_op jit(solution)/shard_map/ppermute | solution.py:279
  7.1 0.0 copy-done.8
  7.1 0.2 collective-permute-start.2
  7.4 0.0 copy-done.7
  7.4 1.5 %collective-permute-start.3 = (f32[3,4,152]{2,1,0:T(4,128)S(1)}, f32[3,4,152]{2,1,0:T(4,128)S(1)}, u32[]{:S(2)}, u32[]{:S(2)}) collective-permute-start(f32[3,4,152]{2,1,0:T(4,128)S(1)} %copy-done.7), channel_id=1, source_target_pairs={{0,4},{8,12},{16,20},{24,28},{4,0},{12,8},{20,16},{28,24},{1,5},{9... | collective-permute-start | bytes 21896 | tf_op jit(solution)/shard_map/ppermute | solution.py:283
  8.9 0.0 copy-done.6
  8.9 0.0 copy-start
  8.9 0.0 copy-start.1
  8.9 3.7 %collective-permute-start.4 = (f32[3,4,152]{2,1,0:T(4,128)S(1)}, f32[3,4,152]{2,1,0:T(4,128)S(1)}, u32[]{:S(2)}, u32[]{:S(2)}) collective-permute-start(f32[3,4,152]{2,1,0:T(4,128)S(1)} %copy-done.6), channel_id=1, source_target_pairs={{4,8},{12,16},{20,24},{8,4},{16,12},{24,20},{5,9},{13,17},{21,25},... | collective-permute-start | bytes 21896 | tf_op jit(solution)/shard_map/ppermute | solution.py:283
  12.7 0.9 %prepare.1.hat = f32[316,40,128]{2,1,0:T(8,128)S(1)} custom-call(bf16[2,316,2304]{2,1,0:T(8,128)(2,1)S(1)} %bitcast.7), custom_call_target="tpu_custom_call" | custom-call | flops 1456128 | bytes 8736768 | tf_op jit(solution)/shard_map/prepare/pallas_call | solution.py:293
  13.6 0.0 copy-start.4
  13.6 0.0 copy-start.5
  13.6 0.0 collective-permute-done.2.refs_0_
  13.6 0.0 collective-permute-done.3.refs_1_
  13.7 0.5 %collective-permute-done.4.refs_2_ = f32[3,4,152]{2,1,0:T(4,128)S(1)} collective-permute-done((f32[3,4,152]{2,1,0:T(4,128)S(1)}, f32[3,4,152]{2,1,0:T(4,128)S(1)}, u32[]{:S(2)}, u32[]{:S(2)}) %collective-permute-start.4) | collective-permute-done | bytes 7328 | tf_op jit(solution)/shard_map/ppermute | solution.py:283
  14.2 0.0 collective-permute-done.1.relayed
  14.2 0.0 copy-done
  14.2 0.0 copy-done.1
  14.2 0.0 copy-done.3
  14.2 1.8 %forward.1.main = f32[40,120,128]{2,1,0:T(8,128)S(1)} custom-call(s32[4,4]{1,0:T(4,128)S(1)} %bitcast.11, f32[3,16,152]{2,1,0:T(8,128)S(1)} %bitcast.9, f32[2,3,4,152]{3,2,1,0:T(4,128)S(1)} %collective-permute-done.from_near, f32[2,3,4,152]{3,2,1,0:T(4,128)S(1)} %collective-permute-done.1.relayed, f32[3,4,152]{2,1,0:T(4,128)S(1)} %collective-permute-done.2.refs_0_, ...), custom_call_target="tpu_custom_call" | custom-call | tf_op jit(solution)/shard_map/forward/pallas_call | solution.py:308
  16.0 0.0 copy-done.4
  16.0 0.0 copy-done.5
  16.1 0.0 copy-start.2
  16.1 6.2 %interact.1 = (f32[1632,128]{1,0:T(8,128)S(1)}, f32[2,126,128]{2,1,0:T(8,128)S(1)}) custom-call(s32[16,32]{1,0:T(8,128)S(1)} %copy-done.4, s32[16,32]{1,0:T(8,128)S(1)} %copy-done.5, f32[316,40,128]{2,1,0:T(8,128)S(1)} %prepare.1.hat, f32[40,120,128]{2,1,0:T(8,128)S(1)} %forward.1.main), custom_call_target="tpu_custom_call" | custom-call | tf_op jit(solution)/shard_map/interact/pallas_call | solution.py:317
  22.3 0.0 copy-done.2
  22.3 1.6 %inverse.1 = f32[3,16,152]{2,1,0:T(8,128)} custom-call(f32[1632,128]{1,0:T(8,128)S(1)} %get-tuple-element.19.total, f32[2,126,128]{2,1,0:T(8,128)S(1)} %get-tuple-element.20.total_tail, bf16[320,4608]{1,0:T(8,128)(2,1)S(1)} %copy-done, f32[1,4608]{1,0:T(1,128)S(1)} %copy-done.2), custom_call_target="tpu_custom_call" | custom-call | tf_op jit(solution)/shard_map/inverse/pallas_call | solution.py:328
  (2 shorter events, 0.0 us)
Async XLA Ops:
  1.6 5.5 %copy-start.8 = (f32[3,4,152]{2,1,0:T(4,128)S(1)}, f32[3,4,152]{2,1,0:T(4,128)}, u32[]{:S(2)}) copy-start(f32[3,4,152]{2,1,0:T(4,128)} %get-tuple-element.16) | copy-start | bytes 21892
  1.6 5.8 %copy-start.7 = (f32[3,4,152]{2,1,0:T(4,128)S(1)}, f32[3,4,152]{2,1,0:T(4,128)}, u32[]{:S(2)}) copy-start(f32[3,4,152]{2,1,0:T(4,128)} %get-tuple-element.17) | copy-start | bytes 21892
  1.6 7.3 %copy-start.6 = (f32[3,4,152]{2,1,0:T(4,128)S(1)}, f32[3,4,152]{2,1,0:T(4,128)}, u32[]{:S(2)}) copy-start(f32[3,4,152]{2,1,0:T(4,128)} %get-tuple-element.18) | copy-start | bytes 21892
  1.6 4.2 %collective-permute-start = (f32[2,3,4,152]{3,2,1,0:T(4,128)}, f32[2,3,4,152]{3,2,1,0:T(4,128)S(1)}, u32[]{:S(2)}, u32[]{:S(2)}) collective-permute-start(f32[2,3,4,152]{3,2,1,0:T(4,128)} %get-tuple-element.13), channel_id=1, source_target_pairs={{0,1},{1,0},{2,3},{3,2},{4,5},{5,4},{6,7},{7,6},{8,9},{9,8},{10,11... | collective-permute-start | bytes 43784 | tf_op jit(solution)/shard_map/ppermute | solution.py:279
  5.8 8.3 %collective-permute-start.1 = (f32[2,3,4,152]{3,2,1,0:T(4,128)S(1)}, f32[2,3,4,152]{3,2,1,0:T(4,128)S(1)}, u32[]{:S(2)}, u32[]{:S(2)}) collective-permute-start(f32[2,3,4,152]{3,2,1,0:T(4,128)S(1)} %collective-permute-done.from_near), channel_id=1, source_target_pairs={{0,2},{1,3},{2,0},{3,1},{4,6},{5,7},{6,4},{7,5},{8,10},{9,11},{10,... | collective-permute-start | bytes 43784 | tf_op jit(solution)/shard_map/ppermute | solution.py:279
  7.1 6.5 %collective-permute-start.2 = (f32[3,4,152]{2,1,0:T(4,128)S(1)}, f32[3,4,152]{2,1,0:T(4,128)S(1)}, u32[]{:S(2)}, u32[]{:S(2)}) collective-permute-start(f32[3,4,152]{2,1,0:T(4,128)S(1)} %copy-done.8), channel_id=1, source_target_pairs={{0,2},{1,3},{2,0},{3,1},{4,6},{5,7},{6,4},{7,5},{8,10},{9,11},{10,... | collective-permute-start | bytes 21896 | tf_op jit(solution)/shard_map/ppermute | solution.py:279
  7.4 6.3 %collective-permute-start.3 = (f32[3,4,152]{2,1,0:T(4,128)S(1)}, f32[3,4,152]{2,1,0:T(4,128)S(1)}, u32[]{:S(2)}, u32[]{:S(2)}) collective-permute-start(f32[3,4,152]{2,1,0:T(4,128)S(1)} %copy-done.7), channel_id=1, source_target_pairs={{0,4},{8,12},{16,20},{24,28},{4,0},{12,8},{20,16},{28,24},{1,5},{9... | collective-permute-start | bytes 21896 | tf_op jit(solution)/shard_map/ppermute | solution.py:283
  8.9 5.3 %copy-start = (bf16[320,4608]{1,0:T(8,128)(2,1)S(1)}, bf16[320,4608]{1,0:T(8,128)(2,1)}, u32[]{:S(2)}) copy-start(bf16[320,4608]{1,0:T(8,128)(2,1)} %constant.4.clone.refs_3_.table) | copy-start | bytes 8847364
  8.9 5.3 %copy-start.1 = (f32[16,3,152]{2,0,1:T(8,128)S(1)}, f32[16,3,152]{2,0,1:T(8,128)}, u32[]{:S(2)}) copy-start(f32[16,3,152]{2,0,1:T(8,128)} %param.8) | copy-start | bytes 87556
  8.9 5.3 %copy-start.3 = (s32[1,4,4]{2,1,0:T(4,128)S(1)}, s32[1,4,4]{2,1,0:T(4,128)}, u32[]{:S(2)}) copy-start(s32[1,4,4]{2,1,0:T(4,128)} %param.10) | copy-start | bytes 196
  8.9 5.3 %collective-permute-start.4 = (f32[3,4,152]{2,1,0:T(4,128)S(1)}, f32[3,4,152]{2,1,0:T(4,128)S(1)}, u32[]{:S(2)}, u32[]{:S(2)}) collective-permute-start(f32[3,4,152]{2,1,0:T(4,128)S(1)} %copy-done.6), channel_id=1, source_target_pairs={{4,8},{12,16},{20,24},{8,4},{16,12},{24,20},{5,9},{13,17},{21,25},... | collective-permute-start | bytes 21896 | tf_op jit(solution)/shard_map/ppermute | solution.py:283
  13.6 2.4 %copy-start.4 = (s32[16,32]{1,0:T(8,128)S(1)}, s32[16,32]{1,0:T(8,128)}, u32[]{:S(2)}) copy-start(s32[16,32]{1,0:T(8,128)} %source.1) | copy-start | bytes 6148
  13.6 2.4 %copy-start.5 = (s32[16,32]{1,0:T(8,128)S(1)}, s32[16,32]{1,0:T(8,128)}, u32[]{:S(2)}) copy-start(s32[16,32]{1,0:T(8,128)} %offset.1) | copy-start | bytes 6148
  16.1 6.3 %copy-start.2 = (f32[1,4608]{1,0:T(1,128)S(1)}, f32[1,4608]{1,0:T(1,128)}, u32[]{:S(2)}) copy-start(f32[1,4608]{1,0:T(1,128)} %constant.5.clone.factor) | copy-start | bytes 55300

commit v12 on v8

--- a/solution.py
+++ b/solution.py
@@ -66,6 +66,10 @@
     return 2 * comp_count * MAIN + (tile - MAIN) * 8 + which
 
 
+def kernel_row(part, tile):
+    return part * MAIN + tile if tile < MAIN else 2 * MAIN + (tile - MAIN) * 2 + part
+
+
 def pack_kernel(density, send_list, halo_list, *outs):
     peers, cap = send_list.shape
     rim = halo_list.shape[1]
@@ -93,7 +97,7 @@
                 for g in range(0, height, 8):
                     size = min(8, height - g)
                     piece = x[g : g + size]
-                    row = (first + g) * HAT_ROWS + part * TILES + j
+                    row = (first + g) * HAT_ROWS + kernel_row(part, j)
                     hat[pl.ds(row, size, stride=HAT_ROWS), :] = piece
 
     whole = count // 16
@@ -168,7 +172,7 @@
             )
 
         def pair(s, o, accs):
-            k = [[hat[pl.ds(o + (r * TILES + 8 * h), 8), :] for h in range(halves)] for r in range(2)]
+            k = [[hat[pl.ds(o + kernel_row(r, 8 * h), 8), :] for h in range(halves)] for r in range(2)]
             accs = list(accs)
             at = 0
             for c in range(comp_count):
@@ -178,12 +182,12 @@
                     accs[at] = accs[at] + (k[0][h] * s_re - k[1][h] * s_im)
                     accs[at + 1] = accs[at + 1] + (k[0][h] * s_im + k[1][h] * s_re)
                     at += 2
-            for j in range(MAIN, TILES):
-                x = main[pl.ds(s + source_row(comp_count, 0, j), 8), :]
-                k_re = hat[pl.ds(o + j, 8, stride=0), :]
-                k_im = hat[pl.ds(o + TILES + j, 8, stride=0), :]
-                accs[at] = accs[at] + k_re * x
-                accs[at + 1] = accs[at + 1] + k_im * x
+            k_tail = hat[pl.ds(o + kernel_row(0, MAIN), 8), :]
+            for j in range(TAIL):
+                x = main[pl.ds(s + source_row(comp_count, 0, MAIN + j), 8), :]
+                for r in range(2):
+                    row = 2 * j + r
+                    accs[at + r] = accs[at + r] + jnp.broadcast_to(k_tail[row : row + 1], (8, LANES)) * x
                 at += 2
             return tuple(accs)
 
@@ -263,7 +267,6 @@
         out_shape=(jax.ShapeDtypeStruct((2, *boxes.shape), f32),) + (boxes,) * (peers - 3) + (side,) * 2,
         in_specs=[vmem, smem, smem],
         out_specs=(vmem,) * peers,
-        compiler_params=pltpu.CompilerParams(vmem_limit_bytes=4 * 1024 * 1024),
         name="pack",
     )(density, send_list[0], halo_list[0])
 

time: 24.7 us -> 23.7 us (0.960)
  local copies, waits for them, and re-layouts: 4.3 us -> 2.15 us
  Pallas kernels: 10.1 us -> 11.3 us
    unnamed x19, local copies, waits for them, and re-layouts: 4.3 us -> 2.15 us
    pallas_call x1, Pallas kernels: 0.71 us -> 1.6 us  [on_device(): pl.pallas_call(pack_kernel, out_shape=(jax.ShapeDtypeStruct((2, *boxes.sh...]
where the time goes in v12:
time: 23.7 us; the launch traced here: 23.5 us
  Pallas kernels  11.3 us (48%)
  starting transfers between devices  8.9 us (38%)
  local copies, waits for them, and re-layouts  2.15 us (9%)
  waiting for transfers between devices  1.02 us (4%)
    pallas_call x1, Pallas kernels, on_device(): pl.pallas_call(functools.partial(interact_kernel, comp_count), out_shape=...  5.77 us
    ppermute x2, starting transfers between devices, swap_groups(): return lax.ppermute(x, 'group', pairs + [(j, i) for i, j in pairs])  5.26 us
    ppermute x3, starting transfers between devices, swap(): return lax.ppermute(x, 'dev', [(i, i ^ k) for i in range(peers)])  3.64 us
    unnamed x19, local copies, waits for them, and re-layouts  2.15 us
    pallas_call x1, Pallas kernels, on_device(): pl.pallas_call(forward_kernel, out_shape=jax.ShapeDtypeStruct((slots * so...  1.76 us
    pallas_call x1, Pallas kernels, on_device(): pl.pallas_call(inverse_kernel, out_shape=jax.ShapeDtypeStruct((comp_count...  1.66 us
    pallas_call x1, Pallas kernels, on_device(): pl.pallas_call(pack_kernel, out_shape=(jax.ShapeDtypeStruct((2, *boxes.sh...  1.6 us
    ppermute x2, waiting for transfers between devices, swap_groups(): return lax.ppermute(x, 'group', pairs + [(j, i) for i, j in pairs])  1.01 us
  transfers between devices with their start and end apart: 5, of which 1 were waited for; matrix products, arithmetic and copies ran while one was open for 9% of the time, Pallas kernels for 2%

profile of v12, /device:TPU:1, one launch (start us, length us, event | category | flops | bytes accessed | tf_op | source)
XLA Modules:
  0.0 23.5 jit_solution(14185870854153193539)
XLA Ops:
  0.0 1.6 %pack.1 = (f32[2,3,4,152]{3,2,1,0:T(4,128)}, f32[3,4,152]{2,1,0:T(4,128)}, f32[3,4,152]{2,1,0:T(4,128)}, f32[3,4,152]{2,1,0:T(4,128)}) custom-call(f32[3,16,152]{2,1,0:T(8,128)} %bitcast.8, s32[4,4]{1,0:T(4,128)} %bitcast.10, s32[2,4]{1,0:T(2,128)} %bitcast.12), custom_call_target="tpu_custom_call" | custom-call | tf_op jit(solution)/shard_map/pack/pallas_call | solution.py:265
  1.6 0.0 copy-start.8
  1.6 0.0 copy-start.7
  1.6 0.0 copy-start.6
  1.6 2.1 %collective-permute-start = (f32[2,3,4,152]{3,2,1,0:T(4,128)}, f32[2,3,4,152]{3,2,1,0:T(4,128)S(1)}, u32[]{:S(2)}, u32[]{:S(2)}) collective-permute-start(f32[2,3,4,152]{3,2,1,0:T(4,128)} %get-tuple-element.13), channel_id=1, source_target_pairs={{0,1},{1,0},{2,3},{3,2},{4,5},{5,4},{6,7},{7,6},{8,9},{9,8},{10,11... | collective-permute-start | bytes 43784 | tf_op jit(solution)/shard_map/ppermute | solution.py:274
  3.7 2.1 %copy.11 = bf16[316,2,2304]{2,0,1:T(8,128)(2,1)S(1)} copy(bf16[316,2,2304]{2,1,0:T(2,128)(2,1)} %param.9) | data formatting | bytes 5824512 | tf_op args[1]
  5.8 0.0 collective-permute-done.from_near
  5.8 1.3 %collective-permute-start.1 = (f32[2,3,4,152]{3,2,1,0:T(4,128)S(1)}, f32[2,3,4,152]{3,2,1,0:T(4,128)S(1)}, u32[]{:S(2)}, u32[]{:S(2)}) collective-permute-start(f32[2,3,4,152]{3,2,1,0:T(4,128)S(1)} %collective-permute-done.from_near), channel_id=1, source_target_pairs={{0,2},{1,3},{2,0},{3,1},{4,6},{5,7},{6,4},{7,5},{8,10},{9,11},{10,... | collective-permute-start | bytes 43784 | tf_op jit(solution)/shard_map/ppermute | solution.py:274
  7.1 0.0 copy-done.8
  7.1 0.2 collective-permute-start.2
  7.4 0.0 copy-done.7
  7.4 1.5 %collective-permute-start.3 = (f32[3,4,152]{2,1,0:T(4,128)S(1)}, f32[3,4,152]{2,1,0:T(4,128)S(1)}, u32[]{:S(2)}, u32[]{:S(2)}) collective-permute-start(f32[3,4,152]{2,1,0:T(4,128)S(1)} %copy-done.7), channel_id=1, source_target_pairs={{0,4},{8,12},{16,20},{24,28},{4,0},{12,8},{20,16},{28,24},{1,5},{9... | collective-permute-start | bytes 21896 | tf_op jit(solution)/shard_map/ppermute | solution.py:278
  8.9 0.0 copy-done.6
  8.9 0.0 copy-start
  8.9 3.7 %collective-permute-start.4 = (f32[3,4,152]{2,1,0:T(4,128)S(1)}, f32[3,4,152]{2,1,0:T(4,128)S(1)}, u32[]{:S(2)}, u32[]{:S(2)}) collective-permute-start(f32[3,4,152]{2,1,0:T(4,128)S(1)} %copy-done.6), channel_id=1, source_target_pairs={{4,8},{12,16},{20,24},{8,4},{16,12},{24,20},{5,9},{13,17},{21,25},... | collective-permute-start | bytes 21896 | tf_op jit(solution)/shard_map/ppermute | solution.py:278
  12.7 0.5 %prepare.1.hat = f32[11700,128]{1,0:T(8,128)S(1)} custom-call(bf16[2,316,2304]{2,1,0:T(8,128)(2,1)S(1)} %bitcast.7), custom_call_target="tpu_custom_call" | custom-call | flops 1456128 | bytes 8736768 | tf_op jit(solution)/shard_map/prepare/pallas_call | solution.py:288
  13.1 0.0 copy-start.4
  13.1 0.0 copy-start.5
  13.2 0.0 collective-permute-done.2.refs_0_
  13.2 0.0 collective-permute-done.3.refs_1_
  13.2 1.0 %collective-permute-done.4.refs_2_ = f32[3,4,152]{2,1,0:T(4,128)S(1)} collective-permute-done((f32[3,4,152]{2,1,0:T(4,128)S(1)}, f32[3,4,152]{2,1,0:T(4,128)S(1)}, u32[]{:S(2)}, u32[]{:S(2)}) %collective-permute-start.4) | collective-permute-done | bytes 7328 | tf_op jit(solution)/shard_map/ppermute | solution.py:278
  14.2 0.0 collective-permute-done.1.relayed
  14.2 0.0 copy-done
  14.2 0.0 copy-done.1
  14.2 0.0 copy-done.3
  14.2 1.8 %forward.1.main = f32[4528,128]{1,0:T(8,128)S(1)} custom-call(s32[4,4]{1,0:T(4,128)S(1)} %bitcast.11, f32[3,16,152]{2,1,0:T(8,128)S(1)} %bitcast.9, f32[2,3,4,152]{3,2,1,0:T(4,128)S(1)} %collective-permute-done.from_near, f32[2,3,4,152]{3,2,1,0:T(4,128)S(1)} %collective-permute-done.1.relayed, f32[3,4,152]{2,1,0:T(4,128)S(1)} %collective-permute-done.2.refs_0_, ...), custom_call_target="tpu_custom_call" | custom-call | tf_op jit(solution)/shard_map/forward/pallas_call | solution.py:303
  16.0 0.0 copy-done.4
  16.0 0.0 copy-done.5
  16.0 0.0 copy-start.2
  16.0 5.8 %interact.1 = (f32[1632,128]{1,0:T(8,128)S(1)}, f32[2,126,128]{2,1,0:T(8,128)S(1)}) custom-call(s32[16,32]{1,0:T(8,128)S(1)} %copy-done.4, s32[16,32]{1,0:T(8,128)S(1)} %copy-done.5, f32[11700,128]{1,0:T(8,128)S(1)} %prepare.1.hat, f32[4528,128]{1,0:T(8,128)S(1)} %forward.1.main), custom_call_target="tpu_custom_call" | custom-call | tf_op jit(solution)/shard_map/interact/pallas_call | solution.py:312
  21.8 0.0 copy-done.2
  21.8 1.7 %inverse.1 = f32[3,16,152]{2,1,0:T(8,128)} custom-call(f32[1632,128]{1,0:T(8,128)S(1)} %get-tuple-element.19.total, f32[2,126,128]{2,1,0:T(8,128)S(1)} %get-tuple-element.20.total_tail, bf16[320,4608]{1,0:T(8,128)(2,1)S(1)} %copy-done, f32[1,4608]{1,0:T(1,128)S(1)} %copy-done.2), custom_call_target="tpu_custom_call" | custom-call | tf_op jit(solution)/shard_map/inverse/pallas_call | solution.py:323
  (2 shorter events, 0.0 us)
Async XLA Ops:
  1.6 5.5 %copy-start.8 = (f32[3,4,152]{2,1,0:T(4,128)S(1)}, f32[3,4,152]{2,1,0:T(4,128)}, u32[]{:S(2)}) copy-start(f32[3,4,152]{2,1,0:T(4,128)} %get-tuple-element.16) | copy-start | bytes 21892
  1.6 5.8 %copy-start.7 = (f32[3,4,152]{2,1,0:T(4,128)S(1)}, f32[3,4,152]{2,1,0:T(4,128)}, u32[]{:S(2)}) copy-start(f32[3,4,152]{2,1,0:T(4,128)} %get-tuple-element.17) | copy-start | bytes 21892
  1.6 7.3 %copy-start.6 = (f32[3,4,152]{2,1,0:T(4,128)S(1)}, f32[3,4,152]{2,1,0:T(4,128)}, u32[]{:S(2)}) copy-start(f32[3,4,152]{2,1,0:T(4,128)} %get-tuple-element.18) | copy-start | bytes 21892
  1.6 4.2 %collective-permute-start = (f32[2,3,4,152]{3,2,1,0:T(4,128)}, f32[2,3,4,152]{3,2,1,0:T(4,128)S(1)}, u32[]{:S(2)}, u32[]{:S(2)}) collective-permute-start(f32[2,3,4,152]{3,2,1,0:T(4,128)} %get-tuple-element.13), channel_id=1, source_target_pairs={{0,1},{1,0},{2,3},{3,2},{4,5},{5,4},{6,7},{7,6},{8,9},{9,8},{10,11... | collective-permute-start | bytes 43784 | tf_op jit(solution)/shard_map/ppermute | solution.py:274
  5.8 8.3 %collective-permute-start.1 = (f32[2,3,4,152]{3,2,1,0:T(4,128)S(1)}, f32[2,3,4,152]{3,2,1,0:T(4,128)S(1)}, u32[]{:S(2)}, u32[]{:S(2)}) collective-permute-start(f32[2,3,4,152]{3,2,1,0:T(4,128)S(1)} %collective-permute-done.from_near), channel_id=1, source_target_pairs={{0,2},{1,3},{2,0},{3,1},{4,6},{5,7},{6,4},{7,5},{8,10},{9,11},{10,... | collective-permute-start | bytes 43784 | tf_op jit(solution)/shard_map/ppermute | solution.py:274
  7.1 6.0 %collective-permute-start.2 = (f32[3,4,152]{2,1,0:T(4,128)S(1)}, f32[3,4,152]{2,1,0:T(4,128)S(1)}, u32[]{:S(2)}, u32[]{:S(2)}) collective-permute-start(f32[3,4,152]{2,1,0:T(4,128)S(1)} %copy-done.8), channel_id=1, source_target_pairs={{0,2},{1,3},{2,0},{3,1},{4,6},{5,7},{6,4},{7,5},{8,10},{9,11},{10,... | collective-permute-start | bytes 21896 | tf_op jit(solution)/shard_map/ppermute | solution.py:274
  7.4 5.8 %collective-permute-start.3 = (f32[3,4,152]{2,1,0:T(4,128)S(1)}, f32[3,4,152]{2,1,0:T(4,128)S(1)}, u32[]{:S(2)}, u32[]{:S(2)}) collective-permute-start(f32[3,4,152]{2,1,0:T(4,128)S(1)} %copy-done.7), channel_id=1, source_target_pairs={{0,4},{8,12},{16,20},{24,28},{4,0},{12,8},{20,16},{28,24},{1,5},{9... | collective-permute-start | bytes 21896 | tf_op jit(solution)/shard_map/ppermute | solution.py:278
  8.9 5.3 %copy-start = (bf16[320,4608]{1,0:T(8,128)(2,1)S(1)}, bf16[320,4608]{1,0:T(8,128)(2,1)}, u32[]{:S(2)}) copy-start(bf16[320,4608]{1,0:T(8,128)(2,1)} %constant.4.clone.refs_3_.table) | copy-start | bytes 8847364
  8.9 5.3 %copy-start.1 = (f32[16,3,152]{2,0,1:T(8,128)S(1)}, f32[16,3,152]{2,0,1:T(8,128)}, u32[]{:S(2)}) copy-start(f32[16,3,152]{2,0,1:T(8,128)} %param.8) | copy-start | bytes 87556
  8.9 5.3 %copy-start.3 = (s32[1,4,4]{2,1,0:T(4,128)S(1)}, s32[1,4,4]{2,1,0:T(4,128)}, u32[]{:S(2)}) copy-start(s32[1,4,4]{2,1,0:T(4,128)} %param.10) | copy-start | bytes 196
  8.9 5.3 %collective-permute-start.4 = (f32[3,4,152]{2,1,0:T(4,128)S(1)}, f32[3,4,152]{2,1,0:T(4,128)S(1)}, u32[]{:S(2)}, u32[]{:S(2)}) collective-permute-start(f32[3,4,152]{2,1,0:T(4,128)S(1)} %copy-done.6), channel_id=1, source_target_pairs={{4,8},{12,16},{20,24},{8,4},{16,12},{24,20},{5,9},{13,17},{21,25},... | collective-permute-start | bytes 21896 | tf_op jit(solution)/shard_map/ppermute | solution.py:278
  13.1 2.8 %copy-start.4 = (s32[16,32]{1,0:T(8,128)S(1)}, s32[16,32]{1,0:T(8,128)}, u32[]{:S(2)}) copy-start(s32[16,32]{1,0:T(8,128)} %source.1) | copy-start | bytes 6148
  13.1 2.8 %copy-start.5 = (s32[16,32]{1,0:T(8,128)S(1)}, s32[16,32]{1,0:T(8,128)}, u32[]{:S(2)}) copy-start(s32[16,32]{1,0:T(8,128)} %offset.1) | copy-start | bytes 6148
  16.0 5.8 %copy-start.2 = (f32[1,4608]{1,0:T(1,128)S(1)}, f32[1,4608]{1,0:T(1,128)}, u32[]{:S(2)}) copy-start(f32[1,4608]{1,0:T(1,128)} %constant.5.clone.factor) | copy-start | bytes 55300

commit v13 on v12

--- a/solution.py
+++ b/solution.py
@@ -20,7 +20,7 @@
 TAIL = TILES - MAIN
 PITCH = MAIN + 1
 TAIL_PITCH = 7
-HAT_ROWS = 2 * TILES + 1
+HAT_ROWS = 3 * MAIN + 2 * TAIL + 1
 POINTS_PAD = 160
 CHUNK = 256
 PIECE = 512
@@ -57,17 +57,17 @@
 
 
 def source_rows(comp_count):
-    return (2 * comp_count * MAIN + TAIL * 8) | 1
+    return (3 * comp_count * MAIN + TAIL * 8) | 1
 
 
 def source_row(comp_count, which, tile):
     if tile < MAIN:
         return which * MAIN + tile
-    return 2 * comp_count * MAIN + (tile - MAIN) * 8 + which
-
-
-def kernel_row(part, tile):
-    return part * MAIN + tile if tile < MAIN else 2 * MAIN + (tile - MAIN) * 2 + part
+    return 3 * comp_count * MAIN + (tile - MAIN) * 8 + which
+
+
+def kernel_row(which, tile):
+    return which * MAIN + tile if tile < MAIN else 3 * MAIN + (tile - MAIN) * 2 + which
 
 
 def pack_kernel(density, send_list, halo_list, *outs):
@@ -91,14 +91,16 @@
     parts, count, _ = kernel_hat.shape
 
     def move(first, height):
-        for part in range(parts):
-            for j in range(TILES):
-                x = kernel_hat[part, pl.ds(first, height), j * LANES : (j + 1) * LANES].astype(jnp.float32)
+        for j in range(TILES):
+            re, im = (
+                kernel_hat[part, pl.ds(first, height), j * LANES : (j + 1) * LANES].astype(jnp.float32)
+                for part in range(parts)
+            )
+            for which, x in enumerate((re, re + im, im - re) if j < MAIN else (re, im)):
                 for g in range(0, height, 8):
                     size = min(8, height - g)
-                    piece = x[g : g + size]
-                    row = (first + g) * HAT_ROWS + kernel_row(part, j)
-                    hat[pl.ds(row, size, stride=HAT_ROWS), :] = piece
+                    row = (first + g) * HAT_ROWS + kernel_row(which, j)
+                    hat[pl.ds(row, size, stride=HAT_ROWS), :] = x[g : g + size]
 
     whole = count // 16
 
@@ -142,19 +144,27 @@
     high = value.astype(bf16)
     low = (value - high.astype(f32)).astype(bf16)
     both = jnp.concatenate([high, low], axis=0)
-    for n in range(2 * FREQ // CHUNK):
-        columns = slice(n * CHUNK, (n + 1) * CHUNK)
+
+    def spectrum(first):
+        columns = slice(first, first + CHUNK)
         x = jnp.dot(both, table[:POINTS_PAD, columns], preferred_element_type=f32)
         x = x[:row_count] + x[row_count:]
         x = x + jnp.dot(high, table[POINTS_PAD:, columns], preferred_element_type=f32)
-        x = x.astype(bf16).astype(f32)
+        return x.astype(bf16).astype(f32)
+
+    for n in range(FREQ // CHUNK):
+        re, im = spectrum(n * CHUNK), spectrum(FREQ + n * CHUNK)
         for m in range(CHUNK // LANES):
-            part, j = divmod(n * (CHUNK // LANES) + m, TILES)
+            j = n * (CHUNK // LANES) + m
             for g in range(row_count // 8):
-                piece = x[g * 8 : (g + 1) * 8, m * LANES : (m + 1) * LANES]
+                at = (slice(g * 8, (g + 1) * 8), slice(m * LANES, (m + 1) * LANES))
                 c, s = divmod(g * 8, slots)
-                row = source_row(comp_count, part * comp_count + c, j)
-                main[pl.ds(s * pitch + row, 8, stride=pitch), :] = piece
+                pieces = [re[at], im[at]]
+                if j < MAIN:
+                    pieces.append(pieces[0] + pieces[1])
+                for part, piece in enumerate(pieces):
+                    row = source_row(comp_count, part * comp_count + c, j)
+                    main[pl.ds(s * pitch + row, 8, stride=pitch), :] = piece
 
 
 def interact_kernel(comp_count, source, offset, hat, main, total, total_tail):
@@ -172,16 +182,18 @@
             )
 
         def pair(s, o, accs):
-            k = [[hat[pl.ds(o + kernel_row(r, 8 * h), 8), :] for h in range(halves)] for r in range(2)]
+            k = [[hat[pl.ds(o + kernel_row(r, 8 * h), 8), :] for h in range(halves)] for r in range(3)]
             accs = list(accs)
             at = 0
             for c in range(comp_count):
                 for h in range(halves):
-                    s_re = main[pl.ds(s + (source_row(comp_count, c, 8 * h)), 8), :]
-                    s_im = main[pl.ds(s + (source_row(comp_count, comp_count + c, 8 * h)), 8), :]
-                    accs[at] = accs[at] + (k[0][h] * s_re - k[1][h] * s_im)
-                    accs[at + 1] = accs[at + 1] + (k[0][h] * s_im + k[1][h] * s_re)
-                    at += 2
+                    s_re, s_im, s_sum = (
+                        main[pl.ds(s + source_row(comp_count, r * comp_count + c, 8 * h), 8), :] for r in range(3)
+                    )
+                    accs[at] = accs[at] + k[0][h] * s_sum
+                    accs[at + 1] = accs[at + 1] + k[1][h] * s_im
+                    accs[at + 2] = accs[at + 2] + k[2][h] * s_re
+                    at += 3
             k_tail = hat[pl.ds(o + kernel_row(0, MAIN), 8), :]
             for j in range(TAIL):
                 x = main[pl.ds(s + source_row(comp_count, 0, MAIN + j), 8), :]
@@ -191,7 +203,7 @@
                 at += 2
             return tuple(accs)
 
-        count = 2 * (comp_count * halves + TAIL)
+        count = 3 * comp_count * halves + 2 * TAIL
         zero = jnp.zeros((8, LANES), f32)
 
         def block(i, carry):
@@ -205,10 +217,10 @@
         at = 0
         for c in range(comp_count):
             for h in range(halves):
-                for part in range(2):
+                for part, value in enumerate((accs[at] - accs[at + 1], accs[at] + accs[at + 2])):
                     row = (part * comp_count + c) * box_count + t
-                    total[pl.ds(row * PITCH + 8 * h, 8), :] = accs[at + part]
-                at += 2
+                    total[pl.ds(row * PITCH + 8 * h, 8), :] = value
+                at += 3
         for j in range(TAIL):
             own, cross = accs[at], accs[at + 1]
             up = jnp.concatenate([cross[comp_count:], cross[:comp_count]], axis=0)

time: 23.7 us -> 23.1 us (0.975)
  Pallas kernels: 11.3 us -> 10.9 us
    pallas_call x1, Pallas kernels: 5.77 us -> 5.19 us  [on_device(): pl.pallas_call(functools.partial(interact_kernel, comp_count), out_shape=...]
  transfers between devices with their start and end apart: 5 -> 5, of which waited for: 1 -> 1; matrix products, arithmetic and copies ran while one was open for 9% -> 9% of each run, Pallas kernels for 2% -> 3%
where the time goes in v13:
time: 23.1 us; the launch traced here: 22.9 us
  Pallas kernels  10.9 us (47%)
  starting transfers between devices  8.9 us (39%)
  local copies, waits for them, and re-layouts  2.15 us (9%)
  waiting for transfers between devices  0.84 us (4%)
    ppermute x2, starting transfers between devices, swap_groups(): return lax.ppermute(x, 'group', pairs + [(j, i) for i, j in pairs])  5.26 us
    pallas_call x1, Pallas kernels, on_device(): pl.pallas_call(functools.partial(interact_kernel, comp_count), out_shape=...  5.19 us
    ppermute x3, starting transfers between devices, swap(): return lax.ppermute(x, 'dev', [(i, i ^ k) for i in range(peers)])  3.64 us
    unnamed x19, local copies, waits for them, and re-layouts  2.15 us
    pallas_call x1, Pallas kernels, on_device(): pl.pallas_call(forward_kernel, out_shape=jax.ShapeDtypeStruct((slots * so...  1.76 us
    pallas_call x1, Pallas kernels, on_device(): pl.pallas_call(inverse_kernel, out_shape=jax.ShapeDtypeStruct((comp_count...  1.66 us
    pallas_call x1, Pallas kernels, on_device(): pl.pallas_call(pack_kernel, out_shape=(jax.ShapeDtypeStruct((2, *boxes.sh...  1.6 us
    ppermute x2, waiting for transfers between devices, swap_groups(): return lax.ppermute(x, 'group', pairs + [(j, i) for i, j in pairs])  0.83 us
  transfers between devices with their start and end apart: 5, of which 1 were waited for; matrix products, arithmetic and copies ran while one was open for 9% of the time, Pallas kernels for 3%

profile of v13, /device:TPU:1, one launch (start us, length us, event | category | flops | bytes accessed | tf_op | source)
XLA Modules:
  0.0 22.9 jit_solution(16030800464706642386)
XLA Ops:
  0.0 1.6 %pack.1 = (f32[2,3,4,152]{3,2,1,0:T(4,128)}, f32[3,4,152]{2,1,0:T(4,128)}, f32[3,4,152]{2,1,0:T(4,128)}, f32[3,4,152]{2,1,0:T(4,128)}) custom-call(f32[3,16,152]{2,1,0:T(8,128)} %bitcast.8, s32[4,4]{1,0:T(4,128)} %bitcast.10, s32[2,4]{1,0:T(2,128)} %bitcast.12), custom_call_target="tpu_custom_call" | custom-call | tf_op jit(solution)/shard_map/pack/pallas_call | solution.py:277
  1.6 0.0 copy-start.8
  1.6 0.0 copy-start.7
  1.6 0.0 copy-start.6
  1.6 2.1 %collective-permute-start = (f32[2,3,4,152]{3,2,1,0:T(4,128)}, f32[2,3,4,152]{3,2,1,0:T(4,128)S(1)}, u32[]{:S(2)}, u32[]{:S(2)}) collective-permute-start(f32[2,3,4,152]{3,2,1,0:T(4,128)} %get-tuple-element.13), channel_id=1, source_target_pairs={{0,1},{1,0},{2,3},{3,2},{4,5},{5,4},{6,7},{7,6},{8,9},{9,8},{10,11... | collective-permute-start | bytes 43784 | tf_op jit(solution)/shard_map/ppermute | solution.py:286
  3.7 2.1 %copy.11 = bf16[316,2,2304]{2,0,1:T(8,128)(2,1)S(1)} copy(bf16[316,2,2304]{2,1,0:T(2,128)(2,1)} %param.9) | data formatting | bytes 5824512 | tf_op args[1]
  5.8 0.0 collective-permute-done.from_near
  5.8 1.3 %collective-permute-start.1 = (f32[2,3,4,152]{3,2,1,0:T(4,128)S(1)}, f32[2,3,4,152]{3,2,1,0:T(4,128)S(1)}, u32[]{:S(2)}, u32[]{:S(2)}) collective-permute-start(f32[2,3,4,152]{3,2,1,0:T(4,128)S(1)} %collective-permute-done.from_near), channel_id=1, source_target_pairs={{0,2},{1,3},{2,0},{3,1},{4,6},{5,7},{6,4},{7,5},{8,10},{9,11},{10,... | collective-permute-start | bytes 43784 | tf_op jit(solution)/shard_map/ppermute | solution.py:286
  7.1 0.0 copy-done.8
  7.1 0.2 collective-permute-start.2
  7.4 0.0 copy-done.7
  7.4 1.5 %collective-permute-start.3 = (f32[3,4,152]{2,1,0:T(4,128)S(1)}, f32[3,4,152]{2,1,0:T(4,128)S(1)}, u32[]{:S(2)}, u32[]{:S(2)}) collective-permute-start(f32[3,4,152]{2,1,0:T(4,128)S(1)} %copy-done.7), channel_id=1, source_target_pairs={{0,4},{8,12},{16,20},{24,28},{4,0},{12,8},{20,16},{28,24},{1,5},{9... | collective-permute-start | bytes 21896 | tf_op jit(solution)/shard_map/ppermute | solution.py:290
  8.9 0.0 copy-done.6
  8.9 0.0 copy-start
  8.9 3.7 %collective-permute-start.4 = (f32[3,4,152]{2,1,0:T(4,128)S(1)}, f32[3,4,152]{2,1,0:T(4,128)S(1)}, u32[]{:S(2)}, u32[]{:S(2)}) collective-permute-start(f32[3,4,152]{2,1,0:T(4,128)S(1)} %copy-done.6), channel_id=1, source_target_pairs={{4,8},{12,16},{20,24},{8,4},{16,12},{24,20},{5,9},{13,17},{21,25},... | collective-permute-start | bytes 21896 | tf_op jit(solution)/shard_map/ppermute | solution.py:290
  12.7 0.6 %prepare.1.hat = f32[16756,128]{1,0:T(8,128)S(1)} custom-call(bf16[2,316,2304]{2,1,0:T(8,128)(2,1)S(1)} %bitcast.7), custom_call_target="tpu_custom_call" | custom-call | flops 1456128 | bytes 8736768 | tf_op jit(solution)/shard_map/prepare/pallas_call | solution.py:300
  13.3 0.0 copy-start.4
  13.3 0.0 copy-start.5
  13.3 0.0 collective-permute-done.2.refs_0_
  13.3 0.0 collective-permute-done.3.refs_1_
  13.4 0.8 %collective-permute-done.4.refs_2_ = f32[3,4,152]{2,1,0:T(4,128)S(1)} collective-permute-done((f32[3,4,152]{2,1,0:T(4,128)S(1)}, f32[3,4,152]{2,1,0:T(4,128)S(1)}, u32[]{:S(2)}, u32[]{:S(2)}) %collective-permute-start.4) | collective-permute-done | bytes 7328 | tf_op jit(solution)/shard_map/ppermute | solution.py:290
  14.2 0.0 collective-permute-done.1.relayed
  14.2 0.0 copy-done
  14.2 0.0 copy-done.1
  14.2 0.0 copy-done.3
  14.2 1.8 %forward.1.main = f32[6448,128]{1,0:T(8,128)S(1)} custom-call(s32[4,4]{1,0:T(4,128)S(1)} %bitcast.11, f32[3,16,152]{2,1,0:T(8,128)S(1)} %bitcast.9, f32[2,3,4,152]{3,2,1,0:T(4,128)S(1)} %collective-permute-done.from_near, f32[2,3,4,152]{3,2,1,0:T(4,128)S(1)} %collective-permute-done.1.relayed, f32[3,4,152]{2,1,0:T(4,128)S(1)} %collective-permute-done.2.refs_0_, ...), custom_call_target="tpu_custom_call" | custom-call | tf_op jit(solution)/shard_map/forward/pallas_call | solution.py:315
  16.0 0.0 copy-done.4
  16.0 0.0 copy-done.5
  16.0 0.0 copy-start.2
  16.0 5.2 %interact.1 = (f32[1632,128]{1,0:T(8,128)S(1)}, f32[2,126,128]{2,1,0:T(8,128)S(1)}) custom-call(s32[16,32]{1,0:T(8,128)S(1)} %copy-done.4, s32[16,32]{1,0:T(8,128)S(1)} %copy-done.5, f32[16756,128]{1,0:T(8,128)S(1)} %prepare.1.hat, f32[6448,128]{1,0:T(8,128)S(1)} %forward.1.main), custom_call_target="tpu_custom_call" | custom-call | tf_op jit(solution)/shard_map/interact/pallas_call | solution.py:324
  21.2 0.0 copy-done.2
  21.2 1.7 %inverse.1 = f32[3,16,152]{2,1,0:T(8,128)} custom-call(f32[1632,128]{1,0:T(8,128)S(1)} %get-tuple-element.19.total, f32[2,126,128]{2,1,0:T(8,128)S(1)} %get-tuple-element.20.total_tail, bf16[320,4608]{1,0:T(8,128)(2,1)S(1)} %copy-done, f32[1,4608]{1,0:T(1,128)S(1)} %copy-done.2), custom_call_target="tpu_custom_call" | custom-call | tf_op jit(solution)/shard_map/inverse/pallas_call | solution.py:335
  (2 shorter events, 0.0 us)
Async XLA Ops:
  1.6 5.5 %copy-start.8 = (f32[3,4,152]{2,1,0:T(4,128)S(1)}, f32[3,4,152]{2,1,0:T(4,128)}, u32[]{:S(2)}) copy-start(f32[3,4,152]{2,1,0:T(4,128)} %get-tuple-element.16) | copy-start | bytes 21892
  1.6 5.8 %copy-start.7 = (f32[3,4,152]{2,1,0:T(4,128)S(1)}, f32[3,4,152]{2,1,0:T(4,128)}, u32[]{:S(2)}) copy-start(f32[3,4,152]{2,1,0:T(4,128)} %get-tuple-element.17) | copy-start | bytes 21892
  1.6 7.3 %copy-start.6 = (f32[3,4,152]{2,1,0:T(4,128)S(1)}, f32[3,4,152]{2,1,0:T(4,128)}, u32[]{:S(2)}) copy-start(f32[3,4,152]{2,1,0:T(4,128)} %get-tuple-element.18) | copy-start | bytes 21892
  1.6 4.2 %collective-permute-start = (f32[2,3,4,152]{3,2,1,0:T(4,128)}, f32[2,3,4,152]{3,2,1,0:T(4,128)S(1)}, u32[]{:S(2)}, u32[]{:S(2)}) collective-permute-start(f32[2,3,4,152]{3,2,1,0:T(4,128)} %get-tuple-element.13), channel_id=1, source_target_pairs={{0,1},{1,0},{2,3},{3,2},{4,5},{5,4},{6,7},{7,6},{8,9},{9,8},{10,11... | collective-permute-start | bytes 43784 | tf_op jit(solution)/shard_map/ppermute | solution.py:286
  5.8 8.3 %collective-permute-start.1 = (f32[2,3,4,152]{3,2,1,0:T(4,128)S(1)}, f32[2,3,4,152]{3,2,1,0:T(4,128)S(1)}, u32[]{:S(2)}, u32[]{:S(2)}) collective-permute-start(f32[2,3,4,152]{3,2,1,0:T(4,128)S(1)} %collective-permute-done.from_near), channel_id=1, source_target_pairs={{0,2},{1,3},{2,0},{3,1},{4,6},{5,7},{6,4},{7,5},{8,10},{9,11},{10,... | collective-permute-start | bytes 43784 | tf_op jit(solution)/shard_map/ppermute | solution.py:286
  7.1 6.2 %collective-permute-start.2 = (f32[3,4,152]{2,1,0:T(4,128)S(1)}, f32[3,4,152]{2,1,0:T(4,128)S(1)}, u32[]{:S(2)}, u32[]{:S(2)}) collective-permute-start(f32[3,4,152]{2,1,0:T(4,128)S(1)} %copy-done.8), channel_id=1, source_target_pairs={{0,2},{1,3},{2,0},{3,1},{4,6},{5,7},{6,4},{7,5},{8,10},{9,11},{10,... | collective-permute-start | bytes 21896 | tf_op jit(solution)/shard_map/ppermute | solution.py:286
  7.4 6.0 %collective-permute-start.3 = (f32[3,4,152]{2,1,0:T(4,128)S(1)}, f32[3,4,152]{2,1,0:T(4,128)S(1)}, u32[]{:S(2)}, u32[]{:S(2)}) collective-permute-start(f32[3,4,152]{2,1,0:T(4,128)S(1)} %copy-done.7), channel_id=1, source_target_pairs={{0,4},{8,12},{16,20},{24,28},{4,0},{12,8},{20,16},{28,24},{1,5},{9... | collective-permute-start | bytes 21896 | tf_op jit(solution)/shard_map/ppermute | solution.py:290
  8.9 5.3 %copy-start = (bf16[320,4608]{1,0:T(8,128)(2,1)S(1)}, bf16[320,4608]{1,0:T(8,128)(2,1)}, u32[]{:S(2)}) copy-start(bf16[320,4608]{1,0:T(8,128)(2,1)} %constant.4.clone.refs_3_.table) | copy-start | bytes 8847364
  8.9 5.3 %copy-start.1 = (f32[16,3,152]{2,0,1:T(8,128)S(1)}, f32[16,3,152]{2,0,1:T(8,128)}, u32[]{:S(2)}) copy-start(f32[16,3,152]{2,0,1:T(8,128)} %param.8) | copy-start | bytes 87556
  8.9 5.3 %copy-start.3 = (s32[1,4,4]{2,1,0:T(4,128)S(1)}, s32[1,4,4]{2,1,0:T(4,128)}, u32[]{:S(2)}) copy-start(s32[1,4,4]{2,1,0:T(4,128)} %param.10) | copy-start | bytes 196
  8.9 5.3 %collective-permute-start.4 = (f32[3,4,152]{2,1,0:T(4,128)S(1)}, f32[3,4,152]{2,1,0:T(4,128)S(1)}, u32[]{:S(2)}, u32[]{:S(2)}) collective-permute-start(f32[3,4,152]{2,1,0:T(4,128)S(1)} %copy-done.6), channel_id=1, source_target_pairs={{4,8},{12,16},{20,24},{8,4},{16,12},{24,20},{5,9},{13,17},{21,25},... | collective-permute-start | bytes 21896 | tf_op jit(solution)/shard_map/ppermute | solution.py:290
  13.3 2.7 %copy-start.4 = (s32[16,32]{1,0:T(8,128)S(1)}, s32[16,32]{1,0:T(8,128)}, u32[]{:S(2)}) copy-start(s32[16,32]{1,0:T(8,128)} %source.1) | copy-start | bytes 6148
  13.3 2.7 %copy-start.5 = (s32[16,32]{1,0:T(8,128)S(1)}, s32[16,32]{1,0:T(8,128)}, u32[]{:S(2)}) copy-start(s32[16,32]{1,0:T(8,128)} %offset.1) | copy-start | bytes 6148
  16.0 5.2 %copy-start.2 = (f32[1,4608]{1,0:T(1,128)S(1)}, f32[1,4608]{1,0:T(1,128)}, u32[]{:S(2)}) copy-start(f32[1,4608]{1,0:T(1,128)} %constant.5.clone.factor) | copy-start | bytes 55300

commit v14 on v13

--- a/solution.py
+++ b/solution.py
@@ -262,6 +262,13 @@
         out[c] = result[c * box_count : (c + 1) * box_count, :surf]
 
 
+def translate_kernel(send_list, source, offset, density, from_near, relayed, *refs):
+    *pieces, table, factor, hat, out, main, rows, total, total_tail = refs
+    forward_kernel(send_list, density, from_near, relayed, *pieces, table, main, rows)
+    interact_kernel(density.shape[0], source, offset, hat, main, total, total_tail)
+    inverse_kernel(total, total_tail, table, factor, out)
+
+
 def on_device(density, kernel_hat, send_list, halo_list, inter_src, inter_off):
     table, factor = transform_tables()
     box_count, comp_count, surf = density.shape
@@ -309,37 +316,24 @@
 
     slots = box_count + peers * cap + 2 * rim
     row_count = comp_count * slots
-    params = pltpu.CompilerParams(vmem_limit_bytes=24 * 1024 * 1024)
-    table = jnp.asarray(table)
-    arrays = (send_list[0], density, from_near, relayed, *from_far, from_first, from_second, table)
-    main = pl.pallas_call(
-        forward_kernel,
-        out_shape=jax.ShapeDtypeStruct((slots * source_rows(comp_count) + 8, LANES), f32),
-        in_specs=[smem] + [vmem] * (len(arrays) - 1),
+    arrays = (
+        send_list[0], inter_src, inter_off, density, from_near, relayed, *from_far, from_first, from_second,
+        jnp.asarray(table), jnp.asarray(factor), hat,
+    )
+    potential = pl.pallas_call(
+        translate_kernel,
+        out_shape=jax.ShapeDtypeStruct((comp_count, box_count, surf), f32),
+        in_specs=[smem] * 3 + [vmem] * (len(arrays) - 3),
         out_specs=vmem,
-        scratch_shapes=[pltpu.VMEM((row_count, POINTS_PAD), f32)],
-        compiler_params=params,
-        name="forward",
+        scratch_shapes=[
+            pltpu.VMEM((slots * source_rows(comp_count) + 8, LANES), f32),
+            pltpu.VMEM((row_count, POINTS_PAD), f32),
+            pltpu.VMEM((2 * comp_count * box_count * PITCH, LANES), f32),
+            pltpu.VMEM((TAIL, (box_count + 2) * TAIL_PITCH, LANES), f32),
+        ],
+        compiler_params=pltpu.CompilerParams(vmem_limit_bytes=24 * 1024 * 1024),
+        name="translate",
     )(*arrays)
-    total, total_tail = pl.pallas_call(
-        functools.partial(interact_kernel, comp_count),
-        out_shape=(
-            jax.ShapeDtypeStruct((2 * comp_count * box_count * PITCH, LANES), f32),
-            jax.ShapeDtypeStruct((TAIL, (box_count + 2) * TAIL_PITCH, LANES), f32),
-        ),
-        in_specs=[smem, smem] + [vmem] * 2,
-        out_specs=(vmem, vmem),
-        compiler_params=params,
-        name="interact",
-    )(inter_src, inter_off, hat, main)
-    potential = pl.pallas_call(
-        inverse_kernel,
-        out_shape=jax.ShapeDtypeStruct((comp_count, box_count, surf), f32),
-        in_specs=[vmem] * 4,
-        out_specs=vmem,
-        compiler_params=params,
-        name="inverse",
-    )(total, total_tail, table, jnp.asarray(factor))
     return potential.transpose(1, 0, 2)
 
 

time: 23.1 us -> 22.7 us (0.983)
  Pallas kernels: 10.9 us -> 10.5 us
    pallas_call x3 -> x1, Pallas kernels: 8.61 us -> 8.24 us  [on_device(): pl.pallas_call(translate_kernel, out_shape=jax.ShapeDtypeStruct((comp_cou...]
where the time goes in v14:
time: 22.7 us; the launch traced here: 22.5 us
  Pallas kernels  10.5 us (46%)
  starting transfers between devices  8.9 us (39%)
  local copies, waits for them, and re-layouts  2.15 us (9%)
  waiting for transfers between devices  0.86 us (4%)
    pallas_call x1, Pallas kernels, on_device(): pl.pallas_call(translate_kernel, out_shape=jax.ShapeDtypeStruct((comp_cou...  8.24 us
    ppermute x2, starting transfers between devices, swap_groups(): return lax.ppermute(x, 'group', pairs + [(j, i) for i, j in pairs])  5.26 us
    ppermute x3, starting transfers between devices, swap(): return lax.ppermute(x, 'dev', [(i, i ^ k) for i in range(peers)])  3.64 us
    unnamed x19, local copies, waits for them, and re-layouts  2.15 us
    pallas_call x1, Pallas kernels, on_device(): pl.pallas_call(pack_kernel, out_shape=(jax.ShapeDtypeStruct((2, *boxes.sh...  1.59 us
    ppermute x2, waiting for transfers between devices, swap_groups(): return lax.ppermute(x, 'group', pairs + [(j, i) for i, j in pairs])  0.86 us
    pallas_call x1, Pallas kernels, on_device(): pl.pallas_call(prepare_kernel, out_shape=jax.ShapeDtypeStruct((offsets *...  0.64 us
  transfers between devices with their start and end apart: 5, of which 1 were waited for; matrix products, arithmetic and copies ran while one was open for 9% of the time, Pallas kernels for 3%

profile of v14, /device:TPU:1, one launch (start us, length us, event | category | flops | bytes accessed | tf_op | source)
XLA Modules:
  0.0 22.5 jit_solution(675451240961856130)
XLA Ops:
  0.0 1.6 %pack.1 = (f32[2,3,4,152]{3,2,1,0:T(4,128)}, f32[3,4,152]{2,1,0:T(4,128)}, f32[3,4,152]{2,1,0:T(4,128)}, f32[3,4,152]{2,1,0:T(4,128)}) custom-call(f32[3,16,152]{2,1,0:T(8,128)} %bitcast.8, s32[4,4]{1,0:T(4,128)} %bitcast.10, s32[2,4]{1,0:T(2,128)} %bitcast.12), custom_call_target="tpu_custom_call" | custom-call | tf_op jit(solution)/shard_map/pack/pallas_call | solution.py:284
  1.6 0.0 copy-start.8
  1.6 0.0 copy-start.7
  1.6 0.0 copy-start.6
  1.6 2.1 %collective-permute-start = (f32[2,3,4,152]{3,2,1,0:T(4,128)}, f32[2,3,4,152]{3,2,1,0:T(4,128)S(1)}, u32[]{:S(2)}, u32[]{:S(2)}) collective-permute-start(f32[2,3,4,152]{3,2,1,0:T(4,128)} %get-tuple-element.11), channel_id=1, source_target_pairs={{0,1},{1,0},{2,3},{3,2},{4,5},{5,4},{6,7},{7,6},{8,9},{9,8},{10,11... | collective-permute-start | bytes 43784 | tf_op jit(solution)/shard_map/ppermute | solution.py:293
  3.7 2.1 %copy.11 = bf16[316,2,2304]{2,0,1:T(8,128)(2,1)S(1)} copy(bf16[316,2,2304]{2,1,0:T(2,128)(2,1)} %param.9) | data formatting | bytes 5824512 | tf_op args[1]
  5.8 0.0 collective-permute-done.from_near
  5.8 1.3 %collective-permute-start.1 = (f32[2,3,4,152]{3,2,1,0:T(4,128)S(1)}, f32[2,3,4,152]{3,2,1,0:T(4,128)S(1)}, u32[]{:S(2)}, u32[]{:S(2)}) collective-permute-start(f32[2,3,4,152]{3,2,1,0:T(4,128)S(1)} %collective-permute-done.from_near), channel_id=1, source_target_pairs={{0,2},{1,3},{2,0},{3,1},{4,6},{5,7},{6,4},{7,5},{8,10},{9,11},{10,... | collective-permute-start | bytes 43784 | tf_op jit(solution)/shard_map/ppermute | solution.py:293
  7.1 0.0 copy-done.8
  7.1 0.2 %collective-permute-start.2 = (f32[3,4,152]{2,1,0:T(4,128)S(1)}, f32[3,4,152]{2,1,0:T(4,128)S(1)}, u32[]{:S(2)}, u32[]{:S(2)}) collective-permute-start(f32[3,4,152]{2,1,0:T(4,128)S(1)} %copy-done.8), channel_id=1, source_target_pairs={{0,2},{1,3},{2,0},{3,1},{4,6},{5,7},{6,4},{7,5},{8,10},{9,11},{10,... | collective-permute-start | bytes 21896 | tf_op jit(solution)/shard_map/ppermute | solution.py:293
  7.4 0.0 copy-done.7
  7.4 1.5 %collective-permute-start.3 = (f32[3,4,152]{2,1,0:T(4,128)S(1)}, f32[3,4,152]{2,1,0:T(4,128)S(1)}, u32[]{:S(2)}, u32[]{:S(2)}) collective-permute-start(f32[3,4,152]{2,1,0:T(4,128)S(1)} %copy-done.7), channel_id=1, source_target_pairs={{0,4},{8,12},{16,20},{24,28},{4,0},{12,8},{20,16},{28,24},{1,5},{9... | collective-permute-start | bytes 21896 | tf_op jit(solution)/shard_map/ppermute | solution.py:297
  8.9 0.0 copy-done.6
  8.9 0.0 copy-start
  8.9 0.0 copy-start.1
  8.9 0.0 copy-start.2
  8.9 0.0 copy-start.3
  8.9 0.0 copy-start.4
  8.9 0.0 copy-start.5
  8.9 3.7 %collective-permute-start.4 = (f32[3,4,152]{2,1,0:T(4,128)S(1)}, f32[3,4,152]{2,1,0:T(4,128)S(1)}, u32[]{:S(2)}, u32[]{:S(2)}) collective-permute-start(f32[3,4,152]{2,1,0:T(4,128)S(1)} %copy-done.6), channel_id=1, source_target_pairs={{4,8},{12,16},{20,24},{8,4},{16,12},{24,20},{5,9},{13,17},{21,25},... | collective-permute-start | bytes 21896 | tf_op jit(solution)/shard_map/ppermute | solution.py:297
  12.7 0.6 %prepare.1.refs_5_ = f32[16756,128]{1,0:T(8,128)S(1)} custom-call(bf16[2,316,2304]{2,1,0:T(8,128)(2,1)S(1)} %bitcast.7), custom_call_target="tpu_custom_call" | custom-call | flops 1456128 | bytes 8736768 | tf_op jit(solution)/shard_map/prepare/pallas_call | solution.py:307
  13.3 0.0 collective-permute-done.2.refs_0_
  13.4 0.0 collective-permute-done.3.refs_1_
  13.4 0.9 %collective-permute-done.4.refs_2_ = f32[3,4,152]{2,1,0:T(4,128)S(1)} collective-permute-done((f32[3,4,152]{2,1,0:T(4,128)S(1)}, f32[3,4,152]{2,1,0:T(4,128)S(1)}, u32[]{:S(2)}, u32[]{:S(2)}) %collective-permute-start.4) | collective-permute-done | bytes 7328 | tf_op jit(solution)/shard_map/ppermute | solution.py:297
  14.2 0.0 collective-permute-done.1.relayed
  14.2 0.0 copy-done
  14.2 0.0 copy-done.1
  14.2 0.0 copy-done.2
  14.2 0.0 copy-done.3
  14.3 0.0 copy-done.4
  14.3 0.0 copy-done.5
  14.3 8.2 %translate.1 = f32[3,16,152]{2,1,0:T(8,128)} custom-call(s32[4,4]{1,0:T(4,128)S(1)} %bitcast.11, s32[16,32]{1,0:T(8,128)S(1)} %copy-done.3, s32[16,32]{1,0:T(8,128)S(1)} %copy-done.4, f32[3,16,152]{2,1,0:T(8,128)S(1)} %bitcast.9, f32[2,3,4,152]{3,2,1,0:T(4,128)S(1)} %collective-permute-done.from_near, f32[2,3,4,152]{3,2,1,0:T(4,128)S(1)} %collective-permute-done.1.relayed, ...), custom_call_target="tpu_custom_call" | custom-call | tf_op jit(solution)/shard_map/translate/pallas_call | solution.py:323
Async XLA Ops:
  1.6 5.6 %copy-start.8 = (f32[3,4,152]{2,1,0:T(4,128)S(1)}, f32[3,4,152]{2,1,0:T(4,128)}, u32[]{:S(2)}) copy-start(f32[3,4,152]{2,1,0:T(4,128)} %get-tuple-element.13) | copy-start | bytes 21892
  1.6 5.8 %copy-start.7 = (f32[3,4,152]{2,1,0:T(4,128)S(1)}, f32[3,4,152]{2,1,0:T(4,128)}, u32[]{:S(2)}) copy-start(f32[3,4,152]{2,1,0:T(4,128)} %get-tuple-element.14) | copy-start | bytes 21892
  1.6 7.3 %copy-start.6 = (f32[3,4,152]{2,1,0:T(4,128)S(1)}, f32[3,4,152]{2,1,0:T(4,128)}, u32[]{:S(2)}) copy-start(f32[3,4,152]{2,1,0:T(4,128)} %get-tuple-element.15) | copy-start | bytes 21892
  1.6 4.2 %collective-permute-start = (f32[2,3,4,152]{3,2,1,0:T(4,128)}, f32[2,3,4,152]{3,2,1,0:T(4,128)S(1)}, u32[]{:S(2)}, u32[]{:S(2)}) collective-permute-start(f32[2,3,4,152]{3,2,1,0:T(4,128)} %get-tuple-element.11), channel_id=1, source_target_pairs={{0,1},{1,0},{2,3},{3,2},{4,5},{5,4},{6,7},{7,6},{8,9},{9,8},{10,11... | collective-permute-start | bytes 43784 | tf_op jit(solution)/shard_map/ppermute | solution.py:293
  5.8 8.4 %collective-permute-start.1 = (f32[2,3,4,152]{3,2,1,0:T(4,128)S(1)}, f32[2,3,4,152]{3,2,1,0:T(4,128)S(1)}, u32[]{:S(2)}, u32[]{:S(2)}) collective-permute-start(f32[2,3,4,152]{3,2,1,0:T(4,128)S(1)} %collective-permute-done.from_near), channel_id=1, source_target_pairs={{0,2},{1,3},{2,0},{3,1},{4,6},{5,7},{6,4},{7,5},{8,10},{9,11},{10,... | collective-permute-start | bytes 43784 | tf_op jit(solution)/shard_map/ppermute | solution.py:293
  7.1 6.2 %collective-permute-start.2 = (f32[3,4,152]{2,1,0:T(4,128)S(1)}, f32[3,4,152]{2,1,0:T(4,128)S(1)}, u32[]{:S(2)}, u32[]{:S(2)}) collective-permute-start(f32[3,4,152]{2,1,0:T(4,128)S(1)} %copy-done.8), channel_id=1, source_target_pairs={{0,2},{1,3},{2,0},{3,1},{4,6},{5,7},{6,4},{7,5},{8,10},{9,11},{10,... | collective-permute-start | bytes 21896 | tf_op jit(solution)/shard_map/ppermute | solution.py:293
  7.4 6.0 %collective-permute-start.3 = (f32[3,4,152]{2,1,0:T(4,128)S(1)}, f32[3,4,152]{2,1,0:T(4,128)S(1)}, u32[]{:S(2)}, u32[]{:S(2)}) collective-permute-start(f32[3,4,152]{2,1,0:T(4,128)S(1)} %copy-done.7), channel_id=1, source_target_pairs={{0,4},{8,12},{16,20},{24,28},{4,0},{12,8},{20,16},{28,24},{1,5},{9... | collective-permute-start | bytes 21896 | tf_op jit(solution)/shard_map/ppermute | solution.py:297
  8.9 5.3 %copy-start = (bf16[320,4608]{1,0:T(8,128)(2,1)S(1)}, bf16[320,4608]{1,0:T(8,128)(2,1)}, u32[]{:S(2)}) copy-start(bf16[320,4608]{1,0:T(8,128)(2,1)} %constant.4.clone.refs_3_) | copy-start | bytes 8847364
  8.9 5.3 %copy-start.1 = (f32[16,3,152]{2,0,1:T(8,128)S(1)}, f32[16,3,152]{2,0,1:T(8,128)}, u32[]{:S(2)}) copy-start(f32[16,3,152]{2,0,1:T(8,128)} %param.8) | copy-start | bytes 87556
  8.9 5.3 %copy-start.2 = (f32[1,4608]{1,0:T(1,128)S(1)}, f32[1,4608]{1,0:T(1,128)}, u32[]{:S(2)}) copy-start(f32[1,4608]{1,0:T(1,128)} %constant.5.clone.refs_4_) | copy-start | bytes 55300
  8.9 5.3 %copy-start.3 = (s32[16,32]{1,0:T(8,128)S(1)}, s32[16,32]{1,0:T(8,128)}, u32[]{:S(2)}) copy-start(s32[16,32]{1,0:T(8,128)} %source.1) | copy-start | bytes 6148
  8.9 5.3 %copy-start.4 = (s32[16,32]{1,0:T(8,128)S(1)}, s32[16,32]{1,0:T(8,128)}, u32[]{:S(2)}) copy-start(s32[16,32]{1,0:T(8,128)} %offset.1) | copy-start | bytes 6148
  8.9 5.3 %copy-start.5 = (s32[1,4,4]{2,1,0:T(4,128)S(1)}, s32[1,4,4]{2,1,0:T(4,128)}, u32[]{:S(2)}) copy-start(s32[1,4,4]{2,1,0:T(4,128)} %param.10) | copy-start | bytes 196
  8.9 5.3 %collective-permute-start.4 = (f32[3,4,152]{2,1,0:T(4,128)S(1)}, f32[3,4,152]{2,1,0:T(4,128)S(1)}, u32[]{:S(2)}, u32[]{:S(2)}) collective-permute-start(f32[3,4,152]{2,1,0:T(4,128)S(1)} %copy-done.6), channel_id=1, source_target_pairs={{4,8},{12,16},{20,24},{8,4},{16,12},{24,20},{5,9},{13,17},{21,25},... | collective-permute-start | bytes 21896 | tf_op jit(solution)/shard_map/ppermute | solution.py:297

commit v15 on v14

--- a/solution.py
+++ b/solution.py
@@ -24,7 +24,7 @@
 POINTS_PAD = 160
 CHUNK = 256
 PIECE = 512
-UNROLL = 8
+UNROLL = 16
 
 
 def surface_points(edge_count):
@@ -125,8 +125,8 @@
     member = lax.axis_index("dev")
     parity = lax.rem(lax.axis_index("group"), 2)
     rows[...] = jnp.zeros_like(rows)
-    pieces = {1: from_near.at[0], 3: relayed.at[1]}
-    pieces.update(zip((2, *range(4, peers)), from_far))
+    pieces = {1: from_near.at[0], 2: relayed.at[0], 3: relayed.at[1]}
+    pieces.update(zip(range(4, peers), from_far))
     for c in range(comp_count):
         base = c * slots
         rows[base : base + box_count, :surf] = density[c]
@@ -281,7 +281,7 @@
 
     boxes = jax.ShapeDtypeStruct((comp_count, cap, surf), f32)
     side = jax.ShapeDtypeStruct((comp_count, rim, surf), f32)
-    to_near, *to_far, to_first, to_second = pl.pallas_call(
+    to_near, to_two, *to_far, to_first, to_second = pl.pallas_call(
         pack_kernel,
         out_shape=(jax.ShapeDtypeStruct((2, *boxes.shape), f32),) + (boxes,) * (peers - 3) + (side,) * 2,
         in_specs=[vmem, smem, smem],
@@ -297,11 +297,11 @@
         return lax.ppermute(x, "group", pairs + [(j, i) for i, j in pairs])
 
     from_near = swap(to_near, 1)
-    from_far = [swap(x, k) for x, k in zip(to_far, (2, *range(4, peers)))]
+    from_far = [swap(x, k) for x, k in zip(to_far, range(4, peers))]
     from_first = swap_groups(to_first, 0)
     from_second = swap_groups(to_second, 1)
     by_part, near = lax.optimization_barrier((kernel_hat.transpose(1, 0, 2), from_near))
-    relayed = swap(near, 2)
+    relayed = swap(jnp.stack([to_two, near[1]]), 2)
 
     offsets = kernel_hat.shape[0]
     hat = pl.pallas_call(

time: 22.7 us -> 24.8 us (1.093)
  Pallas kernels: 10.5 us -> 12.6 us
  starting transfers between devices: 8.9 us -> 8.44 us
  waiting for transfers between devices: 0.86 us -> 1.23 us
    pallas_call x1, Pallas kernels: 8.24 us -> 10.4 us  [on_device(): pl.pallas_call(translate_kernel, out_shape=jax.ShapeDtypeStruct((comp_cou...]
    ppermute x2, waiting for transfers between devices: 0.86 us -> 1.23 us  [swap_groups(): return lax.ppermute(x, 'group', pairs + [(j, i) for i, j in pairs])]
    ppermute x3 -> x2, starting transfers between devices: 3.64 us -> 3.41 us  [swap(): return lax.ppermute(x, 'dev', [(i, i ^ k) for i in range(peers)])]
  transfers between devices with their start and end apart: 5 -> 4, of which waited for: 1 -> 1; matrix products, arithmetic and copies ran while one was open for 9% -> 9% of each run, Pallas kernels for 3% -> 3%
where the time goes in v15:
time: 24.8 us; the launch traced here: 24.6 us
  Pallas kernels  12.6 us (51%)
  starting transfers between devices  8.44 us (34%)
  local copies, waits for them, and re-layouts  2.15 us (9%)
  waiting for transfers between devices  1.23 us (5%)
    pallas_call x1, Pallas kernels, on_device(): pl.pallas_call(translate_kernel, out_shape=jax.ShapeDtypeStruct((comp_cou...  10.4 us
    ppermute x2, starting transfers between devices, swap_groups(): return lax.ppermute(x, 'group', pairs + [(j, i) for i, j in pairs])  5.03 us
    ppermute x2, starting transfers between devices, swap(): return lax.ppermute(x, 'dev', [(i, i ^ k) for i in range(peers)])  3.41 us
    unnamed x19, local copies, waits for them, and re-layouts  2.15 us
    pallas_call x1, Pallas kernels, on_device(): pl.pallas_call(pack_kernel, out_shape=(jax.ShapeDtypeStruct((2, *boxes.sh...  1.59 us
    ppermute x2, waiting for transfers between devices, swap_groups(): return lax.ppermute(x, 'group', pairs + [(j, i) for i, j in pairs])  1.23 us
    pallas_call x1, Pallas kernels, on_device(): pl.pallas_call(prepare_kernel, out_shape=jax.ShapeDtypeStruct((offsets *...  0.64 us
  transfers between devices with their start and end apart: 4, of which 1 were waited for; matrix products, arithmetic and copies ran while one was open for 9% of the time, Pallas kernels for 3%

profile of v15, /device:TPU:1, one launch (start us, length us, event | category | flops | bytes accessed | tf_op | source)
XLA Modules:
  0.0 24.6 jit_solution(6192610574956142649)
XLA Ops:
  0.0 1.6 %pack.1 = (f32[2,3,4,152]{3,2,1,0:T(4,128)}, f32[3,4,152]{2,1,0:T(4,128)}, f32[3,4,152]{2,1,0:T(4,128)}, f32[3,4,152]{2,1,0:T(4,128)}) custom-call(f32[3,16,152]{2,1,0:T(8,128)} %bitcast.9, s32[4,4]{1,0:T(4,128)} %bitcast.11, s32[2,4]{1,0:T(2,128)} %bitcast.14), custom_call_target="tpu_custom_call" | custom-call | tf_op jit(solution)/shard_map/pack/pallas_call | solution.py:284
  1.6 0.0 copy-start.6
  1.6 0.0 copy-start.8
  1.6 0.0 copy-start.7
  1.6 2.1 %collective-permute-start = (f32[2,3,4,152]{3,2,1,0:T(4,128)}, f32[2,3,4,152]{3,2,1,0:T(4,128)S(1)}, u32[]{:S(2)}, u32[]{:S(2)}) collective-permute-start(f32[2,3,4,152]{3,2,1,0:T(4,128)} %get-tuple-element.11), channel_id=1, source_target_pairs={{0,1},{1,0},{2,3},{3,2},{4,5},{5,4},{6,7},{7,6},{8,9},{9,8},{10,11... | collective-permute-start | bytes 43784 | tf_op jit(solution)/shard_map/ppermute | solution.py:293
  3.7 2.1 %copy.11 = bf16[316,2,2304]{2,0,1:T(8,128)(2,1)S(1)} copy(bf16[316,2,2304]{2,1,0:T(2,128)(2,1)} %param.9) | data formatting | bytes 5824512 | tf_op args[1]
  5.8 0.0 collective-permute-done.from_near
  5.9 0.0 copy-done.6
  5.9 1.3 %collective-permute-start.1 = (f32[2,3,4,152]{3,2,1,0:T(4,128)S(1)}, f32[2,3,4,152]{3,2,1,0:T(4,128)S(1)}, u32[]{:S(2)}, u32[]{:S(2)}) collective-permute-start(f32[2,3,4,152]{3,2,1,0:T(4,128)S(1)} %pad_maximum_fusion), channel_id=1, source_target_pairs={{0,2},{1,3},{2,0},{3,1},{4,6},{5,7},{6,4},{7,5},{8,10},{9,11},{10,... | collective-permute-start | bytes 43784 | tf_op jit(solution)/shard_map/ppermute | solution.py:293
  7.2 0.0 copy-done.8
  7.2 1.6 %collective-permute-start.2 = (f32[3,4,152]{2,1,0:T(4,128)S(1)}, f32[3,4,152]{2,1,0:T(4,128)S(1)}, u32[]{:S(2)}, u32[]{:S(2)}) collective-permute-start(f32[3,4,152]{2,1,0:T(4,128)S(1)} %copy-done.8), channel_id=1, source_target_pairs={{0,4},{8,12},{16,20},{24,28},{4,0},{12,8},{20,16},{28,24},{1,5},{9... | collective-permute-start | bytes 21896 | tf_op jit(solution)/shard_map/ppermute | solution.py:297
  8.8 0.0 copy-done.7
  8.8 0.0 copy-start
  8.8 0.0 copy-start.1
  8.8 0.0 copy-start.2
  8.8 0.0 copy-start.3
  8.8 0.0 copy-start.4
  8.9 0.0 copy-start.5
  8.9 3.4 %collective-permute-start.3 = (f32[3,4,152]{2,1,0:T(4,128)S(1)}, f32[3,4,152]{2,1,0:T(4,128)S(1)}, u32[]{:S(2)}, u32[]{:S(2)}) collective-permute-start(f32[3,4,152]{2,1,0:T(4,128)S(1)} %copy-done.7), channel_id=1, source_target_pairs={{4,8},{12,16},{20,24},{8,4},{16,12},{24,20},{5,9},{13,17},{21,25},... | collective-permute-start | bytes 21896 | tf_op jit(solution)/shard_map/ppermute | solution.py:297
  12.3 0.6 %prepare.1.refs_4_ = f32[16756,128]{1,0:T(8,128)S(1)} custom-call(bf16[2,316,2304]{2,1,0:T(8,128)(2,1)S(1)} %bitcast.8), custom_call_target="tpu_custom_call" | custom-call | flops 1456128 | bytes 8736768 | tf_op jit(solution)/shard_map/prepare/pallas_call | solution.py:307
  12.9 0.0 collective-permute-done.2.refs_0_
  12.9 1.2 %collective-permute-done.3.refs_1_ = f32[3,4,152]{2,1,0:T(4,128)S(1)} collective-permute-done((f32[3,4,152]{2,1,0:T(4,128)S(1)}, f32[3,4,152]{2,1,0:T(4,128)S(1)}, u32[]{:S(2)}, u32[]{:S(2)}) %collective-permute-start.3) | collective-permute-done | bytes 7328 | tf_op jit(solution)/shard_map/ppermute | solution.py:297
  14.2 0.0 collective-permute-done.1.relayed
  14.2 0.0 copy-done
  14.2 0.0 copy-done.1
  14.2 0.0 copy-done.2
  14.2 0.0 copy-done.3
  14.2 0.0 copy-done.4
  14.2 0.0 copy-done.5
  14.2 10.4 %translate.1 = f32[3,16,152]{2,1,0:T(8,128)} custom-call(s32[4,4]{1,0:T(4,128)S(1)} %bitcast.12, s32[16,32]{1,0:T(8,128)S(1)} %copy-done.3, s32[16,32]{1,0:T(8,128)S(1)} %copy-done.4, f32[3,16,152]{2,1,0:T(8,128)S(1)} %bitcast.10, f32[2,3,4,152]{3,2,1,0:T(4,128)S(1)} %collective-permute-done.from_near, f32[2,3,4,152]{3,2,1,0:T(4,128)S(1)} %collective-permute-done.1.relayed, ...), custom_call_target="tpu_custom_call" | custom-call | tf_op jit(solution)/shard_map/translate/pallas_call | solution.py:323
  (2 shorter events, 0.0 us)
Async XLA Ops:
  1.6 4.3 %copy-start.6 = (f32[3,4,152]{2,1,0:T(4,128)S(1)}, f32[3,4,152]{2,1,0:T(4,128)}, u32[]{:S(2)}) copy-start(f32[3,4,152]{2,1,0:T(4,128)} %get-tuple-element.12) | copy-start | bytes 21892
  1.6 5.6 %copy-start.8 = (f32[3,4,152]{2,1,0:T(4,128)S(1)}, f32[3,4,152]{2,1,0:T(4,128)}, u32[]{:S(2)}) copy-start(f32[3,4,152]{2,1,0:T(4,128)} %get-tuple-element.14) | copy-start | bytes 21892
  1.6 7.2 %copy-start.7 = (f32[3,4,152]{2,1,0:T(4,128)S(1)}, f32[3,4,152]{2,1,0:T(4,128)}, u32[]{:S(2)}) copy-start(f32[3,4,152]{2,1,0:T(4,128)} %get-tuple-element.15) | copy-start | bytes 21892
  1.6 4.2 %collective-permute-start = (f32[2,3,4,152]{3,2,1,0:T(4,128)}, f32[2,3,4,152]{3,2,1,0:T(4,128)S(1)}, u32[]{:S(2)}, u32[]{:S(2)}) collective-permute-start(f32[2,3,4,152]{3,2,1,0:T(4,128)} %get-tuple-element.11), channel_id=1, source_target_pairs={{0,1},{1,0},{2,3},{3,2},{4,5},{5,4},{6,7},{7,6},{8,9},{9,8},{10,11... | collective-permute-start | bytes 43784 | tf_op jit(solution)/shard_map/ppermute | solution.py:293
  5.9 8.3 %collective-permute-start.1 = (f32[2,3,4,152]{3,2,1,0:T(4,128)S(1)}, f32[2,3,4,152]{3,2,1,0:T(4,128)S(1)}, u32[]{:S(2)}, u32[]{:S(2)}) collective-permute-start(f32[2,3,4,152]{3,2,1,0:T(4,128)S(1)} %pad_maximum_fusion), channel_id=1, source_target_pairs={{0,2},{1,3},{2,0},{3,1},{4,6},{5,7},{6,4},{7,5},{8,10},{9,11},{10,... | collective-permute-start | bytes 43784 | tf_op jit(solution)/shard_map/ppermute | solution.py:293
  7.2 5.7 %collective-permute-start.2 = (f32[3,4,152]{2,1,0:T(4,128)S(1)}, f32[3,4,152]{2,1,0:T(4,128)S(1)}, u32[]{:S(2)}, u32[]{:S(2)}) collective-permute-start(f32[3,4,152]{2,1,0:T(4,128)S(1)} %copy-done.8), channel_id=1, source_target_pairs={{0,4},{8,12},{16,20},{24,28},{4,0},{12,8},{20,16},{28,24},{1,5},{9... | collective-permute-start | bytes 21896 | tf_op jit(solution)/shard_map/ppermute | solution.py:297
  8.8 5.3 %copy-start = (bf16[320,4608]{1,0:T(8,128)(2,1)S(1)}, bf16[320,4608]{1,0:T(8,128)(2,1)}, u32[]{:S(2)}) copy-start(bf16[320,4608]{1,0:T(8,128)(2,1)} %constant.4.clone.refs_2_) | copy-start | bytes 8847364
  8.8 5.3 %copy-start.1 = (f32[16,3,152]{2,0,1:T(8,128)S(1)}, f32[16,3,152]{2,0,1:T(8,128)}, u32[]{:S(2)}) copy-start(f32[16,3,152]{2,0,1:T(8,128)} %param.8) | copy-start | bytes 87556
  8.8 5.3 %copy-start.2 = (f32[1,4608]{1,0:T(1,128)S(1)}, f32[1,4608]{1,0:T(1,128)}, u32[]{:S(2)}) copy-start(f32[1,4608]{1,0:T(1,128)} %constant.5.clone.refs_3_) | copy-start | bytes 55300
  8.8 5.3 %copy-start.3 = (s32[16,32]{1,0:T(8,128)S(1)}, s32[16,32]{1,0:T(8,128)}, u32[]{:S(2)}) copy-start(s32[16,32]{1,0:T(8,128)} %source.1) | copy-start | bytes 6148
  8.8 5.3 %copy-start.4 = (s32[16,32]{1,0:T(8,128)S(1)}, s32[16,32]{1,0:T(8,128)}, u32[]{:S(2)}) copy-start(s32[16,32]{1,0:T(8,128)} %offset.1) | copy-start | bytes 6148
  8.9 5.3 %copy-start.5 = (s32[1,4,4]{2,1,0:T(4,128)S(1)}, s32[1,4,4]{2,1,0:T(4,128)}, u32[]{:S(2)}) copy-start(s32[1,4,4]{2,1,0:T(4,128)} %param.10) | copy-start | bytes 196
  8.9 5.3 %collective-permute-start.3 = (f32[3,4,152]{2,1,0:T(4,128)S(1)}, f32[3,4,152]{2,1,0:T(4,128)S(1)}, u32[]{:S(2)}, u32[]{:S(2)}) collective-permute-start(f32[3,4,152]{2,1,0:T(4,128)S(1)} %copy-done.7), channel_id=1, source_target_pairs={{4,8},{12,16},{20,24},{8,4},{16,12},{24,20},{5,9},{13,17},{21,25},... | collective-permute-start | bytes 21896 | tf_op jit(solution)/shard_map/ppermute | solution.py:297

commit v16 on v15

--- a/solution.py
+++ b/solution.py
@@ -24,7 +24,7 @@
 POINTS_PAD = 160
 CHUNK = 256
 PIECE = 512
-UNROLL = 16
+UNROLL = 4
 
 
 def surface_points(edge_count):

time: 24.8 us -> 22.8 us (0.919)
  Pallas kernels: 12.6 us -> 10.6 us
    pallas_call x1, Pallas kernels: 10.4 us -> 8.39 us  [on_device(): pl.pallas_call(translate_kernel, out_shape=jax.ShapeDtypeStruct((comp_cou...]
where the time goes in v16:
time: 22.8 us; the launch traced here: 22.6 us
  Pallas kernels  10.6 us (46%)
  starting transfers between devices  8.44 us (37%)
  local copies, waits for them, and re-layouts  2.15 us (9%)
  waiting for transfers between devices  1.23 us (5%)
    pallas_call x1, Pallas kernels, on_device(): pl.pallas_call(translate_kernel, out_shape=jax.ShapeDtypeStruct((comp_cou...  8.39 us
    ppermute x2, starting transfers between devices, swap_groups(): return lax.ppermute(x, 'group', pairs + [(j, i) for i, j in pairs])  5.03 us
    ppermute x2, starting transfers between devices, swap(): return lax.ppermute(x, 'dev', [(i, i ^ k) for i in range(peers)])  3.41 us
    unnamed x19, local copies, waits for them, and re-layouts  2.15 us
    pallas_call x1, Pallas kernels, on_device(): pl.pallas_call(pack_kernel, out_shape=(jax.ShapeDtypeStruct((2, *boxes.sh...  1.59 us
    ppermute x2, waiting for transfers between devices, swap_groups(): return lax.ppermute(x, 'group', pairs + [(j, i) for i, j in pairs])  1.23 us
    pallas_call x1, Pallas kernels, on_device(): pl.pallas_call(prepare_kernel, out_shape=jax.ShapeDtypeStruct((offsets *...  0.64 us
  transfers between devices with their start and end apart: 4, of which 1 were waited for; matrix products, arithmetic and copies ran while one was open for 9% of the time, Pallas kernels for 3%

profile of v16, /device:TPU:1, one launch (start us, length us, event | category | flops | bytes accessed | tf_op | source)
XLA Modules:
  0.0 22.6 jit_solution(16690740870129625535)
XLA Ops:
  0.0 1.6 %pack.1 = (f32[2,3,4,152]{3,2,1,0:T(4,128)}, f32[3,4,152]{2,1,0:T(4,128)}, f32[3,4,152]{2,1,0:T(4,128)}, f32[3,4,152]{2,1,0:T(4,128)}) custom-call(f32[3,16,152]{2,1,0:T(8,128)} %bitcast.9, s32[4,4]{1,0:T(4,128)} %bitcast.11, s32[2,4]{1,0:T(2,128)} %bitcast.14), custom_call_target="tpu_custom_call" | custom-call | tf_op jit(solution)/shard_map/pack/pallas_call | solution.py:284
  1.6 0.0 copy-start.6
  1.6 0.0 copy-start.8
  1.6 0.0 copy-start.7
  1.6 2.1 %collective-permute-start = (f32[2,3,4,152]{3,2,1,0:T(4,128)}, f32[2,3,4,152]{3,2,1,0:T(4,128)S(1)}, u32[]{:S(2)}, u32[]{:S(2)}) collective-permute-start(f32[2,3,4,152]{3,2,1,0:T(4,128)} %get-tuple-element.11), channel_id=1, source_target_pairs={{0,1},{1,0},{2,3},{3,2},{4,5},{5,4},{6,7},{7,6},{8,9},{9,8},{10,11... | collective-permute-start | bytes 43784 | tf_op jit(solution)/shard_map/ppermute | solution.py:293
  3.7 2.1 %copy.11 = bf16[316,2,2304]{2,0,1:T(8,128)(2,1)S(1)} copy(bf16[316,2,2304]{2,1,0:T(2,128)(2,1)} %param.9) | data formatting | bytes 5824512 | tf_op args[1]
  5.8 0.0 collective-permute-done.from_near
  5.9 0.0 copy-done.6
  5.9 1.3 %collective-permute-start.1 = (f32[2,3,4,152]{3,2,1,0:T(4,128)S(1)}, f32[2,3,4,152]{3,2,1,0:T(4,128)S(1)}, u32[]{:S(2)}, u32[]{:S(2)}) collective-permute-start(f32[2,3,4,152]{3,2,1,0:T(4,128)S(1)} %pad_maximum_fusion), channel_id=1, source_target_pairs={{0,2},{1,3},{2,0},{3,1},{4,6},{5,7},{6,4},{7,5},{8,10},{9,11},{10,... | collective-permute-start | bytes 43784 | tf_op jit(solution)/shard_map/ppermute | solution.py:293
  7.2 0.0 copy-done.8
  7.2 1.6 %collective-permute-start.2 = (f32[3,4,152]{2,1,0:T(4,128)S(1)}, f32[3,4,152]{2,1,0:T(4,128)S(1)}, u32[]{:S(2)}, u32[]{:S(2)}) collective-permute-start(f32[3,4,152]{2,1,0:T(4,128)S(1)} %copy-done.8), channel_id=1, source_target_pairs={{0,4},{8,12},{16,20},{24,28},{4,0},{12,8},{20,16},{28,24},{1,5},{9... | collective-permute-start | bytes 21896 | tf_op jit(solution)/shard_map/ppermute | solution.py:297
  8.8 0.0 copy-done.7
  8.8 0.0 copy-start
  8.8 0.0 copy-start.1
  8.8 0.0 copy-start.2
  8.8 0.0 copy-start.3
  8.8 0.0 copy-start.4
  8.9 0.0 copy-start.5
  8.9 3.4 %collective-permute-start.3 = (f32[3,4,152]{2,1,0:T(4,128)S(1)}, f32[3,4,152]{2,1,0:T(4,128)S(1)}, u32[]{:S(2)}, u32[]{:S(2)}) collective-permute-start(f32[3,4,152]{2,1,0:T(4,128)S(1)} %copy-done.7), channel_id=1, source_target_pairs={{4,8},{12,16},{20,24},{8,4},{16,12},{24,20},{5,9},{13,17},{21,25},... | collective-permute-start | bytes 21896 | tf_op jit(solution)/shard_map/ppermute | solution.py:297
  12.3 0.6 %prepare.1.refs_4_ = f32[16756,128]{1,0:T(8,128)S(1)} custom-call(bf16[2,316,2304]{2,1,0:T(8,128)(2,1)S(1)} %bitcast.8), custom_call_target="tpu_custom_call" | custom-call | flops 1456128 | bytes 8736768 | tf_op jit(solution)/shard_map/prepare/pallas_call | solution.py:307
  12.9 0.0 collective-permute-done.2.refs_0_
  12.9 1.2 %collective-permute-done.3.refs_1_ = f32[3,4,152]{2,1,0:T(4,128)S(1)} collective-permute-done((f32[3,4,152]{2,1,0:T(4,128)S(1)}, f32[3,4,152]{2,1,0:T(4,128)S(1)}, u32[]{:S(2)}, u32[]{:S(2)}) %collective-permute-start.3) | collective-permute-done | bytes 7328 | tf_op jit(solution)/shard_map/ppermute | solution.py:297
  14.2 0.0 collective-permute-done.1.relayed
  14.2 0.0 copy-done
  14.2 0.0 copy-done.1
  14.2 0.0 copy-done.2
  14.2 0.0 copy-done.3
  14.2 0.0 copy-done.4
  14.2 0.0 copy-done.5
  14.2 8.4 %translate.1 = f32[3,16,152]{2,1,0:T(8,128)} custom-call(s32[4,4]{1,0:T(4,128)S(1)} %bitcast.12, s32[16,32]{1,0:T(8,128)S(1)} %copy-done.3, s32[16,32]{1,0:T(8,128)S(1)} %copy-done.4, f32[3,16,152]{2,1,0:T(8,128)S(1)} %bitcast.10, f32[2,3,4,152]{3,2,1,0:T(4,128)S(1)} %collective-permute-done.from_near, f32[2,3,4,152]{3,2,1,0:T(4,128)S(1)} %collective-permute-done.1.relayed, ...), custom_call_target="tpu_custom_call" | custom-call | tf_op jit(solution)/shard_map/translate/pallas_call | solution.py:323
  (2 shorter events, 0.0 us)
Async XLA Ops:
  1.6 4.3 %copy-start.6 = (f32[3,4,152]{2,1,0:T(4,128)S(1)}, f32[3,4,152]{2,1,0:T(4,128)}, u32[]{:S(2)}) copy-start(f32[3,4,152]{2,1,0:T(4,128)} %get-tuple-element.12) | copy-start | bytes 21892
  1.6 5.6 %copy-start.8 = (f32[3,4,152]{2,1,0:T(4,128)S(1)}, f32[3,4,152]{2,1,0:T(4,128)}, u32[]{:S(2)}) copy-start(f32[3,4,152]{2,1,0:T(4,128)} %get-tuple-element.14) | copy-start | bytes 21892
  1.6 7.2 %copy-start.7 = (f32[3,4,152]{2,1,0:T(4,128)S(1)}, f32[3,4,152]{2,1,0:T(4,128)}, u32[]{:S(2)}) copy-start(f32[3,4,152]{2,1,0:T(4,128)} %get-tuple-element.15) | copy-start | bytes 21892
  1.6 4.2 %collective-permute-start = (f32[2,3,4,152]{3,2,1,0:T(4,128)}, f32[2,3,4,152]{3,2,1,0:T(4,128)S(1)}, u32[]{:S(2)}, u32[]{:S(2)}) collective-permute-start(f32[2,3,4,152]{3,2,1,0:T(4,128)} %get-tuple-element.11), channel_id=1, source_target_pairs={{0,1},{1,0},{2,3},{3,2},{4,5},{5,4},{6,7},{7,6},{8,9},{9,8},{10,11... | collective-permute-start | bytes 43784 | tf_op jit(solution)/shard_map/ppermute | solution.py:293
  5.9 8.3 %collective-permute-start.1 = (f32[2,3,4,152]{3,2,1,0:T(4,128)S(1)}, f32[2,3,4,152]{3,2,1,0:T(4,128)S(1)}, u32[]{:S(2)}, u32[]{:S(2)}) collective-permute-start(f32[2,3,4,152]{3,2,1,0:T(4,128)S(1)} %pad_maximum_fusion), channel_id=1, source_target_pairs={{0,2},{1,3},{2,0},{3,1},{4,6},{5,7},{6,4},{7,5},{8,10},{9,11},{10,... | collective-permute-start | bytes 43784 | tf_op jit(solution)/shard_map/ppermute | solution.py:293
  7.2 5.7 %collective-permute-start.2 = (f32[3,4,152]{2,1,0:T(4,128)S(1)}, f32[3,4,152]{2,1,0:T(4,128)S(1)}, u32[]{:S(2)}, u32[]{:S(2)}) collective-permute-start(f32[3,4,152]{2,1,0:T(4,128)S(1)} %copy-done.8), channel_id=1, source_target_pairs={{0,4},{8,12},{16,20},{24,28},{4,0},{12,8},{20,16},{28,24},{1,5},{9... | collective-permute-start | bytes 21896 | tf_op jit(solution)/shard_map/ppermute | solution.py:297
  8.8 5.3 %copy-start = (bf16[320,4608]{1,0:T(8,128)(2,1)S(1)}, bf16[320,4608]{1,0:T(8,128)(2,1)}, u32[]{:S(2)}) copy-start(bf16[320,4608]{1,0:T(8,128)(2,1)} %constant.4.clone.refs_2_) | copy-start | bytes 8847364
  8.8 5.3 %copy-start.1 = (f32[16,3,152]{2,0,1:T(8,128)S(1)}, f32[16,3,152]{2,0,1:T(8,128)}, u32[]{:S(2)}) copy-start(f32[16,3,152]{2,0,1:T(8,128)} %param.8) | copy-start | bytes 87556
  8.8 5.3 %copy-start.2 = (f32[1,4608]{1,0:T(1,128)S(1)}, f32[1,4608]{1,0:T(1,128)}, u32[]{:S(2)}) copy-start(f32[1,4608]{1,0:T(1,128)} %constant.5.clone.refs_3_) | copy-start | bytes 55300
  8.8 5.3 %copy-start.3 = (s32[16,32]{1,0:T(8,128)S(1)}, s32[16,32]{1,0:T(8,128)}, u32[]{:S(2)}) copy-start(s32[16,32]{1,0:T(8,128)} %source.1) | copy-start | bytes 6148
  8.8 5.3 %copy-start.4 = (s32[16,32]{1,0:T(8,128)S(1)}, s32[16,32]{1,0:T(8,128)}, u32[]{:S(2)}) copy-start(s32[16,32]{1,0:T(8,128)} %offset.1) | copy-start | bytes 6148
  8.9 5.3 %copy-start.5 = (s32[1,4,4]{2,1,0:T(4,128)S(1)}, s32[1,4,4]{2,1,0:T(4,128)}, u32[]{:S(2)}) copy-start(s32[1,4,4]{2,1,0:T(4,128)} %param.10) | copy-start | bytes 196
  8.9 5.3 %collective-permute-start.3 = (f32[3,4,152]{2,1,0:T(4,128)S(1)}, f32[3,4,152]{2,1,0:T(4,128)S(1)}, u32[]{:S(2)}, u32[]{:S(2)}) collective-permute-start(f32[3,4,152]{2,1,0:T(4,128)S(1)} %copy-done.7), channel_id=1, source_target_pairs={{4,8},{12,16},{20,24},{8,4},{16,12},{24,20},{5,9},{13,17},{21,25},... | collective-permute-start | bytes 21896 | tf_op jit(solution)/shard_map/ppermute | solution.py:297

commit v17 on v16

--- a/solution.py
+++ b/solution.py
@@ -24,7 +24,7 @@
 POINTS_PAD = 160
 CHUNK = 256
 PIECE = 512
-UNROLL = 4
+UNROLL = 8
 
 
 def surface_points(edge_count):

time: 22.8 us -> 22.7 us (level)
  no operation moved by 1% of the time
where the time goes in v17:
time: 22.7 us; the launch traced here: 22.5 us
  Pallas kernels  10.5 us (46%)
  starting transfers between devices  8.44 us (37%)
  local copies, waits for them, and re-layouts  2.15 us (9%)
  waiting for transfers between devices  1.23 us (5%)
    pallas_call x1, Pallas kernels, on_device(): pl.pallas_call(translate_kernel, out_shape=jax.ShapeDtypeStruct((comp_cou...  8.29 us
    ppermute x2, starting transfers between devices, swap_groups(): return lax.ppermute(x, 'group', pairs + [(j, i) for i, j in pairs])  5.03 us
    ppermute x2, starting transfers between devices, swap(): return lax.ppermute(x, 'dev', [(i, i ^ k) for i in range(peers)])  3.41 us
    unnamed x19, local copies, waits for them, and re-layouts  2.15 us
    pallas_call x1, Pallas kernels, on_device(): pl.pallas_call(pack_kernel, out_shape=(jax.ShapeDtypeStruct((2, *boxes.sh...  1.59 us
    ppermute x2, waiting for transfers between devices, swap_groups(): return lax.ppermute(x, 'group', pairs + [(j, i) for i, j in pairs])  1.23 us
    pallas_call x1, Pallas kernels, on_device(): pl.pallas_call(prepare_kernel, out_shape=jax.ShapeDtypeStruct((offsets *...  0.64 us
  transfers between devices with their start and end apart: 4, of which 1 were waited for; matrix products, arithmetic and copies ran while one was open for 9% of the time, Pallas kernels for 3%

profile of v17, /device:TPU:1, one launch (start us, length us, event | category | flops | bytes accessed | tf_op | source)
XLA Modules:
  0.0 22.5 jit_solution(7049716318129494613)
XLA Ops:
  0.0 1.6 %pack.1 = (f32[2,3,4,152]{3,2,1,0:T(4,128)}, f32[3,4,152]{2,1,0:T(4,128)}, f32[3,4,152]{2,1,0:T(4,128)}, f32[3,4,152]{2,1,0:T(4,128)}) custom-call(f32[3,16,152]{2,1,0:T(8,128)} %bitcast.9, s32[4,4]{1,0:T(4,128)} %bitcast.11, s32[2,4]{1,0:T(2,128)} %bitcast.14), custom_call_target="tpu_custom_call" | custom-call | tf_op jit(solution)/shard_map/pack/pallas_call | solution.py:284
  1.6 0.0 copy-start.6
  1.6 0.0 copy-start.8
  1.6 0.0 copy-start.7
  1.6 2.1 %collective-permute-start = (f32[2,3,4,152]{3,2,1,0:T(4,128)}, f32[2,3,4,152]{3,2,1,0:T(4,128)S(1)}, u32[]{:S(2)}, u32[]{:S(2)}) collective-permute-start(f32[2,3,4,152]{3,2,1,0:T(4,128)} %get-tuple-element.11), channel_id=1, source_target_pairs={{0,1},{1,0},{2,3},{3,2},{4,5},{5,4},{6,7},{7,6},{8,9},{9,8},{10,11... | collective-permute-start | bytes 43784 | tf_op jit(solution)/shard_map/ppermute | solution.py:293
  3.7 2.1 %copy.11 = bf16[316,2,2304]{2,0,1:T(8,128)(2,1)S(1)} copy(bf16[316,2,2304]{2,1,0:T(2,128)(2,1)} %param.9) | data formatting | bytes 5824512 | tf_op args[1]
  5.8 0.0 collective-permute-done.from_near
  5.9 0.0 copy-done.6
  5.9 1.3 %collective-permute-start.1 = (f32[2,3,4,152]{3,2,1,0:T(4,128)S(1)}, f32[2,3,4,152]{3,2,1,0:T(4,128)S(1)}, u32[]{:S(2)}, u32[]{:S(2)}) collective-permute-start(f32[2,3,4,152]{3,2,1,0:T(4,128)S(1)} %pad_maximum_fusion), channel_id=1, source_target_pairs={{0,2},{1,3},{2,0},{3,1},{4,6},{5,7},{6,4},{7,5},{8,10},{9,11},{10,... | collective-permute-start | bytes 43784 | tf_op jit(solution)/shard_map/ppermute | solution.py:293
  7.2 0.0 copy-done.8
  7.2 1.6 %collective-permute-start.2 = (f32[3,4,152]{2,1,0:T(4,128)S(1)}, f32[3,4,152]{2,1,0:T(4,128)S(1)}, u32[]{:S(2)}, u32[]{:S(2)}) collective-permute-start(f32[3,4,152]{2,1,0:T(4,128)S(1)} %copy-done.8), channel_id=1, source_target_pairs={{0,4},{8,12},{16,20},{24,28},{4,0},{12,8},{20,16},{28,24},{1,5},{9... | collective-permute-start | bytes 21896 | tf_op jit(solution)/shard_map/ppermute | solution.py:297
  8.8 0.0 copy-done.7
  8.8 0.0 copy-start
  8.8 0.0 copy-start.1
  8.8 0.0 copy-start.2
  8.8 0.0 copy-start.3
  8.8 0.0 copy-start.4
  8.9 0.0 copy-start.5
  8.9 3.4 %collective-permute-start.3 = (f32[3,4,152]{2,1,0:T(4,128)S(1)}, f32[3,4,152]{2,1,0:T(4,128)S(1)}, u32[]{:S(2)}, u32[]{:S(2)}) collective-permute-start(f32[3,4,152]{2,1,0:T(4,128)S(1)} %copy-done.7), channel_id=1, source_target_pairs={{4,8},{12,16},{20,24},{8,4},{16,12},{24,20},{5,9},{13,17},{21,25},... | collective-permute-start | bytes 21896 | tf_op jit(solution)/shard_map/ppermute | solution.py:297
  12.3 0.6 %prepare.1.refs_4_ = f32[16756,128]{1,0:T(8,128)S(1)} custom-call(bf16[2,316,2304]{2,1,0:T(8,128)(2,1)S(1)} %bitcast.8), custom_call_target="tpu_custom_call" | custom-call | flops 1456128 | bytes 8736768 | tf_op jit(solution)/shard_map/prepare/pallas_call | solution.py:307
  12.9 0.0 collective-permute-done.2.refs_0_
  12.9 1.2 %collective-permute-done.3.refs_1_ = f32[3,4,152]{2,1,0:T(4,128)S(1)} collective-permute-done((f32[3,4,152]{2,1,0:T(4,128)S(1)}, f32[3,4,152]{2,1,0:T(4,128)S(1)}, u32[]{:S(2)}, u32[]{:S(2)}) %collective-permute-start.3) | collective-permute-done | bytes 7328 | tf_op jit(solution)/shard_map/ppermute | solution.py:297
  14.2 0.0 collective-permute-done.1.relayed
  14.2 0.0 copy-done
  14.2 0.0 copy-done.1
  14.2 0.0 copy-done.2
  14.2 0.0 copy-done.3
  14.2 0.0 copy-done.4
  14.2 0.0 copy-done.5
  14.2 8.3 %translate.1 = f32[3,16,152]{2,1,0:T(8,128)} custom-call(s32[4,4]{1,0:T(4,128)S(1)} %bitcast.12, s32[16,32]{1,0:T(8,128)S(1)} %copy-done.3, s32[16,32]{1,0:T(8,128)S(1)} %copy-done.4, f32[3,16,152]{2,1,0:T(8,128)S(1)} %bitcast.10, f32[2,3,4,152]{3,2,1,0:T(4,128)S(1)} %collective-permute-done.from_near, f32[2,3,4,152]{3,2,1,0:T(4,128)S(1)} %collective-permute-done.1.relayed, ...), custom_call_target="tpu_custom_call" | custom-call | tf_op jit(solution)/shard_map/translate/pallas_call | solution.py:323
  (2 shorter events, 0.0 us)
Async XLA Ops:
  1.6 4.3 %copy-start.6 = (f32[3,4,152]{2,1,0:T(4,128)S(1)}, f32[3,4,152]{2,1,0:T(4,128)}, u32[]{:S(2)}) copy-start(f32[3,4,152]{2,1,0:T(4,128)} %get-tuple-element.12) | copy-start | bytes 21892
  1.6 5.6 %copy-start.8 = (f32[3,4,152]{2,1,0:T(4,128)S(1)}, f32[3,4,152]{2,1,0:T(4,128)}, u32[]{:S(2)}) copy-start(f32[3,4,152]{2,1,0:T(4,128)} %get-tuple-element.14) | copy-start | bytes 21892
  1.6 7.2 %copy-start.7 = (f32[3,4,152]{2,1,0:T(4,128)S(1)}, f32[3,4,152]{2,1,0:T(4,128)}, u32[]{:S(2)}) copy-start(f32[3,4,152]{2,1,0:T(4,128)} %get-tuple-element.15) | copy-start | bytes 21892
  1.6 4.2 %collective-permute-start = (f32[2,3,4,152]{3,2,1,0:T(4,128)}, f32[2,3,4,152]{3,2,1,0:T(4,128)S(1)}, u32[]{:S(2)}, u32[]{:S(2)}) collective-permute-start(f32[2,3,4,152]{3,2,1,0:T(4,128)} %get-tuple-element.11), channel_id=1, source_target_pairs={{0,1},{1,0},{2,3},{3,2},{4,5},{5,4},{6,7},{7,6},{8,9},{9,8},{10,11... | collective-permute-start | bytes 43784 | tf_op jit(solution)/shard_map/ppermute | solution.py:293
  5.9 8.3 %collective-permute-start.1 = (f32[2,3,4,152]{3,2,1,0:T(4,128)S(1)}, f32[2,3,4,152]{3,2,1,0:T(4,128)S(1)}, u32[]{:S(2)}, u32[]{:S(2)}) collective-permute-start(f32[2,3,4,152]{3,2,1,0:T(4,128)S(1)} %pad_maximum_fusion), channel_id=1, source_target_pairs={{0,2},{1,3},{2,0},{3,1},{4,6},{5,7},{6,4},{7,5},{8,10},{9,11},{10,... | collective-permute-start | bytes 43784 | tf_op jit(solution)/shard_map/ppermute | solution.py:293
  7.2 5.7 %collective-permute-start.2 = (f32[3,4,152]{2,1,0:T(4,128)S(1)}, f32[3,4,152]{2,1,0:T(4,128)S(1)}, u32[]{:S(2)}, u32[]{:S(2)}) collective-permute-start(f32[3,4,152]{2,1,0:T(4,128)S(1)} %copy-done.8), channel_id=1, source_target_pairs={{0,4},{8,12},{16,20},{24,28},{4,0},{12,8},{20,16},{28,24},{1,5},{9... | collective-permute-start | bytes 21896 | tf_op jit(solution)/shard_map/ppermute | solution.py:297
  8.8 5.3 %copy-start = (bf16[320,4608]{1,0:T(8,128)(2,1)S(1)}, bf16[320,4608]{1,0:T(8,128)(2,1)}, u32[]{:S(2)}) copy-start(bf16[320,4608]{1,0:T(8,128)(2,1)} %constant.4.clone.refs_2_) | copy-start | bytes 8847364
  8.8 5.3 %copy-start.1 = (f32[16,3,152]{2,0,1:T(8,128)S(1)}, f32[16,3,152]{2,0,1:T(8,128)}, u32[]{:S(2)}) copy-start(f32[16,3,152]{2,0,1:T(8,128)} %param.8) | copy-start | bytes 87556
  8.8 5.3 %copy-start.2 = (f32[1,4608]{1,0:T(1,128)S(1)}, f32[1,4608]{1,0:T(1,128)}, u32[]{:S(2)}) copy-start(f32[1,4608]{1,0:T(1,128)} %constant.5.clone.refs_3_) | copy-start | bytes 55300
  8.8 5.3 %copy-start.3 = (s32[16,32]{1,0:T(8,128)S(1)}, s32[16,32]{1,0:T(8,128)}, u32[]{:S(2)}) copy-start(s32[16,32]{1,0:T(8,128)} %source.1) | copy-start | bytes 6148
  8.8 5.3 %copy-start.4 = (s32[16,32]{1,0:T(8,128)S(1)}, s32[16,32]{1,0:T(8,128)}, u32[]{:S(2)}) copy-start(s32[16,32]{1,0:T(8,128)} %offset.1) | copy-start | bytes 6148
  8.9 5.3 %copy-start.5 = (s32[1,4,4]{2,1,0:T(4,128)S(1)}, s32[1,4,4]{2,1,0:T(4,128)}, u32[]{:S(2)}) copy-start(s32[1,4,4]{2,1,0:T(4,128)} %param.10) | copy-start | bytes 196
  8.9 5.3 %collective-permute-start.3 = (f32[3,4,152]{2,1,0:T(4,128)S(1)}, f32[3,4,152]{2,1,0:T(4,128)S(1)}, u32[]{:S(2)}, u32[]{:S(2)}) collective-permute-start(f32[3,4,152]{2,1,0:T(4,128)S(1)} %copy-done.7), channel_id=1, source_target_pairs={{4,8},{12,16},{20,24},{8,4},{16,12},{24,20},{5,9},{13,17},{21,25},... | collective-permute-start | bytes 21896 | tf_op jit(solution)/shard_map/ppermute | solution.py:297

commit v18 on v17

--- a/solution.py
+++ b/solution.py
@@ -23,7 +23,7 @@
 HAT_ROWS = 3 * MAIN + 2 * TAIL + 1
 POINTS_PAD = 160
 CHUNK = 256
-PIECE = 512
+PIECE = 2304
 UNROLL = 8
 
 

time: 22.7 us -> 22.7 us (level)
  no operation moved by 1% of the time
where the time goes in v18:
time: 22.7 us; the launch traced here: 22.5 us
  Pallas kernels  10.5 us (46%)
  starting transfers between devices  8.44 us (37%)
  local copies, waits for them, and re-layouts  2.15 us (9%)
  waiting for transfers between devices  1.23 us (5%)
    pallas_call x1, Pallas kernels, on_device(): pl.pallas_call(translate_kernel, out_shape=jax.ShapeDtypeStruct((comp_cou...  8.26 us
    ppermute x2, starting transfers between devices, swap_groups(): return lax.ppermute(x, 'group', pairs + [(j, i) for i, j in pairs])  5.03 us
    ppermute x2, starting transfers between devices, swap(): return lax.ppermute(x, 'dev', [(i, i ^ k) for i in range(peers)])  3.41 us
    unnamed x19, local copies, waits for them, and re-layouts  2.15 us
    pallas_call x1, Pallas kernels, on_device(): pl.pallas_call(pack_kernel, out_shape=(jax.ShapeDtypeStruct((2, *boxes.sh...  1.59 us
    ppermute x2, waiting for transfers between devices, swap_groups(): return lax.ppermute(x, 'group', pairs + [(j, i) for i, j in pairs])  1.23 us
    pallas_call x1, Pallas kernels, on_device(): pl.pallas_call(prepare_kernel, out_shape=jax.ShapeDtypeStruct((offsets *...  0.64 us
  transfers between devices with their start and end apart: 4, of which 1 were waited for; matrix products, arithmetic and copies ran while one was open for 9% of the time, Pallas kernels for 3%

profile of v18, /device:TPU:1, one launch (start us, length us, event | category | flops | bytes accessed | tf_op | source)
XLA Modules:
  0.0 22.5 jit_solution(15853000107692020595)
XLA Ops:
  0.0 1.6 %pack.1 = (f32[2,3,4,152]{3,2,1,0:T(4,128)}, f32[3,4,152]{2,1,0:T(4,128)}, f32[3,4,152]{2,1,0:T(4,128)}, f32[3,4,152]{2,1,0:T(4,128)}) custom-call(f32[3,16,152]{2,1,0:T(8,128)} %bitcast.9, s32[4,4]{1,0:T(4,128)} %bitcast.11, s32[2,4]{1,0:T(2,128)} %bitcast.14), custom_call_target="tpu_custom_call" | custom-call | tf_op jit(solution)/shard_map/pack/pallas_call | solution.py:284
  1.6 0.0 copy-start.6
  1.6 0.0 copy-start.8
  1.6 0.0 copy-start.7
  1.6 2.1 %collective-permute-start = (f32[2,3,4,152]{3,2,1,0:T(4,128)}, f32[2,3,4,152]{3,2,1,0:T(4,128)S(1)}, u32[]{:S(2)}, u32[]{:S(2)}) collective-permute-start(f32[2,3,4,152]{3,2,1,0:T(4,128)} %get-tuple-element.11), channel_id=1, source_target_pairs={{0,1},{1,0},{2,3},{3,2},{4,5},{5,4},{6,7},{7,6},{8,9},{9,8},{10,11... | collective-permute-start | bytes 43784 | tf_op jit(solution)/shard_map/ppermute | solution.py:293
  3.7 2.1 %copy.11 = bf16[316,2,2304]{2,0,1:T(8,128)(2,1)S(1)} copy(bf16[316,2,2304]{2,1,0:T(2,128)(2,1)} %param.9) | data formatting | bytes 5824512 | tf_op args[1]
  5.8 0.0 collective-permute-done.from_near
  5.9 0.0 copy-done.6
  5.9 1.3 %collective-permute-start.1 = (f32[2,3,4,152]{3,2,1,0:T(4,128)S(1)}, f32[2,3,4,152]{3,2,1,0:T(4,128)S(1)}, u32[]{:S(2)}, u32[]{:S(2)}) collective-permute-start(f32[2,3,4,152]{3,2,1,0:T(4,128)S(1)} %pad_maximum_fusion), channel_id=1, source_target_pairs={{0,2},{1,3},{2,0},{3,1},{4,6},{5,7},{6,4},{7,5},{8,10},{9,11},{10,... | collective-permute-start | bytes 43784 | tf_op jit(solution)/shard_map/ppermute | solution.py:293
  7.2 0.0 copy-done.8
  7.2 1.6 %collective-permute-start.2 = (f32[3,4,152]{2,1,0:T(4,128)S(1)}, f32[3,4,152]{2,1,0:T(4,128)S(1)}, u32[]{:S(2)}, u32[]{:S(2)}) collective-permute-start(f32[3,4,152]{2,1,0:T(4,128)S(1)} %copy-done.8), channel_id=1, source_target_pairs={{0,4},{8,12},{16,20},{24,28},{4,0},{12,8},{20,16},{28,24},{1,5},{9... | collective-permute-start | bytes 21896 | tf_op jit(solution)/shard_map/ppermute | solution.py:297
  8.8 0.0 copy-done.7
  8.8 0.0 copy-start
  8.8 0.0 copy-start.1
  8.8 0.0 copy-start.2
  8.8 0.0 copy-start.3
  8.8 0.0 copy-start.4
  8.9 0.0 copy-start.5
  8.9 3.4 %collective-permute-start.3 = (f32[3,4,152]{2,1,0:T(4,128)S(1)}, f32[3,4,152]{2,1,0:T(4,128)S(1)}, u32[]{:S(2)}, u32[]{:S(2)}) collective-permute-start(f32[3,4,152]{2,1,0:T(4,128)S(1)} %copy-done.7), channel_id=1, source_target_pairs={{4,8},{12,16},{20,24},{8,4},{16,12},{24,20},{5,9},{13,17},{21,25},... | collective-permute-start | bytes 21896 | tf_op jit(solution)/shard_map/ppermute | solution.py:297
  12.3 0.6 %prepare.1.refs_4_ = f32[16756,128]{1,0:T(8,128)S(1)} custom-call(bf16[2,316,2304]{2,1,0:T(8,128)(2,1)S(1)} %bitcast.8), custom_call_target="tpu_custom_call" | custom-call | flops 1456128 | bytes 8736768 | tf_op jit(solution)/shard_map/prepare/pallas_call | solution.py:307
  12.9 0.0 collective-permute-done.2.refs_0_
  12.9 1.2 %collective-permute-done.3.refs_1_ = f32[3,4,152]{2,1,0:T(4,128)S(1)} collective-permute-done((f32[3,4,152]{2,1,0:T(4,128)S(1)}, f32[3,4,152]{2,1,0:T(4,128)S(1)}, u32[]{:S(2)}, u32[]{:S(2)}) %collective-permute-start.3) | collective-permute-done | bytes 7328 | tf_op jit(solution)/shard_map/ppermute | solution.py:297
  14.2 0.0 collective-permute-done.1.relayed
  14.2 0.0 copy-done
  14.2 0.0 copy-done.1
  14.2 0.0 copy-done.2
  14.2 0.0 copy-done.3
  14.2 0.0 copy-done.4
  14.2 0.0 copy-done.5
  14.2 8.3 %translate.1 = f32[3,16,152]{2,1,0:T(8,128)} custom-call(s32[4,4]{1,0:T(4,128)S(1)} %bitcast.12, s32[16,32]{1,0:T(8,128)S(1)} %copy-done.3, s32[16,32]{1,0:T(8,128)S(1)} %copy-done.4, f32[3,16,152]{2,1,0:T(8,128)S(1)} %bitcast.10, f32[2,3,4,152]{3,2,1,0:T(4,128)S(1)} %collective-permute-done.from_near, f32[2,3,4,152]{3,2,1,0:T(4,128)S(1)} %collective-permute-done.1.relayed, ...), custom_call_target="tpu_custom_call" | custom-call | tf_op jit(solution)/shard_map/translate/pallas_call | solution.py:323
  (2 shorter events, 0.0 us)
Async XLA Ops:
  1.6 4.3 %copy-start.6 = (f32[3,4,152]{2,1,0:T(4,128)S(1)}, f32[3,4,152]{2,1,0:T(4,128)}, u32[]{:S(2)}) copy-start(f32[3,4,152]{2,1,0:T(4,128)} %get-tuple-element.12) | copy-start | bytes 21892
  1.6 5.6 %copy-start.8 = (f32[3,4,152]{2,1,0:T(4,128)S(1)}, f32[3,4,152]{2,1,0:T(4,128)}, u32[]{:S(2)}) copy-start(f32[3,4,152]{2,1,0:T(4,128)} %get-tuple-element.14) | copy-start | bytes 21892
  1.6 7.2 %copy-start.7 = (f32[3,4,152]{2,1,0:T(4,128)S(1)}, f32[3,4,152]{2,1,0:T(4,128)}, u32[]{:S(2)}) copy-start(f32[3,4,152]{2,1,0:T(4,128)} %get-tuple-element.15) | copy-start | bytes 21892
  1.6 4.2 %collective-permute-start = (f32[2,3,4,152]{3,2,1,0:T(4,128)}, f32[2,3,4,152]{3,2,1,0:T(4,128)S(1)}, u32[]{:S(2)}, u32[]{:S(2)}) collective-permute-start(f32[2,3,4,152]{3,2,1,0:T(4,128)} %get-tuple-element.11), channel_id=1, source_target_pairs={{0,1},{1,0},{2,3},{3,2},{4,5},{5,4},{6,7},{7,6},{8,9},{9,8},{10,11... | collective-permute-start | bytes 43784 | tf_op jit(solution)/shard_map/ppermute | solution.py:293
  5.9 8.3 %collective-permute-start.1 = (f32[2,3,4,152]{3,2,1,0:T(4,128)S(1)}, f32[2,3,4,152]{3,2,1,0:T(4,128)S(1)}, u32[]{:S(2)}, u32[]{:S(2)}) collective-permute-start(f32[2,3,4,152]{3,2,1,0:T(4,128)S(1)} %pad_maximum_fusion), channel_id=1, source_target_pairs={{0,2},{1,3},{2,0},{3,1},{4,6},{5,7},{6,4},{7,5},{8,10},{9,11},{10,... | collective-permute-start | bytes 43784 | tf_op jit(solution)/shard_map/ppermute | solution.py:293
  7.2 5.7 %collective-permute-start.2 = (f32[3,4,152]{2,1,0:T(4,128)S(1)}, f32[3,4,152]{2,1,0:T(4,128)S(1)}, u32[]{:S(2)}, u32[]{:S(2)}) collective-permute-start(f32[3,4,152]{2,1,0:T(4,128)S(1)} %copy-done.8), channel_id=1, source_target_pairs={{0,4},{8,12},{16,20},{24,28},{4,0},{12,8},{20,16},{28,24},{1,5},{9... | collective-permute-start | bytes 21896 | tf_op jit(solution)/shard_map/ppermute | solution.py:297
  8.8 5.3 %copy-start = (bf16[320,4608]{1,0:T(8,128)(2,1)S(1)}, bf16[320,4608]{1,0:T(8,128)(2,1)}, u32[]{:S(2)}) copy-start(bf16[320,4608]{1,0:T(8,128)(2,1)} %constant.4.clone.refs_2_) | copy-start | bytes 8847364
  8.8 5.3 %copy-start.1 = (f32[16,3,152]{2,0,1:T(8,128)S(1)}, f32[16,3,152]{2,0,1:T(8,128)}, u32[]{:S(2)}) copy-start(f32[16,3,152]{2,0,1:T(8,128)} %param.8) | copy-start | bytes 87556
  8.8 5.3 %copy-start.2 = (f32[1,4608]{1,0:T(1,128)S(1)}, f32[1,4608]{1,0:T(1,128)}, u32[]{:S(2)}) copy-start(f32[1,4608]{1,0:T(1,128)} %constant.5.clone.refs_3_) | copy-start | bytes 55300
  8.8 5.3 %copy-start.3 = (s32[16,32]{1,0:T(8,128)S(1)}, s32[16,32]{1,0:T(8,128)}, u32[]{:S(2)}) copy-start(s32[16,32]{1,0:T(8,128)} %source.1) | copy-start | bytes 6148
  8.8 5.3 %copy-start.4 = (s32[16,32]{1,0:T(8,128)S(1)}, s32[16,32]{1,0:T(8,128)}, u32[]{:S(2)}) copy-start(s32[16,32]{1,0:T(8,128)} %offset.1) | copy-start | bytes 6148
  8.9 5.3 %copy-start.5 = (s32[1,4,4]{2,1,0:T(4,128)S(1)}, s32[1,4,4]{2,1,0:T(4,128)}, u32[]{:S(2)}) copy-start(s32[1,4,4]{2,1,0:T(4,128)} %param.10) | copy-start | bytes 196
  8.9 5.3 %collective-permute-start.3 = (f32[3,4,152]{2,1,0:T(4,128)S(1)}, f32[3,4,152]{2,1,0:T(4,128)S(1)}, u32[]{:S(2)}, u32[]{:S(2)}) collective-permute-start(f32[3,4,152]{2,1,0:T(4,128)S(1)} %copy-done.7), channel_id=1, source_target_pairs={{4,8},{12,16},{20,24},{8,4},{16,12},{24,20},{5,9},{13,17},{21,25},... | collective-permute-start | bytes 21896 | tf_op jit(solution)/shard_map/ppermute | solution.py:297

commit v19 on v17

--- a/solution.py
+++ b/solution.py
@@ -300,7 +300,7 @@
     from_far = [swap(x, k) for x, k in zip(to_far, range(4, peers))]
     from_first = swap_groups(to_first, 0)
     from_second = swap_groups(to_second, 1)
-    by_part, near = lax.optimization_barrier((kernel_hat.transpose(1, 0, 2), from_near))
+    kernels, near = lax.optimization_barrier((kernel_hat, from_near))
     relayed = swap(jnp.stack([to_two, near[1]]), 2)
 
     offsets = kernel_hat.shape[0]
@@ -312,7 +312,7 @@
         compiler_params=pltpu.CompilerParams(vmem_limit_bytes=16 * 1024 * 1024),
         cost_estimate=pl.CostEstimate(flops=kernel_hat.size, bytes_accessed=6 * kernel_hat.size, transcendentals=0),
         name="prepare",
-    )(by_part)
+    )(kernels.transpose(1, 0, 2))
 
     slots = box_count + peers * cap + 2 * rim
     row_count = comp_count * slots

time: 22.7 us -> 25 us (1.10)
  local copies, waits for them, and re-layouts: 2.15 us -> 3.23 us
  other arithmetic: 0.01 us -> 0.71 us
  starting transfers between devices: 8.44 us -> 8.72 us
    optimization_barrier x0 -> x1, local copies, waits for them, and re-layouts: none -> 2.11 us  [on_device(): kernels, near = lax.optimization_barrier((kernel_hat, from_near))]
    ppermute x2, waiting for transfers between devices: 0.01 us -> 1.43 us  [swap(): return lax.ppermute(x, 'dev', [(i, i ^ k) for i in range(peers)])]
    ppermute x2, waiting for transfers between devices: 1.23 us -> 0.01 us  [swap_groups(): return lax.ppermute(x, 'group', pairs + [(j, i) for i, j in pairs])]
    unnamed x19 -> x12, local copies, waits for them, and re-layouts: 2.15 us -> 1.12 us
    another operation x1, other arithmetic: 0.01 us -> 0.71 us  [on_device(): relayed = swap(jnp.stack([to_two, near[1]]), 2)]
where the time goes in v19:
time: 25 us; the launch traced here: 24.7 us
  Pallas kernels  10.5 us (42%)
  starting transfers between devices  8.72 us (35%)
  local copies, waits for them, and re-layouts  3.23 us (13%)
  waiting for transfers between devices  1.43 us (6%)
  other arithmetic  0.71 us (3%)
    pallas_call x1, Pallas kernels, on_device(): pl.pallas_call(translate_kernel, out_shape=jax.ShapeDtypeStruct((comp_cou...  8.27 us
    ppermute x2, starting transfers between devices, swap_groups(): return lax.ppermute(x, 'group', pairs + [(j, i) for i, j in pairs])  5.19 us
    ppermute x2, starting transfers between devices, swap(): return lax.ppermute(x, 'dev', [(i, i ^ k) for i in range(peers)])  3.53 us
    optimization_barrier x1, local copies, waits for them, and re-layouts, on_device(): kernels, near = lax.optimization_barrier((kernel_hat, from_near))  2.11 us
    pallas_call x1, Pallas kernels, on_device(): pl.pallas_call(pack_kernel, out_shape=(jax.ShapeDtypeStruct((2, *boxes.sh...  1.59 us
    ppermute x2, waiting for transfers between devices, swap(): return lax.ppermute(x, 'dev', [(i, i ^ k) for i in range(peers)])  1.43 us
    unnamed x12, local copies, waits for them, and re-layouts  1.12 us
    another operation x1, other arithmetic, on_device(): relayed = swap(jnp.stack([to_two, near[1]]), 2)  0.71 us
  transfers between devices with their start and end apart: 4, of which 1 were waited for; matrix products, arithmetic and copies ran while one was open for 9% of the time, Pallas kernels for 3%

profile of v19, /device:TPU:1, one launch (start us, length us, event | category | flops | bytes accessed | tf_op | source)
XLA Modules:
  0.0 24.7 jit_solution(2676487657671725526)
XLA Ops:
  0.0 1.6 %pack.1 = (f32[2,3,4,152]{3,2,1,0:T(4,128)}, f32[3,4,152]{2,1,0:T(4,128)}, f32[3,4,152]{2,1,0:T(4,128)}, f32[3,4,152]{2,1,0:T(4,128)}) custom-call(f32[3,16,152]{2,1,0:T(8,128)} %bitcast.9, s32[4,4]{1,0:T(4,128)} %bitcast.11, s32[2,4]{1,0:T(2,128)} %bitcast.14), custom_call_target="tpu_custom_call" | custom-call | tf_op jit(solution)/shard_map/pack/pallas_call | solution.py:284
  1.6 2.0 %collective-permute-start = (f32[2,3,4,152]{3,2,1,0:T(4,128)}, f32[2,3,4,152]{3,2,1,0:T(4,128)S(1)}, u32[]{:S(2)}, u32[]{:S(2)}) collective-permute-start(f32[2,3,4,152]{3,2,1,0:T(4,128)} %get-tuple-element.11), channel_id=1, source_target_pairs={{0,1},{1,0},{2,3},{3,2},{4,5},{5,4},{6,7},{7,6},{8,9},{9,8},{10,11... | collective-permute-start | bytes 43784 | tf_op jit(solution)/shard_map/ppermute | solution.py:293
  3.6 1.4 %collective-permute-done.from_near = f32[2,3,4,152]{3,2,1,0:T(4,128)S(1)} collective-permute-done((f32[2,3,4,152]{3,2,1,0:T(4,128)}, f32[2,3,4,152]{3,2,1,0:T(4,128)S(1)}, u32[]{:S(2)}, u32[]{:S(2)}) %collective-permute-start) | collective-permute-done | bytes 14624 | tf_op jit(solution)/shard_map/ppermute | solution.py:293
  5.1 0.7 %pad_maximum_fusion = f32[2,3,4,152]{3,2,1,0:T(4,128)S(1)} fusion(f32[1,3,4,152]{3,2,1,0:T(4,128)S(1)} %slice.3, f32[1,3,4,152]{3,2,1,0:T(4,128)} %bitcast.13), kind=kLoop, calls=%fused_computation.1 | loop fusion | flops 3648 | bytes 29184 | tf_op jit(solution)/shard_map/stack | solution.py:304
  5.8 1.5 %collective-permute-start.1 = (f32[2,3,4,152]{3,2,1,0:T(4,128)S(1)}, f32[2,3,4,152]{3,2,1,0:T(4,128)S(1)}, u32[]{:S(2)}, u32[]{:S(2)}) collective-permute-start(f32[2,3,4,152]{3,2,1,0:T(4,128)S(1)} %pad_maximum_fusion), channel_id=1, source_target_pairs={{0,2},{1,3},{2,0},{3,1},{4,6},{5,7},{6,4},{7,5},{8,10},{9,11},{10,... | collective-permute-start | bytes 43784 | tf_op jit(solution)/shard_map/ppermute | solution.py:293
  7.3 2.1 %collective-permute-start.2 = (f32[3,4,152]{2,1,0:T(4,128)}, f32[3,4,152]{2,1,0:T(4,128)S(1)}, u32[]{:S(2)}, u32[]{:S(2)}) collective-permute-start(f32[3,4,152]{2,1,0:T(4,128)} %get-tuple-element.14), channel_id=1, source_target_pairs={{0,4},{8,12},{16,20},{24,28},{4,0},{12,8},{20,16},{28,24},{1,5},{9... | collective-permute-start | bytes 21896 | tf_op jit(solution)/shard_map/ppermute | solution.py:297
  9.4 3.1 %collective-permute-start.3 = (f32[3,4,152]{2,1,0:T(4,128)}, f32[3,4,152]{2,1,0:T(4,128)S(1)}, u32[]{:S(2)}, u32[]{:S(2)}) collective-permute-start(f32[3,4,152]{2,1,0:T(4,128)} %get-tuple-element.15), channel_id=1, source_target_pairs={{4,8},{12,16},{20,24},{8,4},{16,12},{24,20},{5,9},{13,17},{21,25},... | collective-permute-start | bytes 21896 | tf_op jit(solution)/shard_map/ppermute | solution.py:297
  12.5 2.1 %copy.11 = bf16[316,2,2304]{2,0,1:T(8,128)(2,1)S(1)} copy(bf16[316,2,2304]{2,1,0:T(2,128)(2,1)} %param.9) | data formatting | bytes 5824512 | tf_op jit(solution)/shard_map/optimization_barrier | solution.py:303
  14.6 0.0 copy-start
  14.6 0.0 copy-start.1
  14.6 0.0 copy-start.2
  14.6 0.0 copy-start.3
  14.6 0.0 copy-start.4
  14.6 0.0 copy-start.5
  14.7 0.6 %prepare.1.refs_4_ = f32[16756,128]{1,0:T(8,128)S(1)} custom-call(bf16[2,316,2304]{2,1,0:T(8,128)(2,1)S(1)} %bitcast.8), custom_call_target="tpu_custom_call" | custom-call | flops 1456128 | bytes 8736768 | tf_op jit(solution)/shard_map/prepare/pallas_call | solution.py:307
  15.3 0.0 collective-permute-done.2.refs_0_
  15.3 0.0 collective-permute-done.3.refs_1_
  15.3 0.0 collective-permute-done.1.relayed
  15.3 1.1 %copy-done = bf16[320,4608]{1,0:T(8,128)(2,1)S(1)} copy-done((bf16[320,4608]{1,0:T(8,128)(2,1)S(1)}, bf16[320,4608]{1,0:T(8,128)(2,1)}, u32[]{:S(2)}) %copy-start) | copy-done | bytes 2949144
  16.4 0.0 copy-done.1
  16.4 0.0 copy-done.2
  16.4 0.0 copy-done.3
  16.4 0.0 copy-done.4
  16.4 0.0 copy-done.5
  16.4 8.3 %translate.1 = f32[3,16,152]{2,1,0:T(8,128)} custom-call(s32[4,4]{1,0:T(4,128)S(1)} %bitcast.12, s32[16,32]{1,0:T(8,128)S(1)} %copy-done.3, s32[16,32]{1,0:T(8,128)S(1)} %copy-done.4, f32[3,16,152]{2,1,0:T(8,128)S(1)} %bitcast.10, f32[2,3,4,152]{3,2,1,0:T(4,128)S(1)} %collective-permute-done.from_near, f32[2,3,4,152]{3,2,1,0:T(4,128)S(1)} %collective-permute-done.1.relayed, ...), custom_call_target="tpu_custom_call" | custom-call | tf_op jit(solution)/shard_map/translate/pallas_call | solution.py:323
  (1 shorter events, 0.0 us)
Async XLA Ops:
  1.6 3.5 %collective-permute-start = (f32[2,3,4,152]{3,2,1,0:T(4,128)}, f32[2,3,4,152]{3,2,1,0:T(4,128)S(1)}, u32[]{:S(2)}, u32[]{:S(2)}) collective-permute-start(f32[2,3,4,152]{3,2,1,0:T(4,128)} %get-tuple-element.11), channel_id=1, source_target_pairs={{0,1},{1,0},{2,3},{3,2},{4,5},{5,4},{6,7},{7,6},{8,9},{9,8},{10,11... | collective-permute-start | bytes 43784 | tf_op jit(solution)/shard_map/ppermute | solution.py:293
  5.8 9.5 %collective-permute-start.1 = (f32[2,3,4,152]{3,2,1,0:T(4,128)S(1)}, f32[2,3,4,152]{3,2,1,0:T(4,128)S(1)}, u32[]{:S(2)}, u32[]{:S(2)}) collective-permute-start(f32[2,3,4,152]{3,2,1,0:T(4,128)S(1)} %pad_maximum_fusion), channel_id=1, source_target_pairs={{0,2},{1,3},{2,0},{3,1},{4,6},{5,7},{6,4},{7,5},{8,10},{9,11},{10,... | collective-permute-start | bytes 43784 | tf_op jit(solution)/shard_map/ppermute | solution.py:293
  7.3 8.0 %collective-permute-start.2 = (f32[3,4,152]{2,1,0:T(4,128)}, f32[3,4,152]{2,1,0:T(4,128)S(1)}, u32[]{:S(2)}, u32[]{:S(2)}) collective-permute-start(f32[3,4,152]{2,1,0:T(4,128)} %get-tuple-element.14), channel_id=1, source_target_pairs={{0,4},{8,12},{16,20},{24,28},{4,0},{12,8},{20,16},{28,24},{1,5},{9... | collective-permute-start | bytes 21896 | tf_op jit(solution)/shard_map/ppermute | solution.py:297
  9.4 5.9 %collective-permute-start.3 = (f32[3,4,152]{2,1,0:T(4,128)}, f32[3,4,152]{2,1,0:T(4,128)S(1)}, u32[]{:S(2)}, u32[]{:S(2)}) collective-permute-start(f32[3,4,152]{2,1,0:T(4,128)} %get-tuple-element.15), channel_id=1, source_target_pairs={{4,8},{12,16},{20,24},{8,4},{16,12},{24,20},{5,9},{13,17},{21,25},... | collective-permute-start | bytes 21896 | tf_op jit(solution)/shard_map/ppermute | solution.py:297
  14.6 1.8 %copy-start = (bf16[320,4608]{1,0:T(8,128)(2,1)S(1)}, bf16[320,4608]{1,0:T(8,128)(2,1)}, u32[]{:S(2)}) copy-start(bf16[320,4608]{1,0:T(8,128)(2,1)} %constant.4.clone.refs_2_) | copy-start | bytes 8847364
  14.6 1.8 %copy-start.1 = (f32[16,3,152]{2,0,1:T(8,128)S(1)}, f32[16,3,152]{2,0,1:T(8,128)}, u32[]{:S(2)}) copy-start(f32[16,3,152]{2,0,1:T(8,128)} %param.8) | copy-start | bytes 87556
  14.6 1.8 %copy-start.2 = (f32[1,4608]{1,0:T(1,128)S(1)}, f32[1,4608]{1,0:T(1,128)}, u32[]{:S(2)}) copy-start(f32[1,4608]{1,0:T(1,128)} %constant.5.clone.refs_3_) | copy-start | bytes 55300
  14.6 1.8 %copy-start.3 = (s32[16,32]{1,0:T(8,128)S(1)}, s32[16,32]{1,0:T(8,128)}, u32[]{:S(2)}) copy-start(s32[16,32]{1,0:T(8,128)} %source.1) | copy-start | bytes 6148
  14.6 1.8 %copy-start.4 = (s32[16,32]{1,0:T(8,128)S(1)}, s32[16,32]{1,0:T(8,128)}, u32[]{:S(2)}) copy-start(s32[16,32]{1,0:T(8,128)} %offset.1) | copy-start | bytes 6148
  14.6 1.8 %copy-start.5 = (s32[1,4,4]{2,1,0:T(4,128)S(1)}, s32[1,4,4]{2,1,0:T(4,128)}, u32[]{:S(2)}) copy-start(s32[1,4,4]{2,1,0:T(4,128)} %param.10) | copy-start | bytes 196

commit v20 on v17

--- a/solution.py
+++ b/solution.py
@@ -298,8 +298,8 @@
 
     from_near = swap(to_near, 1)
     from_far = [swap(x, k) for x, k in zip(to_far, range(4, peers))]
+    from_second = swap_groups(to_second, 1)
     from_first = swap_groups(to_first, 0)
-    from_second = swap_groups(to_second, 1)
     by_part, near = lax.optimization_barrier((kernel_hat.transpose(1, 0, 2), from_near))
     relayed = swap(jnp.stack([to_two, near[1]]), 2)
 

time: 22.7 us -> 22.7 us (level)
  no operation moved by 1% of the time
where the time goes in v20:
time: 22.7 us; the launch traced here: 22.5 us
  Pallas kernels  10.5 us (46%)
  starting transfers between devices  8.44 us (37%)
  local copies, waits for them, and re-layouts  2.15 us (9%)
  waiting for transfers between devices  1.23 us (5%)
    pallas_call x1, Pallas kernels, on_device(): pl.pallas_call(translate_kernel, out_shape=jax.ShapeDtypeStruct((comp_cou...  8.26 us
    ppermute x2, starting transfers between devices, swap_groups(): return lax.ppermute(x, 'group', pairs + [(j, i) for i, j in pairs])  5.03 us
    ppermute x2, starting transfers between devices, swap(): return lax.ppermute(x, 'dev', [(i, i ^ k) for i in range(peers)])  3.41 us
    unnamed x19, local copies, waits for them, and re-layouts  2.15 us
    pallas_call x1, Pallas kernels, on_device(): pl.pallas_call(pack_kernel, out_shape=(jax.ShapeDtypeStruct((2, *boxes.sh...  1.59 us
    ppermute x2, waiting for transfers between devices, swap_groups(): return lax.ppermute(x, 'group', pairs + [(j, i) for i, j in pairs])  1.23 us
    pallas_call x1, Pallas kernels, on_device(): pl.pallas_call(prepare_kernel, out_shape=jax.ShapeDtypeStruct((offsets *...  0.64 us
  transfers between devices with their start and end apart: 4, of which 1 were waited for; matrix products, arithmetic and copies ran while one was open for 9% of the time, Pallas kernels for 3%

profile of v20, /device:TPU:1, one launch (start us, length us, event | category | flops | bytes accessed | tf_op | source)
XLA Modules:
  0.0 22.5 jit_solution(7049716318129494613)
XLA Ops:
  0.0 1.6 %pack.1 = (f32[2,3,4,152]{3,2,1,0:T(4,128)}, f32[3,4,152]{2,1,0:T(4,128)}, f32[3,4,152]{2,1,0:T(4,128)}, f32[3,4,152]{2,1,0:T(4,128)}) custom-call(f32[3,16,152]{2,1,0:T(8,128)} %bitcast.9, s32[4,4]{1,0:T(4,128)} %bitcast.11, s32[2,4]{1,0:T(2,128)} %bitcast.14), custom_call_target="tpu_custom_call" | custom-call | tf_op jit(solution)/shard_map/pack/pallas_call | solution.py:284
  1.6 0.0 copy-start.6
  1.6 0.0 copy-start.8
  1.6 0.0 copy-start.7
  1.6 2.1 %collective-permute-start = (f32[2,3,4,152]{3,2,1,0:T(4,128)}, f32[2,3,4,152]{3,2,1,0:T(4,128)S(1)}, u32[]{:S(2)}, u32[]{:S(2)}) collective-permute-start(f32[2,3,4,152]{3,2,1,0:T(4,128)} %get-tuple-element.11), channel_id=1, source_target_pairs={{0,1},{1,0},{2,3},{3,2},{4,5},{5,4},{6,7},{7,6},{8,9},{9,8},{10,11... | collective-permute-start | bytes 43784 | tf_op jit(solution)/shard_map/ppermute | solution.py:293
  3.7 2.1 %copy.11 = bf16[316,2,2304]{2,0,1:T(8,128)(2,1)S(1)} copy(bf16[316,2,2304]{2,1,0:T(2,128)(2,1)} %param.9) | data formatting | bytes 5824512 | tf_op args[1]
  5.8 0.0 collective-permute-done.from_near
  5.9 0.0 copy-done.6
  5.9 1.3 %collective-permute-start.1 = (f32[2,3,4,152]{3,2,1,0:T(4,128)S(1)}, f32[2,3,4,152]{3,2,1,0:T(4,128)S(1)}, u32[]{:S(2)}, u32[]{:S(2)}) collective-permute-start(f32[2,3,4,152]{3,2,1,0:T(4,128)S(1)} %pad_maximum_fusion), channel_id=1, source_target_pairs={{0,2},{1,3},{2,0},{3,1},{4,6},{5,7},{6,4},{7,5},{8,10},{9,11},{10,... | collective-permute-start | bytes 43784 | tf_op jit(solution)/shard_map/ppermute | solution.py:293
  7.2 0.0 copy-done.8
  7.2 1.6 %collective-permute-start.2 = (f32[3,4,152]{2,1,0:T(4,128)S(1)}, f32[3,4,152]{2,1,0:T(4,128)S(1)}, u32[]{:S(2)}, u32[]{:S(2)}) collective-permute-start(f32[3,4,152]{2,1,0:T(4,128)S(1)} %copy-done.8), channel_id=1, source_target_pairs={{0,4},{8,12},{16,20},{24,28},{4,0},{12,8},{20,16},{28,24},{1,5},{9... | collective-permute-start | bytes 21896 | tf_op jit(solution)/shard_map/ppermute | solution.py:297
  8.8 0.0 copy-done.7
  8.8 0.0 copy-start
  8.8 0.0 copy-start.1
  8.8 0.0 copy-start.2
  8.8 0.0 copy-start.3
  8.8 0.0 copy-start.4
  8.9 0.0 copy-start.5
  8.9 3.4 %collective-permute-start.3 = (f32[3,4,152]{2,1,0:T(4,128)S(1)}, f32[3,4,152]{2,1,0:T(4,128)S(1)}, u32[]{:S(2)}, u32[]{:S(2)}) collective-permute-start(f32[3,4,152]{2,1,0:T(4,128)S(1)} %copy-done.7), channel_id=1, source_target_pairs={{4,8},{12,16},{20,24},{8,4},{16,12},{24,20},{5,9},{13,17},{21,25},... | collective-permute-start | bytes 21896 | tf_op jit(solution)/shard_map/ppermute | solution.py:297
  12.3 0.6 %prepare.1.refs_4_ = f32[16756,128]{1,0:T(8,128)S(1)} custom-call(bf16[2,316,2304]{2,1,0:T(8,128)(2,1)S(1)} %bitcast.8), custom_call_target="tpu_custom_call" | custom-call | flops 1456128 | bytes 8736768 | tf_op jit(solution)/shard_map/prepare/pallas_call | solution.py:307
  12.9 0.0 collective-permute-done.2.refs_0_
  12.9 1.2 %collective-permute-done.3.refs_1_ = f32[3,4,152]{2,1,0:T(4,128)S(1)} collective-permute-done((f32[3,4,152]{2,1,0:T(4,128)S(1)}, f32[3,4,152]{2,1,0:T(4,128)S(1)}, u32[]{:S(2)}, u32[]{:S(2)}) %collective-permute-start.3) | collective-permute-done | bytes 7328 | tf_op jit(solution)/shard_map/ppermute | solution.py:297
  14.2 0.0 collective-permute-done.1.relayed
  14.2 0.0 copy-done
  14.2 0.0 copy-done.1
  14.2 0.0 copy-done.2
  14.2 0.0 copy-done.3
  14.2 0.0 copy-done.4
  14.2 0.0 copy-done.5
  14.2 8.3 %translate.1 = f32[3,16,152]{2,1,0:T(8,128)} custom-call(s32[4,4]{1,0:T(4,128)S(1)} %bitcast.12, s32[16,32]{1,0:T(8,128)S(1)} %copy-done.3, s32[16,32]{1,0:T(8,128)S(1)} %copy-done.4, f32[3,16,152]{2,1,0:T(8,128)S(1)} %bitcast.10, f32[2,3,4,152]{3,2,1,0:T(4,128)S(1)} %collective-permute-done.from_near, f32[2,3,4,152]{3,2,1,0:T(4,128)S(1)} %collective-permute-done.1.relayed, ...), custom_call_target="tpu_custom_call" | custom-call | tf_op jit(solution)/shard_map/translate/pallas_call | solution.py:323
  (2 shorter events, 0.0 us)
Async XLA Ops:
  1.6 4.3 %copy-start.6 = (f32[3,4,152]{2,1,0:T(4,128)S(1)}, f32[3,4,152]{2,1,0:T(4,128)}, u32[]{:S(2)}) copy-start(f32[3,4,152]{2,1,0:T(4,128)} %get-tuple-element.12) | copy-start | bytes 21892
  1.6 5.6 %copy-start.8 = (f32[3,4,152]{2,1,0:T(4,128)S(1)}, f32[3,4,152]{2,1,0:T(4,128)}, u32[]{:S(2)}) copy-start(f32[3,4,152]{2,1,0:T(4,128)} %get-tuple-element.14) | copy-start | bytes 21892
  1.6 7.2 %copy-start.7 = (f32[3,4,152]{2,1,0:T(4,128)S(1)}, f32[3,4,152]{2,1,0:T(4,128)}, u32[]{:S(2)}) copy-start(f32[3,4,152]{2,1,0:T(4,128)} %get-tuple-element.15) | copy-start | bytes 21892
  1.6 4.2 %collective-permute-start = (f32[2,3,4,152]{3,2,1,0:T(4,128)}, f32[2,3,4,152]{3,2,1,0:T(4,128)S(1)}, u32[]{:S(2)}, u32[]{:S(2)}) collective-permute-start(f32[2,3,4,152]{3,2,1,0:T(4,128)} %get-tuple-element.11), channel_id=1, source_target_pairs={{0,1},{1,0},{2,3},{3,2},{4,5},{5,4},{6,7},{7,6},{8,9},{9,8},{10,11... | collective-permute-start | bytes 43784 | tf_op jit(solution)/shard_map/ppermute | solution.py:293
  5.9 8.3 %collective-permute-start.1 = (f32[2,3,4,152]{3,2,1,0:T(4,128)S(1)}, f32[2,3,4,152]{3,2,1,0:T(4,128)S(1)}, u32[]{:S(2)}, u32[]{:S(2)}) collective-permute-start(f32[2,3,4,152]{3,2,1,0:T(4,128)S(1)} %pad_maximum_fusion), channel_id=1, source_target_pairs={{0,2},{1,3},{2,0},{3,1},{4,6},{5,7},{6,4},{7,5},{8,10},{9,11},{10,... | collective-permute-start | bytes 43784 | tf_op jit(solution)/shard_map/ppermute | solution.py:293
  7.2 5.7 %collective-permute-start.2 = (f32[3,4,152]{2,1,0:T(4,128)S(1)}, f32[3,4,152]{2,1,0:T(4,128)S(1)}, u32[]{:S(2)}, u32[]{:S(2)}) collective-permute-start(f32[3,4,152]{2,1,0:T(4,128)S(1)} %copy-done.8), channel_id=1, source_target_pairs={{0,4},{8,12},{16,20},{24,28},{4,0},{12,8},{20,16},{28,24},{1,5},{9... | collective-permute-start | bytes 21896 | tf_op jit(solution)/shard_map/ppermute | solution.py:297
  8.8 5.3 %copy-start = (bf16[320,4608]{1,0:T(8,128)(2,1)S(1)}, bf16[320,4608]{1,0:T(8,128)(2,1)}, u32[]{:S(2)}) copy-start(bf16[320,4608]{1,0:T(8,128)(2,1)} %constant.4.clone.refs_2_) | copy-start | bytes 8847364
  8.8 5.3 %copy-start.1 = (f32[16,3,152]{2,0,1:T(8,128)S(1)}, f32[16,3,152]{2,0,1:T(8,128)}, u32[]{:S(2)}) copy-start(f32[16,3,152]{2,0,1:T(8,128)} %param.8) | copy-start | bytes 87556
  8.8 5.3 %copy-start.2 = (f32[1,4608]{1,0:T(1,128)S(1)}, f32[1,4608]{1,0:T(1,128)}, u32[]{:S(2)}) copy-start(f32[1,4608]{1,0:T(1,128)} %constant.5.clone.refs_3_) | copy-start | bytes 55300
  8.8 5.3 %copy-start.3 = (s32[16,32]{1,0:T(8,128)S(1)}, s32[16,32]{1,0:T(8,128)}, u32[]{:S(2)}) copy-start(s32[16,32]{1,0:T(8,128)} %source.1) | copy-start | bytes 6148
  8.8 5.3 %copy-start.4 = (s32[16,32]{1,0:T(8,128)S(1)}, s32[16,32]{1,0:T(8,128)}, u32[]{:S(2)}) copy-start(s32[16,32]{1,0:T(8,128)} %offset.1) | copy-start | bytes 6148
  8.9 5.3 %copy-start.5 = (s32[1,4,4]{2,1,0:T(4,128)S(1)}, s32[1,4,4]{2,1,0:T(4,128)}, u32[]{:S(2)}) copy-start(s32[1,4,4]{2,1,0:T(4,128)} %param.10) | copy-start | bytes 196
  8.9 5.3 %collective-permute-start.3 = (f32[3,4,152]{2,1,0:T(4,128)S(1)}, f32[3,4,152]{2,1,0:T(4,128)S(1)}, u32[]{:S(2)}, u32[]{:S(2)}) collective-permute-start(f32[3,4,152]{2,1,0:T(4,128)S(1)} %copy-done.7), channel_id=1, source_target_pairs={{4,8},{12,16},{20,24},{8,4},{16,12},{24,20},{5,9},{13,17},{21,25},... | collective-permute-start | bytes 21896 | tf_op jit(solution)/shard_map/ppermute | solution.py:297

commit v21 on v18

--- a/solution.py
+++ b/solution.py
@@ -23,7 +23,7 @@
 HAT_ROWS = 3 * MAIN + 2 * TAIL + 1
 POINTS_PAD = 160
 CHUNK = 256
-PIECE = 2304
+PIECE = 256
 UNROLL = 8
 
 

time: 22.7 us -> 22.7 us (level)
  no operation moved by 1% of the time
where the time goes in v21:
time: 22.7 us; the launch traced here: 22.5 us
  Pallas kernels  10.5 us (46%)
  starting transfers between devices  8.44 us (37%)
  local copies, waits for them, and re-layouts  2.15 us (9%)
  waiting for transfers between devices  1.23 us (5%)
    pallas_call x1, Pallas kernels, on_device(): pl.pallas_call(translate_kernel, out_shape=jax.ShapeDtypeStruct((comp_cou...  8.25 us
    ppermute x2, starting transfers between devices, swap_groups(): return lax.ppermute(x, 'group', pairs + [(j, i) for i, j in pairs])  5.03 us
    ppermute x2, starting transfers between devices, swap(): return lax.ppermute(x, 'dev', [(i, i ^ k) for i in range(peers)])  3.41 us
    unnamed x19, local copies, waits for them, and re-layouts  2.15 us
    pallas_call x1, Pallas kernels, on_device(): pl.pallas_call(pack_kernel, out_shape=(jax.ShapeDtypeStruct((2, *boxes.sh...  1.59 us
    ppermute x2, waiting for transfers between devices, swap_groups(): return lax.ppermute(x, 'group', pairs + [(j, i) for i, j in pairs])  1.23 us
    pallas_call x1, Pallas kernels, on_device(): pl.pallas_call(prepare_kernel, out_shape=jax.ShapeDtypeStruct((offsets *...  0.64 us
  transfers between devices with their start and end apart: 4, of which 1 were waited for; matrix products, arithmetic and copies ran while one was open for 9% of the time, Pallas kernels for 3%

profile of v21, /device:TPU:1, one launch (start us, length us, event | category | flops | bytes accessed | tf_op | source)
XLA Modules:
  0.0 22.5 jit_solution(8953345950969384760)
XLA Ops:
  0.0 1.6 %pack.1 = (f32[2,3,4,152]{3,2,1,0:T(4,128)}, f32[3,4,152]{2,1,0:T(4,128)}, f32[3,4,152]{2,1,0:T(4,128)}, f32[3,4,152]{2,1,0:T(4,128)}) custom-call(f32[3,16,152]{2,1,0:T(8,128)} %bitcast.9, s32[4,4]{1,0:T(4,128)} %bitcast.11, s32[2,4]{1,0:T(2,128)} %bitcast.14), custom_call_target="tpu_custom_call" | custom-call | tf_op jit(solution)/shard_map/pack/pallas_call | solution.py:284
  1.6 0.0 copy-start.6
  1.6 0.0 copy-start.8
  1.6 0.0 copy-start.7
  1.6 2.1 %collective-permute-start = (f32[2,3,4,152]{3,2,1,0:T(4,128)}, f32[2,3,4,152]{3,2,1,0:T(4,128)S(1)}, u32[]{:S(2)}, u32[]{:S(2)}) collective-permute-start(f32[2,3,4,152]{3,2,1,0:T(4,128)} %get-tuple-element.11), channel_id=1, source_target_pairs={{0,1},{1,0},{2,3},{3,2},{4,5},{5,4},{6,7},{7,6},{8,9},{9,8},{10,11... | collective-permute-start | bytes 43784 | tf_op jit(solution)/shard_map/ppermute | solution.py:293
  3.7 2.1 %copy.11 = bf16[316,2,2304]{2,0,1:T(8,128)(2,1)S(1)} copy(bf16[316,2,2304]{2,1,0:T(2,128)(2,1)} %param.9) | data formatting | bytes 5824512 | tf_op args[1]
  5.8 0.0 collective-permute-done.from_near
  5.9 0.0 copy-done.6
  5.9 1.3 %collective-permute-start.1 = (f32[2,3,4,152]{3,2,1,0:T(4,128)S(1)}, f32[2,3,4,152]{3,2,1,0:T(4,128)S(1)}, u32[]{:S(2)}, u32[]{:S(2)}) collective-permute-start(f32[2,3,4,152]{3,2,1,0:T(4,128)S(1)} %pad_maximum_fusion), channel_id=1, source_target_pairs={{0,2},{1,3},{2,0},{3,1},{4,6},{5,7},{6,4},{7,5},{8,10},{9,11},{10,... | collective-permute-start | bytes 43784 | tf_op jit(solution)/shard_map/ppermute | solution.py:293
  7.2 0.0 copy-done.8
  7.2 1.6 %collective-permute-start.2 = (f32[3,4,152]{2,1,0:T(4,128)S(1)}, f32[3,4,152]{2,1,0:T(4,128)S(1)}, u32[]{:S(2)}, u32[]{:S(2)}) collective-permute-start(f32[3,4,152]{2,1,0:T(4,128)S(1)} %copy-done.8), channel_id=1, source_target_pairs={{0,4},{8,12},{16,20},{24,28},{4,0},{12,8},{20,16},{28,24},{1,5},{9... | collective-permute-start | bytes 21896 | tf_op jit(solution)/shard_map/ppermute | solution.py:297
  8.8 0.0 copy-done.7
  8.8 0.0 copy-start
  8.8 0.0 copy-start.1
  8.8 0.0 copy-start.2
  8.8 0.0 copy-start.3
  8.8 0.0 copy-start.4
  8.9 0.0 copy-start.5
  8.9 3.4 %collective-permute-start.3 = (f32[3,4,152]{2,1,0:T(4,128)S(1)}, f32[3,4,152]{2,1,0:T(4,128)S(1)}, u32[]{:S(2)}, u32[]{:S(2)}) collective-permute-start(f32[3,4,152]{2,1,0:T(4,128)S(1)} %copy-done.7), channel_id=1, source_target_pairs={{4,8},{12,16},{20,24},{8,4},{16,12},{24,20},{5,9},{13,17},{21,25},... | collective-permute-start | bytes 21896 | tf_op jit(solution)/shard_map/ppermute | solution.py:297
  12.3 0.6 %prepare.1.refs_4_ = f32[16756,128]{1,0:T(8,128)S(1)} custom-call(bf16[2,316,2304]{2,1,0:T(8,128)(2,1)S(1)} %bitcast.8), custom_call_target="tpu_custom_call" | custom-call | flops 1456128 | bytes 8736768 | tf_op jit(solution)/shard_map/prepare/pallas_call | solution.py:307
  12.9 0.0 collective-permute-done.2.refs_0_
  12.9 1.2 %collective-permute-done.3.refs_1_ = f32[3,4,152]{2,1,0:T(4,128)S(1)} collective-permute-done((f32[3,4,152]{2,1,0:T(4,128)S(1)}, f32[3,4,152]{2,1,0:T(4,128)S(1)}, u32[]{:S(2)}, u32[]{:S(2)}) %collective-permute-start.3) | collective-permute-done | bytes 7328 | tf_op jit(solution)/shard_map/ppermute | solution.py:297
  14.2 0.0 collective-permute-done.1.relayed
  14.2 0.0 copy-done
  14.2 0.0 copy-done.1
  14.2 0.0 copy-done.2
  14.2 0.0 copy-done.3
  14.2 0.0 copy-done.4
  14.2 0.0 copy-done.5
  14.2 8.3 %translate.1 = f32[3,16,152]{2,1,0:T(8,128)} custom-call(s32[4,4]{1,0:T(4,128)S(1)} %bitcast.12, s32[16,32]{1,0:T(8,128)S(1)} %copy-done.3, s32[16,32]{1,0:T(8,128)S(1)} %copy-done.4, f32[3,16,152]{2,1,0:T(8,128)S(1)} %bitcast.10, f32[2,3,4,152]{3,2,1,0:T(4,128)S(1)} %collective-permute-done.from_near, f32[2,3,4,152]{3,2,1,0:T(4,128)S(1)} %collective-permute-done.1.relayed, ...), custom_call_target="tpu_custom_call" | custom-call | tf_op jit(solution)/shard_map/translate/pallas_call | solution.py:323
  (2 shorter events, 0.0 us)
Async XLA Ops:
  1.6 4.3 %copy-start.6 = (f32[3,4,152]{2,1,0:T(4,128)S(1)}, f32[3,4,152]{2,1,0:T(4,128)}, u32[]{:S(2)}) copy-start(f32[3,4,152]{2,1,0:T(4,128)} %get-tuple-element.12) | copy-start | bytes 21892
  1.6 5.6 %copy-start.8 = (f32[3,4,152]{2,1,0:T(4,128)S(1)}, f32[3,4,152]{2,1,0:T(4,128)}, u32[]{:S(2)}) copy-start(f32[3,4,152]{2,1,0:T(4,128)} %get-tuple-element.14) | copy-start | bytes 21892
  1.6 7.2 %copy-start.7 = (f32[3,4,152]{2,1,0:T(4,128)S(1)}, f32[3,4,152]{2,1,0:T(4,128)}, u32[]{:S(2)}) copy-start(f32[3,4,152]{2,1,0:T(4,128)} %get-tuple-element.15) | copy-start | bytes 21892
  1.6 4.2 %collective-permute-start = (f32[2,3,4,152]{3,2,1,0:T(4,128)}, f32[2,3,4,152]{3,2,1,0:T(4,128)S(1)}, u32[]{:S(2)}, u32[]{:S(2)}) collective-permute-start(f32[2,3,4,152]{3,2,1,0:T(4,128)} %get-tuple-element.11), channel_id=1, source_target_pairs={{0,1},{1,0},{2,3},{3,2},{4,5},{5,4},{6,7},{7,6},{8,9},{9,8},{10,11... | collective-permute-start | bytes 43784 | tf_op jit(solution)/shard_map/ppermute | solution.py:293
  5.9 8.3 %collective-permute-start.1 = (f32[2,3,4,152]{3,2,1,0:T(4,128)S(1)}, f32[2,3,4,152]{3,2,1,0:T(4,128)S(1)}, u32[]{:S(2)}, u32[]{:S(2)}) collective-permute-start(f32[2,3,4,152]{3,2,1,0:T(4,128)S(1)} %pad_maximum_fusion), channel_id=1, source_target_pairs={{0,2},{1,3},{2,0},{3,1},{4,6},{5,7},{6,4},{7,5},{8,10},{9,11},{10,... | collective-permute-start | bytes 43784 | tf_op jit(solution)/shard_map/ppermute | solution.py:293
  7.2 5.7 %collective-permute-start.2 = (f32[3,4,152]{2,1,0:T(4,128)S(1)}, f32[3,4,152]{2,1,0:T(4,128)S(1)}, u32[]{:S(2)}, u32[]{:S(2)}) collective-permute-start(f32[3,4,152]{2,1,0:T(4,128)S(1)} %copy-done.8), channel_id=1, source_target_pairs={{0,4},{8,12},{16,20},{24,28},{4,0},{12,8},{20,16},{28,24},{1,5},{9... | collective-permute-start | bytes 21896 | tf_op jit(solution)/shard_map/ppermute | solution.py:297
  8.8 5.3 %copy-start = (bf16[320,4608]{1,0:T(8,128)(2,1)S(1)}, bf16[320,4608]{1,0:T(8,128)(2,1)}, u32[]{:S(2)}) copy-start(bf16[320,4608]{1,0:T(8,128)(2,1)} %constant.4.clone.refs_2_) | copy-start | bytes 8847364
  8.8 5.3 %copy-start.1 = (f32[16,3,152]{2,0,1:T(8,128)S(1)}, f32[16,3,152]{2,0,1:T(8,128)}, u32[]{:S(2)}) copy-start(f32[16,3,152]{2,0,1:T(8,128)} %param.8) | copy-start | bytes 87556
  8.8 5.3 %copy-start.2 = (f32[1,4608]{1,0:T(1,128)S(1)}, f32[1,4608]{1,0:T(1,128)}, u32[]{:S(2)}) copy-start(f32[1,4608]{1,0:T(1,128)} %constant.5.clone.refs_3_) | copy-start | bytes 55300
  8.8 5.3 %copy-start.3 = (s32[16,32]{1,0:T(8,128)S(1)}, s32[16,32]{1,0:T(8,128)}, u32[]{:S(2)}) copy-start(s32[16,32]{1,0:T(8,128)} %source.1) | copy-start | bytes 6148
  8.8 5.3 %copy-start.4 = (s32[16,32]{1,0:T(8,128)S(1)}, s32[16,32]{1,0:T(8,128)}, u32[]{:S(2)}) copy-start(s32[16,32]{1,0:T(8,128)} %offset.1) | copy-start | bytes 6148
  8.9 5.3 %copy-start.5 = (s32[1,4,4]{2,1,0:T(4,128)S(1)}, s32[1,4,4]{2,1,0:T(4,128)}, u32[]{:S(2)}) copy-start(s32[1,4,4]{2,1,0:T(4,128)} %param.10) | copy-start | bytes 196
  8.9 5.3 %collective-permute-start.3 = (f32[3,4,152]{2,1,0:T(4,128)S(1)}, f32[3,4,152]{2,1,0:T(4,128)S(1)}, u32[]{:S(2)}, u32[]{:S(2)}) collective-permute-start(f32[3,4,152]{2,1,0:T(4,128)S(1)} %copy-done.7), channel_id=1, source_target_pairs={{4,8},{12,16},{20,24},{8,4},{16,12},{24,20},{5,9},{13,17},{21,25},... | collective-permute-start | bytes 21896 | tf_op jit(solution)/shard_map/ppermute | solution.py:297

commit v22 on v17

--- a/solution.py
+++ b/solution.py
@@ -309,7 +309,7 @@
         out_shape=jax.ShapeDtypeStruct((offsets * HAT_ROWS + 8, LANES), f32),
         in_specs=[vmem],
         out_specs=vmem,
-        compiler_params=pltpu.CompilerParams(vmem_limit_bytes=16 * 1024 * 1024),
+        compiler_params=pltpu.CompilerParams(vmem_limit_bytes=13 * 1024 * 1024),
         cost_estimate=pl.CostEstimate(flops=kernel_hat.size, bytes_accessed=6 * kernel_hat.size, transcendentals=0),
         name="prepare",
     )(by_part)
@@ -331,7 +331,7 @@
             pltpu.VMEM((2 * comp_count * box_count * PITCH, LANES), f32),
             pltpu.VMEM((TAIL, (box_count + 2) * TAIL_PITCH, LANES), f32),
         ],
-        compiler_params=pltpu.CompilerParams(vmem_limit_bytes=24 * 1024 * 1024),
+        compiler_params=pltpu.CompilerParams(vmem_limit_bytes=14 * 1024 * 1024),
         name="translate",
     )(*arrays)
     return potential.transpose(1, 0, 2)

time: 22.7 us -> 22.6 us (level)
  no operation moved by 1% of the time
where the time goes in v22:
time: 22.6 us; the launch traced here: 22.4 us
  Pallas kernels  10.4 us (46%)
  starting transfers between devices  8.44 us (37%)
  local copies, waits for them, and re-layouts  2.15 us (10%)
  waiting for transfers between devices  1.23 us (5%)
    pallas_call x1, Pallas kernels, on_device(): pl.pallas_call(translate_kernel, out_shape=jax.ShapeDtypeStruct((comp_cou...  8.21 us
    ppermute x2, starting transfers between devices, swap_groups(): return lax.ppermute(x, 'group', pairs + [(j, i) for i, j in pairs])  5.03 us
    ppermute x2, starting transfers between devices, swap(): return lax.ppermute(x, 'dev', [(i, i ^ k) for i in range(peers)])  3.41 us
    unnamed x19, local copies, waits for them, and re-layouts  2.15 us
    pallas_call x1, Pallas kernels, on_device(): pl.pallas_call(pack_kernel, out_shape=(jax.ShapeDtypeStruct((2, *boxes.sh...  1.59 us
    ppermute x2, waiting for transfers between devices, swap_groups(): return lax.ppermute(x, 'group', pairs + [(j, i) for i, j in pairs])  1.23 us
    pallas_call x1, Pallas kernels, on_device(): pl.pallas_call(prepare_kernel, out_shape=jax.ShapeDtypeStruct((offsets *...  0.64 us
  transfers between devices with their start and end apart: 4, of which 1 were waited for; matrix products, arithmetic and copies ran while one was open for 9% of the time, Pallas kernels for 3%

profile of v22, /device:TPU:1, one launch (start us, length us, event | category | flops | bytes accessed | tf_op | source)
XLA Modules:
  0.0 22.4 jit_solution(5417111799672692445)
XLA Ops:
  0.0 1.6 %pack.1 = (f32[2,3,4,152]{3,2,1,0:T(4,128)}, f32[3,4,152]{2,1,0:T(4,128)}, f32[3,4,152]{2,1,0:T(4,128)}, f32[3,4,152]{2,1,0:T(4,128)}) custom-call(f32[3,16,152]{2,1,0:T(8,128)} %bitcast.9, s32[4,4]{1,0:T(4,128)} %bitcast.11, s32[2,4]{1,0:T(2,128)} %bitcast.14), custom_call_target="tpu_custom_call" | custom-call | tf_op jit(solution)/shard_map/pack/pallas_call | solution.py:284
  1.6 0.0 copy-start.6
  1.6 0.0 copy-start.8
  1.6 0.0 copy-start.7
  1.6 2.1 %collective-permute-start = (f32[2,3,4,152]{3,2,1,0:T(4,128)}, f32[2,3,4,152]{3,2,1,0:T(4,128)S(1)}, u32[]{:S(2)}, u32[]{:S(2)}) collective-permute-start(f32[2,3,4,152]{3,2,1,0:T(4,128)} %get-tuple-element.11), channel_id=1, source_target_pairs={{0,1},{1,0},{2,3},{3,2},{4,5},{5,4},{6,7},{7,6},{8,9},{9,8},{10,11... | collective-permute-start | bytes 43784 | tf_op jit(solution)/shard_map/ppermute | solution.py:293
  3.7 2.1 %copy.11 = bf16[316,2,2304]{2,0,1:T(8,128)(2,1)S(1)} copy(bf16[316,2,2304]{2,1,0:T(2,128)(2,1)} %param.9) | data formatting | bytes 5824512 | tf_op args[1]
  5.8 0.0 collective-permute-done.from_near
  5.9 0.0 copy-done.6
  5.9 1.3 %collective-permute-start.1 = (f32[2,3,4,152]{3,2,1,0:T(4,128)S(1)}, f32[2,3,4,152]{3,2,1,0:T(4,128)S(1)}, u32[]{:S(2)}, u32[]{:S(2)}) collective-permute-start(f32[2,3,4,152]{3,2,1,0:T(4,128)S(1)} %pad_maximum_fusion), channel_id=1, source_target_pairs={{0,2},{1,3},{2,0},{3,1},{4,6},{5,7},{6,4},{7,5},{8,10},{9,11},{10,... | collective-permute-start | bytes 43784 | tf_op jit(solution)/shard_map/ppermute | solution.py:293
  7.2 0.0 copy-done.8
  7.2 1.6 %collective-permute-start.2 = (f32[3,4,152]{2,1,0:T(4,128)S(1)}, f32[3,4,152]{2,1,0:T(4,128)S(1)}, u32[]{:S(2)}, u32[]{:S(2)}) collective-permute-start(f32[3,4,152]{2,1,0:T(4,128)S(1)} %copy-done.8), channel_id=1, source_target_pairs={{0,4},{8,12},{16,20},{24,28},{4,0},{12,8},{20,16},{28,24},{1,5},{9... | collective-permute-start | bytes 21896 | tf_op jit(solution)/shard_map/ppermute | solution.py:297
  8.8 0.0 copy-done.7
  8.8 0.0 copy-start
  8.8 0.0 copy-start.1
  8.8 0.0 copy-start.2
  8.8 0.0 copy-start.3
  8.8 0.0 copy-start.4
  8.9 0.0 copy-start.5
  8.9 3.4 %collective-permute-start.3 = (f32[3,4,152]{2,1,0:T(4,128)S(1)}, f32[3,4,152]{2,1,0:T(4,128)S(1)}, u32[]{:S(2)}, u32[]{:S(2)}) collective-permute-start(f32[3,4,152]{2,1,0:T(4,128)S(1)} %copy-done.7), channel_id=1, source_target_pairs={{4,8},{12,16},{20,24},{8,4},{16,12},{24,20},{5,9},{13,17},{21,25},... | collective-permute-start | bytes 21896 | tf_op jit(solution)/shard_map/ppermute | solution.py:297
  12.3 0.6 %prepare.1.refs_4_ = f32[16756,128]{1,0:T(8,128)S(1)} custom-call(bf16[2,316,2304]{2,1,0:T(8,128)(2,1)S(1)} %bitcast.8), custom_call_target="tpu_custom_call" | custom-call | flops 1456128 | bytes 8736768 | tf_op jit(solution)/shard_map/prepare/pallas_call | solution.py:307
  12.9 0.0 collective-permute-done.2.refs_0_
  12.9 1.2 %collective-permute-done.3.refs_1_ = f32[3,4,152]{2,1,0:T(4,128)S(1)} collective-permute-done((f32[3,4,152]{2,1,0:T(4,128)S(1)}, f32[3,4,152]{2,1,0:T(4,128)S(1)}, u32[]{:S(2)}, u32[]{:S(2)}) %collective-permute-start.3) | collective-permute-done | bytes 7328 | tf_op jit(solution)/shard_map/ppermute | solution.py:297
  14.2 0.0 collective-permute-done.1.relayed
  14.2 0.0 copy-done
  14.2 0.0 copy-done.1
  14.2 0.0 copy-done.2
  14.2 0.0 copy-done.3
  14.2 0.0 copy-done.4
  14.2 0.0 copy-done.5
  14.2 8.2 %translate.1 = f32[3,16,152]{2,1,0:T(8,128)} custom-call(s32[4,4]{1,0:T(4,128)S(1)} %bitcast.12, s32[16,32]{1,0:T(8,128)S(1)} %copy-done.3, s32[16,32]{1,0:T(8,128)S(1)} %copy-done.4, f32[3,16,152]{2,1,0:T(8,128)S(1)} %bitcast.10, f32[2,3,4,152]{3,2,1,0:T(4,128)S(1)} %collective-permute-done.from_near, f32[2,3,4,152]{3,2,1,0:T(4,128)S(1)} %collective-permute-done.1.relayed, ...), custom_call_target="tpu_custom_call" | custom-call | tf_op jit(solution)/shard_map/translate/pallas_call | solution.py:323
  (2 shorter events, 0.0 us)
Async XLA Ops:
  1.6 4.3 %copy-start.6 = (f32[3,4,152]{2,1,0:T(4,128)S(1)}, f32[3,4,152]{2,1,0:T(4,128)}, u32[]{:S(2)}) copy-start(f32[3,4,152]{2,1,0:T(4,128)} %get-tuple-element.12) | copy-start | bytes 21892
  1.6 5.6 %copy-start.8 = (f32[3,4,152]{2,1,0:T(4,128)S(1)}, f32[3,4,152]{2,1,0:T(4,128)}, u32[]{:S(2)}) copy-start(f32[3,4,152]{2,1,0:T(4,128)} %get-tuple-element.14) | copy-start | bytes 21892
  1.6 7.2 %copy-start.7 = (f32[3,4,152]{2,1,0:T(4,128)S(1)}, f32[3,4,152]{2,1,0:T(4,128)}, u32[]{:S(2)}) copy-start(f32[3,4,152]{2,1,0:T(4,128)} %get-tuple-element.15) | copy-start | bytes 21892
  1.6 4.2 %collective-permute-start = (f32[2,3,4,152]{3,2,1,0:T(4,128)}, f32[2,3,4,152]{3,2,1,0:T(4,128)S(1)}, u32[]{:S(2)}, u32[]{:S(2)}) collective-permute-start(f32[2,3,4,152]{3,2,1,0:T(4,128)} %get-tuple-element.11), channel_id=1, source_target_pairs={{0,1},{1,0},{2,3},{3,2},{4,5},{5,4},{6,7},{7,6},{8,9},{9,8},{10,11... | collective-permute-start | bytes 43784 | tf_op jit(solution)/shard_map/ppermute | solution.py:293
  5.9 8.3 %collective-permute-start.1 = (f32[2,3,4,152]{3,2,1,0:T(4,128)S(1)}, f32[2,3,4,152]{3,2,1,0:T(4,128)S(1)}, u32[]{:S(2)}, u32[]{:S(2)}) collective-permute-start(f32[2,3,4,152]{3,2,1,0:T(4,128)S(1)} %pad_maximum_fusion), channel_id=1, source_target_pairs={{0,2},{1,3},{2,0},{3,1},{4,6},{5,7},{6,4},{7,5},{8,10},{9,11},{10,... | collective-permute-start | bytes 43784 | tf_op jit(solution)/shard_map/ppermute | solution.py:293
  7.2 5.7 %collective-permute-start.2 = (f32[3,4,152]{2,1,0:T(4,128)S(1)}, f32[3,4,152]{2,1,0:T(4,128)S(1)}, u32[]{:S(2)}, u32[]{:S(2)}) collective-permute-start(f32[3,4,152]{2,1,0:T(4,128)S(1)} %copy-done.8), channel_id=1, source_target_pairs={{0,4},{8,12},{16,20},{24,28},{4,0},{12,8},{20,16},{28,24},{1,5},{9... | collective-permute-start | bytes 21896 | tf_op jit(solution)/shard_map/ppermute | solution.py:297
  8.8 5.3 %copy-start = (bf16[320,4608]{1,0:T(8,128)(2,1)S(1)}, bf16[320,4608]{1,0:T(8,128)(2,1)}, u32[]{:S(2)}) copy-start(bf16[320,4608]{1,0:T(8,128)(2,1)} %constant.4.clone.refs_2_) | copy-start | bytes 8847364
  8.8 5.3 %copy-start.1 = (f32[16,3,152]{2,0,1:T(8,128)S(1)}, f32[16,3,152]{2,0,1:T(8,128)}, u32[]{:S(2)}) copy-start(f32[16,3,152]{2,0,1:T(8,128)} %param.8) | copy-start | bytes 87556
  8.8 5.3 %copy-start.2 = (f32[1,4608]{1,0:T(1,128)S(1)}, f32[1,4608]{1,0:T(1,128)}, u32[]{:S(2)}) copy-start(f32[1,4608]{1,0:T(1,128)} %constant.5.clone.refs_3_) | copy-start | bytes 55300
  8.8 5.3 %copy-start.3 = (s32[16,32]{1,0:T(8,128)S(1)}, s32[16,32]{1,0:T(8,128)}, u32[]{:S(2)}) copy-start(s32[16,32]{1,0:T(8,128)} %source.1) | copy-start | bytes 6148
  8.8 5.3 %copy-start.4 = (s32[16,32]{1,0:T(8,128)S(1)}, s32[16,32]{1,0:T(8,128)}, u32[]{:S(2)}) copy-start(s32[16,32]{1,0:T(8,128)} %offset.1) | copy-start | bytes 6148
  8.9 5.3 %copy-start.5 = (s32[1,4,4]{2,1,0:T(4,128)S(1)}, s32[1,4,4]{2,1,0:T(4,128)}, u32[]{:S(2)}) copy-start(s32[1,4,4]{2,1,0:T(4,128)} %param.10) | copy-start | bytes 196
  8.9 5.3 %collective-permute-start.3 = (f32[3,4,152]{2,1,0:T(4,128)S(1)}, f32[3,4,152]{2,1,0:T(4,128)S(1)}, u32[]{:S(2)}, u32[]{:S(2)}) collective-permute-start(f32[3,4,152]{2,1,0:T(4,128)S(1)} %copy-done.7), channel_id=1, source_target_pairs={{4,8},{12,16},{20,24},{8,4},{16,12},{24,20},{5,9},{13,17},{21,25},... | collective-permute-start | bytes 21896 | tf_op jit(solution)/shard_map/ppermute | solution.py:297

commit v23 on v17

--- a/solution.py
+++ b/solution.py
@@ -22,7 +22,7 @@
 TAIL_PITCH = 7
 HAT_ROWS = 3 * MAIN + 2 * TAIL + 1
 POINTS_PAD = 160
-CHUNK = 256
+CHUNK = 128
 PIECE = 512
 UNROLL = 8
 

time: 22.7 us -> 23.6 us (1.040)
  Pallas kernels: 10.5 us -> 11.4 us
    pallas_call x1, Pallas kernels: 8.29 us -> 9.14 us  [on_device(): pl.pallas_call(translate_kernel, out_shape=jax.ShapeDtypeStruct((comp_cou...]
where the time goes in v23:
time: 23.6 us; the launch traced here: 23.3 us
  Pallas kernels  11.4 us (48%)
  starting transfers between devices  8.44 us (36%)
  local copies, waits for them, and re-layouts  2.15 us (9%)
  waiting for transfers between devices  1.23 us (5%)
    pallas_call x1, Pallas kernels, on_device(): pl.pallas_call(translate_kernel, out_shape=jax.ShapeDtypeStruct((comp_cou...  9.14 us
    ppermute x2, starting transfers between devices, swap_groups(): return lax.ppermute(x, 'group', pairs + [(j, i) for i, j in pairs])  5.03 us
    ppermute x2, starting transfers between devices, swap(): return lax.ppermute(x, 'dev', [(i, i ^ k) for i in range(peers)])  3.41 us
    unnamed x19, local copies, waits for them, and re-layouts  2.15 us
    pallas_call x1, Pallas kernels, on_device(): pl.pallas_call(pack_kernel, out_shape=(jax.ShapeDtypeStruct((2, *boxes.sh...  1.59 us
    ppermute x2, waiting for transfers between devices, swap_groups(): return lax.ppermute(x, 'group', pairs + [(j, i) for i, j in pairs])  1.23 us
    pallas_call x1, Pallas kernels, on_device(): pl.pallas_call(prepare_kernel, out_shape=jax.ShapeDtypeStruct((offsets *...  0.64 us
  transfers between devices with their start and end apart: 4, of which 1 were waited for; matrix products, arithmetic and copies ran while one was open for 9% of the time, Pallas kernels for 3%

profile of v23, /device:TPU:1, one launch (start us, length us, event | category | flops | bytes accessed | tf_op | source)
XLA Modules:
  0.0 23.3 jit_solution(10144821082957066758)
XLA Ops:
  0.0 1.6 %pack.1 = (f32[2,3,4,152]{3,2,1,0:T(4,128)}, f32[3,4,152]{2,1,0:T(4,128)}, f32[3,4,152]{2,1,0:T(4,128)}, f32[3,4,152]{2,1,0:T(4,128)}) custom-call(f32[3,16,152]{2,1,0:T(8,128)} %bitcast.9, s32[4,4]{1,0:T(4,128)} %bitcast.11, s32[2,4]{1,0:T(2,128)} %bitcast.14), custom_call_target="tpu_custom_call" | custom-call | tf_op jit(solution)/shard_map/pack/pallas_call | solution.py:284
  1.6 0.0 copy-start.6
  1.6 0.0 copy-start.8
  1.6 0.0 copy-start.7
  1.6 2.1 %collective-permute-start = (f32[2,3,4,152]{3,2,1,0:T(4,128)}, f32[2,3,4,152]{3,2,1,0:T(4,128)S(1)}, u32[]{:S(2)}, u32[]{:S(2)}) collective-permute-start(f32[2,3,4,152]{3,2,1,0:T(4,128)} %get-tuple-element.11), channel_id=1, source_target_pairs={{0,1},{1,0},{2,3},{3,2},{4,5},{5,4},{6,7},{7,6},{8,9},{9,8},{10,11... | collective-permute-start | bytes 43784 | tf_op jit(solution)/shard_map/ppermute | solution.py:293
  3.7 2.1 %copy.11 = bf16[316,2,2304]{2,0,1:T(8,128)(2,1)S(1)} copy(bf16[316,2,2304]{2,1,0:T(2,128)(2,1)} %param.9) | data formatting | bytes 5824512 | tf_op args[1]
  5.8 0.0 collective-permute-done.from_near
  5.9 0.0 copy-done.6
  5.9 1.3 %collective-permute-start.1 = (f32[2,3,4,152]{3,2,1,0:T(4,128)S(1)}, f32[2,3,4,152]{3,2,1,0:T(4,128)S(1)}, u32[]{:S(2)}, u32[]{:S(2)}) collective-permute-start(f32[2,3,4,152]{3,2,1,0:T(4,128)S(1)} %pad_maximum_fusion), channel_id=1, source_target_pairs={{0,2},{1,3},{2,0},{3,1},{4,6},{5,7},{6,4},{7,5},{8,10},{9,11},{10,... | collective-permute-start | bytes 43784 | tf_op jit(solution)/shard_map/ppermute | solution.py:293
  7.2 0.0 copy-done.8
  7.2 1.6 %collective-permute-start.2 = (f32[3,4,152]{2,1,0:T(4,128)S(1)}, f32[3,4,152]{2,1,0:T(4,128)S(1)}, u32[]{:S(2)}, u32[]{:S(2)}) collective-permute-start(f32[3,4,152]{2,1,0:T(4,128)S(1)} %copy-done.8), channel_id=1, source_target_pairs={{0,4},{8,12},{16,20},{24,28},{4,0},{12,8},{20,16},{28,24},{1,5},{9... | collective-permute-start | bytes 21896 | tf_op jit(solution)/shard_map/ppermute | solution.py:297
  8.8 0.0 copy-done.7
  8.8 0.0 copy-start
  8.8 0.0 copy-start.1
  8.8 0.0 copy-start.2
  8.8 0.0 copy-start.3
  8.8 0.0 copy-start.4
  8.9 0.0 copy-start.5
  8.9 3.4 %collective-permute-start.3 = (f32[3,4,152]{2,1,0:T(4,128)S(1)}, f32[3,4,152]{2,1,0:T(4,128)S(1)}, u32[]{:S(2)}, u32[]{:S(2)}) collective-permute-start(f32[3,4,152]{2,1,0:T(4,128)S(1)} %copy-done.7), channel_id=1, source_target_pairs={{4,8},{12,16},{20,24},{8,4},{16,12},{24,20},{5,9},{13,17},{21,25},... | collective-permute-start | bytes 21896 | tf_op jit(solution)/shard_map/ppermute | solution.py:297
  12.3 0.6 %prepare.1.refs_4_ = f32[16756,128]{1,0:T(8,128)S(1)} custom-call(bf16[2,316,2304]{2,1,0:T(8,128)(2,1)S(1)} %bitcast.8), custom_call_target="tpu_custom_call" | custom-call | flops 1456128 | bytes 8736768 | tf_op jit(solution)/shard_map/prepare/pallas_call | solution.py:307
  12.9 0.0 collective-permute-done.2.refs_0_
  12.9 1.2 %collective-permute-done.3.refs_1_ = f32[3,4,152]{2,1,0:T(4,128)S(1)} collective-permute-done((f32[3,4,152]{2,1,0:T(4,128)S(1)}, f32[3,4,152]{2,1,0:T(4,128)S(1)}, u32[]{:S(2)}, u32[]{:S(2)}) %collective-permute-start.3) | collective-permute-done | bytes 7328 | tf_op jit(solution)/shard_map/ppermute | solution.py:297
  14.2 0.0 collective-permute-done.1.relayed
  14.2 0.0 copy-done
  14.2 0.0 copy-done.1
  14.2 0.0 copy-done.2
  14.2 0.0 copy-done.3
  14.2 0.0 copy-done.4
  14.2 0.0 copy-done.5
  14.2 9.1 %translate.1 = f32[3,16,152]{2,1,0:T(8,128)} custom-call(s32[4,4]{1,0:T(4,128)S(1)} %bitcast.12, s32[16,32]{1,0:T(8,128)S(1)} %copy-done.3, s32[16,32]{1,0:T(8,128)S(1)} %copy-done.4, f32[3,16,152]{2,1,0:T(8,128)S(1)} %bitcast.10, f32[2,3,4,152]{3,2,1,0:T(4,128)S(1)} %collective-permute-done.from_near, f32[2,3,4,152]{3,2,1,0:T(4,128)S(1)} %collective-permute-done.1.relayed, ...), custom_call_target="tpu_custom_call" | custom-call | tf_op jit(solution)/shard_map/translate/pallas_call | solution.py:323
  (2 shorter events, 0.0 us)
Async XLA Ops:
  1.6 4.3 %copy-start.6 = (f32[3,4,152]{2,1,0:T(4,128)S(1)}, f32[3,4,152]{2,1,0:T(4,128)}, u32[]{:S(2)}) copy-start(f32[3,4,152]{2,1,0:T(4,128)} %get-tuple-element.12) | copy-start | bytes 21892
  1.6 5.6 %copy-start.8 = (f32[3,4,152]{2,1,0:T(4,128)S(1)}, f32[3,4,152]{2,1,0:T(4,128)}, u32[]{:S(2)}) copy-start(f32[3,4,152]{2,1,0:T(4,128)} %get-tuple-element.14) | copy-start | bytes 21892
  1.6 7.2 %copy-start.7 = (f32[3,4,152]{2,1,0:T(4,128)S(1)}, f32[3,4,152]{2,1,0:T(4,128)}, u32[]{:S(2)}) copy-start(f32[3,4,152]{2,1,0:T(4,128)} %get-tuple-element.15) | copy-start | bytes 21892
  1.6 4.2 %collective-permute-start = (f32[2,3,4,152]{3,2,1,0:T(4,128)}, f32[2,3,4,152]{3,2,1,0:T(4,128)S(1)}, u32[]{:S(2)}, u32[]{:S(2)}) collective-permute-start(f32[2,3,4,152]{3,2,1,0:T(4,128)} %get-tuple-element.11), channel_id=1, source_target_pairs={{0,1},{1,0},{2,3},{3,2},{4,5},{5,4},{6,7},{7,6},{8,9},{9,8},{10,11... | collective-permute-start | bytes 43784 | tf_op jit(solution)/shard_map/ppermute | solution.py:293
  5.9 8.3 %collective-permute-start.1 = (f32[2,3,4,152]{3,2,1,0:T(4,128)S(1)}, f32[2,3,4,152]{3,2,1,0:T(4,128)S(1)}, u32[]{:S(2)}, u32[]{:S(2)}) collective-permute-start(f32[2,3,4,152]{3,2,1,0:T(4,128)S(1)} %pad_maximum_fusion), channel_id=1, source_target_pairs={{0,2},{1,3},{2,0},{3,1},{4,6},{5,7},{6,4},{7,5},{8,10},{9,11},{10,... | collective-permute-start | bytes 43784 | tf_op jit(solution)/shard_map/ppermute | solution.py:293
  7.2 5.7 %collective-permute-start.2 = (f32[3,4,152]{2,1,0:T(4,128)S(1)}, f32[3,4,152]{2,1,0:T(4,128)S(1)}, u32[]{:S(2)}, u32[]{:S(2)}) collective-permute-start(f32[3,4,152]{2,1,0:T(4,128)S(1)} %copy-done.8), channel_id=1, source_target_pairs={{0,4},{8,12},{16,20},{24,28},{4,0},{12,8},{20,16},{28,24},{1,5},{9... | collective-permute-start | bytes 21896 | tf_op jit(solution)/shard_map/ppermute | solution.py:297
  8.8 5.3 %copy-start = (bf16[320,4608]{1,0:T(8,128)(2,1)S(1)}, bf16[320,4608]{1,0:T(8,128)(2,1)}, u32[]{:S(2)}) copy-start(bf16[320,4608]{1,0:T(8,128)(2,1)} %constant.4.clone.refs_2_) | copy-start | bytes 8847364
  8.8 5.3 %copy-start.1 = (f32[16,3,152]{2,0,1:T(8,128)S(1)}, f32[16,3,152]{2,0,1:T(8,128)}, u32[]{:S(2)}) copy-start(f32[16,3,152]{2,0,1:T(8,128)} %param.8) | copy-start | bytes 87556
  8.8 5.3 %copy-start.2 = (f32[1,4608]{1,0:T(1,128)S(1)}, f32[1,4608]{1,0:T(1,128)}, u32[]{:S(2)}) copy-start(f32[1,4608]{1,0:T(1,128)} %constant.5.clone.refs_3_) | copy-start | bytes 55300
  8.8 5.3 %copy-start.3 = (s32[16,32]{1,0:T(8,128)S(1)}, s32[16,32]{1,0:T(8,128)}, u32[]{:S(2)}) copy-start(s32[16,32]{1,0:T(8,128)} %source.1) | copy-start | bytes 6148
  8.8 5.3 %copy-start.4 = (s32[16,32]{1,0:T(8,128)S(1)}, s32[16,32]{1,0:T(8,128)}, u32[]{:S(2)}) copy-start(s32[16,32]{1,0:T(8,128)} %offset.1) | copy-start | bytes 6148
  8.9 5.3 %copy-start.5 = (s32[1,4,4]{2,1,0:T(4,128)S(1)}, s32[1,4,4]{2,1,0:T(4,128)}, u32[]{:S(2)}) copy-start(s32[1,4,4]{2,1,0:T(4,128)} %param.10) | copy-start | bytes 196
  8.9 5.3 %collective-permute-start.3 = (f32[3,4,152]{2,1,0:T(4,128)S(1)}, f32[3,4,152]{2,1,0:T(4,128)S(1)}, u32[]{:S(2)}, u32[]{:S(2)}) collective-permute-start(f32[3,4,152]{2,1,0:T(4,128)S(1)} %copy-done.7), channel_id=1, source_target_pairs={{4,8},{12,16},{20,24},{8,4},{16,12},{24,20},{5,9},{13,17},{21,25},... | collective-permute-start | bytes 21896 | tf_op jit(solution)/shard_map/ppermute | solution.py:297
